TPU v7x, 128 devices: a whole 4x4x4 slice. The times are simulated.
128 devices in a mesh: morton: 32 (over y, x, core), chan: 4 (over z).
Axes of the slice: x: 4, y: 4, z: 4, core: 2. Of those that a mesh axis runs over, the one named last changes fastest.
Arguments:
- features: bfloat16 [256, 65536], P('chan', 'morton'), may hold values from -6 to 6
- conv_weight: bfloat16 [27, 256, 256], P(None, 'chan'), may hold values from -0.078125 to 0.078125
- coarse_weight: bfloat16 [256, 256], P('chan'), may hold values from -0.375 to 0.375
- out_grad: bfloat16 [256, 65536], P('chan', 'morton'), may hold values from -6 to 6
- send_block: int32 [32, 32], P('morton'), may hold values from 0 to 15
- send_count: int32 [32, 32], P('morton'), may hold values from 0 to 1, as said below
- neighbour: int32 [27, 512], P(None, 'morton'), may hold values from -1 to 47, as said below
Outputs:
- output: bfloat16 [256, 65536], P('chan', 'morton')
- input_grad: float32 [256, 65536], P('chan', 'morton')
- conv_grad: float32 [27, 256, 256], P(None, 'chan')
- coarse_grad: float32 [256, 256], P('chan')
Inputs may be any that keep to these rules, and one draw needn't show every extreme that they name: send_count[s, d] is 0 where d = s, 1 where d = s - 1 or s + 1, else 0 or 1. neighbour[13, g] = g % 16 (the block itself). A value 16 + s in a column of owner m appears only where send_count[s, m] = 1, and every such pair (s, m) appears in some column of owner m.
All inputs are finite; a program needn't handle non-finite values.
Results may differ from a plain program's by a relative error of at most 0.0065.
Values may be sent and summed in bfloat16 or wider, within the bound.
No kernel may reach another device: no remote copies, remote signals or barrier semaphores. Data moves between devices by JAX's collectives and lax.ppermute only.
A program may use at most 128 MiB of HBM per device.

v0:
```python
import jax
import jax.numpy as jnp
from jax import lax
from jax.sharding import PartitionSpec as P

OFFSETS = 27


def selector(table_index, offset, extent):
    wanted = lax.dynamic_index_in_dim(table_index, offset, 0, keepdims=False)
    slots = jnp.arange(extent + 1, dtype=jnp.int32)
    return (slots[:, None] == wanted[None, :]).astype(jnp.bfloat16)


def build_table(weight_cols, grad_rows, coarse_rows, table_index, nblocks, extent):
    row_total = weight_cols.shape[2]
    partial_value = jnp.zeros((row_total, extent + 1, 128), jnp.float32)
    partial_value = partial_value.at[:, :nblocks].add(coarse_rows.reshape(row_total, nblocks, 128))

    def spread_step(offset, current):
        weight_now = lax.dynamic_index_in_dim(weight_cols, offset, 0, keepdims=False)
        contrib = lax.dot_general(
            weight_now, grad_rows, (((0,), (0,)), ((), ())), preferred_element_type=jnp.float32
        )
        contrib = contrib.reshape(row_total, nblocks, 128)
        high = contrib.astype(jnp.bfloat16)
        rest = contrib - high.astype(jnp.float32)
        middle = rest.astype(jnp.bfloat16)
        low = (rest - middle.astype(jnp.float32)).astype(jnp.bfloat16)
        stacked = jnp.stack([high, middle, low])
        picks = selector(table_index, offset, extent)
        return current + jnp.einsum(
            "srnq,bn->rbq", stacked, picks, preferred_element_type=jnp.float32
        )

    return lax.fori_loop(0, OFFSETS, spread_step, partial_value)


def send_back(grad_table, send_rows, live_mask, nblocks, extent):
    halo_grad = grad_table[:, nblocks:extent]
    returned = lax.all_to_all(halo_grad, "morton", split_axis=1, concat_axis=1, tiled=True)
    returned = returned * live_mask.astype(jnp.float32)[None, :, None]
    return grad_table[:, :nblocks].at[:, send_rows, :].add(returned)


def local(features, conv_weight, coarse_weight, out_grad, send_block, send_count, neighbour):
    n_morton = lax.axis_size("morton")
    quarter, row_count = features.shape
    nblocks = row_count // 128
    channels = conv_weight.shape[2]
    extent = nblocks + n_morton
    send_rows = send_block[0]
    live_mask = send_count[0]
    local_grid = features.reshape(quarter, nblocks, 128)
    outgoing = (
        jnp.take(local_grid, send_rows, axis=1) * live_mask.astype(jnp.bfloat16)[None, :, None]
    )
    incoming = lax.all_to_all(outgoing, "morton", split_axis=1, concat_axis=1, tiled=True)
    part_table = jnp.concatenate(
        [local_grid, incoming, jnp.zeros((quarter, 1, 128), jnp.bfloat16)], axis=1
    )
    block_table = lax.all_gather(part_table, "chan", axis=0, tiled=True)
    table_index = jnp.where(neighbour < 0, extent, neighbour)

    def gather_offset(offset):
        picks = selector(table_index, offset, extent)
        picked = jnp.einsum("cbr,bn->cnr", block_table, picks, preferred_element_type=jnp.float32)
        return picked.astype(jnp.bfloat16).reshape(channels, row_count)

    def forward_step(offset, total):
        weight_now = lax.dynamic_index_in_dim(conv_weight, offset, 0, keepdims=False)
        return total + jnp.dot(
            weight_now, gather_offset(offset), preferred_element_type=jnp.float32
        )

    conv_out = lax.fori_loop(0, OFFSETS, forward_step, jnp.zeros((quarter, row_count), jnp.float32))
    local_values = block_table[:, :nblocks].reshape(channels, row_count).astype(jnp.float32)
    pooled = jnp.mean(local_values.reshape(channels, row_count // 8, 8), axis=2).astype(
        jnp.bfloat16
    )
    coarse = jnp.dot(coarse_weight, pooled, preferred_element_type=jnp.float32)
    pre_act = conv_out + jnp.repeat(coarse, 8, axis=1)
    output = jax.nn.silu(pre_act).astype(jnp.bfloat16)
    sigma = jax.nn.sigmoid(pre_act)
    grad_pre = out_grad.astype(jnp.float32) * sigma * (1.0 + pre_act * (1.0 - sigma))
    grad_pre_bf = grad_pre.astype(jnp.bfloat16)
    grad_parent = jnp.sum(grad_pre.reshape(quarter, row_count // 8, 8), axis=2)
    coarse_local = lax.dot_general(
        grad_parent,
        pooled.astype(jnp.float32),
        (((1,), (1,)), ((), ())),
        precision=lax.Precision.HIGHEST,
    )

    def weight_step(offset, weight_grad):
        single = lax.dot_general(
            grad_pre_bf,
            gather_offset(offset),
            (((1,), (1,)), ((), ())),
            preferred_element_type=jnp.float32,
        )
        return weight_grad.at[offset].set(single)

    conv_local = lax.fori_loop(
        0, OFFSETS, weight_step, jnp.zeros((OFFSETS, quarter, channels), jnp.float32)
    )
    conv_total, coarse_total = lax.psum((conv_local, coarse_local), "morton")
    scale = float(row_count * n_morton) ** (-0.5)
    conv_grad = conv_total * scale
    coarse_grad = coarse_total * scale
    coarse_input = lax.dot_general(
        coarse_weight.astype(jnp.float32),
        grad_parent,
        (((0,), (0,)), ((), ())),
        precision=lax.Precision.HIGHEST,
    )
    spread_coarse = jnp.repeat(coarse_input, 8, axis=1) / 8.0
    grad_table = lax.psum_scatter(
        build_table(conv_weight, grad_pre_bf, spread_coarse, table_index, nblocks, extent),
        "chan",
        scatter_dimension=0,
        tiled=True,
    )
    input_grad = send_back(grad_table, send_rows, live_mask, nblocks, extent).reshape(
        quarter, row_count
    )
    return (output, input_grad, conv_grad, coarse_grad)


def solution(mesh):
    placed = (
        P("chan", "morton"),
        P(None, "chan", None),
        P("chan", None),
        P("chan", "morton"),
        P("morton", None),
        P("morton", None),
        P(None, "morton"),
    )
    return jax.shard_map(
        local,
        mesh=mesh,
        in_specs=placed,
        out_specs=(
            P("chan", "morton"),
            P("chan", "morton"),
            P(None, "chan", None),
            P("chan", None),
        ),
        check_vma=False,
    )
```

profile of v0, /device:TPU:1, one launch (start us, length us, event | category | flops | bytes accessed | tf_op | source)
XLA Modules:
  0.0 693.3 jit_solution(16878327394354296786)
XLA Ops:
  11.0 8.6 %all-to-all-start = ((bf16[64,32,128]{2,0,1:T(8,128)(2,1)}), bf16[64,32,128]{2,0,1:T(8,128)(2,1)S(1)}, u32[]{:S(2)}, u32[]{:S(2)}) async-start(bf16[64,32,128]{2,0,1:T(8,128)(2,1)} %multiply_bitcast_fusion.1), calls=%async_computation | async-start | bytes 1048576 | tf_op jit(solution)/shard_map/all_to_all | solution.py:58
  19.7 11.4 %all-to-all-done = bf16[64,32,128]{2,0,1:T(8,128)(2,1)S(1)} async-done(((bf16[64,32,128]{2,0,1:T(8,128)(2,1)}), bf16[64,32,128]{2,0,1:T(8,128)(2,1)S(1)}, u32[]{:S(2)}, u32[]{:S(2)}) %all-to-all-start) | async-done | bytes 524320 | tf_op jit(solution)/shard_map/all_to_all | solution.py:58
  33.3 37.8 %all-gather.2.cloned.1.call-done = bf16[256,49,128]{2,0,1:T(8,128)(2,1)} async-done(((bf16[64,49,128]{2,0,1:T(8,128)(2,1)}), bf16[256,49,128]{2,0,1:T(8,128)(2,1)}) %all-gather.2.cloned.1.call-update) | async-done | bytes 3211280 | tf_op jit(solution)/shard_map/all_gather | solution.py:62
  71.1 2.8 slice_convert_fusion
  76.7 5.8 copy.54
  82.5 104.3 %while.44 = (s32[]{:T(128)}, f32[64,2048]{1,0:T(8,128)S(1)}, bf16[27,64,256]{2,1,0:T(8,128)(2,1)}, s32[27,16]{1,0:T(8,128)S(1)}, bf16[256,49,128]{2,1,0:T(8,128)(2,1)}, /*index=5*/s32[]{:T(128)}, s32[]{:T(128)}) while((s32[]{:T(128)}, f32[64,2048]{1,0:T(8,128)S(1)}, bf16[27,64,256]{2,1,0:T(8,128)(2,1)}, s32[27,16]{1,0:T(8,128)S(1)}, ...), condition=%wide.region_1.2_spmd.clone, body=%wide.region_0.1_spmd.clone.sunk | while | flops 119276304 | bytes 6390055 | solution.py:76
  82.6 2.8 convolution_convert_fusion.5
  195.0 3.4 scatter-add.12.clone
  198.4 235.8 %while.42 = (s32[]{:T(128)}, f32[256,49,128]{2,1,0:T(8,128)}, s32[27,16]{1,0:T(8,128)S(1)}, bf16[27,64,256]{2,1,0:T(8,128)(2,1)}, bf16[64,2048]{1,0:T(8,128)(2,1)S(1)}, /*index=5*/s32[]{:T(128)}) while((s32[]{:T(128)}, f32[256,49,128]{2,1,0:T(8,128)}, s32[27,16]{1,0:T(8,128)S(1)}, bf16[27,64,256]{2,1,0:T(8,128)(2,1)}, ...), condition=%wide.region_6.7_spmd, body=%wide.region_4.6_spmd.sunk | while | flops 134251280 | bytes 72909128 | solution.py:36
  204.2 2.9 copy-done.2
  212.9 2.9 copy-done.2
  221.7 2.9 copy-done.2
  230.4 2.9 copy-done.2
  239.1 2.9 copy-done.2
  247.9 2.9 copy-done.2
  256.6 2.9 copy-done.2
  265.3 2.9 copy-done.2
  274.0 2.9 copy-done.2
  282.8 2.9 copy-done.2
  291.5 2.9 copy-done.2
  300.2 2.9 copy-done.2
  309.0 2.9 copy-done.2
  317.7 2.9 copy-done.2
  326.4 2.9 copy-done.2
  335.2 2.9 copy-done.2
  343.9 2.9 copy-done.2
  352.6 2.9 copy-done.2
  361.4 2.9 copy-done.2
  370.1 2.9 copy-done.2
  378.8 2.9 copy-done.2
  387.6 2.9 copy-done.2
  396.3 2.9 copy-done.2
  405.0 2.9 copy-done.2
  413.8 2.9 copy-done.2
  422.5 2.9 copy-done.2
  431.2 2.9 copy-done.2
  434.2 7.1 %copy.62 = f32[256,49,128]{2,0,1:T(8,128)} copy(f32[256,49,128]{2,1,0:T(8,128)} %get-tuple-element.321) | data formatting | bytes 12845056 | tf_op jit(solution)/shard_map/while | solution.py:36
  441.9 123.4 %while.43 = (s32[]{:T(128)}, f32[27,64,256]{2,1,0:T(8,128)S(1)}, s32[27,16]{1,0:T(8,128)S(1)}, bf16[256,49,128]{2,1,0:T(8,128)(2,1)}, bf16[64,2048]{1,0:T(8,128)...) while((s32[]{:T(128)}, f32[27,64,256]{2,1,0:T(8,128)S(1)}, s32[27,16]{1,0:T(8,128)S(1)}, ...), condition=%wide.region_11.12_spmd, body=%wide.region_9.11_spmd.sunk | while | flops 119030560 | bytes 5701947 | solution.py:104
  451.8 2.8 convolution_convert_fusion.4
  474.6 2.7 convolution_convert_fusion.4
  479.2 2.8 convolution_convert_fusion.4
  483.8 2.8 convolution_convert_fusion.4
  493.0 2.8 convolution_convert_fusion.4
  497.7 2.8 convolution_convert_fusion.4
  502.3 2.7 convolution_convert_fusion.4
  568.9 7.5 %all-to-all-start.1 = ((f32[64,32,128]{2,0,1:T(8,128)}), f32[64,32,128]{2,0,1:T(8,128)S(1)}, u32[]{:S(2)}, u32[]{:S(2)}) async-start(f32[64,32,128]{2,0,1:T(8,128)} %slice.72), calls=%async_computation.2 | async-start | bytes 2097152 | tf_op jit(solution)/shard_map/all_to_all | solution.py:41
  577.3 101.9 %all-reduce.4.cloned.1.call-done = (f32[27,64,256]{2,1,0:T(8,128)}, f32[64,256]{1,0:T(8,128)}) async-done(((f32[27,64,256]{2,1,0:T(8,128)}, f32[64,256]{1,0:T(8,128)}), (f32[27,64,256]{2,1,0:T(8,128)}, f32[64,256]{1,0:T(8,128)})) %all-reduce.4.cloned.1.call-update) | async-done | bytes 1835024 | tf_op jit(solution)/shard_map/psum | solution.py:107
  680.7 2.9 broadcast_multiply_fusion
  (427 shorter events, 386.0 us)
Async XLA Ops:
  7.2 25.1 %copy-start.8 = (s32[27,16]{0,1:T(8,128)S(1)}, s32[27,16]{0,1:T(8,128)}, u32[]{:S(2)}) copy-start(s32[27,16]{0,1:T(8,128)} %param.23) | copy-start | bytes 5188
  7.2 25.1 %copy-start.5 = (bf16[64,2048]{1,0:T(8,128)(2,1)S(1)}, bf16[64,2048]{1,0:T(8,128)(2,1)}, u32[]{:S(2)}) copy-start(bf16[64,2048]{1,0:T(8,128)(2,1)} %param.20) | copy-start | bytes 786436
  11.0 20.1 %all-to-all-start = ((bf16[64,32,128]{2,0,1:T(8,128)(2,1)}), bf16[64,32,128]{2,0,1:T(8,128)(2,1)S(1)}, u32[]{:S(2)}, u32[]{:S(2)}) async-start(bf16[64,32,128]{2,0,1:T(8,128)(2,1)} %multiply_bitcast_fusion.1), calls=%async_computation | async-start | bytes 1048576 | tf_op jit(solution)/shard_map/all_to_all | solution.py:58
  19.6 51.5 %all-gather.2.cloned.1.call-start = ((), (), s32[]{:S(2)}) async-start(), calls=%async_computation.3 | async-start | bytes 4014080 | tf_op jit(solution)/shard_map/all_gather | solution.py:62
  32.2 534.4 %reduce-scatter.2.cloned.1.call-start = ((), (), s32[]{:S(2)}) async-start(), calls=%async_computation.4 | async-start | bytes 8028160 | tf_op jit(solution)/shard_map/reduce_scatter | solution.py:118
  82.5 104.7 %copy-start.4 = (bf16[64,2048]{0,1:T(8,128)(2,1)S(1)}, bf16[64,2048]{0,1:T(8,128)(2,1)}, u32[]{:S(2)}) copy-start(bf16[64,2048]{0,1:T(8,128)(2,1)} %copy.59) | copy-start | bytes 786436
  198.4 3.1 copy-start.1
  204.2 2.9 copy-start.2
  207.1 3.1 copy-start.1
  212.9 2.9 copy-start.2
  215.9 3.1 copy-start.1
  221.6 2.9 copy-start.2
  224.6 3.1 copy-start.1
  230.4 2.9 copy-start.2
  233.3 3.1 copy-start.1
  242.1 3.1 copy-start.1
  247.8 2.9 copy-start.2
  250.8 3.1 copy-start.1
  256.6 2.9 copy-start.2
  259.5 3.1 copy-start.1
  265.3 2.9 copy-start.2
  268.3 3.1 copy-start.1
  274.0 2.9 copy-start.2
  277.0 3.1 copy-start.1
  285.7 3.1 copy-start.1
  291.5 2.9 copy-start.2
  294.5 3.1 copy-start.1
  303.2 3.1 copy-start.1
  309.0 2.9 copy-start.2
  311.9 3.1 copy-start.1
  317.7 2.9 copy-start.2
  320.7 3.1 copy-start.1
  326.4 2.9 copy-start.2
  329.4 3.1 copy-start.1
  338.1 3.1 copy-start.1
  346.9 3.1 copy-start.1
  355.6 3.1 copy-start.1
  364.3 3.1 copy-start.1
  373.1 3.1 copy-start.1
  381.8 3.1 copy-start.1
  390.5 3.1 copy-start.1
  399.3 3.1 copy-start.1
  408.0 3.1 copy-start.1
  416.7 3.1 copy-start.1
  425.4 3.1 copy-start.1
  441.3 238.0 %all-reduce.4.cloned.1.call-start = ((), (), s32[]{:S(2)}) async-start(), calls=%async_computation.5 | async-start | bytes 3670016 | tf_op jit(solution)/shard_map/psum | solution.py:107
  568.9 114.7 %all-to-all-start.1 = ((f32[64,32,128]{2,0,1:T(8,128)}), f32[64,32,128]{2,0,1:T(8,128)S(1)}, u32[]{:S(2)}, u32[]{:S(2)}) async-start(f32[64,32,128]{2,0,1:T(8,128)} %slice.72), calls=%async_computation.2 | async-start | bytes 2097152 | tf_op jit(solution)/shard_map/all_to_all | solution.py:41
  680.7 3.1 slice-start
  (19 other events, 50.8 us)
Sparse Core Ops, SparseCore 0:
  32.3 38.7 all-gather.1
  441.4 65.3 reduce-scatter.1
  566.7 112.4 all-reduce.3
where the time goes:
time: 699 us; the launch traced here: 693 us
  matrix products  325 us (46%)
  waiting for transfers between devices  151 us (22%)
  local copies, waits for them, and re-layouts  135 us (19%)
  other arithmetic  48.9 us (7%)
  starting transfers between devices  16.4 us (2%)
  between operations  14 us (2%)
    dot_general x54, matrix products, gather_offset(): jnp.einsum('cbr,bn->cnr', block_table, picks, preferred_element_type=jnp....  148 us
    while x108, local copies, waits for them, and re-layouts  104 us
    psum x1, waiting for transfers between devices, local(): conv_total, coarse_total = lax.psum((conv_local, coarse_local), 'morton')  102 us
    dot_general x27, matrix products, spread_step(): jnp.einsum('srnq,bn->rbq', stacked, picks, preferred_element_type=jnp.flo...  72.1 us
    dot_general x27, matrix products, spread_step(): lax.dot_general(weight_now, grad_rows, (((0,), (0,)), ((), ())), preferre...  45.1 us
    all_gather x1, waiting for transfers between devices, local(): block_table = lax.all_gather(part_table, 'chan', axis=0, tiled=True)  37.8 us
    dot_general x27, matrix products, weight_step(): lax.dot_general(grad_pre_bf, gather_offset(offset), (((1,), (1,)), ((), (...  29.4 us
    dot_general x27, matrix products, forward_step(): jnp.dot(weight_now, gather_offset(offset), preferred_element_type=jnp.flo...  29.4 us
  transfers between devices with their start and end apart: 5, of which 3 were waited for; matrix products, arithmetic and copies ran while one was open for 19% of the time, Pallas kernels for 0%

commit v1 on v0

v1 whole, which is shorter than its diff:
```python
import functools

import jax
import jax.numpy as jnp
from jax import lax
from jax.experimental import pallas as pl
from jax.experimental.pallas import tpu as pltpu
from jax.sharding import PartitionSpec as P

OFFSETS = 27
TERMS = 28
PAIRS = TERMS // 2
BLOCK = 128
BF = jnp.bfloat16
F32 = jnp.float32


def call(kernel, name, outs, kinds, scratch=(), flops=0, size=0, limit=48 << 20):
    space = {"s": pltpu.SMEM, "v": pltpu.VMEM}
    many = isinstance(outs, (list, tuple))
    spec = pl.BlockSpec(memory_space=pltpu.VMEM)
    return pl.pallas_call(
        kernel,
        name=name,
        out_shape=outs,
        in_specs=[pl.BlockSpec(memory_space=space[k]) for k in kinds],
        out_specs=[spec] * len(outs) if many else spec,
        scratch_shapes=list(scratch),
        compiler_params=pltpu.CompilerParams(vmem_limit_bytes=limit),
        cost_estimate=pl.CostEstimate(flops=flops, bytes_accessed=size, transcendentals=0),
    )


def mean_matrix():
    row = lax.broadcasted_iota(jnp.int32, (BLOCK, BLOCK), 0) // 8
    column = lax.broadcasted_iota(jnp.int32, (BLOCK, BLOCK), 1) // 8
    return jnp.where(row == column, 0.125, 0.0).astype(BF)


def columns(index):
    return pl.ds(pl.multiple_of(index * BLOCK, BLOCK), BLOCK)


def pack_kernel(send_block, send_count, features, outgoing):
    for peer in range(outgoing.shape[0]):
        block = features[:, columns(send_block[0, peer])]
        outgoing[peer] = block * send_count[0, peer].astype(F32).astype(BF)


def split_kernel(place, conv_weight, coarse_weight, pieces):
    quarter = conv_weight.shape[1]
    for pair in range(PAIRS):
        first = conv_weight[2 * pair]
        second = conv_weight[2 * pair + 1] if 2 * pair + 1 < OFFSETS else coarse_weight[...]
        cuts = [slice(t * quarter, (t + 1) * quarter) for t in range(4)]
        tiles = [jnp.concatenate([first[:, c], second[:, c]], axis=1) for c in cuts]
        for step in range(4):
            target = lax.rem(place[0] + step, 4)
            low = jnp.where(target == 0, tiles[0], tiles[1])
            high = jnp.where(target == 2, tiles[2], tiles[3])
            pieces[step * PAIRS + pair] = jnp.where(target < 2, low, high)


def join_kernel(piece0, piece1, piece2, piece3, weight, flipped):
    for pair in range(PAIRS):
        tile = jnp.concatenate([p[pair] for p in (piece0, piece1, piece2, piece3)], axis=0)
        weight[:, pair * BLOCK : (pair + 1) * BLOCK] = tile
        flipped[pair * BLOCK : (pair + 1) * BLOCK, :] = tile.T


def fill_table(features, incoming, table, nblocks):
    for block in range(nblocks):
        table[block] = features[:, block * BLOCK : (block + 1) * BLOCK]
    table[nblocks : nblocks + incoming.shape[0]] = incoming[...]
    table[nblocks + incoming.shape[0]] = jnp.zeros(table.shape[1:], BF)


def slot(neighbour, offset, block, extent):
    named = neighbour[offset, block]
    return jnp.where(named < 0, extent, named)


def fill_gathered(neighbour, table, gathered, nblocks, extent):
    quarter = table.shape[1]

    def step(offset, carry):
        rows = pl.ds(pl.multiple_of(offset * quarter, quarter), quarter)
        for block in range(nblocks):
            picked = table[slot(neighbour, offset, block, extent)]
            gathered[rows, block * BLOCK : (block + 1) * BLOCK] = picked
        return carry

    lax.fori_loop(0, OFFSETS, step, 0)
    mean = mean_matrix()
    for block in range(nblocks):
        pooled = jnp.dot(table[block], mean, preferred_element_type=F32).astype(BF)
        gathered[OFFSETS * quarter :, block * BLOCK : (block + 1) * BLOCK] = pooled


def forward_kernel(
    neighbour, features, incoming, weight, out0, out1, out2, out3, table, gathered
):
    quarter, row_count = features.shape
    nblocks = row_count // BLOCK
    extent = nblocks + incoming.shape[0]
    fill_table(features, incoming, table, nblocks)
    fill_gathered(neighbour, table, gathered, nblocks, extent)
    for tile in range(row_count // 256):
        cut = slice(tile * 256, (tile + 1) * 256)
        total = jnp.dot(weight[...], gathered[:, cut], preferred_element_type=F32)
        for step, out in enumerate((out0, out1, out2, out3)):
            out[:, cut] = total[step * quarter : (step + 1) * quarter].astype(out.dtype)


def activation_kernel(own, part1, part2, part3, out_grad, output, grad):
    pre = (own[...] + part1[...].astype(F32)) + (part2[...].astype(F32) + part3[...].astype(F32))
    sigma = 1.0 / (1.0 + jnp.exp(-pre))
    output[...] = (pre * sigma).astype(BF)
    grad[...] = (out_grad[...].astype(F32) * sigma * (1.0 + pre * (1.0 - sigma))).astype(BF)


def weight_kernel(
    place, neighbour, features, incoming, grad0, grad1, grad2, grad3, parts, table, gathered, flipped
):
    quarter, row_count = features.shape
    nblocks = row_count // BLOCK
    extent = nblocks + incoming.shape[0]
    fill_table(features, incoming, table, nblocks)
    fill_gathered(neighbour, table, gathered, nblocks, extent)
    for block in range(nblocks):
        cut = slice(block * BLOCK, (block + 1) * BLOCK)
        tall = jnp.concatenate([g[:, cut] for g in (grad0, grad1, grad2, grad3)], axis=0)
        flipped[cut, :] = tall.T
    half = quarter // 2
    for pair in range(PAIRS):
        rows = slice(pair * BLOCK, (pair + 1) * BLOCK)
        product = jnp.dot(gathered[rows, :], flipped[...], preferred_element_type=F32)
        upright = product.T.astype(BF)
        for step in range(4):
            target = lax.rem(place[0] - step + 4, 4)
            for side in range(2):
                start = step * quarter + side * half
                parts[2 * pair + side, target] = upright[start : start + half]
    for spare in range(2 * PAIRS, parts.shape[0]):
        parts[spare] = jnp.zeros(parts.shape[1:], BF)


def table_kernel(neighbour, weight_t, grad0, grad1, grad2, grad3, local, returned, total):
    quarter, row_count = grad0.shape
    nblocks = row_count // BLOCK
    extent = nblocks + returned.shape[0]
    total[...] = jnp.zeros_like(total)
    mean = mean_matrix()
    for tile in range(nblocks // 2):
        cut = slice(tile * 256, (tile + 1) * 256)
        tall = jnp.concatenate([g[:, cut] for g in (grad0, grad1, grad2, grad3)], axis=0)

        def step(offset, carry, tall=tall, tile=tile):
            rows = pl.ds(pl.multiple_of(offset * quarter, quarter), quarter)
            product = jnp.dot(weight_t[rows, :], tall, preferred_element_type=F32)
            for side in range(2):
                place = slot(neighbour, offset, 2 * tile + side, extent)
                total[place] += product[:, side * BLOCK : (side + 1) * BLOCK]
            return carry

        lax.fori_loop(0, OFFSETS, step, 0)
        coarse = jnp.dot(weight_t[OFFSETS * quarter :, :], tall, preferred_element_type=F32)
        for side in range(2):
            value = coarse[:, side * BLOCK : (side + 1) * BLOCK]
            high = value.astype(BF)
            low = (value - high.astype(F32)).astype(BF)
            total[2 * tile + side] += jnp.dot(high, mean, preferred_element_type=F32) + jnp.dot(
                low, mean, preferred_element_type=F32
            )
    for block in range(nblocks):
        local[:, block * BLOCK : (block + 1) * BLOCK] = total[block]
    returned[...] = total[nblocks:extent].astype(BF)


def return_kernel(send_block, send_count, local, returned, input_grad):
    input_grad[...] = local[...]
    for peer in range(returned.shape[0]):
        factor = send_count[0, peer].astype(F32)
        input_grad[:, columns(send_block[0, peer])] += returned[peer].astype(F32) * factor


def sum_kernel(scale, parts, chunk):
    quarter = 64
    total = parts[0].astype(F32)
    for source in range(1, parts.shape[0]):
        total = total + parts[source].astype(F32)
    total = total * scale
    for side in range(2):
        cut = slice(side * quarter, (side + 1) * quarter)
        chunk[side] = jnp.concatenate([total[c, :, cut] for c in range(4)], axis=1).astype(BF)


def unpack_kernel(chunks, conv_grad, coarse_grad):
    half = chunks.shape[2]
    for piece in range(2 * PAIRS):
        rows = slice((piece % 2) * half, (piece % 2 + 1) * half)
        for side in range(2):
            offset = 2 * (piece // 2) + side
            value = chunks[piece, side].astype(F32)
            if offset < OFFSETS:
                conv_grad[offset, rows, :] = value
            else:
                coarse_grad[rows, :] = value


def shift(value, axis, step):
    size = lax.axis_size(axis)
    return lax.ppermute(value, axis, [(i, (i + step) % size) for i in range(size)])


def local_step(features, conv_weight, coarse_weight, out_grad, send_block, send_count, neighbour):
    n_morton = lax.axis_size("morton")
    quarter, row_count = features.shape
    channels = conv_weight.shape[2]
    nblocks = row_count // BLOCK
    extent = nblocks + n_morton
    depth = TERMS * quarter
    flops = 2 * depth * channels * row_count
    place = lax.axis_index("chan").astype(jnp.int32).reshape(1)
    shape = jax.ShapeDtypeStruct

    outgoing = call(
        pack_kernel, "pack", shape((n_morton, quarter, BLOCK), BF), "ssv", size=1 << 20
    )(send_block, send_count, features)
    incoming = lax.all_to_all(outgoing, "morton", 0, 0, tiled=True)

    pieces = call(
        split_kernel, "split", shape((4 * PAIRS, quarter, BLOCK), BF), "svv", size=2 << 20
    )(place, conv_weight, coarse_weight)
    pieces = pieces.reshape(4, PAIRS, quarter, BLOCK)
    weights = [pieces[0]] + [shift(pieces[s], "chan", s) for s in (1, 2, 3)]
    weight, weight_t = call(
        join_kernel,
        "join",
        [shape((channels, depth), BF), shape((depth, channels), BF)],
        "vvvv",
        size=3 << 20,
    )(*weights)

    big = [pltpu.VMEM((extent + 1, quarter, BLOCK), BF), pltpu.VMEM((depth, row_count), BF)]
    wide = (quarter, row_count)
    partial = call(
        forward_kernel,
        "forward",
        [shape(wide, F32)] + [shape(wide, BF)] * 3,
        "svvv",
        big,
        flops,
        4 << 20,
    )(neighbour, features, incoming, weight)
    arrived = [shift(partial[s], "chan", -s) for s in (1, 2, 3)]
    output, grad = call(
        activation_kernel, "activation", [shape(wide, BF)] * 2, "vvvvv", size=2 << 20
    )(partial[0], *arrived, out_grad)
    grads = [grad] + [shift(grad, "chan", s) for s in (1, 2, 3)]

    parts = call(
        weight_kernel,
        "weight_grad",
        shape((n_morton, 4, quarter // 2, BLOCK), BF),
        "ssvvvvvv",
        big + [pltpu.VMEM((row_count, channels), BF)],
        flops,
        4 << 20,
    )(place, neighbour, features, incoming, *grads)
    received = lax.all_to_all(
        parts.reshape(n_morton * 4, quarter // 2, BLOCK), ("morton", "chan"), 0, 0, tiled=True
    ).reshape(parts.shape)

    local, outward = call(
        table_kernel,
        "table_grad",
        [shape(wide, F32), shape((n_morton, quarter, BLOCK), BF)],
        "svvvvv",
        [pltpu.VMEM((extent + 1, quarter, BLOCK), F32)],
        flops,
        4 << 20,
    )(neighbour, weight_t, *grads)
    returned = lax.all_to_all(outward, "morton", 0, 0, tiled=True)
    input_grad = call(return_kernel, "return_add", shape(wide, F32), "ssvv", size=2 << 20)(
        send_block, send_count, local, returned
    )

    scale = float(row_count * n_morton) ** (-0.5)
    chunk = call(
        functools.partial(sum_kernel, scale),
        "sum_parts",
        shape((2, quarter // 2, channels), BF),
        "v",
        size=1 << 20,
    )(received)
    chunks = lax.all_to_all(
        jnp.broadcast_to(chunk, (n_morton,) + chunk.shape), "morton", 0, 0, tiled=True
    )
    conv_grad, coarse_grad = call(
        unpack_kernel,
        "unpack",
        [shape((OFFSETS, quarter, channels), F32), shape((quarter, channels), F32)],
        "v",
        size=3 << 20,
    )(chunks)
    return output, input_grad, conv_grad, coarse_grad


def solution(mesh):
    placed = (
        P("chan", "morton"),
        P(None, "chan", None),
        P("chan", None),
        P("chan", "morton"),
        P("morton", None),
        P("morton", None),
        P(None, "morton"),
    )
    return jax.shard_map(
        local_step,
        mesh=mesh,
        in_specs=placed,
        out_specs=(
            P("chan", "morton"),
            P("chan", "morton"),
            P(None, "chan", None),
            P("chan", None),
        ),
        check_vma=False,
    )
```

time: 699 us -> 167 us (0.24)
  matrix products: 325 us -> 0 us
  local copies, waits for them, and re-layouts: 135 us -> 5.72 us
  waiting for transfers between devices: 151 us -> 63.1 us
  Pallas kernels: 0 us -> 55.2 us
  other arithmetic: 48.9 us -> 0 us
  starting transfers between devices: 16.4 us -> 41.5 us
  between operations: 14 us -> 0.81 us
    dot_general x165 -> x0, matrix products: 325 us -> none  [the longest x54 148 us: gather_offset(): jnp.einsum('cbr,bn->cnr', block_table, picks, preferred_element_type=jnp....]
    while x111 -> x0, local copies, waits for them, and re-layouts: 112 us -> none
    psum x1 -> x0, waiting for transfers between devices: 102 us -> none  [local(): conv_total, coarse_total = lax.psum((conv_local, coarse_local), 'morton')]
    pallas_call x0 -> x10, Pallas kernels: none -> 55.2 us  [the longest x1 38 us: local_step(): call(table_kernel, 'table_grad', [shape(wide, F32), shape((n_morton, quar...]
    all_gather x1 -> x0, waiting for transfers between devices: 37.8 us -> none  [local(): block_table = lax.all_gather(part_table, 'chan', axis=0, tiled=True)]
    ppermute x0 -> x9, waiting for transfers between devices: none -> 36.2 us  [shift(): lax.ppermute(value, axis, [(i, (i + step) % size) for i in range(size)])]
    another operation x27 -> x0, other arithmetic: 19.2 us -> none
    all_to_all x2 -> x4, waiting for transfers between devices: 11.4 us -> 26.9 us  [the longest x1 15.6 us: local_step(): lax.all_to_all(jnp.broadcast_to(chunk, (n_morton,) + chunk.shape), 'morto...]
  transfers between devices with their start and end apart: 5 -> 13, of which waited for: 3 -> 9; matrix products, arithmetic and copies ran while one was open for 19% -> 0% of each run, Pallas kernels for 0% -> 24%
where the time goes in v1:
time: 167 us; the launch traced here: 166 us
  waiting for transfers between devices  63.1 us (38%)
  Pallas kernels  55.2 us (33%)
  starting transfers between devices  41.5 us (25%)
  local copies, waits for them, and re-layouts  5.72 us (3%)
    pallas_call x1, Pallas kernels, local_step(): call(table_kernel, 'table_grad', [shape(wide, F32), shape((n_morton, quar...  38 us
    ppermute x9, waiting for transfers between devices, shift(): lax.ppermute(value, axis, [(i, (i + step) % size) for i in range(size)])  36.2 us
    all_to_all x1, waiting for transfers between devices, local_step(): lax.all_to_all(jnp.broadcast_to(chunk, (n_morton,) + chunk.shape), 'morto...  15.6 us
    ppermute x9, starting transfers between devices, shift(): lax.ppermute(value, axis, [(i, (i + step) % size) for i in range(size)])  11.6 us
    all_to_all x1, waiting for transfers between devices, local_step(): returned = lax.all_to_all(outward, 'morton', 0, 0, tiled=True)  11.3 us
    all_to_all x1, starting transfers between devices, local_step(): lax.all_to_all(parts.reshape(n_morton * 4, quarter // 2, BLOCK), ('morton...  9.85 us
    all_to_all x1, starting transfers between devices, local_step(): incoming = lax.all_to_all(outgoing, 'morton', 0, 0, tiled=True)  8.59 us
    all_to_all x1, starting transfers between devices, local_step(): returned = lax.all_to_all(outward, 'morton', 0, 0, tiled=True)  7.41 us
  transfers between devices with their start and end apart: 13, of which 9 were waited for; matrix products, arithmetic and copies ran while one was open for 0% of the time, Pallas kernels for 24%

profile of v1, /device:TPU:1, one launch (start us, length us, event | category | flops | bytes accessed | tf_op | source)
XLA Modules:
  0.0 166.2 jit_solution(5957801748793788052)
XLA Ops:
  0.6 0.0 copy-start.1
  0.7 1.0 copy-done.1
  1.7 0.7 copy-done.5
  2.3 0.7 copy-done.7
  3.0 1.5 pack.1
  4.5 8.6 %all-to-all-start = ((bf16[32,64,128]{2,1,0:T(8,128)(2,1)}), bf16[32,64,128]{2,1,0:T(8,128)(2,1)S(1)}, u32[]{:S(2)}, u32[]{:S(2)}) async-start(bf16[32,64,128]{2,1,0:T(8,128)(2,1)} %pack.1), calls=%async_computation | async-start | bytes 1048576 | tf_op jit(solution)/shard_map/all_to_all | solution.py:230
  13.1 0.0 copy-start.15
  13.1 0.3 split.1
  13.4 0.0 copy-start.2
  13.4 0.1 fusion
  13.5 1.7 %collective-permute-start = (bf16[14,64,128]{2,1,0:T(8,128)(2,1)S(1)}, bf16[14,64,128]{2,1,0:T(8,128)(2,1)S(1)}, u32[]{:S(2)}, u32[]{:S(2)}) collective-permute-start(bf16[14,64,128]{2,1,0:T(8,128)(2,1)S(1)} %get-tuple-element.30), channel_id=1, source_target_pairs={{0,1},{1,2},{2,3},{3,0},{4,5},{5,6},{6,7},{7,4},{8,9},{9,10},{10,1... | collective-permute-start | bytes 688136 | tf_op jit(solution)/shard_map/ppermute | solution.py:213
  15.2 3.3 %collective-permute-start.1 = (bf16[14,64,128]{2,1,0:T(8,128)(2,1)S(1)}, bf16[14,64,128]{2,1,0:T(8,128)(2,1)S(1)}, u32[]{:S(2)}, u32[]{:S(2)}) collective-permute-start(bf16[14,64,128]{2,1,0:T(8,128)(2,1)S(1)} %get-tuple-element.29), channel_id=1, source_target_pairs={{0,2},{1,3},{2,0},{3,1},{4,6},{5,7},{6,4},{7,5},{8,10},{9,11},{10,... | collective-permute-start | bytes 688136 | tf_op jit(solution)/shard_map/ppermute | solution.py:213
  18.5 0.7 collective-permute-start.2
  19.2 0.1 copy.11.neighbour
  19.3 3.8 %collective-permute-done.piece1 = bf16[14,64,128]{2,1,0:T(8,128)(2,1)S(1)} collective-permute-done((bf16[14,64,128]{2,1,0:T(8,128)(2,1)S(1)}, bf16[14,64,128]{2,1,0:T(8,128)(2,1)S(1)}, u32[]{:S(2)}, u32[]{:S(2)}) %collective-permute-start) | collective-permute-done | bytes 229408 | tf_op jit(solution)/shard_map/ppermute | solution.py:213
  23.2 5.8 %collective-permute-done.1.piece2 = bf16[14,64,128]{2,1,0:T(8,128)(2,1)S(1)} collective-permute-done((bf16[14,64,128]{2,1,0:T(8,128)(2,1)S(1)}, bf16[14,64,128]{2,1,0:T(8,128)(2,1)S(1)}, u32[]{:S(2)}, u32[]{:S(2)}) %collective-permute-start.1) | collective-permute-done | bytes 229408 | tf_op jit(solution)/shard_map/ppermute | solution.py:213
  28.9 0.0 collective-permute-done.2.piece3
  28.9 0.3 join.1
  29.3 0.0 copy-start.9
  29.3 0.9 copy-done.9
  30.2 0.0 all-to-all-done.incoming
  30.2 1.2 copy-done.10
  31.4 4.9 %forward.1 = (f32[64,2048]{1,0:T(8,128)S(1)}, bf16[64,2048]{1,0:T(8,128)(2,1)S(1)}, bf16[64,2048]{1,0:T(8,128)(2,1)S(1)}, bf16[64,2048]{1,0:T(8,128)(2,1)S(1)}) custom-call(s32[27,16]{1,0:T(8,128)S(1)} %copy.11.neighbour, bf16[64,2048]{1,0:T(8,128)(2,1)S(1)} %copy-done.2, bf16[32,64,128]{2,1,0:T(8,128)(2,1)S(1)} %all-to-all-done.incoming, ...), custom_call_target="tpu_custom_call" | custom-call | flops 1879048192 | bytes 4194304 | tf_op jit(solution)/shard_map/forward/pallas_call | solution.py:247
  36.3 2.5 %collective-permute-start.3 = (bf16[64,2048]{1,0:T(8,128)(2,1)S(1)}, bf16[64,2048]{1,0:T(8,128)(2,1)S(1)}, u32[]{:S(2)}, u32[]{:S(2)}) collective-permute-start(bf16[64,2048]{1,0:T(8,128)(2,1)S(1)} %get-tuple-element.18), channel_id=1, source_target_pairs={{0,3},{1,0},{2,1},{3,2},{4,7},{5,4},{6,5},{7,6},{8,11},{9,8},{10,9... | collective-permute-start | bytes 786440 | tf_op jit(solution)/shard_map/ppermute | solution.py:213
  38.8 0.5 collective-permute-start.4
  39.3 0.2 collective-permute-start.5
  39.5 5.9 %collective-permute-done.3.part1 = bf16[64,2048]{1,0:T(8,128)(2,1)S(1)} collective-permute-done((bf16[64,2048]{1,0:T(8,128)(2,1)S(1)}, bf16[64,2048]{1,0:T(8,128)(2,1)S(1)}, u32[]{:S(2)}, u32[]{:S(2)}) %collective-permute-start.3) | collective-permute-done | bytes 262176 | tf_op jit(solution)/shard_map/ppermute | solution.py:213
  45.4 2.0 %collective-permute-done.4.part2 = bf16[64,2048]{1,0:T(8,128)(2,1)S(1)} collective-permute-done((bf16[64,2048]{1,0:T(8,128)(2,1)S(1)}, bf16[64,2048]{1,0:T(8,128)(2,1)S(1)}, u32[]{:S(2)}, u32[]{:S(2)}) %collective-permute-start.4) | collective-permute-done | bytes 262176 | tf_op jit(solution)/shard_map/ppermute | solution.py:213
  47.4 6.7 %collective-permute-done.5.part3 = bf16[64,2048]{1,0:T(8,128)(2,1)S(1)} collective-permute-done((bf16[64,2048]{1,0:T(8,128)(2,1)S(1)}, bf16[64,2048]{1,0:T(8,128)(2,1)S(1)}, u32[]{:S(2)}, u32[]{:S(2)}) %collective-permute-start.5) | collective-permute-done | bytes 262176 | tf_op jit(solution)/shard_map/ppermute | solution.py:213
  54.2 0.9 activation.1
  55.1 0.0 collective-permute-start.6
  55.1 0.5 collective-permute-start.7
  55.6 2.2 %collective-permute-start.8 = (bf16[64,2048]{1,0:T(8,128)(2,1)S(1)}, bf16[64,2048]{1,0:T(8,128)(2,1)S(1)}, u32[]{:S(2)}, u32[]{:S(2)}) collective-permute-start(bf16[64,2048]{1,0:T(8,128)(2,1)S(1)} %get-tuple-element.23.grad0), channel_id=1, source_target_pairs={{0,3},{1,0},{2,1},{3,2},{4,7},{5,4},{6,5},{7,6},{8,11},{9,8},{10,9... | collective-permute-start | bytes 786440 | tf_op jit(solution)/shard_map/ppermute | solution.py:213
  57.8 11.5 %collective-permute-done.6.grad1 = bf16[64,2048]{1,0:T(8,128)(2,1)S(1)} collective-permute-done((bf16[64,2048]{1,0:T(8,128)(2,1)S(1)}, bf16[64,2048]{1,0:T(8,128)(2,1)S(1)}, u32[]{:S(2)}, u32[]{:S(2)}) %collective-permute-start.6) | collective-permute-done | bytes 262176 | tf_op jit(solution)/shard_map/ppermute | solution.py:213
  69.3 0.0 collective-permute-done.7.grad2
  69.3 0.3 collective-permute-done.8.grad3
  69.7 6.0 %weight_grad.1 = bf16[32,4,32,128]{3,2,1,0:T(8,128)(2,1)} custom-call(s32[1]{0:T(128)} %bitcast.place, s32[27,16]{1,0:T(8,128)S(1)} %copy.11.neighbour, bf16[64,2048]{1,0:T(8,128)(2,1)S(1)} %copy-done.2, bf16[32,64,128]{2,1,0:T(8,128)(2,1)S(1)} %all-to-all-done.incoming, bf16[64,2048]{1,0:T(8,128)(2,1)S(1)} %get-tuple-element.23.grad0, ...), custom_call_target="tpu_custom_call" | custom-call | flops 1879048192 | bytes 4194304 | tf_op jit(solution)/shard_map/weight_grad/pallas_call | solution.py:262
  75.7 9.8 %all-to-all-start.2 = ((bf16[128,32,128]{2,1,0:T(8,128)(2,1)}), bf16[128,32,128]{2,1,0:T(8,128)(2,1)S(1)}, u32[]{:S(2)}, u32[]{:S(2)}) async-start(bf16[128,32,128]{2,1,0:T(8,128)(2,1)} %bitcast.1), calls=%async_computation.2 | async-start | bytes 2097152 | tf_op jit(solution)/shard_map/all_to_all | solution.py:271
  85.5 38.0 %table_grad.1 = (f32[64,2048]{1,0:T(8,128)S(1)}, bf16[32,64,128]{2,1,0:T(8,128)(2,1)}) custom-call(s32[27,16]{1,0:T(8,128)S(1)} %copy.11.neighbour, bf16[1792,256]{1,0:T(8,128)(2,1)S(1)} %get-tuple-element.22.weight_t, bf16[64,2048]{1,0:T(8,128)(2,1)S(1)} %get-tuple-element.23.grad0, bf16[64,2048]{1,0:T(8,128)(2,1)S(1)} %collective-permute-done.6.grad1, ...), custom_call_target="tpu_custom_call" | custom-call | flops 1879048192 | bytes 4194304 | tf_op jit(solution)/shard_map/table_grad/pallas_call | solution.py:275
  123.5 0.0 all-to-all-done.2
  123.5 7.4 %all-to-all-start.1 = ((bf16[32,64,128]{2,1,0:T(8,128)(2,1)}), bf16[32,64,128]{2,1,0:T(8,128)(2,1)S(1)}, u32[]{:S(2)}, u32[]{:S(2)}) async-start(bf16[32,64,128]{2,1,0:T(8,128)(2,1)} %get-tuple-element.25), calls=%async_computation.1 | async-start | bytes 1048576 | tf_op jit(solution)/shard_map/all_to_all | solution.py:284
  130.9 0.2 sum_parts.1
  131.2 11.3 %all-to-all-done.1.returned = bf16[32,64,128]{2,1,0:T(8,128)(2,1)S(1)} async-done(((bf16[32,64,128]{2,1,0:T(8,128)(2,1)}), bf16[32,64,128]{2,1,0:T(8,128)(2,1)S(1)}, u32[]{:S(2)}, u32[]{:S(2)}) %all-to-all-start.1) | async-done | bytes 524320 | tf_op jit(solution)/shard_map/all_to_all | solution.py:284
  142.5 1.1 broadcast_in_dim.3
  143.6 4.0 %all-to-all-start.3 = ((bf16[32,2,32,256]{3,2,1,0:T(8,128)(2,1)}), bf16[32,2,32,256]{3,2,1,0:T(8,128)(2,1)S(1)}, u32[]{:S(2)}, u32[]{:S(2)}) async-start(bf16[32,2,32,256]{3,2,1,0:T(8,128)(2,1)} %broadcast_in_dim.3), calls=%async_computation.3 | async-start | bytes 2097152 | tf_op jit(solution)/shard_map/all_to_all | solution.py:297
  147.6 1.7 return_add.1
  149.3 15.6 %all-to-all-done.3.chunks = bf16[32,2,32,256]{3,2,1,0:T(8,128)(2,1)S(1)} async-done(((bf16[32,2,32,256]{3,2,1,0:T(8,128)(2,1)}), bf16[32,2,32,256]{3,2,1,0:T(8,128)(2,1)S(1)}, u32[]{:S(2)}, u32[]{:S(2)}) %all-to-all-start.3) | async-done | bytes 1048608 | tf_op jit(solution)/shard_map/all_to_all | solution.py:297
  164.9 1.3 unpack.1
  (23 shorter events, 0.0 us)
Async XLA Ops:
  0.6 12.4 %copy-start = (bf16[27,64,256]{2,1,0:T(8,128)(2,1)S(1)}, bf16[27,64,256]{2,1,0:T(8,128)(2,1)}, u32[]{:S(2)}) copy-start(bf16[27,64,256]{2,1,0:T(8,128)(2,1)} %conv_weight.1) | copy-start | bytes 2654212
  0.6 1.0 copy-start.1
  1.7 0.7 copy-start.5
  2.3 0.7 copy-start.7
  3.0 10.1 %copy-start.4 = (bf16[64,256]{1,0:T(8,128)(2,1)S(1)}, bf16[64,256]{1,0:T(8,128)(2,1)}, u32[]{:S(2)}) copy-start(bf16[64,256]{1,0:T(8,128)(2,1)} %coarse_weight.1) | copy-start | bytes 98308
  4.5 25.7 %all-to-all-start = ((bf16[32,64,128]{2,1,0:T(8,128)(2,1)}), bf16[32,64,128]{2,1,0:T(8,128)(2,1)S(1)}, u32[]{:S(2)}, u32[]{:S(2)}) async-start(bf16[32,64,128]{2,1,0:T(8,128)(2,1)} %pack.1), calls=%async_computation | async-start | bytes 1048576 | tf_op jit(solution)/shard_map/all_to_all | solution.py:230
  13.1 6.2 %copy-start.15 = (s32[27,16]{0,1:T(8,128)S(1)}, s32[27,16]{0,1:T(8,128)}, u32[]{:S(2)}) copy-start(s32[27,16]{0,1:T(8,128)} %param.13) | copy-start | bytes 5188
  13.4 16.8 %copy-start.2 = (bf16[64,2048]{1,0:T(8,128)(2,1)S(1)}, bf16[64,2048]{1,0:T(8,128)(2,1)}, u32[]{:S(2)}) copy-start(bf16[64,2048]{1,0:T(8,128)(2,1)} %features.5) | copy-start | bytes 786436
  13.5 9.7 %collective-permute-start = (bf16[14,64,128]{2,1,0:T(8,128)(2,1)S(1)}, bf16[14,64,128]{2,1,0:T(8,128)(2,1)S(1)}, u32[]{:S(2)}, u32[]{:S(2)}) collective-permute-start(bf16[14,64,128]{2,1,0:T(8,128)(2,1)S(1)} %get-tuple-element.30), channel_id=1, source_target_pairs={{0,1},{1,2},{2,3},{3,0},{4,5},{5,6},{6,7},{7,4},{8,9},{9,10},{10,1... | collective-permute-start | bytes 688136 | tf_op jit(solution)/shard_map/ppermute | solution.py:213
  15.2 13.7 %collective-permute-start.1 = (bf16[14,64,128]{2,1,0:T(8,128)(2,1)S(1)}, bf16[14,64,128]{2,1,0:T(8,128)(2,1)S(1)}, u32[]{:S(2)}, u32[]{:S(2)}) collective-permute-start(bf16[14,64,128]{2,1,0:T(8,128)(2,1)S(1)} %get-tuple-element.29), channel_id=1, source_target_pairs={{0,2},{1,3},{2,0},{3,1},{4,6},{5,7},{6,4},{7,5},{8,10},{9,11},{10,... | collective-permute-start | bytes 688136 | tf_op jit(solution)/shard_map/ppermute | solution.py:213
  18.5 10.4 %collective-permute-start.2 = (bf16[14,64,128]{2,1,0:T(8,128)(2,1)S(1)}, bf16[14,64,128]{2,1,0:T(8,128)(2,1)S(1)}, u32[]{:S(2)}, u32[]{:S(2)}) collective-permute-start(bf16[14,64,128]{2,1,0:T(8,128)(2,1)S(1)} %get-tuple-element.28), channel_id=1, source_target_pairs={{0,3},{1,0},{2,1},{3,2},{4,7},{5,4},{6,5},{7,6},{8,11},{9,8},{10,9... | collective-permute-start | bytes 688136 | tf_op jit(solution)/shard_map/ppermute | solution.py:213
  29.3 0.9 copy-start.9
  30.2 1.2 copy-start.10
  31.4 22.8 %copy-start.3 = (bf16[64,2048]{1,0:T(8,128)(2,1)S(1)}, bf16[64,2048]{1,0:T(8,128)(2,1)}, u32[]{:S(2)}) copy-start(bf16[64,2048]{1,0:T(8,128)(2,1)} %out_grad.1) | copy-start | bytes 786436
  36.3 9.1 %collective-permute-start.3 = (bf16[64,2048]{1,0:T(8,128)(2,1)S(1)}, bf16[64,2048]{1,0:T(8,128)(2,1)S(1)}, u32[]{:S(2)}, u32[]{:S(2)}) collective-permute-start(bf16[64,2048]{1,0:T(8,128)(2,1)S(1)} %get-tuple-element.18), channel_id=1, source_target_pairs={{0,3},{1,0},{2,1},{3,2},{4,7},{5,4},{6,5},{7,6},{8,11},{9,8},{10,9... | collective-permute-start | bytes 786440 | tf_op jit(solution)/shard_map/ppermute | solution.py:213
  38.8 8.6 %collective-permute-start.4 = (bf16[64,2048]{1,0:T(8,128)(2,1)S(1)}, bf16[64,2048]{1,0:T(8,128)(2,1)S(1)}, u32[]{:S(2)}, u32[]{:S(2)}) collective-permute-start(bf16[64,2048]{1,0:T(8,128)(2,1)S(1)} %get-tuple-element.19), channel_id=1, source_target_pairs={{0,2},{1,3},{2,0},{3,1},{4,6},{5,7},{6,4},{7,5},{8,10},{9,11},{10,... | collective-permute-start | bytes 786440 | tf_op jit(solution)/shard_map/ppermute | solution.py:213
  39.3 14.8 %collective-permute-start.5 = (bf16[64,2048]{1,0:T(8,128)(2,1)S(1)}, bf16[64,2048]{1,0:T(8,128)(2,1)S(1)}, u32[]{:S(2)}, u32[]{:S(2)}) collective-permute-start(bf16[64,2048]{1,0:T(8,128)(2,1)S(1)} %get-tuple-element.20), channel_id=1, source_target_pairs={{0,1},{1,2},{2,3},{3,0},{4,5},{5,6},{6,7},{7,4},{8,9},{9,10},{10,1... | collective-permute-start | bytes 786440 | tf_op jit(solution)/shard_map/ppermute | solution.py:213
  55.1 14.2 %collective-permute-start.6 = (bf16[64,2048]{1,0:T(8,128)(2,1)S(1)}, bf16[64,2048]{1,0:T(8,128)(2,1)S(1)}, u32[]{:S(2)}, u32[]{:S(2)}) collective-permute-start(bf16[64,2048]{1,0:T(8,128)(2,1)S(1)} %get-tuple-element.23.grad0), channel_id=1, source_target_pairs={{0,1},{1,2},{2,3},{3,0},{4,5},{5,6},{6,7},{7,4},{8,9},{9,10},{10,1... | collective-permute-start | bytes 786440 | tf_op jit(solution)/shard_map/ppermute | solution.py:213
  55.1 14.2 %collective-permute-start.7 = (bf16[64,2048]{1,0:T(8,128)(2,1)S(1)}, bf16[64,2048]{1,0:T(8,128)(2,1)S(1)}, u32[]{:S(2)}, u32[]{:S(2)}) collective-permute-start(bf16[64,2048]{1,0:T(8,128)(2,1)S(1)} %get-tuple-element.23.grad0), channel_id=1, source_target_pairs={{0,2},{1,3},{2,0},{3,1},{4,6},{5,7},{6,4},{7,5},{8,10},{9,11},{10,... | collective-permute-start | bytes 786440 | tf_op jit(solution)/shard_map/ppermute | solution.py:213
  55.6 14.0 %collective-permute-start.8 = (bf16[64,2048]{1,0:T(8,128)(2,1)S(1)}, bf16[64,2048]{1,0:T(8,128)(2,1)S(1)}, u32[]{:S(2)}, u32[]{:S(2)}) collective-permute-start(bf16[64,2048]{1,0:T(8,128)(2,1)S(1)} %get-tuple-element.23.grad0), channel_id=1, source_target_pairs={{0,3},{1,0},{2,1},{3,2},{4,7},{5,4},{6,5},{7,6},{8,11},{9,8},{10,9... | collective-permute-start | bytes 786440 | tf_op jit(solution)/shard_map/ppermute | solution.py:213
  69.3 6.3 %copy-start.11 = (bf16[64,2048]{1,0:T(8,128)(2,1)}, bf16[64,2048]{1,0:T(8,128)(2,1)S(1)}, u32[]{:S(2)}) copy-start(bf16[64,2048]{1,0:T(8,128)(2,1)S(1)} %collective-permute-done.7.grad2) | copy-start | bytes 786436
  69.7 6.0 %copy-start.13 = (bf16[64,2048]{1,0:T(8,128)(2,1)}, bf16[64,2048]{1,0:T(8,128)(2,1)S(1)}, u32[]{:S(2)}) copy-start(bf16[64,2048]{1,0:T(8,128)(2,1)S(1)} %collective-permute-done.8.grad3) | copy-start | bytes 786436
  75.7 9.9 %copy-start.12 = (bf16[64,2048]{1,0:T(8,128)(2,1)S(1)}, bf16[64,2048]{1,0:T(8,128)(2,1)}, u32[]{:S(2)}) copy-start(bf16[64,2048]{1,0:T(8,128)(2,1)} %copy-done.11) | copy-start | bytes 786436
  75.7 9.9 %copy-start.14 = (bf16[64,2048]{1,0:T(8,128)(2,1)S(1)}, bf16[64,2048]{1,0:T(8,128)(2,1)}, u32[]{:S(2)}) copy-start(bf16[64,2048]{1,0:T(8,128)(2,1)} %copy-done.13) | copy-start | bytes 786436
  75.7 47.8 %all-to-all-start.2 = ((bf16[128,32,128]{2,1,0:T(8,128)(2,1)}), bf16[128,32,128]{2,1,0:T(8,128)(2,1)S(1)}, u32[]{:S(2)}, u32[]{:S(2)}) async-start(bf16[128,32,128]{2,1,0:T(8,128)(2,1)} %bitcast.1), calls=%async_computation.2 | async-start | bytes 2097152 | tf_op jit(solution)/shard_map/all_to_all | solution.py:271
  123.5 19.0 %all-to-all-start.1 = ((bf16[32,64,128]{2,1,0:T(8,128)(2,1)}), bf16[32,64,128]{2,1,0:T(8,128)(2,1)S(1)}, u32[]{:S(2)}, u32[]{:S(2)}) async-start(bf16[32,64,128]{2,1,0:T(8,128)(2,1)} %get-tuple-element.25), calls=%async_computation.1 | async-start | bytes 1048576 | tf_op jit(solution)/shard_map/all_to_all | solution.py:284
  131.2 16.5 %copy-start.6 = (s32[1,32]{1,0:T(1,128)S(1)}, s32[1,32]{1,0:T(1,128)}, u32[]{:S(2)}) copy-start(s32[1,32]{1,0:T(1,128)} %send_block.3) | copy-start | bytes 388
  131.2 16.5 %copy-start.8 = (s32[1,32]{1,0:T(1,128)S(1)}, s32[1,32]{1,0:T(1,128)}, u32[]{:S(2)}) copy-start(s32[1,32]{1,0:T(1,128)} %send_count.3) | copy-start | bytes 388
  143.6 21.3 %all-to-all-start.3 = ((bf16[32,2,32,256]{3,2,1,0:T(8,128)(2,1)}), bf16[32,2,32,256]{3,2,1,0:T(8,128)(2,1)S(1)}, u32[]{:S(2)}, u32[]{:S(2)}) async-start(bf16[32,2,32,256]{3,2,1,0:T(8,128)(2,1)} %broadcast_in_dim.3), calls=%async_computation.3 | async-start | bytes 2097152 | tf_op jit(solution)/shard_map/all_to_all | solution.py:297

commit v2 on v1

--- a/solution.py
+++ b/solution.py
@@ -90,7 +90,7 @@
             gathered[rows, block * BLOCK : (block + 1) * BLOCK] = picked
         return carry
 
-    lax.fori_loop(0, OFFSETS, step, 0)
+    lax.fori_loop(0, OFFSETS, step, 0, unroll=27)
     mean = mean_matrix()
     for block in range(nblocks):
         pooled = jnp.dot(table[block], mean, preferred_element_type=F32).astype(BF)
@@ -145,7 +145,7 @@
         parts[spare] = jnp.zeros(parts.shape[1:], BF)
 
 
-def table_kernel(neighbour, weight_t, grad0, grad1, grad2, grad3, local, returned, total):
+def table_kernel(neighbour, weight_t, grad0, grad1, grad2, grad3, local, returned, total, spread):
     quarter, row_count = grad0.shape
     nblocks = row_count // BLOCK
     extent = nblocks + returned.shape[0]
@@ -154,17 +154,18 @@
     for tile in range(nblocks // 2):
         cut = slice(tile * 256, (tile + 1) * 256)
         tall = jnp.concatenate([g[:, cut] for g in (grad0, grad1, grad2, grad3)], axis=0)
-
-        def step(offset, carry, tall=tall, tile=tile):
+        product = jnp.dot(weight_t[...], tall, preferred_element_type=F32)
+        spread[...] = product[: OFFSETS * quarter]
+
+        def step(offset, carry, tile=tile):
             rows = pl.ds(pl.multiple_of(offset * quarter, quarter), quarter)
-            product = jnp.dot(weight_t[rows, :], tall, preferred_element_type=F32)
             for side in range(2):
                 place = slot(neighbour, offset, 2 * tile + side, extent)
-                total[place] += product[:, side * BLOCK : (side + 1) * BLOCK]
+                total[place] += spread[rows, side * BLOCK : (side + 1) * BLOCK]
             return carry
 
-        lax.fori_loop(0, OFFSETS, step, 0)
-        coarse = jnp.dot(weight_t[OFFSETS * quarter :, :], tall, preferred_element_type=F32)
+        lax.fori_loop(0, OFFSETS, step, 0, unroll=27)
+        coarse = product[OFFSETS * quarter :]
         for side in range(2):
             value = coarse[:, side * BLOCK : (side + 1) * BLOCK]
             high = value.astype(BF)
@@ -195,13 +196,12 @@
         chunk[side] = jnp.concatenate([total[c, :, cut] for c in range(4)], axis=1).astype(BF)
 
 
-def unpack_kernel(chunks, conv_grad, coarse_grad):
-    half = chunks.shape[2]
-    for piece in range(2 * PAIRS):
-        rows = slice((piece % 2) * half, (piece % 2 + 1) * half)
-        for side in range(2):
-            offset = 2 * (piece // 2) + side
-            value = chunks[piece, side].astype(F32)
+def unpack_kernel(core, mine, other, conv_grad, coarse_grad):
+    half = mine.shape[2]
+    for chunks, side in ((mine, core[0]), (other, 1 - core[0])):
+        rows = pl.ds(pl.multiple_of(side * half, half), half)
+        for offset in range(TERMS):
+            value = chunks[offset // 2, offset % 2].astype(F32)
             if offset < OFFSETS:
                 conv_grad[offset, rows, :] = value
             else:
@@ -277,7 +277,7 @@
         "table_grad",
         [shape(wide, F32), shape((n_morton, quarter, BLOCK), BF)],
         "svvvvv",
-        [pltpu.VMEM((extent + 1, quarter, BLOCK), F32)],
+        [pltpu.VMEM((extent + 1, quarter, BLOCK), F32), pltpu.VMEM((OFFSETS * quarter, 256), F32)],
         flops,
         4 << 20,
     )(neighbour, weight_t, *grads)
@@ -294,16 +294,25 @@
         "v",
         size=1 << 20,
     )(received)
-    chunks = lax.all_to_all(
-        jnp.broadcast_to(chunk, (n_morton,) + chunk.shape), "morton", 0, 0, tiled=True
-    )
+    chips = n_morton // 2
+    same_core = [[2 * chip + core for chip in range(chips)] for core in range(2)]
+    mine = lax.all_to_all(
+        jnp.broadcast_to(chunk, (chips,) + chunk.shape),
+        "morton",
+        0,
+        0,
+        axis_index_groups=same_core,
+        tiled=True,
+    )
+    other = lax.ppermute(mine, "morton", [(i, i ^ 1) for i in range(n_morton)])
+    core = lax.rem(lax.axis_index("morton"), 2).astype(jnp.int32).reshape(1)
     conv_grad, coarse_grad = call(
         unpack_kernel,
         "unpack",
         [shape((OFFSETS, quarter, channels), F32), shape((quarter, channels), F32)],
-        "v",
+        "svv",
         size=3 << 20,
-    )(chunks)
+    )(core, mine, other)
     return output, input_grad, conv_grad, coarse_grad
 
 

time: 167 us -> 141 us (0.84)
  blocking collectives: 0 us -> 42.3 us
  Pallas kernels: 55.2 us -> 19.2 us
  starting transfers between devices: 41.5 us -> 25.7 us
  waiting for transfers between devices: 63.1 us -> 47.7 us
    all_to_all x0 -> x2, blocking collectives: none -> 42.3 us  [the longest x1 29.1 us: local_step(): lax.all_to_all(parts.reshape(n_morton * 4, quarter // 2, BLOCK), ('morton...]
    pallas_call x1, Pallas kernels: 38 us -> 6.49 us  [local_step(): call(table_kernel, 'table_grad', [shape(wide, F32), shape((n_morton, quar...]
    all_to_all x2 -> x0, waiting for transfers between devices: 15.6 us -> none  [the longest x1 15.6 us: local_step(): lax.all_to_all(jnp.broadcast_to(chunk, (n_morton,) + chunk.shape), 'morto...]
    all_to_all x2 -> x0, starting transfers between devices: 13.9 us -> none  [the longest x1 9.85 us: local_step(): lax.all_to_all(parts.reshape(n_morton * 4, quarter // 2, BLOCK), ('morton...]
    all_to_all x1, starting transfers between devices: 7.41 us -> 3.68 us  [local_step(): returned = lax.all_to_all(outward, 'morton', 0, 0, tiled=True)]
    pallas_call x1, Pallas kernels: 6 us -> 3.25 us  [local_step(): call(weight_kernel, 'weight_grad', shape((n_morton, 4, quarter // 2, BLOC...]
    ppermute x0 -> x1, starting transfers between devices: none -> 1.88 us  [local_step(): other = lax.ppermute(mine, 'morton', [(i, i ^ 1) for i in range(n_morton)])]
    pallas_call x1, Pallas kernels: 4.91 us -> 3.15 us  [local_step(): call(forward_kernel, 'forward', [shape(wide, F32)] + [shape(wide, BF)] *...]
  transfers between devices with their start and end apart: 13 -> 12, of which waited for: 9 -> 8; matrix products, arithmetic and copies ran while one was open for 0% -> 0% of each run, Pallas kernels for 24% -> 6%
where the time goes in v2:
time: 141 us; the launch traced here: 140 us
  waiting for transfers between devices  47.7 us (34%)
  blocking collectives  42.3 us (30%)
  starting transfers between devices  25.7 us (18%)
  Pallas kernels  19.2 us (14%)
  local copies, waits for them, and re-layouts  4.66 us (3%)
    ppermute x9, waiting for transfers between devices, shift(): lax.ppermute(value, axis, [(i, (i + step) % size) for i in range(size)])  36.2 us
    all_to_all x1, blocking collectives, local_step(): lax.all_to_all(parts.reshape(n_morton * 4, quarter // 2, BLOCK), ('morton...  29.1 us
    all_to_all x1, blocking collectives, local_step(): lax.all_to_all(jnp.broadcast_to(chunk, (chips,) + chunk.shape), 'morton',...  13.2 us
    ppermute x9, starting transfers between devices, shift(): lax.ppermute(value, axis, [(i, (i + step) % size) for i in range(size)])  11.6 us
    all_to_all x1, waiting for transfers between devices, local_step(): returned = lax.all_to_all(outward, 'morton', 0, 0, tiled=True)  11.5 us
    all_to_all x1, starting transfers between devices, local_step(): incoming = lax.all_to_all(outgoing, 'morton', 0, 0, tiled=True)  8.59 us
    pallas_call x1, Pallas kernels, local_step(): call(table_kernel, 'table_grad', [shape(wide, F32), shape((n_morton, quar...  6.49 us
    unnamed x25, local copies, waits for them, and re-layouts  4.55 us
  transfers between devices with their start and end apart: 12, of which 8 were waited for; matrix products, arithmetic and copies ran while one was open for 0% of the time, Pallas kernels for 6%

profile of v2, /device:TPU:1, one launch (start us, length us, event | category | flops | bytes accessed | tf_op | source)
XLA Modules:
  0.0 140.3 jit_solution(589124827439959520)
XLA Ops:
  0.6 0.0 copy-start.1
  0.7 1.0 copy-done.1
  1.7 0.7 copy-done.5
  2.3 0.7 copy-done.7
  3.0 1.5 %pack.1 = bf16[32,64,128]{2,1,0:T(8,128)(2,1)} custom-call(s32[1,32]{1,0:T(1,128)S(1)} %copy-done.5, s32[1,32]{1,0:T(1,128)S(1)} %copy-done.7, bf16[64,2048]{1,0:T(8,128)(2,1)S(1)} %copy-done.1), custom_call_target="tpu_custom_call" | custom-call | bytes 1048576 | tf_op jit(solution)/shard_map/pack/pallas_call | solution.py:227
  4.5 8.6 %all-to-all-start = ((bf16[32,64,128]{2,1,0:T(8,128)(2,1)}), bf16[32,64,128]{2,1,0:T(8,128)(2,1)S(1)}, u32[]{:S(2)}, u32[]{:S(2)}) async-start(bf16[32,64,128]{2,1,0:T(8,128)(2,1)} %pack.1), calls=%async_computation | async-start | bytes 1048576 | tf_op jit(solution)/shard_map/all_to_all | solution.py:230
  13.1 0.0 copy-start.11
  13.1 0.3 split.1
  13.4 0.0 copy-start.2
  13.4 0.1 fusion
  13.5 1.7 %collective-permute-start = (bf16[14,64,128]{2,1,0:T(8,128)(2,1)S(1)}, bf16[14,64,128]{2,1,0:T(8,128)(2,1)S(1)}, u32[]{:S(2)}, u32[]{:S(2)}) collective-permute-start(bf16[14,64,128]{2,1,0:T(8,128)(2,1)S(1)} %get-tuple-element.30), channel_id=1, source_target_pairs={{0,1},{1,2},{2,3},{3,0},{4,5},{5,6},{6,7},{7,4},{8,9},{9,10},{10,1... | collective-permute-start | bytes 688136 | tf_op jit(solution)/shard_map/ppermute | solution.py:213
  15.2 3.3 %collective-permute-start.1 = (bf16[14,64,128]{2,1,0:T(8,128)(2,1)S(1)}, bf16[14,64,128]{2,1,0:T(8,128)(2,1)S(1)}, u32[]{:S(2)}, u32[]{:S(2)}) collective-permute-start(bf16[14,64,128]{2,1,0:T(8,128)(2,1)S(1)} %get-tuple-element.29), channel_id=1, source_target_pairs={{0,2},{1,3},{2,0},{3,1},{4,6},{5,7},{6,4},{7,5},{8,10},{9,11},{10,... | collective-permute-start | bytes 688136 | tf_op jit(solution)/shard_map/ppermute | solution.py:213
  18.5 0.7 collective-permute-start.2
  19.2 0.1 copy.11.neighbour
  19.3 3.8 %collective-permute-done.piece1 = bf16[14,64,128]{2,1,0:T(8,128)(2,1)S(1)} collective-permute-done((bf16[14,64,128]{2,1,0:T(8,128)(2,1)S(1)}, bf16[14,64,128]{2,1,0:T(8,128)(2,1)S(1)}, u32[]{:S(2)}, u32[]{:S(2)}) %collective-permute-start) | collective-permute-done | bytes 229408 | tf_op jit(solution)/shard_map/ppermute | solution.py:213
  23.2 5.8 %collective-permute-done.1.piece2 = bf16[14,64,128]{2,1,0:T(8,128)(2,1)S(1)} collective-permute-done((bf16[14,64,128]{2,1,0:T(8,128)(2,1)S(1)}, bf16[14,64,128]{2,1,0:T(8,128)(2,1)S(1)}, u32[]{:S(2)}, u32[]{:S(2)}) %collective-permute-start.1) | collective-permute-done | bytes 229408 | tf_op jit(solution)/shard_map/ppermute | solution.py:213
  28.9 0.0 collective-permute-done.2.piece3
  28.9 0.3 join.1
  29.3 0.0 copy-start.9
  29.3 0.9 copy-done.9
  30.2 0.0 all-to-all-done.incoming
  30.2 1.2 copy-done.10
  31.4 3.2 %forward.1 = (f32[64,2048]{1,0:T(8,128)S(1)}, bf16[64,2048]{1,0:T(8,128)(2,1)S(1)}, bf16[64,2048]{1,0:T(8,128)(2,1)S(1)}, bf16[64,2048]{1,0:T(8,128)(2,1)S(1)}) custom-call(s32[27,16]{1,0:T(8,128)S(1)} %copy.11.neighbour, bf16[64,2048]{1,0:T(8,128)(2,1)S(1)} %copy-done.2, bf16[32,64,128]{2,1,0:T(8,128)(2,1)S(1)} %all-to-all-done.incoming, ...), custom_call_target="tpu_custom_call" | custom-call | flops 1879048192 | bytes 4194304 | tf_op jit(solution)/shard_map/forward/pallas_call | solution.py:247
  34.6 2.5 %collective-permute-start.3 = (bf16[64,2048]{1,0:T(8,128)(2,1)S(1)}, bf16[64,2048]{1,0:T(8,128)(2,1)S(1)}, u32[]{:S(2)}, u32[]{:S(2)}) collective-permute-start(bf16[64,2048]{1,0:T(8,128)(2,1)S(1)} %get-tuple-element.18), channel_id=1, source_target_pairs={{0,3},{1,0},{2,1},{3,2},{4,7},{5,4},{6,5},{7,6},{8,11},{9,8},{10,9... | collective-permute-start | bytes 786440 | tf_op jit(solution)/shard_map/ppermute | solution.py:213
  37.1 0.5 collective-permute-start.4
  37.6 0.2 collective-permute-start.5
  37.7 5.9 %collective-permute-done.3.part1 = bf16[64,2048]{1,0:T(8,128)(2,1)S(1)} collective-permute-done((bf16[64,2048]{1,0:T(8,128)(2,1)S(1)}, bf16[64,2048]{1,0:T(8,128)(2,1)S(1)}, u32[]{:S(2)}, u32[]{:S(2)}) %collective-permute-start.3) | collective-permute-done | bytes 262176 | tf_op jit(solution)/shard_map/ppermute | solution.py:213
  43.6 2.1 %collective-permute-done.4.part2 = bf16[64,2048]{1,0:T(8,128)(2,1)S(1)} collective-permute-done((bf16[64,2048]{1,0:T(8,128)(2,1)S(1)}, bf16[64,2048]{1,0:T(8,128)(2,1)S(1)}, u32[]{:S(2)}, u32[]{:S(2)}) %collective-permute-start.4) | collective-permute-done | bytes 262176 | tf_op jit(solution)/shard_map/ppermute | solution.py:213
  45.7 6.7 %collective-permute-done.5.part3 = bf16[64,2048]{1,0:T(8,128)(2,1)S(1)} collective-permute-done((bf16[64,2048]{1,0:T(8,128)(2,1)S(1)}, bf16[64,2048]{1,0:T(8,128)(2,1)S(1)}, u32[]{:S(2)}, u32[]{:S(2)}) %collective-permute-start.5) | collective-permute-done | bytes 262176 | tf_op jit(solution)/shard_map/ppermute | solution.py:213
  52.4 0.9 activation.1
  53.3 0.0 collective-permute-start.6
  53.3 0.5 collective-permute-start.7
  53.9 2.2 %collective-permute-start.8 = (bf16[64,2048]{1,0:T(8,128)(2,1)S(1)}, bf16[64,2048]{1,0:T(8,128)(2,1)S(1)}, u32[]{:S(2)}, u32[]{:S(2)}) collective-permute-start(bf16[64,2048]{1,0:T(8,128)(2,1)S(1)} %get-tuple-element.23.grad0), channel_id=1, source_target_pairs={{0,3},{1,0},{2,1},{3,2},{4,7},{5,4},{6,5},{7,6},{8,11},{9,8},{10,9... | collective-permute-start | bytes 786440 | tf_op jit(solution)/shard_map/ppermute | solution.py:213
  56.0 11.5 %collective-permute-done.6.grad1 = bf16[64,2048]{1,0:T(8,128)(2,1)S(1)} collective-permute-done((bf16[64,2048]{1,0:T(8,128)(2,1)S(1)}, bf16[64,2048]{1,0:T(8,128)(2,1)S(1)}, u32[]{:S(2)}, u32[]{:S(2)}) %collective-permute-start.6) | collective-permute-done | bytes 262176 | tf_op jit(solution)/shard_map/ppermute | solution.py:213
  67.6 0.0 collective-permute-done.7.grad2
  67.6 0.3 collective-permute-done.8.grad3
  67.9 3.3 %weight_grad.1 = bf16[32,4,32,128]{3,2,1,0:T(8,128)(2,1)S(1)} custom-call(s32[1]{0:T(128)} %bitcast.place, s32[27,16]{1,0:T(8,128)S(1)} %copy.11.neighbour, bf16[64,2048]{1,0:T(8,128)(2,1)S(1)} %copy-done.2, bf16[32,64,128]{2,1,0:T(8,128)(2,1)S(1)} %all-to-all-done.incoming, bf16[64,2048]{1,0:T(8,128)(2,1)S(1)} %get-tuple-element.23.grad0, ...), custom_call_target="tpu_custom_call" | custom-call | flops 1879048192 | bytes 4194304 | tf_op jit(solution)/shard_map/weight_grad/pallas_call | solution.py:262
  71.2 29.1 %all_to_all.20 = bf16[128,32,128]{2,1,0:T(8,128)(2,1)S(1)} all-to-all(bf16[128,32,128]{2,1,0:T(8,128)(2,1)S(1)} %bitcast.5), channel_id=1, replica_groups=mesh['morton'=32,'chan'=4] {'morton','chan'}, dimensions={0} | all-to-all | bytes 2097152 | tf_op jit(solution)/shard_map/all_to_all | solution.py:271
  100.2 0.2 sum_parts.1
  100.5 0.1 broadcast_in_dim.3
  100.5 13.2 %all_to_all.21.mine = bf16[16,2,32,256]{3,2,1,0:T(8,128)(2,1)S(1)} all-to-all(bf16[16,2,32,256]{3,2,1,0:T(8,128)(2,1)S(1)} %broadcast_in_dim.3), channel_id=1, replica_groups={{0,8,16,24,32,40,48,56,64,72,80,88,96,104,112,120},{4,12,20,28,36,44,52..., dimensions={0} | all-to-all | bytes 1048576 | tf_op jit(solution)/shard_map/all_to_all | solution.py:299
  113.7 1.9 %collective-permute-start.9 = (bf16[16,2,32,256]{3,2,1,0:T(8,128)(2,1)S(1)}, bf16[16,2,32,256]{3,2,1,0:T(8,128)(2,1)S(1)}, u32[]{:S(2)}, u32[]{:S(2)}) collective-permute-start(bf16[16,2,32,256]{3,2,1,0:T(8,128)(2,1)S(1)} %all_to_all.21.mine), channel_id=1, source_target_pairs={{0,4},{4,0},{8,12},{12,8},{16,20},{20,16},{24,28},{28,24},{32,36},... | collective-permute-start | bytes 1572872 | tf_op jit(solution)/shard_map/ppermute | solution.py:307
  115.6 6.5 %table_grad.1 = (f32[64,2048]{1,0:T(8,128)S(1)}, bf16[32,64,128]{2,1,0:T(8,128)(2,1)}) custom-call(s32[27,16]{1,0:T(8,128)S(1)} %copy.11.neighbour, bf16[1792,256]{1,0:T(8,128)(2,1)S(1)} %get-tuple-element.22.weight_t, bf16[64,2048]{1,0:T(8,128)(2,1)S(1)} %get-tuple-element.23.grad0, bf16[64,2048]{1,0:T(8,128)(2,1)S(1)} %collective-permute-done.6.grad1, ...), custom_call_target="tpu_custom_call" | custom-call | flops 1879048192 | bytes 4194304 | tf_op jit(solution)/shard_map/table_grad/pallas_call | solution.py:275
  122.1 3.7 %all-to-all-start.1 = ((bf16[32,64,128]{2,1,0:T(8,128)(2,1)}), bf16[32,64,128]{2,1,0:T(8,128)(2,1)S(1)}, u32[]{:S(2)}, u32[]{:S(2)}) async-start(bf16[32,64,128]{2,1,0:T(8,128)(2,1)} %get-tuple-element.25), calls=%async_computation.1 | async-start | bytes 1048576 | tf_op jit(solution)/shard_map/all_to_all | solution.py:284
  125.8 11.5 %all-to-all-done.1.returned = bf16[32,64,128]{2,1,0:T(8,128)(2,1)S(1)} async-done(((bf16[32,64,128]{2,1,0:T(8,128)(2,1)}), bf16[32,64,128]{2,1,0:T(8,128)(2,1)S(1)}, u32[]{:S(2)}, u32[]{:S(2)}) %all-to-all-start.1) | async-done | bytes 524320 | tf_op jit(solution)/shard_map/all_to_all | solution.py:284
  137.3 1.7 %return_add.1 = f32[64,2048]{1,0:T(8,128)} custom-call(s32[1,32]{1,0:T(1,128)S(1)} %copy-done.6, s32[1,32]{1,0:T(1,128)S(1)} %copy-done.8, f32[64,2048]{1,0:T(8,128)S(1)} %get-tuple-element.24.local, bf16[32,64,128]{2,1,0:T(8,128)(2,1)S(1)} %all-to-all-done.1.returned), custom_call_target="tpu_custom_call" | custom-call | bytes 2097152 | tf_op jit(solution)/shard_map/return_add/pallas_call | solution.py:285
  139.0 0.0 collective-permute-done.9.other
  139.0 1.3 unpack.1
  (15 shorter events, 0.0 us)
Async XLA Ops:
  0.6 12.4 %copy-start = (bf16[27,64,256]{2,1,0:T(8,128)(2,1)S(1)}, bf16[27,64,256]{2,1,0:T(8,128)(2,1)}, u32[]{:S(2)}) copy-start(bf16[27,64,256]{2,1,0:T(8,128)(2,1)} %conv_weight.1) | copy-start | bytes 2654212
  0.6 1.0 copy-start.1
  1.7 0.7 copy-start.5
  2.3 0.7 copy-start.7
  3.0 10.1 %copy-start.4 = (bf16[64,256]{1,0:T(8,128)(2,1)S(1)}, bf16[64,256]{1,0:T(8,128)(2,1)}, u32[]{:S(2)}) copy-start(bf16[64,256]{1,0:T(8,128)(2,1)} %coarse_weight.1) | copy-start | bytes 98308
  4.5 25.7 %all-to-all-start = ((bf16[32,64,128]{2,1,0:T(8,128)(2,1)}), bf16[32,64,128]{2,1,0:T(8,128)(2,1)S(1)}, u32[]{:S(2)}, u32[]{:S(2)}) async-start(bf16[32,64,128]{2,1,0:T(8,128)(2,1)} %pack.1), calls=%async_computation | async-start | bytes 1048576 | tf_op jit(solution)/shard_map/all_to_all | solution.py:230
  13.1 6.2 %copy-start.11 = (s32[27,16]{0,1:T(8,128)S(1)}, s32[27,16]{0,1:T(8,128)}, u32[]{:S(2)}) copy-start(s32[27,16]{0,1:T(8,128)} %param.13) | copy-start | bytes 5188
  13.4 16.8 %copy-start.2 = (bf16[64,2048]{1,0:T(8,128)(2,1)S(1)}, bf16[64,2048]{1,0:T(8,128)(2,1)}, u32[]{:S(2)}) copy-start(bf16[64,2048]{1,0:T(8,128)(2,1)} %features.5) | copy-start | bytes 786436
  13.5 9.7 %collective-permute-start = (bf16[14,64,128]{2,1,0:T(8,128)(2,1)S(1)}, bf16[14,64,128]{2,1,0:T(8,128)(2,1)S(1)}, u32[]{:S(2)}, u32[]{:S(2)}) collective-permute-start(bf16[14,64,128]{2,1,0:T(8,128)(2,1)S(1)} %get-tuple-element.30), channel_id=1, source_target_pairs={{0,1},{1,2},{2,3},{3,0},{4,5},{5,6},{6,7},{7,4},{8,9},{9,10},{10,1... | collective-permute-start | bytes 688136 | tf_op jit(solution)/shard_map/ppermute | solution.py:213
  15.2 13.7 %collective-permute-start.1 = (bf16[14,64,128]{2,1,0:T(8,128)(2,1)S(1)}, bf16[14,64,128]{2,1,0:T(8,128)(2,1)S(1)}, u32[]{:S(2)}, u32[]{:S(2)}) collective-permute-start(bf16[14,64,128]{2,1,0:T(8,128)(2,1)S(1)} %get-tuple-element.29), channel_id=1, source_target_pairs={{0,2},{1,3},{2,0},{3,1},{4,6},{5,7},{6,4},{7,5},{8,10},{9,11},{10,... | collective-permute-start | bytes 688136 | tf_op jit(solution)/shard_map/ppermute | solution.py:213
  18.5 10.4 %collective-permute-start.2 = (bf16[14,64,128]{2,1,0:T(8,128)(2,1)S(1)}, bf16[14,64,128]{2,1,0:T(8,128)(2,1)S(1)}, u32[]{:S(2)}, u32[]{:S(2)}) collective-permute-start(bf16[14,64,128]{2,1,0:T(8,128)(2,1)S(1)} %get-tuple-element.28), channel_id=1, source_target_pairs={{0,3},{1,0},{2,1},{3,2},{4,7},{5,4},{6,5},{7,6},{8,11},{9,8},{10,9... | collective-permute-start | bytes 688136 | tf_op jit(solution)/shard_map/ppermute | solution.py:213
  29.3 0.9 copy-start.9
  30.2 1.2 copy-start.10
  31.4 21.0 %copy-start.3 = (bf16[64,2048]{1,0:T(8,128)(2,1)S(1)}, bf16[64,2048]{1,0:T(8,128)(2,1)}, u32[]{:S(2)}) copy-start(bf16[64,2048]{1,0:T(8,128)(2,1)} %out_grad.1) | copy-start | bytes 786436
  34.6 9.0 %collective-permute-start.3 = (bf16[64,2048]{1,0:T(8,128)(2,1)S(1)}, bf16[64,2048]{1,0:T(8,128)(2,1)S(1)}, u32[]{:S(2)}, u32[]{:S(2)}) collective-permute-start(bf16[64,2048]{1,0:T(8,128)(2,1)S(1)} %get-tuple-element.18), channel_id=1, source_target_pairs={{0,3},{1,0},{2,1},{3,2},{4,7},{5,4},{6,5},{7,6},{8,11},{9,8},{10,9... | collective-permute-start | bytes 786440 | tf_op jit(solution)/shard_map/ppermute | solution.py:213
  37.1 8.6 %collective-permute-start.4 = (bf16[64,2048]{1,0:T(8,128)(2,1)S(1)}, bf16[64,2048]{1,0:T(8,128)(2,1)S(1)}, u32[]{:S(2)}, u32[]{:S(2)}) collective-permute-start(bf16[64,2048]{1,0:T(8,128)(2,1)S(1)} %get-tuple-element.19), channel_id=1, source_target_pairs={{0,2},{1,3},{2,0},{3,1},{4,6},{5,7},{6,4},{7,5},{8,10},{9,11},{10,... | collective-permute-start | bytes 786440 | tf_op jit(solution)/shard_map/ppermute | solution.py:213
  37.6 14.8 %collective-permute-start.5 = (bf16[64,2048]{1,0:T(8,128)(2,1)S(1)}, bf16[64,2048]{1,0:T(8,128)(2,1)S(1)}, u32[]{:S(2)}, u32[]{:S(2)}) collective-permute-start(bf16[64,2048]{1,0:T(8,128)(2,1)S(1)} %get-tuple-element.20), channel_id=1, source_target_pairs={{0,1},{1,2},{2,3},{3,0},{4,5},{5,6},{6,7},{7,4},{8,9},{9,10},{10,1... | collective-permute-start | bytes 786440 | tf_op jit(solution)/shard_map/ppermute | solution.py:213
  53.3 14.2 %collective-permute-start.6 = (bf16[64,2048]{1,0:T(8,128)(2,1)S(1)}, bf16[64,2048]{1,0:T(8,128)(2,1)S(1)}, u32[]{:S(2)}, u32[]{:S(2)}) collective-permute-start(bf16[64,2048]{1,0:T(8,128)(2,1)S(1)} %get-tuple-element.23.grad0), channel_id=1, source_target_pairs={{0,1},{1,2},{2,3},{3,0},{4,5},{5,6},{6,7},{7,4},{8,9},{9,10},{10,1... | collective-permute-start | bytes 786440 | tf_op jit(solution)/shard_map/ppermute | solution.py:213
  53.3 14.2 %collective-permute-start.7 = (bf16[64,2048]{1,0:T(8,128)(2,1)S(1)}, bf16[64,2048]{1,0:T(8,128)(2,1)S(1)}, u32[]{:S(2)}, u32[]{:S(2)}) collective-permute-start(bf16[64,2048]{1,0:T(8,128)(2,1)S(1)} %get-tuple-element.23.grad0), channel_id=1, source_target_pairs={{0,2},{1,3},{2,0},{3,1},{4,6},{5,7},{6,4},{7,5},{8,10},{9,11},{10,... | collective-permute-start | bytes 786440 | tf_op jit(solution)/shard_map/ppermute | solution.py:213
  53.9 14.0 %collective-permute-start.8 = (bf16[64,2048]{1,0:T(8,128)(2,1)S(1)}, bf16[64,2048]{1,0:T(8,128)(2,1)S(1)}, u32[]{:S(2)}, u32[]{:S(2)}) collective-permute-start(bf16[64,2048]{1,0:T(8,128)(2,1)S(1)} %get-tuple-element.23.grad0), channel_id=1, source_target_pairs={{0,3},{1,0},{2,1},{3,2},{4,7},{5,4},{6,5},{7,6},{8,11},{9,8},{10,9... | collective-permute-start | bytes 786440 | tf_op jit(solution)/shard_map/ppermute | solution.py:213
  113.7 25.3 %collective-permute-start.9 = (bf16[16,2,32,256]{3,2,1,0:T(8,128)(2,1)S(1)}, bf16[16,2,32,256]{3,2,1,0:T(8,128)(2,1)S(1)}, u32[]{:S(2)}, u32[]{:S(2)}) collective-permute-start(bf16[16,2,32,256]{3,2,1,0:T(8,128)(2,1)S(1)} %all_to_all.21.mine), channel_id=1, source_target_pairs={{0,4},{4,0},{8,12},{12,8},{16,20},{20,16},{24,28},{28,24},{32,36},... | collective-permute-start | bytes 1572872 | tf_op jit(solution)/shard_map/ppermute | solution.py:307
  115.6 21.7 %copy-start.6 = (s32[1,32]{1,0:T(1,128)S(1)}, s32[1,32]{1,0:T(1,128)}, u32[]{:S(2)}) copy-start(s32[1,32]{1,0:T(1,128)} %send_block.3) | copy-start | bytes 388
  115.6 21.7 %copy-start.8 = (s32[1,32]{1,0:T(1,128)S(1)}, s32[1,32]{1,0:T(1,128)}, u32[]{:S(2)}) copy-start(s32[1,32]{1,0:T(1,128)} %send_count.3) | copy-start | bytes 388
  122.1 15.2 %all-to-all-start.1 = ((bf16[32,64,128]{2,1,0:T(8,128)(2,1)}), bf16[32,64,128]{2,1,0:T(8,128)(2,1)S(1)}, u32[]{:S(2)}, u32[]{:S(2)}) async-start(bf16[32,64,128]{2,1,0:T(8,128)(2,1)} %get-tuple-element.25), calls=%async_computation.1 | async-start | bytes 1048576 | tf_op jit(solution)/shard_map/all_to_all | solution.py:284

commit v3 on v2

--- a/solution.py
+++ b/solution.py
@@ -16,7 +16,7 @@
 
 
 def call(kernel, name, outs, kinds, scratch=(), flops=0, size=0, limit=48 << 20):
-    space = {"s": pltpu.SMEM, "v": pltpu.VMEM}
+    space = {"s": pltpu.SMEM, "v": pltpu.VMEM, "a": pl.ANY}
     many = isinstance(outs, (list, tuple))
     spec = pl.BlockSpec(memory_space=pltpu.VMEM)
     return pl.pallas_call(
@@ -41,7 +41,8 @@
     return pl.ds(pl.multiple_of(index * BLOCK, BLOCK), BLOCK)
 
 
-def pack_kernel(send_block, send_count, features, outgoing):
+def pack_kernel(send_block, send_count, features, after, outgoing):
+    del after
     for peer in range(outgoing.shape[0]):
         block = features[:, columns(send_block[0, peer])]
         outgoing[peer] = block * send_count[0, peer].astype(F32).astype(BF)
@@ -80,62 +81,87 @@
     return jnp.where(named < 0, extent, named)
 
 
-def fill_gathered(neighbour, table, gathered, nblocks, extent):
+def fill_gathered(neighbour, table, gathered, first, extent):
     quarter = table.shape[1]
+    nblocks = gathered.shape[1] // BLOCK
 
     def step(offset, carry):
         rows = pl.ds(pl.multiple_of(offset * quarter, quarter), quarter)
         for block in range(nblocks):
-            picked = table[slot(neighbour, offset, block, extent)]
+            picked = table[slot(neighbour, offset, first + block, extent)]
             gathered[rows, block * BLOCK : (block + 1) * BLOCK] = picked
         return carry
 
     lax.fori_loop(0, OFFSETS, step, 0, unroll=27)
     mean = mean_matrix()
     for block in range(nblocks):
-        pooled = jnp.dot(table[block], mean, preferred_element_type=F32).astype(BF)
+        pooled = jnp.dot(table[first + block], mean, preferred_element_type=F32).astype(BF)
         gathered[OFFSETS * quarter :, block * BLOCK : (block + 1) * BLOCK] = pooled
 
 
 def forward_kernel(
-    neighbour, features, incoming, weight, out0, out1, out2, out3, table, gathered
+    half, neighbour, features, incoming, weight, out0, out1, out2, out3, table, gathered
 ):
     quarter, row_count = features.shape
     nblocks = row_count // BLOCK
     extent = nblocks + incoming.shape[0]
     fill_table(features, incoming, table, nblocks)
-    fill_gathered(neighbour, table, gathered, nblocks, extent)
-    for tile in range(row_count // 256):
+    fill_gathered(neighbour, table, gathered, half * nblocks // 2, extent)
+    for tile in range(row_count // 512):
         cut = slice(tile * 256, (tile + 1) * 256)
         total = jnp.dot(weight[...], gathered[:, cut], preferred_element_type=F32)
         for step, out in enumerate((out0, out1, out2, out3)):
             out[:, cut] = total[step * quarter : (step + 1) * quarter].astype(out.dtype)
 
 
-def activation_kernel(own, part1, part2, part3, out_grad, output, grad):
+def activate(own, part1, part2, part3, out_grad):
     pre = (own[...] + part1[...].astype(F32)) + (part2[...].astype(F32) + part3[...].astype(F32))
     sigma = 1.0 / (1.0 + jnp.exp(-pre))
-    output[...] = (pre * sigma).astype(BF)
-    grad[...] = (out_grad[...].astype(F32) * sigma * (1.0 + pre * (1.0 - sigma))).astype(BF)
-
-
-def weight_kernel(
-    place, neighbour, features, incoming, grad0, grad1, grad2, grad3, parts, table, gathered, flipped
-):
-    quarter, row_count = features.shape
-    nblocks = row_count // BLOCK
+    grad = out_grad.astype(F32) * sigma * (1.0 + pre * (1.0 - sigma))
+    return (pre * sigma).astype(BF), grad.astype(BF)
+
+
+def activation_kernel(own, part1, part2, part3, out_grad, output, grad):
+    middle = own.shape[1]
+    output[...], grad[...] = activate(own, part1, part2, part3, out_grad[:, :middle])
+
+
+def activation_end_kernel(own, part1, part2, part3, out_grad, before, output, grad):
+    middle = own.shape[1]
+    output[:, :middle] = before[...]
+    output[:, middle:], grad[...] = activate(own, part1, part2, part3, out_grad[:, middle:])
+
+
+def prepare_weight(half, neighbour, features, incoming, grads, table, gathered, flipped):
+    nblocks = features.shape[1] // BLOCK
     extent = nblocks + incoming.shape[0]
     fill_table(features, incoming, table, nblocks)
-    fill_gathered(neighbour, table, gathered, nblocks, extent)
-    for block in range(nblocks):
+    fill_gathered(neighbour, table, gathered, half * nblocks // 2, extent)
+    for block in range(nblocks // 2):
         cut = slice(block * BLOCK, (block + 1) * BLOCK)
-        tall = jnp.concatenate([g[:, cut] for g in (grad0, grad1, grad2, grad3)], axis=0)
+        tall = jnp.concatenate([g[:, cut] for g in grads], axis=0)
         flipped[cut, :] = tall.T
+
+
+def weight_first_kernel(
+    neighbour, features, incoming, grad0, grad1, grad2, grad3, held, table, gathered, flipped
+):
+    grads = (grad0, grad1, grad2, grad3)
+    prepare_weight(0, neighbour, features, incoming, grads, table, gathered, flipped)
+    held[...] = jnp.dot(gathered[...], flipped[...], preferred_element_type=F32)
+
+
+def weight_second_kernel(
+    place, neighbour, features, incoming, grad0, grad1, grad2, grad3, held, parts, table, gathered, flipped
+):
+    quarter = features.shape[0]
+    grads = (grad0, grad1, grad2, grad3)
+    prepare_weight(1, neighbour, features, incoming, grads, table, gathered, flipped)
     half = quarter // 2
     for pair in range(PAIRS):
         rows = slice(pair * BLOCK, (pair + 1) * BLOCK)
         product = jnp.dot(gathered[rows, :], flipped[...], preferred_element_type=F32)
-        upright = product.T.astype(BF)
+        upright = (product + held[rows, :]).T.astype(BF)
         for step in range(4):
             target = lax.rem(place[0] - step + 4, 4)
             for side in range(2):
@@ -145,15 +171,18 @@
         parts[spare] = jnp.zeros(parts.shape[1:], BF)
 
 
-def table_kernel(neighbour, weight_t, grad0, grad1, grad2, grad3, local, returned, total, spread):
-    quarter, row_count = grad0.shape
+def table_kernel(
+    neighbour, weight_t, g00, g01, g02, g03, g10, g11, g12, g13, local, returned, total, spread
+):
+    quarter, row_count = local.shape
     nblocks = row_count // BLOCK
     extent = nblocks + returned.shape[0]
     total[...] = jnp.zeros_like(total)
     mean = mean_matrix()
     for tile in range(nblocks // 2):
-        cut = slice(tile * 256, (tile + 1) * 256)
-        tall = jnp.concatenate([g[:, cut] for g in (grad0, grad1, grad2, grad3)], axis=0)
+        grads = (g00, g01, g02, g03) if tile < nblocks // 4 else (g10, g11, g12, g13)
+        start = tile % (nblocks // 4) * 256
+        tall = jnp.concatenate([g[:, start : start + 256] for g in grads], axis=0)
         product = jnp.dot(weight_t[...], tall, preferred_element_type=F32)
         spread[...] = product[: OFFSETS * quarter]
 
@@ -185,7 +214,8 @@
         input_grad[:, columns(send_block[0, peer])] += returned[peer].astype(F32) * factor
 
 
-def sum_kernel(scale, parts, chunk):
+def sum_kernel(scale, parts, after, chunk):
+    del after
     quarter = 64
     total = parts[0].astype(F32)
     for source in range(1, parts.shape[0]):
@@ -224,14 +254,14 @@
     place = lax.axis_index("chan").astype(jnp.int32).reshape(1)
     shape = jax.ShapeDtypeStruct
 
-    outgoing = call(
-        pack_kernel, "pack", shape((n_morton, quarter, BLOCK), BF), "ssv", size=1 << 20
-    )(send_block, send_count, features)
-    incoming = lax.all_to_all(outgoing, "morton", 0, 0, tiled=True)
-
     pieces = call(
         split_kernel, "split", shape((4 * PAIRS, quarter, BLOCK), BF), "svv", size=2 << 20
     )(place, conv_weight, coarse_weight)
+    outgoing = call(
+        pack_kernel, "pack", shape((n_morton, quarter, BLOCK), BF), "ssva", size=64 << 20
+    )(send_block, send_count, features, pieces)
+    incoming = lax.all_to_all(outgoing, "morton", 0, 0, tiled=True)
+
     pieces = pieces.reshape(4, PAIRS, quarter, BLOCK)
     weights = [pieces[0]] + [shift(pieces[s], "chan", s) for s in (1, 2, 3)]
     weight, weight_t = call(
@@ -242,32 +272,50 @@
         size=3 << 20,
     )(*weights)
 
-    big = [pltpu.VMEM((extent + 1, quarter, BLOCK), BF), pltpu.VMEM((depth, row_count), BF)]
-    wide = (quarter, row_count)
-    partial = call(
-        forward_kernel,
-        "forward",
-        [shape(wide, F32)] + [shape(wide, BF)] * 3,
-        "svvv",
-        big,
-        flops,
+    middle = row_count // 2
+    big = [pltpu.VMEM((extent + 1, quarter, BLOCK), BF), pltpu.VMEM((depth, middle), BF)]
+    turned = [pltpu.VMEM((middle, channels), BF)]
+    wide, part = (quarter, row_count), (quarter, middle)
+    grads = []
+    output = ()
+    for half in range(2):
+        partial = call(
+            functools.partial(forward_kernel, half),
+            f"forward{half}",
+            [shape(part, F32)] + [shape(part, BF)] * 3,
+            "svvv",
+            big,
+            flops // 2,
+            3 << 20,
+        )(neighbour, features, incoming, weight)
+        arrived = [shift(partial[s], "chan", -s) for s in (1, 2, 3)]
+        output, grad = call(
+            activation_end_kernel if half else activation_kernel,
+            f"activation{half}",
+            [shape(wide if half else part, BF), shape(part, BF)],
+            "vvvvvv" if half else "vvvvv",
+            size=1 << 20,
+        )(partial[0], *arrived, out_grad, *((output,) if half else ()))
+        grads.append([grad] + [shift(grad, "chan", s) for s in (1, 2, 3)])
+
+    held = call(
+        weight_first_kernel,
+        "weight_grad0",
+        shape((depth, channels), F32),
+        "svvvvvv",
+        big + turned,
+        flops // 2,
         4 << 20,
-    )(neighbour, features, incoming, weight)
-    arrived = [shift(partial[s], "chan", -s) for s in (1, 2, 3)]
-    output, grad = call(
-        activation_kernel, "activation", [shape(wide, BF)] * 2, "vvvvv", size=2 << 20
-    )(partial[0], *arrived, out_grad)
-    grads = [grad] + [shift(grad, "chan", s) for s in (1, 2, 3)]
-
+    )(neighbour, features, incoming, *grads[0])
     parts = call(
-        weight_kernel,
-        "weight_grad",
+        weight_second_kernel,
+        "weight_grad1",
         shape((n_morton, 4, quarter // 2, BLOCK), BF),
-        "ssvvvvvv",
-        big + [pltpu.VMEM((row_count, channels), BF)],
-        flops,
+        "ssvvvvvvv",
+        big + turned,
+        flops // 2,
         4 << 20,
-    )(place, neighbour, features, incoming, *grads)
+    )(place, neighbour, features, incoming, *grads[1], held)
     received = lax.all_to_all(
         parts.reshape(n_morton * 4, quarter // 2, BLOCK), ("morton", "chan"), 0, 0, tiled=True
     ).reshape(parts.shape)
@@ -276,11 +324,14 @@
         table_kernel,
         "table_grad",
         [shape(wide, F32), shape((n_morton, quarter, BLOCK), BF)],
-        "svvvvv",
-        [pltpu.VMEM((extent + 1, quarter, BLOCK), F32), pltpu.VMEM((OFFSETS * quarter, 256), F32)],
+        "s" + "v" * 9,
+        [
+            pltpu.VMEM((extent + 1, quarter, BLOCK), F32),
+            pltpu.VMEM((OFFSETS * quarter, 256), F32),
+        ],
         flops,
         4 << 20,
-    )(neighbour, weight_t, *grads)
+    )(neighbour, weight_t, *grads[0], *grads[1])
     returned = lax.all_to_all(outward, "morton", 0, 0, tiled=True)
     input_grad = call(return_kernel, "return_add", shape(wide, F32), "ssvv", size=2 << 20)(
         send_block, send_count, local, returned
@@ -291,9 +342,9 @@
         functools.partial(sum_kernel, scale),
         "sum_parts",
         shape((2, quarter // 2, channels), BF),
-        "v",
+        "va",
         size=1 << 20,
-    )(received)
+    )(received, outward)
     chips = n_morton // 2
     same_core = [[2 * chip + core for chip in range(chips)] for core in range(2)]
     mine = lax.all_to_all(

time: 141 us -> 130 us (0.922)
  blocking collectives: 42.3 us -> 13.2 us
  starting transfers between devices: 25.7 us -> 41.9 us
  waiting for transfers between devices: 47.7 us -> 44.3 us
  Pallas kernels: 19.2 us -> 22.4 us
  local copies, waits for them, and re-layouts: 4.66 us -> 6.72 us
    all_to_all x1 -> x0, blocking collectives: 29.1 us -> none  [local_step(): lax.all_to_all(parts.reshape(n_morton * 4, quarter // 2, BLOCK), ('morton...]
    ppermute x9 -> x15, waiting for transfers between devices: 36.2 us -> 21 us  [shift(): lax.ppermute(value, axis, [(i, (i + step) % size) for i in range(size)])]
    all_to_all x0 -> x1, starting transfers between devices: none -> 12.5 us  [local_step(): lax.all_to_all(parts.reshape(n_morton * 4, quarter // 2, BLOCK), ('morton...]
    all_to_all x0 -> x1, waiting for transfers between devices: none -> 11.8 us  [local_step(): lax.all_to_all(parts.reshape(n_morton * 4, quarter // 2, BLOCK), ('morton...]
    ppermute x9 -> x15, starting transfers between devices: 11.6 us -> 15.2 us  [shift(): lax.ppermute(value, axis, [(i, (i + step) % size) for i in range(size)])]
    pallas_call x4 -> x7, Pallas kernels: 8.82 us -> 12.1 us  [the longest x2 4.25 us: local_step(): call(functools.partial(forward_kernel, half), f'forward{half}', [shape(pa...]
    unnamed x25 -> x23, local copies, waits for them, and re-layouts: 4.55 us -> 6.61 us
  transfers between devices with their start and end apart: 12 -> 19, of which waited for: 8 -> 9; matrix products, arithmetic and copies ran while one was open for 0% -> 0% of each run, Pallas kernels for 6% -> 11%
where the time goes in v3:
time: 130 us; the launch traced here: 129 us
  waiting for transfers between devices  44.3 us (34%)
  starting transfers between devices  41.9 us (32%)
  Pallas kernels  22.4 us (17%)
  blocking collectives  13.2 us (10%)
  local copies, waits for them, and re-layouts  6.72 us (5%)
    ppermute x15, waiting for transfers between devices, shift(): lax.ppermute(value, axis, [(i, (i + step) % size) for i in range(size)])  21 us
    ppermute x15, starting transfers between devices, shift(): lax.ppermute(value, axis, [(i, (i + step) % size) for i in range(size)])  15.2 us
    all_to_all x1, blocking collectives, local_step(): lax.all_to_all(jnp.broadcast_to(chunk, (chips,) + chunk.shape), 'morton',...  13.2 us
    all_to_all x1, starting transfers between devices, local_step(): lax.all_to_all(parts.reshape(n_morton * 4, quarter // 2, BLOCK), ('morton...  12.5 us
    all_to_all x1, waiting for transfers between devices, local_step(): lax.all_to_all(parts.reshape(n_morton * 4, quarter // 2, BLOCK), ('morton...  11.8 us
    all_to_all x1, waiting for transfers between devices, local_step(): returned = lax.all_to_all(outward, 'morton', 0, 0, tiled=True)  11.5 us
    all_to_all x1, starting transfers between devices, local_step(): incoming = lax.all_to_all(outgoing, 'morton', 0, 0, tiled=True)  8.72 us
    unnamed x23, local copies, waits for them, and re-layouts  6.61 us
  transfers between devices with their start and end apart: 19, of which 9 were waited for; matrix products, arithmetic and copies ran while one was open for 0% of the time, Pallas kernels for 11%

profile of v3, /device:TPU:1, one launch (start us, length us, event | category | flops | bytes accessed | tf_op | source)
XLA Modules:
  0.0 129.4 jit_solution(2726350236839089775)
XLA Ops:
  0.7 1.2 copy-done.2
  1.9 0.8 copy-done.3
  2.6 0.3 split.1.after
  2.9 0.3 copy-done.4
  3.3 1.5 %pack.1 = bf16[32,64,128]{2,1,0:T(8,128)(2,1)} custom-call(s32[1,32]{1,0:T(1,128)S(1)} %copy-done.4, s32[1,32]{1,0:T(1,128)S(1)} %copy-done.5, bf16[64,2048]{1,0:T(8,128)(2,1)S(1)} %copy-done.1, bf16[56,64,128]{2,1,0:T(8,128)(2,1)S(1)} %split.1.after), custom_call_target="tpu_custom_call" | custom-call | bytes 67108864 | tf_op jit(solution)/shard_map/pack/pallas_call | solution.py:260
  4.8 8.7 %all-to-all-start = ((bf16[32,64,128]{2,1,0:T(8,128)(2,1)}), bf16[32,64,128]{2,1,0:T(8,128)(2,1)S(1)}, u32[]{:S(2)}, u32[]{:S(2)}) async-start(bf16[32,64,128]{2,1,0:T(8,128)(2,1)} %pack.1), calls=%async_computation | async-start | bytes 1048576 | tf_op jit(solution)/shard_map/all_to_all | solution.py:263
  13.6 3.8 %collective-permute-start.2 = (bf16[14,64,128]{2,1,0:T(8,128)(2,1)S(1)}, bf16[14,64,128]{2,1,0:T(8,128)(2,1)S(1)}, u32[]{:S(2)}, u32[]{:S(2)}) collective-permute-start(bf16[14,64,128]{2,1,0:T(8,128)(2,1)S(1)} %get-tuple-element.40), channel_id=1, source_target_pairs={{0,3},{1,0},{2,1},{3,2},{4,7},{5,4},{6,5},{7,6},{8,11},{9,8},{10,9... | collective-permute-start | bytes 688136 | tf_op jit(solution)/shard_map/ppermute | solution.py:243
  17.4 0.7 collective-permute-start
  18.1 0.1 copy.11.neighbour
  18.2 8.9 %collective-permute-done.2.piece3 = bf16[14,64,128]{2,1,0:T(8,128)(2,1)S(1)} collective-permute-done((bf16[14,64,128]{2,1,0:T(8,128)(2,1)S(1)}, bf16[14,64,128]{2,1,0:T(8,128)(2,1)S(1)}, u32[]{:S(2)}, u32[]{:S(2)}) %collective-permute-start.2) | collective-permute-done | bytes 229408 | tf_op jit(solution)/shard_map/ppermute | solution.py:243
  27.1 3.7 %collective-permute-done.piece1 = bf16[14,64,128]{2,1,0:T(8,128)(2,1)S(1)} collective-permute-done((bf16[14,64,128]{2,1,0:T(8,128)(2,1)S(1)}, bf16[14,64,128]{2,1,0:T(8,128)(2,1)S(1)}, u32[]{:S(2)}, u32[]{:S(2)}) %collective-permute-start) | collective-permute-done | bytes 229408 | tf_op jit(solution)/shard_map/ppermute | solution.py:243
  30.8 0.3 join.1
  31.1 0.9 copy-done.6
  32.1 0.9 copy-done.8
  33.0 1.2 copy-done.9
  34.2 2.1 %forward0.1 = (f32[64,1024]{1,0:T(8,128)S(1)}, bf16[64,1024]{1,0:T(8,128)(2,1)S(1)}, bf16[64,1024]{1,0:T(8,128)(2,1)S(1)}, bf16[64,1024]{1,0:T(8,128)(2,1)S(1)}) custom-call(s32[27,16]{1,0:T(8,128)S(1)} %copy.11.neighbour, bf16[64,2048]{1,0:T(8,128)(2,1)S(1)} %copy-done.1, bf16[32,64,128]{2,1,0:T(8,128)(2,1)S(1)} %all-to-all-done.incoming, ...), custom_call_target="tpu_custom_call" | custom-call | flops 939524096 | bytes 3145728 | tf_op jit(solution)/shard_map/forward0/pallas_call | solution.py:282
  36.3 0.1 collective-permute-start.6
  36.4 0.6 collective-permute-start.7
  37.0 0.8 collective-permute-start.8
  37.8 2.1 %forward1.1 = (f32[64,1024]{1,0:T(8,128)S(1)}, bf16[64,1024]{1,0:T(8,128)(2,1)S(1)}, bf16[64,1024]{1,0:T(8,128)(2,1)S(1)}, bf16[64,1024]{1,0:T(8,128)(2,1)S(1)}) custom-call(s32[27,16]{1,0:T(8,128)S(1)} %copy.11.neighbour, bf16[64,2048]{1,0:T(8,128)(2,1)S(1)} %copy-done.1, bf16[32,64,128]{2,1,0:T(8,128)(2,1)S(1)} %all-to-all-done.incoming, ...), custom_call_target="tpu_custom_call" | custom-call | flops 939524096 | bytes 3145728 | tf_op jit(solution)/shard_map/forward1/pallas_call | solution.py:282
  40.0 2.5 %collective-permute-start.3 = (bf16[64,1024]{1,0:T(8,128)(2,1)S(1)}, bf16[64,1024]{1,0:T(8,128)(2,1)S(1)}, u32[]{:S(2)}, u32[]{:S(2)}) collective-permute-start(bf16[64,1024]{1,0:T(8,128)(2,1)S(1)} %get-tuple-element.24), channel_id=1, source_target_pairs={{0,3},{1,0},{2,1},{3,2},{4,7},{5,4},{6,5},{7,6},{8,11},{9,8},{10,9... | collective-permute-start | bytes 393224 | tf_op jit(solution)/shard_map/ppermute | solution.py:243
  42.4 1.3 collective-permute-start.4
  43.7 0.8 collective-permute-start.5
  44.5 0.9 collective-permute-done.8.part3
  45.4 0.2 activation0.1
  45.5 1.1 collective-permute-start.11
  46.7 0.5 collective-permute-start.10
  47.1 0.2 collective-permute-start.9
  47.3 0.7 collective-permute-done.4.part2
  48.1 3.4 %collective-permute-done.5.part3 = bf16[64,1024]{1,0:T(8,128)(2,1)S(1)} collective-permute-done((bf16[64,1024]{1,0:T(8,128)(2,1)S(1)}, bf16[64,1024]{1,0:T(8,128)(2,1)S(1)}, u32[]{:S(2)}, u32[]{:S(2)}) %collective-permute-start.5) | collective-permute-done | bytes 131104 | tf_op jit(solution)/shard_map/ppermute | solution.py:243
  51.5 0.8 activation1.1
  52.3 2.0 %collective-permute-start.13 = (bf16[64,1024]{1,0:T(8,128)(2,1)S(1)}, bf16[64,1024]{1,0:T(8,128)(2,1)S(1)}, u32[]{:S(2)}, u32[]{:S(2)}) collective-permute-start(bf16[64,1024]{1,0:T(8,128)(2,1)S(1)} %get-tuple-element.35.g10.grad0), channel_id=1, source_target_pairs={{0,2},{1,3},{2,0},{3,1},{4,6},{5,7},{6,4},{7,5},{8,10},{9,11},{10,... | collective-permute-start | bytes 393224 | tf_op jit(solution)/shard_map/ppermute | solution.py:243
  54.3 0.9 collective-permute-start.12
  55.1 2.0 %collective-permute-done.9.g01.grad1 = bf16[64,1024]{1,0:T(8,128)(2,1)S(1)} collective-permute-done((bf16[64,1024]{1,0:T(8,128)(2,1)S(1)}, bf16[64,1024]{1,0:T(8,128)(2,1)S(1)}, u32[]{:S(2)}, u32[]{:S(2)}) %collective-permute-start.9) | collective-permute-done | bytes 131104 | tf_op jit(solution)/shard_map/ppermute | solution.py:243
  57.1 2.1 %weight_grad0.1.held = f32[1792,256]{1,0:T(8,128)S(1)} custom-call(s32[27,16]{1,0:T(8,128)S(1)} %copy.11.neighbour, bf16[64,2048]{1,0:T(8,128)(2,1)S(1)} %copy-done.1, bf16[32,64,128]{2,1,0:T(8,128)(2,1)S(1)} %all-to-all-done.incoming, bf16[64,1024]{1,0:T(8,128)(2,1)S(1)} %get-tuple-element.34.g00.grad0, ...), custom_call_target="tpu_custom_call" | custom-call | flops 939524096 | bytes 4194304 | tf_op jit(solution)/shard_map/weight_grad0/pallas_call | solution.py:301
  59.3 1.4 %collective-permute-done.12.g11.grad1 = bf16[64,1024]{1,0:T(8,128)(2,1)S(1)} collective-permute-done((bf16[64,1024]{1,0:T(8,128)(2,1)S(1)}, bf16[64,1024]{1,0:T(8,128)(2,1)S(1)}, u32[]{:S(2)}, u32[]{:S(2)}) %collective-permute-start.12) | collective-permute-done | bytes 131104 | tf_op jit(solution)/shard_map/ppermute | solution.py:243
  60.6 3.3 %weight_grad1.1 = bf16[32,4,32,128]{3,2,1,0:T(8,128)(2,1)} custom-call(s32[1]{0:T(128)} %bitcast.place, s32[27,16]{1,0:T(8,128)S(1)} %copy.11.neighbour, bf16[64,2048]{1,0:T(8,128)(2,1)S(1)} %copy-done.1, bf16[32,64,128]{2,1,0:T(8,128)(2,1)S(1)} %all-to-all-done.incoming, bf16[64,1024]{1,0:T(8,128)(2,1)S(1)} %get-tuple-element.35.g10.grad0, ...), custom_call_target="tpu_custom_call" | custom-call | flops 939524096 | bytes 4194304 | tf_op jit(solution)/shard_map/weight_grad1/pallas_call | solution.py:310
  63.9 12.5 %all-to-all-start.2 = ((bf16[128,32,128]{2,1,0:T(8,128)(2,1)}), bf16[128,32,128]{2,1,0:T(8,128)(2,1)S(1)}, u32[]{:S(2)}, u32[]{:S(2)}) async-start(bf16[128,32,128]{2,1,0:T(8,128)(2,1)} %bitcast.2), calls=%async_computation.2 | async-start | bytes 2097152 | tf_op jit(solution)/shard_map/all_to_all | solution.py:319
  76.4 1.2 copy-done.7
  77.5 6.5 %table_grad.1 = (f32[64,2048]{1,0:T(8,128)S(1)}, bf16[32,64,128]{2,1,0:T(8,128)(2,1)}) custom-call(s32[27,16]{1,0:T(8,128)S(1)} %copy.11.neighbour, bf16[1792,256]{1,0:T(8,128)(2,1)S(1)} %copy-done.7, bf16[64,1024]{1,0:T(8,128)(2,1)S(1)} %get-tuple-element.34.g00.grad0, bf16[64,1024]{1,0:T(8,128)(2,1)S(1)} %collective-permute-done.9.g01.grad1, ...), custom_call_target="tpu_custom_call" | custom-call | flops 1879048192 | bytes 4194304 | tf_op jit(solution)/shard_map/table_grad/pallas_call | solution.py:323
  84.0 11.8 %all-to-all-done.2 = bf16[128,32,128]{2,1,0:T(8,128)(2,1)S(1)} async-done(((bf16[128,32,128]{2,1,0:T(8,128)(2,1)}), bf16[128,32,128]{2,1,0:T(8,128)(2,1)S(1)}, u32[]{:S(2)}, u32[]{:S(2)}) %all-to-all-start.2) | async-done | bytes 1048608 | tf_op jit(solution)/shard_map/all_to_all | solution.py:319
  95.8 0.2 sum_parts.1
  96.1 13.2 %all_to_all.20.mine = bf16[16,2,32,256]{3,2,1,0:T(8,128)(2,1)S(1)} all-to-all(bf16[16,2,32,256]{3,2,1,0:T(8,128)(2,1)S(1)} %broadcast_in_dim.3), channel_id=1, replica_groups={{0,8,16,24,32,40,48,56,64,72,80,88,96,104,112,120},{4,12,20,28,36,44,52..., dimensions={0} | all-to-all | bytes 1048576 | tf_op jit(solution)/shard_map/all_to_all | solution.py:350
  109.3 1.9 %collective-permute-start.15 = (bf16[16,2,32,256]{3,2,1,0:T(8,128)(2,1)S(1)}, bf16[16,2,32,256]{3,2,1,0:T(8,128)(2,1)S(1)}, u32[]{:S(2)}, u32[]{:S(2)}) collective-permute-start(bf16[16,2,32,256]{3,2,1,0:T(8,128)(2,1)S(1)} %all_to_all.20.mine), channel_id=1, source_target_pairs={{0,4},{4,0},{8,12},{12,8},{16,20},{20,16},{24,28},{28,24},{32,36},... | collective-permute-start | bytes 1572872 | tf_op jit(solution)/shard_map/ppermute | solution.py:358
  111.2 3.7 %all-to-all-start.1 = ((bf16[32,64,128]{2,1,0:T(8,128)(2,1)}), bf16[32,64,128]{2,1,0:T(8,128)(2,1)S(1)}, u32[]{:S(2)}, u32[]{:S(2)}) async-start(bf16[32,64,128]{2,1,0:T(8,128)(2,1)} %get-tuple-element.37.after), calls=%async_computation.1 | async-start | bytes 1048576 | tf_op jit(solution)/shard_map/all_to_all | solution.py:335
  114.9 11.5 %all-to-all-done.1.returned = bf16[32,64,128]{2,1,0:T(8,128)(2,1)S(1)} async-done(((bf16[32,64,128]{2,1,0:T(8,128)(2,1)}), bf16[32,64,128]{2,1,0:T(8,128)(2,1)S(1)}, u32[]{:S(2)}, u32[]{:S(2)}) %all-to-all-start.1) | async-done | bytes 524320 | tf_op jit(solution)/shard_map/all_to_all | solution.py:335
  126.4 1.6 %return_add.1 = f32[64,2048]{1,0:T(8,128)} custom-call(s32[1,32]{1,0:T(1,128)S(1)} %copy-done.4, s32[1,32]{1,0:T(1,128)S(1)} %copy-done.5, f32[64,2048]{1,0:T(8,128)S(1)} %get-tuple-element.36.local, bf16[32,64,128]{2,1,0:T(8,128)(2,1)S(1)} %all-to-all-done.1.returned), custom_call_target="tpu_custom_call" | custom-call | bytes 2097152 | tf_op jit(solution)/shard_map/return_add/pallas_call | solution.py:336
  128.0 1.3 %unpack.1 = (f32[27,64,256]{2,1,0:T(8,128)}, f32[64,256]{1,0:T(8,128)}) custom-call(s32[1]{0:T(128)} %bitcast.1.core, bf16[16,2,32,256]{3,2,1,0:T(8,128)(2,1)S(1)} %all_to_all.20.mine, bf16[16,2,32,256]{3,2,1,0:T(8,128)(2,1)S(1)} %collective-permute-done.15.other), custom_call_target="tpu_custom_call" | custom-call | bytes 3145728 | tf_op jit(solution)/shard_map/unpack/pallas_call | solution.py:360
  (29 shorter events, 0.2 us)
Async XLA Ops:
  0.6 2.3 %copy-start.1 = (bf16[64,2048]{1,0:T(8,128)(2,1)S(1)}, bf16[64,2048]{1,0:T(8,128)(2,1)}, u32[]{:S(2)}) copy-start(bf16[64,2048]{1,0:T(8,128)(2,1)} %features.9) | copy-start | bytes 786436
  0.6 1.2 copy-start.2
  1.9 0.8 copy-start.3
  2.6 0.7 copy-start.4
  2.6 0.7 copy-start.5
  4.8 13.3 %copy-start.10 = (s32[27,16]{0,1:T(8,128)S(1)}, s32[27,16]{0,1:T(8,128)}, u32[]{:S(2)}) copy-start(s32[27,16]{0,1:T(8,128)} %param.13) | copy-start | bytes 5188
  4.8 28.2 %all-to-all-start = ((bf16[32,64,128]{2,1,0:T(8,128)(2,1)}), bf16[32,64,128]{2,1,0:T(8,128)(2,1)S(1)}, u32[]{:S(2)}, u32[]{:S(2)}) async-start(bf16[32,64,128]{2,1,0:T(8,128)(2,1)} %pack.1), calls=%async_computation | async-start | bytes 1048576 | tf_op jit(solution)/shard_map/all_to_all | solution.py:263
  13.6 13.5 %collective-permute-start.2 = (bf16[14,64,128]{2,1,0:T(8,128)(2,1)S(1)}, bf16[14,64,128]{2,1,0:T(8,128)(2,1)S(1)}, u32[]{:S(2)}, u32[]{:S(2)}) collective-permute-start(bf16[14,64,128]{2,1,0:T(8,128)(2,1)S(1)} %get-tuple-element.40), channel_id=1, source_target_pairs={{0,3},{1,0},{2,1},{3,2},{4,7},{5,4},{6,5},{7,6},{8,11},{9,8},{10,9... | collective-permute-start | bytes 688136 | tf_op jit(solution)/shard_map/ppermute | solution.py:243
  17.4 9.7 %collective-permute-start.1 = (bf16[14,64,128]{2,1,0:T(8,128)(2,1)S(1)}, bf16[14,64,128]{2,1,0:T(8,128)(2,1)S(1)}, u32[]{:S(2)}, u32[]{:S(2)}) collective-permute-start(bf16[14,64,128]{2,1,0:T(8,128)(2,1)S(1)} %get-tuple-element.41), channel_id=1, source_target_pairs={{0,2},{1,3},{2,0},{3,1},{4,6},{5,7},{6,4},{7,5},{8,10},{9,11},{10,... | collective-permute-start | bytes 688136 | tf_op jit(solution)/shard_map/ppermute | solution.py:243
  17.4 13.4 %collective-permute-start = (bf16[14,64,128]{2,1,0:T(8,128)(2,1)S(1)}, bf16[14,64,128]{2,1,0:T(8,128)(2,1)S(1)}, u32[]{:S(2)}, u32[]{:S(2)}) collective-permute-start(bf16[14,64,128]{2,1,0:T(8,128)(2,1)S(1)} %get-tuple-element.42), channel_id=1, source_target_pairs={{0,1},{1,2},{2,3},{3,0},{4,5},{5,6},{6,7},{7,4},{8,9},{9,10},{10,1... | collective-permute-start | bytes 688136 | tf_op jit(solution)/shard_map/ppermute | solution.py:243
  31.1 0.9 copy-start.6
  32.1 0.9 copy-start.8
  33.0 1.2 copy-start.9
  36.3 9.1 %copy-start = (bf16[64,2048]{1,0:T(8,128)(2,1)S(1)}, bf16[64,2048]{1,0:T(8,128)(2,1)}, u32[]{:S(2)}) copy-start(bf16[64,2048]{1,0:T(8,128)(2,1)} %out_grad.3) | copy-start | bytes 786436
  36.3 7.4 %collective-permute-start.6 = (bf16[64,1024]{1,0:T(8,128)(2,1)S(1)}, bf16[64,1024]{1,0:T(8,128)(2,1)S(1)}, u32[]{:S(2)}, u32[]{:S(2)}) collective-permute-start(bf16[64,1024]{1,0:T(8,128)(2,1)S(1)} %get-tuple-element.28), channel_id=1, source_target_pairs={{0,3},{1,0},{2,1},{3,2},{4,7},{5,4},{6,5},{7,6},{8,11},{9,8},{10,9... | collective-permute-start | bytes 393224 | tf_op jit(solution)/shard_map/ppermute | solution.py:243
  36.4 8.1 %collective-permute-start.7 = (bf16[64,1024]{1,0:T(8,128)(2,1)S(1)}, bf16[64,1024]{1,0:T(8,128)(2,1)S(1)}, u32[]{:S(2)}, u32[]{:S(2)}) collective-permute-start(bf16[64,1024]{1,0:T(8,128)(2,1)S(1)} %get-tuple-element.29), channel_id=1, source_target_pairs={{0,2},{1,3},{2,0},{3,1},{4,6},{5,7},{6,4},{7,5},{8,10},{9,11},{10,... | collective-permute-start | bytes 393224 | tf_op jit(solution)/shard_map/ppermute | solution.py:243
  37.0 8.3 %collective-permute-start.8 = (bf16[64,1024]{1,0:T(8,128)(2,1)S(1)}, bf16[64,1024]{1,0:T(8,128)(2,1)S(1)}, u32[]{:S(2)}, u32[]{:S(2)}) collective-permute-start(bf16[64,1024]{1,0:T(8,128)(2,1)S(1)} %get-tuple-element.30), channel_id=1, source_target_pairs={{0,1},{1,2},{2,3},{3,0},{4,5},{5,6},{6,7},{7,4},{8,9},{9,10},{10,1... | collective-permute-start | bytes 393224 | tf_op jit(solution)/shard_map/ppermute | solution.py:243
  40.0 7.2 %collective-permute-start.3 = (bf16[64,1024]{1,0:T(8,128)(2,1)S(1)}, bf16[64,1024]{1,0:T(8,128)(2,1)S(1)}, u32[]{:S(2)}, u32[]{:S(2)}) collective-permute-start(bf16[64,1024]{1,0:T(8,128)(2,1)S(1)} %get-tuple-element.24), channel_id=1, source_target_pairs={{0,3},{1,0},{2,1},{3,2},{4,7},{5,4},{6,5},{7,6},{8,11},{9,8},{10,9... | collective-permute-start | bytes 393224 | tf_op jit(solution)/shard_map/ppermute | solution.py:243
  42.4 5.6 %collective-permute-start.4 = (bf16[64,1024]{1,0:T(8,128)(2,1)S(1)}, bf16[64,1024]{1,0:T(8,128)(2,1)S(1)}, u32[]{:S(2)}, u32[]{:S(2)}) collective-permute-start(bf16[64,1024]{1,0:T(8,128)(2,1)S(1)} %get-tuple-element.25), channel_id=1, source_target_pairs={{0,2},{1,3},{2,0},{3,1},{4,6},{5,7},{6,4},{7,5},{8,10},{9,11},{10,... | collective-permute-start | bytes 393224 | tf_op jit(solution)/shard_map/ppermute | solution.py:243
  43.7 7.8 %collective-permute-start.5 = (bf16[64,1024]{1,0:T(8,128)(2,1)S(1)}, bf16[64,1024]{1,0:T(8,128)(2,1)S(1)}, u32[]{:S(2)}, u32[]{:S(2)}) collective-permute-start(bf16[64,1024]{1,0:T(8,128)(2,1)S(1)} %get-tuple-element.26), channel_id=1, source_target_pairs={{0,1},{1,2},{2,3},{3,0},{4,5},{5,6},{6,7},{7,4},{8,9},{9,10},{10,1... | collective-permute-start | bytes 393224 | tf_op jit(solution)/shard_map/ppermute | solution.py:243
  45.5 8.7 %collective-permute-start.11 = (bf16[64,1024]{1,0:T(8,128)(2,1)S(1)}, bf16[64,1024]{1,0:T(8,128)(2,1)S(1)}, u32[]{:S(2)}, u32[]{:S(2)}) collective-permute-start(bf16[64,1024]{1,0:T(8,128)(2,1)S(1)} %get-tuple-element.34.g00.grad0), channel_id=1, source_target_pairs={{0,3},{1,0},{2,1},{3,2},{4,7},{5,4},{6,5},{7,6},{8,11},{9,8},{10,9... | collective-permute-start | bytes 393224 | tf_op jit(solution)/shard_map/ppermute | solution.py:243
  46.7 8.5 %collective-permute-start.10 = (bf16[64,1024]{1,0:T(8,128)(2,1)S(1)}, bf16[64,1024]{1,0:T(8,128)(2,1)S(1)}, u32[]{:S(2)}, u32[]{:S(2)}) collective-permute-start(bf16[64,1024]{1,0:T(8,128)(2,1)S(1)} %get-tuple-element.34.g00.grad0), channel_id=1, source_target_pairs={{0,2},{1,3},{2,0},{3,1},{4,6},{5,7},{6,4},{7,5},{8,10},{9,11},{10,... | collective-permute-start | bytes 393224 | tf_op jit(solution)/shard_map/ppermute | solution.py:243
  47.1 10.0 %collective-permute-start.9 = (bf16[64,1024]{1,0:T(8,128)(2,1)S(1)}, bf16[64,1024]{1,0:T(8,128)(2,1)S(1)}, u32[]{:S(2)}, u32[]{:S(2)}) collective-permute-start(bf16[64,1024]{1,0:T(8,128)(2,1)S(1)} %get-tuple-element.34.g00.grad0), channel_id=1, source_target_pairs={{0,1},{1,2},{2,3},{3,0},{4,5},{5,6},{6,7},{7,4},{8,9},{9,10},{10,1... | collective-permute-start | bytes 393224 | tf_op jit(solution)/shard_map/ppermute | solution.py:243
  52.3 6.9 %collective-permute-start.14 = (bf16[64,1024]{1,0:T(8,128)(2,1)S(1)}, bf16[64,1024]{1,0:T(8,128)(2,1)S(1)}, u32[]{:S(2)}, u32[]{:S(2)}) collective-permute-start(bf16[64,1024]{1,0:T(8,128)(2,1)S(1)} %get-tuple-element.35.g10.grad0), channel_id=1, source_target_pairs={{0,3},{1,0},{2,1},{3,2},{4,7},{5,4},{6,5},{7,6},{8,11},{9,8},{10,9... | collective-permute-start | bytes 393224 | tf_op jit(solution)/shard_map/ppermute | solution.py:243
  52.3 6.9 %collective-permute-start.13 = (bf16[64,1024]{1,0:T(8,128)(2,1)S(1)}, bf16[64,1024]{1,0:T(8,128)(2,1)S(1)}, u32[]{:S(2)}, u32[]{:S(2)}) collective-permute-start(bf16[64,1024]{1,0:T(8,128)(2,1)S(1)} %get-tuple-element.35.g10.grad0), channel_id=1, source_target_pairs={{0,2},{1,3},{2,0},{3,1},{4,6},{5,7},{6,4},{7,5},{8,10},{9,11},{10,... | collective-permute-start | bytes 393224 | tf_op jit(solution)/shard_map/ppermute | solution.py:243
  54.3 6.3 %collective-permute-start.12 = (bf16[64,1024]{1,0:T(8,128)(2,1)S(1)}, bf16[64,1024]{1,0:T(8,128)(2,1)S(1)}, u32[]{:S(2)}, u32[]{:S(2)}) collective-permute-start(bf16[64,1024]{1,0:T(8,128)(2,1)S(1)} %get-tuple-element.35.g10.grad0), channel_id=1, source_target_pairs={{0,1},{1,2},{2,3},{3,0},{4,5},{5,6},{6,7},{7,4},{8,9},{9,10},{10,1... | collective-permute-start | bytes 393224 | tf_op jit(solution)/shard_map/ppermute | solution.py:243
  63.9 31.9 %all-to-all-start.2 = ((bf16[128,32,128]{2,1,0:T(8,128)(2,1)}), bf16[128,32,128]{2,1,0:T(8,128)(2,1)S(1)}, u32[]{:S(2)}, u32[]{:S(2)}) async-start(bf16[128,32,128]{2,1,0:T(8,128)(2,1)} %bitcast.2), calls=%async_computation.2 | async-start | bytes 2097152 | tf_op jit(solution)/shard_map/all_to_all | solution.py:319
  76.4 1.2 copy-start.7
  109.3 18.7 %collective-permute-start.15 = (bf16[16,2,32,256]{3,2,1,0:T(8,128)(2,1)S(1)}, bf16[16,2,32,256]{3,2,1,0:T(8,128)(2,1)S(1)}, u32[]{:S(2)}, u32[]{:S(2)}) collective-permute-start(bf16[16,2,32,256]{3,2,1,0:T(8,128)(2,1)S(1)} %all_to_all.20.mine), channel_id=1, source_target_pairs={{0,4},{4,0},{8,12},{12,8},{16,20},{20,16},{24,28},{28,24},{32,36},... | collective-permute-start | bytes 1572872 | tf_op jit(solution)/shard_map/ppermute | solution.py:358
  111.2 15.2 %all-to-all-start.1 = ((bf16[32,64,128]{2,1,0:T(8,128)(2,1)}), bf16[32,64,128]{2,1,0:T(8,128)(2,1)S(1)}, u32[]{:S(2)}, u32[]{:S(2)}) async-start(bf16[32,64,128]{2,1,0:T(8,128)(2,1)} %get-tuple-element.37.after), calls=%async_computation.1 | async-start | bytes 1048576 | tf_op jit(solution)/shard_map/all_to_all | solution.py:335

commit v4 on v3

--- a/solution.py
+++ b/solution.py
@@ -15,7 +15,7 @@
 F32 = jnp.float32
 
 
-def call(kernel, name, outs, kinds, scratch=(), flops=0, size=0, limit=48 << 20):
+def call(kernel, name, outs, kinds, scratch=(), flops=0, size=0, limit=24 << 20):
     space = {"s": pltpu.SMEM, "v": pltpu.VMEM, "a": pl.ANY}
     many = isinstance(outs, (list, tuple))
     spec = pl.BlockSpec(memory_space=pltpu.VMEM)
@@ -41,8 +41,7 @@
     return pl.ds(pl.multiple_of(index * BLOCK, BLOCK), BLOCK)
 
 
-def pack_kernel(send_block, send_count, features, after, outgoing):
-    del after
+def pack_kernel(send_block, send_count, features, outgoing):
     for peer in range(outgoing.shape[0]):
         block = features[:, columns(send_block[0, peer])]
         outgoing[peer] = block * send_count[0, peer].astype(F32).astype(BF)
@@ -152,7 +151,7 @@
 
 
 def weight_second_kernel(
-    place, neighbour, features, incoming, grad0, grad1, grad2, grad3, held, parts, table, gathered, flipped
+    core, neighbour, features, incoming, grad0, grad1, grad2, grad3, held, keep, give, table, gathered, flipped
 ):
     quarter = features.shape[0]
     grads = (grad0, grad1, grad2, grad3)
@@ -161,19 +160,23 @@
     for pair in range(PAIRS):
         rows = slice(pair * BLOCK, (pair + 1) * BLOCK)
         product = jnp.dot(gathered[rows, :], flipped[...], preferred_element_type=F32)
-        upright = (product + held[rows, :]).T.astype(BF)
+        upright = (product + held[rows, :]).T
         for step in range(4):
-            target = lax.rem(place[0] - step + 4, 4)
-            for side in range(2):
-                start = step * quarter + side * half
-                parts[2 * pair + side, target] = upright[start : start + half]
-    for spare in range(2 * PAIRS, parts.shape[0]):
-        parts[spare] = jnp.zeros(parts.shape[1:], BF)
+            low = upright[step * quarter : step * quarter + half]
+            high = upright[step * quarter + half : (step + 1) * quarter]
+            keep[pair, step] = jnp.where(core[0] == 0, low, high)
+            give[pair, step] = jnp.where(core[0] == 0, high, low).astype(BF)
+
+
+def pair_kernel(keep, arrived, parts):
+    parts[:PAIRS] = (keep[...] + arrived[...].astype(F32)).astype(BF)
+    parts[PAIRS:] = jnp.zeros((parts.shape[0] - PAIRS,) + parts.shape[1:], BF)
 
 
 def table_kernel(
-    neighbour, weight_t, g00, g01, g02, g03, g10, g11, g12, g13, local, returned, total, spread
+    neighbour, weight_t, g00, g01, g02, g03, g10, g11, g12, g13, after, local, returned, total, spread
 ):
+    del after
     quarter, row_count = local.shape
     nblocks = row_count // BLOCK
     extent = nblocks + returned.shape[0]
@@ -214,33 +217,70 @@
         input_grad[:, columns(send_block[0, peer])] += returned[peer].astype(F32) * factor
 
 
-def sum_kernel(scale, parts, after, chunk):
+def sum_kernel(scale, parts, after, own, sent1, sent2, sent3):
     del after
-    quarter = 64
     total = parts[0].astype(F32)
     for source in range(1, parts.shape[0]):
         total = total + parts[source].astype(F32)
     total = total * scale
+    own[...] = total[0]
+    sent1[...] = total[1].astype(BF)
+    sent2[...] = total[2].astype(BF)
+    sent3[...] = total[3].astype(BF)
+
+
+def assemble_kernel(place, own, part1, part2, part3, chunk):
+    quarter = own.shape[1] // 2
+    pieces = (own[...], part1[...].astype(F32), part2[...].astype(F32), part3[...].astype(F32))
     for side in range(2):
         cut = slice(side * quarter, (side + 1) * quarter)
-        chunk[side] = jnp.concatenate([total[c, :, cut] for c in range(4)], axis=1).astype(BF)
-
-
-def unpack_kernel(core, mine, other, conv_grad, coarse_grad):
-    half = mine.shape[2]
-    for chunks, side in ((mine, core[0]), (other, 1 - core[0])):
+        columns_of = []
+        for source in range(4):
+            step = lax.rem(source - place[0] + 4, 4)
+            low = jnp.where(step == 0, pieces[0][:, cut], pieces[1][:, cut])
+            high = jnp.where(step == 2, pieces[2][:, cut], pieces[3][:, cut])
+            columns_of.append(jnp.where(step < 2, low, high))
+        chunk[side] = jnp.concatenate(columns_of, axis=1).astype(BF)
+
+
+def unpack_kernel(chip, *refs):
+    conv_grad, coarse_grad = refs[-2:]
+    half = refs[0].shape[2]
+    core = chip[2]
+    for index, ref in enumerate(refs[:-2]):
+        side = core if index < 4 else 1 - core
         rows = pl.ds(pl.multiple_of(side * half, half), half)
-        for offset in range(TERMS):
-            value = chunks[offset // 2, offset % 2].astype(F32)
-            if offset < OFFSETS:
-                conv_grad[offset, rows, :] = value
-            else:
-                coarse_grad[rows, :] = value
+        for step in range(4):
+            source_y = lax.rem(chip[0] - step + 4, 4)
+            source_x = lax.rem(chip[1] - index % 4 + 4, 4)
+            pair = source_y * 4 + source_x
+
+            @pl.when(pair < PAIRS)
+            def _(ref=ref, step=step, pair=pair, rows=rows):
+                conv_grad[2 * pair, rows, :] = ref[step, 0].astype(F32)
+
+            @pl.when(pair < PAIRS - 1)
+            def _(ref=ref, step=step, pair=pair, rows=rows):
+                conv_grad[2 * pair + 1, rows, :] = ref[step, 1].astype(F32)
+
+            @pl.when(pair == PAIRS - 1)
+            def _(ref=ref, step=step, rows=rows):
+                coarse_grad[rows, :] = ref[step, 1].astype(F32)
 
 
 def shift(value, axis, step):
     size = lax.axis_size(axis)
     return lax.ppermute(value, axis, [(i, (i + step) % size) for i in range(size)])
+
+
+def move(value, step_y, step_x, flip):
+    moves = []
+    for y in range(4):
+        for x in range(4):
+            for core in range(2):
+                target = ((y + step_y) % 4 * 4 + (x + step_x) % 4) * 2 + (core ^ flip)
+                moves.append(((y * 4 + x) * 2 + core, target))
+    return lax.ppermute(value, "morton", moves)
 
 
 def local_step(features, conv_weight, coarse_weight, out_grad, send_block, send_count, neighbour):
@@ -252,14 +292,17 @@
     depth = TERMS * quarter
     flops = 2 * depth * channels * row_count
     place = lax.axis_index("chan").astype(jnp.int32).reshape(1)
+    spot = lax.axis_index("morton").astype(jnp.int32)
+    chip = jnp.stack([spot // 8, spot // 2 % 4, spot % 2])
+    core = (spot % 2).reshape(1)
     shape = jax.ShapeDtypeStruct
 
     pieces = call(
         split_kernel, "split", shape((4 * PAIRS, quarter, BLOCK), BF), "svv", size=2 << 20
     )(place, conv_weight, coarse_weight)
     outgoing = call(
-        pack_kernel, "pack", shape((n_morton, quarter, BLOCK), BF), "ssva", size=64 << 20
-    )(send_block, send_count, features, pieces)
+        pack_kernel, "pack", shape((n_morton, quarter, BLOCK), BF), "ssv", size=1 << 20
+    )(send_block, send_count, features)
     incoming = lax.all_to_all(outgoing, "morton", 0, 0, tiled=True)
 
     pieces = pieces.reshape(4, PAIRS, quarter, BLOCK)
@@ -307,63 +350,65 @@
         flops // 2,
         4 << 20,
     )(neighbour, features, incoming, *grads[0])
-    parts = call(
+    piece = (4, quarter // 2, BLOCK)
+    keep, give = call(
         weight_second_kernel,
         "weight_grad1",
-        shape((n_morton, 4, quarter // 2, BLOCK), BF),
+        [shape((PAIRS,) + piece, F32), shape((PAIRS,) + piece, BF)],
         "ssvvvvvvv",
         big + turned,
         flops // 2,
         4 << 20,
-    )(place, neighbour, features, incoming, *grads[1], held)
+    )(core, neighbour, features, incoming, *grads[1], held)
+    chips = n_morton // 2
+    parts = call(pair_kernel, "pair_sum", shape((chips,) + piece, BF), "vv", size=3 << 20)(
+        keep, move(give, 0, 0, 1)
+    )
+    same_core = [[2 * c + side for c in range(chips)] for side in range(2)]
     received = lax.all_to_all(
-        parts.reshape(n_morton * 4, quarter // 2, BLOCK), ("morton", "chan"), 0, 0, tiled=True
-    ).reshape(parts.shape)
+        parts, "morton", 0, 0, axis_index_groups=same_core, tiled=True
+    )
 
     local, outward = call(
         table_kernel,
         "table_grad",
         [shape(wide, F32), shape((n_morton, quarter, BLOCK), BF)],
-        "s" + "v" * 9,
+        "s" + "v" * 9 + "a",
         [
             pltpu.VMEM((extent + 1, quarter, BLOCK), F32),
             pltpu.VMEM((OFFSETS * quarter, 256), F32),
         ],
         flops,
         4 << 20,
-    )(neighbour, weight_t, *grads[0], *grads[1])
+    )(neighbour, weight_t, *grads[0], *grads[1], parts)
     returned = lax.all_to_all(outward, "morton", 0, 0, tiled=True)
     input_grad = call(return_kernel, "return_add", shape(wide, F32), "ssvv", size=2 << 20)(
         send_block, send_count, local, returned
     )
 
     scale = float(row_count * n_morton) ** (-0.5)
-    chunk = call(
+    small = piece[1:]
+    own, *sent = call(
         functools.partial(sum_kernel, scale),
         "sum_parts",
-        shape((2, quarter // 2, channels), BF),
+        [shape(small, F32)] + [shape(small, BF)] * 3,
         "va",
         size=1 << 20,
     )(received, outward)
-    chips = n_morton // 2
-    same_core = [[2 * chip + core for chip in range(chips)] for core in range(2)]
-    mine = lax.all_to_all(
-        jnp.broadcast_to(chunk, (chips,) + chunk.shape),
-        "morton",
-        0,
-        0,
-        axis_index_groups=same_core,
-        tiled=True,
-    )
-    other = lax.ppermute(mine, "morton", [(i, i ^ 1) for i in range(n_morton)])
-    core = lax.rem(lax.axis_index("morton"), 2).astype(jnp.int32).reshape(1)
+    sent = [shift(value, "chan", -step) for step, value in zip((1, 2, 3), sent)]
+    chunk = call(
+        assemble_kernel, "assemble", shape((2, quarter // 2, channels), BF), "svvvv", size=1 << 17
+    )(place, own, *sent)
+    column = jnp.stack([chunk] + [move(chunk, step, 0, 0) for step in (1, 2, 3)])
+    mine = [column] + [move(column, 0, step, 0) for step in (1, 2, 3)]
+    other = [move(value, 0, 0, 1) for value in mine]
     conv_grad, coarse_grad = call(
         unpack_kernel,
         "unpack",
         [shape((OFFSETS, quarter, channels), F32), shape((quarter, channels), F32)],
-        "svv",
+        "s" + "v" * 8,
         size=3 << 20,
-    )(core, mine, other)
+    )(chip, *mine, *other)
     return output, input_grad, conv_grad, coarse_grad
 
 

time: 130 us -> 124 us (0.954)
  starting transfers between devices: 41.9 us -> 60.8 us
  blocking collectives: 13.2 us -> 0 us
  waiting for transfers between devices: 44.3 us -> 33.2 us
    ppermute x1 -> x11, starting transfers between devices: 1.88 us -> 22.8 us  [move(): return lax.ppermute(value, 'morton', moves)]
    all_to_all x1 -> x0, blocking collectives: 13.2 us -> none  [local_step(): lax.all_to_all(jnp.broadcast_to(chunk, (chips,) + chunk.shape), 'morton',...]
    all_to_all x1, waiting for transfers between devices: 11.5 us -> 0.01 us  [local_step(): returned = lax.all_to_all(outward, 'morton', 0, 0, tiled=True)]
    all_to_all x1, waiting for transfers between devices: 11.8 us -> 3.37 us  [local_step(): lax.all_to_all(parts, 'morton', 0, 0, axis_index_groups=same_core, tiled=...]
    all_to_all x1, starting transfers between devices: 12.5 us -> 6.7 us  [local_step(): lax.all_to_all(parts, 'morton', 0, 0, axis_index_groups=same_core, tiled=...]
    ppermute x1 -> x11, waiting for transfers between devices: 0.01 us -> 4.98 us  [move(): return lax.ppermute(value, 'morton', moves)]
    ppermute x15 -> x18, waiting for transfers between devices: 21 us -> 24.9 us  [shift(): lax.ppermute(value, axis, [(i, (i + step) % size) for i in range(size)])]
    ppermute x15 -> x18, starting transfers between devices: 15.2 us -> 17.5 us  [shift(): lax.ppermute(value, axis, [(i, (i + step) % size) for i in range(size)])]
  transfers between devices with their start and end apart: 19 -> 32, of which waited for: 9 -> 14; matrix products, arithmetic and copies ran while one was open for 0% -> 0% of each run, Pallas kernels for 11% -> 11%
where the time goes in v4:
time: 124 us
  starting transfers between devices  60.8 us (49%)
  waiting for transfers between devices  33.2 us (27%)
  Pallas kernels  23.4 us (19%)
  local copies, waits for them, and re-layouts  5.52 us (4%)
    ppermute x18, waiting for transfers between devices, shift(): lax.ppermute(value, axis, [(i, (i + step) % size) for i in range(size)])  24.9 us
    ppermute x11, starting transfers between devices, move(): return lax.ppermute(value, 'morton', moves)  22.8 us
    ppermute x18, starting transfers between devices, shift(): lax.ppermute(value, axis, [(i, (i + step) % size) for i in range(size)])  17.5 us
    all_to_all x1, starting transfers between devices, local_step(): incoming = lax.all_to_all(outgoing, 'morton', 0, 0, tiled=True)  8.59 us
    all_to_all x1, starting transfers between devices, local_step(): lax.all_to_all(parts, 'morton', 0, 0, axis_index_groups=same_core, tiled=...  6.7 us
    pallas_call x1, Pallas kernels, local_step(): call(table_kernel, 'table_grad', [shape(wide, F32), shape((n_morton, quar...  6.43 us
    unnamed x31, local copies, waits for them, and re-layouts  5.46 us
    all_to_all x1, starting transfers between devices, local_step(): returned = lax.all_to_all(outward, 'morton', 0, 0, tiled=True)  5.32 us
  transfers between devices with their start and end apart: 32, of which 14 were waited for; matrix products, arithmetic and copies ran while one was open for 0% of the time, Pallas kernels for 11%

profile of v4, /device:TPU:1, one launch (start us, length us, event | category | flops | bytes accessed | tf_op | source)
XLA Modules:
  0.0 124.0 jit_solution(8666124650502669714)
XLA Ops:
  0.7 1.0 copy-done.2
  1.7 0.7 copy-done.5
  2.3 0.7 copy-done.7
  3.0 1.5 %pack.1 = bf16[32,64,128]{2,1,0:T(8,128)(2,1)} custom-call(s32[1,32]{1,0:T(1,128)S(1)} %copy-done.5, s32[1,32]{1,0:T(1,128)S(1)} %copy-done.7, bf16[64,2048]{1,0:T(8,128)(2,1)S(1)} %copy-done.2), custom_call_target="tpu_custom_call" | custom-call | bytes 1048576 | tf_op jit(solution)/shard_map/pack/pallas_call | solution.py:303
  4.5 8.6 %all-to-all-start = ((bf16[32,64,128]{2,1,0:T(8,128)(2,1)}), bf16[32,64,128]{2,1,0:T(8,128)(2,1)S(1)}, u32[]{:S(2)}, u32[]{:S(2)}) async-start(bf16[32,64,128]{2,1,0:T(8,128)(2,1)} %pack.1), calls=%async_computation | async-start | bytes 1048576 | tf_op jit(solution)/shard_map/all_to_all | solution.py:306
  13.5 3.8 %collective-permute-start.2 = (bf16[14,64,128]{2,1,0:T(8,128)(2,1)S(1)}, bf16[14,64,128]{2,1,0:T(8,128)(2,1)S(1)}, u32[]{:S(2)}, u32[]{:S(2)}) collective-permute-start(bf16[14,64,128]{2,1,0:T(8,128)(2,1)S(1)} %get-tuple-element.52), channel_id=1, source_target_pairs={{0,3},{1,0},{2,1},{3,2},{4,7},{5,4},{6,5},{7,6},{8,11},{9,8},{10,9... | collective-permute-start | bytes 688136 | tf_op jit(solution)/shard_map/ppermute | solution.py:273
  17.3 0.7 collective-permute-start
  18.1 8.9 %collective-permute-done.2.piece3 = bf16[14,64,128]{2,1,0:T(8,128)(2,1)S(1)} collective-permute-done((bf16[14,64,128]{2,1,0:T(8,128)(2,1)S(1)}, bf16[14,64,128]{2,1,0:T(8,128)(2,1)S(1)}, u32[]{:S(2)}, u32[]{:S(2)}) %collective-permute-start.2) | collective-permute-done | bytes 229408 | tf_op jit(solution)/shard_map/ppermute | solution.py:273
  27.0 3.7 %collective-permute-done.piece1 = bf16[14,64,128]{2,1,0:T(8,128)(2,1)S(1)} collective-permute-done((bf16[14,64,128]{2,1,0:T(8,128)(2,1)S(1)}, bf16[14,64,128]{2,1,0:T(8,128)(2,1)S(1)}, u32[]{:S(2)}, u32[]{:S(2)}) %collective-permute-start) | collective-permute-done | bytes 229408 | tf_op jit(solution)/shard_map/ppermute | solution.py:273
  31.1 0.9 copy-done.9
  32.0 1.2 copy-done.10
  33.2 2.1 %forward0.1 = (f32[64,1024]{1,0:T(8,128)S(1)}, bf16[64,1024]{1,0:T(8,128)(2,1)S(1)}, bf16[64,1024]{1,0:T(8,128)(2,1)S(1)}, bf16[64,1024]{1,0:T(8,128)(2,1)S(1)}) custom-call(s32[27,16]{1,0:T(8,128)S(1)} %copy.11.neighbour, bf16[64,2048]{1,0:T(8,128)(2,1)S(1)} %copy-done.3, bf16[32,64,128]{2,1,0:T(8,128)(2,1)S(1)} %all-to-all-done.incoming, ...), custom_call_target="tpu_custom_call" | custom-call | flops 939524096 | bytes 3145728 | tf_op jit(solution)/shard_map/forward0/pallas_call | solution.py:325
  36.1 0.8 collective-permute-start.8
  36.9 2.1 %forward1.1 = (f32[64,1024]{1,0:T(8,128)S(1)}, bf16[64,1024]{1,0:T(8,128)(2,1)S(1)}, bf16[64,1024]{1,0:T(8,128)(2,1)S(1)}, bf16[64,1024]{1,0:T(8,128)(2,1)S(1)}) custom-call(s32[27,16]{1,0:T(8,128)S(1)} %copy.11.neighbour, bf16[64,2048]{1,0:T(8,128)(2,1)S(1)} %copy-done.3, bf16[32,64,128]{2,1,0:T(8,128)(2,1)S(1)} %all-to-all-done.incoming, ...), custom_call_target="tpu_custom_call" | custom-call | flops 939524096 | bytes 3145728 | tf_op jit(solution)/shard_map/forward1/pallas_call | solution.py:325
  39.0 2.5 %collective-permute-start.3 = (bf16[64,1024]{1,0:T(8,128)(2,1)S(1)}, bf16[64,1024]{1,0:T(8,128)(2,1)S(1)}, u32[]{:S(2)}, u32[]{:S(2)}) collective-permute-start(bf16[64,1024]{1,0:T(8,128)(2,1)S(1)} %get-tuple-element.30), channel_id=1, source_target_pairs={{0,3},{1,0},{2,1},{3,2},{4,7},{5,4},{6,5},{7,6},{8,11},{9,8},{10,9... | collective-permute-start | bytes 393224 | tf_op jit(solution)/shard_map/ppermute | solution.py:273
  41.4 1.3 %collective-permute-start.4 = (bf16[64,1024]{1,0:T(8,128)(2,1)S(1)}, bf16[64,1024]{1,0:T(8,128)(2,1)S(1)}, u32[]{:S(2)}, u32[]{:S(2)}) collective-permute-start(bf16[64,1024]{1,0:T(8,128)(2,1)S(1)} %get-tuple-element.31), channel_id=1, source_target_pairs={{0,2},{1,3},{2,0},{3,1},{4,6},{5,7},{6,4},{7,5},{8,10},{9,11},{10,... | collective-permute-start | bytes 393224 | tf_op jit(solution)/shard_map/ppermute | solution.py:273
  42.7 0.8 collective-permute-start.5
  43.5 0.9 collective-permute-done.8.part3
  44.5 1.1 collective-permute-start.11
  46.3 0.7 collective-permute-done.4.part2
  47.1 3.4 %collective-permute-done.5.part3 = bf16[64,1024]{1,0:T(8,128)(2,1)S(1)} collective-permute-done((bf16[64,1024]{1,0:T(8,128)(2,1)S(1)}, bf16[64,1024]{1,0:T(8,128)(2,1)S(1)}, u32[]{:S(2)}, u32[]{:S(2)}) %collective-permute-start.5) | collective-permute-done | bytes 131104 | tf_op jit(solution)/shard_map/ppermute | solution.py:273
  50.5 0.8 activation1.1
  51.3 2.0 %collective-permute-start.13 = (bf16[64,1024]{1,0:T(8,128)(2,1)S(1)}, bf16[64,1024]{1,0:T(8,128)(2,1)S(1)}, u32[]{:S(2)}, u32[]{:S(2)}) collective-permute-start(bf16[64,1024]{1,0:T(8,128)(2,1)S(1)} %get-tuple-element.41.grad0.g10), channel_id=1, source_target_pairs={{0,2},{1,3},{2,0},{3,1},{4,6},{5,7},{6,4},{7,5},{8,10},{9,11},{10,... | collective-permute-start | bytes 393224 | tf_op jit(solution)/shard_map/ppermute | solution.py:273
  53.3 0.9 collective-permute-start.12
  54.2 1.9 %collective-permute-done.9.grad1.g01 = bf16[64,1024]{1,0:T(8,128)(2,1)S(1)} collective-permute-done((bf16[64,1024]{1,0:T(8,128)(2,1)S(1)}, bf16[64,1024]{1,0:T(8,128)(2,1)S(1)}, u32[]{:S(2)}, u32[]{:S(2)}) %collective-permute-start.9) | collective-permute-done | bytes 131104 | tf_op jit(solution)/shard_map/ppermute | solution.py:273
  56.1 2.1 %weight_grad0.1.held = f32[1792,256]{1,0:T(8,128)S(1)} custom-call(s32[27,16]{1,0:T(8,128)S(1)} %copy.11.neighbour, bf16[64,2048]{1,0:T(8,128)(2,1)S(1)} %copy-done.3, bf16[32,64,128]{2,1,0:T(8,128)(2,1)S(1)} %all-to-all-done.incoming, bf16[64,1024]{1,0:T(8,128)(2,1)S(1)} %get-tuple-element.40.grad0.g00, ...), custom_call_target="tpu_custom_call" | custom-call | flops 939524096 | bytes 4194304 | tf_op jit(solution)/shard_map/weight_grad0/pallas_call | solution.py:344
  58.2 1.4 %collective-permute-done.12.grad1.g11 = bf16[64,1024]{1,0:T(8,128)(2,1)S(1)} collective-permute-done((bf16[64,1024]{1,0:T(8,128)(2,1)S(1)}, bf16[64,1024]{1,0:T(8,128)(2,1)S(1)}, u32[]{:S(2)}, u32[]{:S(2)}) %collective-permute-start.12) | collective-permute-done | bytes 131104 | tf_op jit(solution)/shard_map/ppermute | solution.py:273
  59.6 2.2 %weight_grad1.1 = (f32[14,4,32,128]{3,2,1,0:T(8,128)S(1)}, bf16[14,4,32,128]{3,2,1,0:T(8,128)(2,1)S(1)}) custom-call(s32[1]{0:T(128)} %bitcast.1.core, s32[27,16]{1,0:T(8,128)S(1)} %copy.11.neighbour, bf16[64,2048]{1,0:T(8,128)(2,1)S(1)} %copy-done.3, bf16[32,64,128]{2,1,0:T(8,128)(2,1)S(1)} %all-to-all-done.incoming, ...), custom_call_target="tpu_custom_call" | custom-call | flops 939524096 | bytes 4194304 | tf_op jit(solution)/shard_map/weight_grad1/pallas_call | solution.py:354
  61.9 4.9 %collective-permute-start.15 = (bf16[14,4,32,128]{3,2,1,0:T(8,128)(2,1)S(1)}, bf16[14,4,32,128]{3,2,1,0:T(8,128)(2,1)S(1)}, u32[]{:S(2)}, u32[]{:S(2)}) collective-permute-start(bf16[14,4,32,128]{3,2,1,0:T(8,128)(2,1)S(1)} %get-tuple-element.43), channel_id=1, source_target_pairs={{0,4},{4,0},{8,12},{12,8},{16,20},{20,16},{24,28},{28,24},{32,36},... | collective-permute-start | bytes 1376264 | tf_op jit(solution)/shard_map/ppermute | solution.py:283
  66.8 1.4 %collective-permute-done.15.arrived = bf16[14,4,32,128]{3,2,1,0:T(8,128)(2,1)S(1)} collective-permute-done((bf16[14,4,32,128]{3,2,1,0:T(8,128)(2,1)S(1)}, bf16[14,4,32,128]{3,2,1,0:T(8,128)(2,1)S(1)}, u32[]{:S(2)}, u32[]{:S(2)}) %collective-permute-start.15) | collective-permute-done | bytes 458784 | tf_op jit(solution)/shard_map/ppermute | solution.py:283
  68.2 0.9 pair_sum.1.after
  69.1 6.7 %all-to-all-start.2 = ((bf16[16,4,32,128]{3,2,1,0:T(8,128)(2,1)}), bf16[16,4,32,128]{3,2,1,0:T(8,128)(2,1)S(1)}, u32[]{:S(2)}, u32[]{:S(2)}) async-start(bf16[16,4,32,128]{3,2,1,0:T(8,128)(2,1)} %pair_sum.1.after), calls=%async_computation.2 | async-start | bytes 1048576 | tf_op jit(solution)/shard_map/all_to_all | solution.py:368
  75.8 0.9 copy-done.13
  76.7 6.4 %table_grad.1 = (f32[64,2048]{1,0:T(8,128)S(1)}, bf16[32,64,128]{2,1,0:T(8,128)(2,1)}) custom-call(s32[27,16]{1,0:T(8,128)S(1)} %copy.11.neighbour, bf16[1792,256]{1,0:T(8,128)(2,1)S(1)} %get-tuple-element.39.weight_t, bf16[64,1024]{1,0:T(8,128)(2,1)S(1)} %get-tuple-element.40.grad0.g00, bf16[64,1024]{1,0:T(8,128)(2,1)S(1)} %collective-permute-done.9.grad1.g01, ...), custom_call_target="tpu_custom_call" | custom-call | flops 1879048192 | bytes 4194304 | tf_op jit(solution)/shard_map/table_grad/pallas_call | solution.py:372
  83.1 3.4 %all-to-all-done.2.parts = bf16[16,4,32,128]{3,2,1,0:T(8,128)(2,1)S(1)} async-done(((bf16[16,4,32,128]{3,2,1,0:T(8,128)(2,1)}), bf16[16,4,32,128]{3,2,1,0:T(8,128)(2,1)S(1)}, u32[]{:S(2)}, u32[]{:S(2)}) %all-to-all-start.2) | async-done | bytes 524320 | tf_op jit(solution)/shard_map/all_to_all | solution.py:368
  86.5 5.3 %all-to-all-start.1 = ((bf16[32,64,128]{2,1,0:T(8,128)(2,1)}), bf16[32,64,128]{2,1,0:T(8,128)(2,1)S(1)}, u32[]{:S(2)}, u32[]{:S(2)}) async-start(bf16[32,64,128]{2,1,0:T(8,128)(2,1)} %get-tuple-element.45.after), calls=%async_computation.1 | async-start | bytes 1048576 | tf_op jit(solution)/shard_map/all_to_all | solution.py:384
  91.9 1.6 %collective-permute-start.16 = (bf16[32,128]{1,0:T(8,128)(2,1)S(1)}, bf16[32,128]{1,0:T(8,128)(2,1)S(1)}, u32[]{:S(2)}, u32[]{:S(2)}) collective-permute-start(bf16[32,128]{1,0:T(8,128)(2,1)S(1)} %get-tuple-element.47), channel_id=1, source_target_pairs={{0,3},{1,0},{2,1},{3,2},{4,7},{5,4},{6,5},{7,6},{8,11},{9,8},{10,9... | collective-permute-start | bytes 24584 | tf_op jit(solution)/shard_map/ppermute | solution.py:273
  94.8 3.1 %collective-permute-done.17.part2 = bf16[32,128]{1,0:T(8,128)(2,1)S(1)} collective-permute-done((bf16[32,128]{1,0:T(8,128)(2,1)S(1)}, bf16[32,128]{1,0:T(8,128)(2,1)S(1)}, u32[]{:S(2)}, u32[]{:S(2)}) %collective-permute-start.17) | collective-permute-done | bytes 8224 | tf_op jit(solution)/shard_map/ppermute | solution.py:273
  98.2 2.8 %collective-permute-start.21 = (bf16[2,32,256]{2,1,0:T(8,128)(2,1)S(1)}, bf16[2,32,256]{2,1,0:T(8,128)(2,1)S(1)}, u32[]{:S(2)}, u32[]{:S(2)}) collective-permute-start(bf16[2,32,256]{2,1,0:T(8,128)(2,1)S(1)} %assemble.1), channel_id=1, source_target_pairs={{0,96},{4,100},{8,104},{12,108},{16,112},{20,116},{24,120},{28,124... | collective-permute-start | bytes 98312 | tf_op jit(solution)/shard_map/ppermute | solution.py:283
  101.5 0.7 collective-permute-start.19
  102.2 3.2 %collective-permute-done.20 = bf16[2,32,256]{2,1,0:T(8,128)(2,1)S(1)} collective-permute-done((bf16[2,32,256]{2,1,0:T(8,128)(2,1)S(1)}, bf16[2,32,256]{2,1,0:T(8,128)(2,1)S(1)}, u32[]{:S(2)}, u32[]{:S(2)}) %collective-permute-start.20) | collective-permute-done | bytes 32800 | tf_op jit(solution)/shard_map/ppermute | solution.py:283
  105.7 2.5 %collective-permute-start.24 = (bf16[4,2,32,256]{3,2,1,0:T(8,128)(2,1)S(1)}, bf16[4,2,32,256]{3,2,1,0:T(8,128)(2,1)S(1)}, u32[]{:S(2)}, u32[]{:S(2)}) collective-permute-start(bf16[4,2,32,256]{3,2,1,0:T(8,128)(2,1)S(1)} %pad_maximum_fusion.refs_0_), channel_id=1, source_target_pairs={{0,24},{4,28},{8,0},{12,4},{16,8},{20,12},{24,16},{28,20},{32,56},... | collective-permute-start | bytes 393224 | tf_op jit(solution)/shard_map/ppermute | solution.py:283
  109.3 4.1 %collective-permute-start.25 = (bf16[4,2,32,256]{3,2,1,0:T(8,128)(2,1)S(1)}, bf16[4,2,32,256]{3,2,1,0:T(8,128)(2,1)S(1)}, u32[]{:S(2)}, u32[]{:S(2)}) collective-permute-start(bf16[4,2,32,256]{3,2,1,0:T(8,128)(2,1)S(1)} %pad_maximum_fusion.refs_0_), channel_id=1, source_target_pairs={{0,4},{4,0},{8,12},{12,8},{16,20},{20,16},{24,28},{28,24},{32,36},... | collective-permute-start | bytes 393224 | tf_op jit(solution)/shard_map/ppermute | solution.py:283
  113.5 0.8 collective-permute-start.28
  114.3 4.0 %collective-permute-start.27 = (bf16[4,2,32,256]{3,2,1,0:T(8,128)(2,1)S(1)}, bf16[4,2,32,256]{3,2,1,0:T(8,128)(2,1)S(1)}, u32[]{:S(2)}, u32[]{:S(2)}) collective-permute-start(bf16[4,2,32,256]{3,2,1,0:T(8,128)(2,1)S(1)} %collective-permute-done.23.refs_2_), channel_id=1, source_target_pairs={{0,4},{4,0},{8,12},{12,8},{16,20},{20,16},{24,28},{28,24},{32,36},... | collective-permute-start | bytes 393224 | tf_op jit(solution)/shard_map/ppermute | solution.py:283
  118.4 1.3 %collective-permute-start.26 = (bf16[4,2,32,256]{3,2,1,0:T(8,128)(2,1)S(1)}, bf16[4,2,32,256]{3,2,1,0:T(8,128)(2,1)S(1)}, u32[]{:S(2)}, u32[]{:S(2)}) collective-permute-start(bf16[4,2,32,256]{3,2,1,0:T(8,128)(2,1)S(1)} %collective-permute-done.22.refs_1_), channel_id=1, source_target_pairs={{0,4},{4,0},{8,12},{12,8},{16,20},{20,16},{24,28},{28,24},{32,36},... | collective-permute-start | bytes 393224 | tf_op jit(solution)/shard_map/ppermute | solution.py:283
  119.8 1.7 %return_add.1 = f32[64,2048]{1,0:T(8,128)} custom-call(s32[1,32]{1,0:T(1,128)S(1)} %copy-done.6, s32[1,32]{1,0:T(1,128)S(1)} %copy-done.8, f32[64,2048]{1,0:T(8,128)S(1)} %get-tuple-element.44.local, bf16[32,64,128]{2,1,0:T(8,128)(2,1)S(1)} %all-to-all-done.1.returned), custom_call_target="tpu_custom_call" | custom-call | bytes 2097152 | tf_op jit(solution)/shard_map/return_add/pallas_call | solution.py:385
  121.4 2.5 %unpack.1 = (f32[27,64,256]{2,1,0:T(8,128)}, f32[64,256]{1,0:T(8,128)}) custom-call(s32[3]{0:T(128)S(1)} %pad_add_fusion.chip, bf16[4,2,32,256]{3,2,1,0:T(8,128)(2,1)S(1)} %pad_maximum_fusion.refs_0_, bf16[4,2,32,256]{3,2,1,0:T(8,128)(2,1)S(1)} %collective-permute-done.22.refs_1_, bf16[4,2,32,256]{3,2,1,0:T(8,128)(2,1)S(1)} %collective-permute-done.23.refs_2_, ...), custom_call_target="tpu_custom_call" | custom-call | bytes 3145728 | tf_op jit(solution)/shard_map/unpack/pallas_call | solution.py:405
  (65 shorter events, 6.2 us)
Async XLA Ops:
  0.6 12.4 %copy-start.1 = (bf16[27,64,256]{2,1,0:T(8,128)(2,1)S(1)}, bf16[27,64,256]{2,1,0:T(8,128)(2,1)}, u32[]{:S(2)}) copy-start(bf16[27,64,256]{2,1,0:T(8,128)(2,1)} %conv_weight.1) | copy-start | bytes 2654212
  0.6 1.0 copy-start.2
  1.7 0.7 copy-start.5
  2.3 0.7 copy-start.7
  3.0 10.1 %copy-start.4 = (bf16[64,256]{1,0:T(8,128)(2,1)S(1)}, bf16[64,256]{1,0:T(8,128)(2,1)}, u32[]{:S(2)}) copy-start(bf16[64,256]{1,0:T(8,128)(2,1)} %coarse_weight.1) | copy-start | bytes 98308
  4.5 27.5 %all-to-all-start = ((bf16[32,64,128]{2,1,0:T(8,128)(2,1)}), bf16[32,64,128]{2,1,0:T(8,128)(2,1)S(1)}, u32[]{:S(2)}, u32[]{:S(2)}) async-start(bf16[32,64,128]{2,1,0:T(8,128)(2,1)} %pack.1), calls=%async_computation | async-start | bytes 1048576 | tf_op jit(solution)/shard_map/all_to_all | solution.py:306
  13.1 4.9 %copy-start.14 = (s32[27,16]{0,1:T(8,128)S(1)}, s32[27,16]{0,1:T(8,128)}, u32[]{:S(2)}) copy-start(s32[27,16]{0,1:T(8,128)} %param.13) | copy-start | bytes 5188
  13.4 18.6 %copy-start.3 = (bf16[64,2048]{1,0:T(8,128)(2,1)S(1)}, bf16[64,2048]{1,0:T(8,128)(2,1)}, u32[]{:S(2)}) copy-start(bf16[64,2048]{1,0:T(8,128)(2,1)} %features.9) | copy-start | bytes 786436
  13.5 13.5 %collective-permute-start.2 = (bf16[14,64,128]{2,1,0:T(8,128)(2,1)S(1)}, bf16[14,64,128]{2,1,0:T(8,128)(2,1)S(1)}, u32[]{:S(2)}, u32[]{:S(2)}) collective-permute-start(bf16[14,64,128]{2,1,0:T(8,128)(2,1)S(1)} %get-tuple-element.52), channel_id=1, source_target_pairs={{0,3},{1,0},{2,1},{3,2},{4,7},{5,4},{6,5},{7,6},{8,11},{9,8},{10,9... | collective-permute-start | bytes 688136 | tf_op jit(solution)/shard_map/ppermute | solution.py:273
  17.3 9.7 %collective-permute-start.1 = (bf16[14,64,128]{2,1,0:T(8,128)(2,1)S(1)}, bf16[14,64,128]{2,1,0:T(8,128)(2,1)S(1)}, u32[]{:S(2)}, u32[]{:S(2)}) collective-permute-start(bf16[14,64,128]{2,1,0:T(8,128)(2,1)S(1)} %get-tuple-element.53), channel_id=1, source_target_pairs={{0,2},{1,3},{2,0},{3,1},{4,6},{5,7},{6,4},{7,5},{8,10},{9,11},{10,... | collective-permute-start | bytes 688136 | tf_op jit(solution)/shard_map/ppermute | solution.py:273
  17.3 13.4 %collective-permute-start = (bf16[14,64,128]{2,1,0:T(8,128)(2,1)S(1)}, bf16[14,64,128]{2,1,0:T(8,128)(2,1)S(1)}, u32[]{:S(2)}, u32[]{:S(2)}) collective-permute-start(bf16[14,64,128]{2,1,0:T(8,128)(2,1)S(1)} %get-tuple-element.54), channel_id=1, source_target_pairs={{0,1},{1,2},{2,3},{3,0},{4,5},{5,6},{6,7},{7,4},{8,9},{9,10},{10,1... | collective-permute-start | bytes 688136 | tf_op jit(solution)/shard_map/ppermute | solution.py:273
  31.1 0.9 copy-start.9
  32.0 1.2 copy-start.10
  33.2 3.7 %copy-start.11 = (bf16[256,1792]{1,0:T(8,128)(2,1)S(1)}, bf16[256,1792]{1,0:T(8,128)(2,1)}, u32[]{:S(2)}) copy-start(bf16[256,1792]{1,0:T(8,128)(2,1)} %copy-done.9) | copy-start | bytes 2752516
  35.3 9.1 %copy-start = (bf16[64,2048]{1,0:T(8,128)(2,1)S(1)}, bf16[64,2048]{1,0:T(8,128)(2,1)}, u32[]{:S(2)}) copy-start(bf16[64,2048]{1,0:T(8,128)(2,1)} %out_grad.3) | copy-start | bytes 786436
  35.3 7.4 %collective-permute-start.6 = (bf16[64,1024]{1,0:T(8,128)(2,1)S(1)}, bf16[64,1024]{1,0:T(8,128)(2,1)S(1)}, u32[]{:S(2)}, u32[]{:S(2)}) collective-permute-start(bf16[64,1024]{1,0:T(8,128)(2,1)S(1)} %get-tuple-element.34), channel_id=1, source_target_pairs={{0,3},{1,0},{2,1},{3,2},{4,7},{5,4},{6,5},{7,6},{8,11},{9,8},{10,9... | collective-permute-start | bytes 393224 | tf_op jit(solution)/shard_map/ppermute | solution.py:273
  35.4 8.1 %collective-permute-start.7 = (bf16[64,1024]{1,0:T(8,128)(2,1)S(1)}, bf16[64,1024]{1,0:T(8,128)(2,1)S(1)}, u32[]{:S(2)}, u32[]{:S(2)}) collective-permute-start(bf16[64,1024]{1,0:T(8,128)(2,1)S(1)} %get-tuple-element.35), channel_id=1, source_target_pairs={{0,2},{1,3},{2,0},{3,1},{4,6},{5,7},{6,4},{7,5},{8,10},{9,11},{10,... | collective-permute-start | bytes 393224 | tf_op jit(solution)/shard_map/ppermute | solution.py:273
  36.1 8.3 %collective-permute-start.8 = (bf16[64,1024]{1,0:T(8,128)(2,1)S(1)}, bf16[64,1024]{1,0:T(8,128)(2,1)S(1)}, u32[]{:S(2)}, u32[]{:S(2)}) collective-permute-start(bf16[64,1024]{1,0:T(8,128)(2,1)S(1)} %get-tuple-element.36), channel_id=1, source_target_pairs={{0,1},{1,2},{2,3},{3,0},{4,5},{5,6},{6,7},{7,4},{8,9},{9,10},{10,1... | collective-permute-start | bytes 393224 | tf_op jit(solution)/shard_map/ppermute | solution.py:273
  39.0 7.2 %collective-permute-start.3 = (bf16[64,1024]{1,0:T(8,128)(2,1)S(1)}, bf16[64,1024]{1,0:T(8,128)(2,1)S(1)}, u32[]{:S(2)}, u32[]{:S(2)}) collective-permute-start(bf16[64,1024]{1,0:T(8,128)(2,1)S(1)} %get-tuple-element.30), channel_id=1, source_target_pairs={{0,3},{1,0},{2,1},{3,2},{4,7},{5,4},{6,5},{7,6},{8,11},{9,8},{10,9... | collective-permute-start | bytes 393224 | tf_op jit(solution)/shard_map/ppermute | solution.py:273
  41.4 5.6 %collective-permute-start.4 = (bf16[64,1024]{1,0:T(8,128)(2,1)S(1)}, bf16[64,1024]{1,0:T(8,128)(2,1)S(1)}, u32[]{:S(2)}, u32[]{:S(2)}) collective-permute-start(bf16[64,1024]{1,0:T(8,128)(2,1)S(1)} %get-tuple-element.31), channel_id=1, source_target_pairs={{0,2},{1,3},{2,0},{3,1},{4,6},{5,7},{6,4},{7,5},{8,10},{9,11},{10,... | collective-permute-start | bytes 393224 | tf_op jit(solution)/shard_map/ppermute | solution.py:273
  42.7 7.7 %collective-permute-start.5 = (bf16[64,1024]{1,0:T(8,128)(2,1)S(1)}, bf16[64,1024]{1,0:T(8,128)(2,1)S(1)}, u32[]{:S(2)}, u32[]{:S(2)}) collective-permute-start(bf16[64,1024]{1,0:T(8,128)(2,1)S(1)} %get-tuple-element.32), channel_id=1, source_target_pairs={{0,1},{1,2},{2,3},{3,0},{4,5},{5,6},{6,7},{7,4},{8,9},{9,10},{10,1... | collective-permute-start | bytes 393224 | tf_op jit(solution)/shard_map/ppermute | solution.py:273
  44.5 8.8 %collective-permute-start.11 = (bf16[64,1024]{1,0:T(8,128)(2,1)S(1)}, bf16[64,1024]{1,0:T(8,128)(2,1)S(1)}, u32[]{:S(2)}, u32[]{:S(2)}) collective-permute-start(bf16[64,1024]{1,0:T(8,128)(2,1)S(1)} %get-tuple-element.40.grad0.g00), channel_id=1, source_target_pairs={{0,3},{1,0},{2,1},{3,2},{4,7},{5,4},{6,5},{7,6},{8,11},{9,8},{10,9... | collective-permute-start | bytes 393224 | tf_op jit(solution)/shard_map/ppermute | solution.py:273
  45.7 8.5 %collective-permute-start.10 = (bf16[64,1024]{1,0:T(8,128)(2,1)S(1)}, bf16[64,1024]{1,0:T(8,128)(2,1)S(1)}, u32[]{:S(2)}, u32[]{:S(2)}) collective-permute-start(bf16[64,1024]{1,0:T(8,128)(2,1)S(1)} %get-tuple-element.40.grad0.g00), channel_id=1, source_target_pairs={{0,2},{1,3},{2,0},{3,1},{4,6},{5,7},{6,4},{7,5},{8,10},{9,11},{10,... | collective-permute-start | bytes 393224 | tf_op jit(solution)/shard_map/ppermute | solution.py:273
  46.1 9.9 %collective-permute-start.9 = (bf16[64,1024]{1,0:T(8,128)(2,1)S(1)}, bf16[64,1024]{1,0:T(8,128)(2,1)S(1)}, u32[]{:S(2)}, u32[]{:S(2)}) collective-permute-start(bf16[64,1024]{1,0:T(8,128)(2,1)S(1)} %get-tuple-element.40.grad0.g00), channel_id=1, source_target_pairs={{0,1},{1,2},{2,3},{3,0},{4,5},{5,6},{6,7},{7,4},{8,9},{9,10},{10,1... | collective-permute-start | bytes 393224 | tf_op jit(solution)/shard_map/ppermute | solution.py:273
  51.3 6.9 %collective-permute-start.14 = (bf16[64,1024]{1,0:T(8,128)(2,1)S(1)}, bf16[64,1024]{1,0:T(8,128)(2,1)S(1)}, u32[]{:S(2)}, u32[]{:S(2)}) collective-permute-start(bf16[64,1024]{1,0:T(8,128)(2,1)S(1)} %get-tuple-element.41.grad0.g10), channel_id=1, source_target_pairs={{0,3},{1,0},{2,1},{3,2},{4,7},{5,4},{6,5},{7,6},{8,11},{9,8},{10,9... | collective-permute-start | bytes 393224 | tf_op jit(solution)/shard_map/ppermute | solution.py:273
  51.3 6.9 %collective-permute-start.13 = (bf16[64,1024]{1,0:T(8,128)(2,1)S(1)}, bf16[64,1024]{1,0:T(8,128)(2,1)S(1)}, u32[]{:S(2)}, u32[]{:S(2)}) collective-permute-start(bf16[64,1024]{1,0:T(8,128)(2,1)S(1)} %get-tuple-element.41.grad0.g10), channel_id=1, source_target_pairs={{0,2},{1,3},{2,0},{3,1},{4,6},{5,7},{6,4},{7,5},{8,10},{9,11},{10,... | collective-permute-start | bytes 393224 | tf_op jit(solution)/shard_map/ppermute | solution.py:273
  53.3 6.3 %collective-permute-start.12 = (bf16[64,1024]{1,0:T(8,128)(2,1)S(1)}, bf16[64,1024]{1,0:T(8,128)(2,1)S(1)}, u32[]{:S(2)}, u32[]{:S(2)}) collective-permute-start(bf16[64,1024]{1,0:T(8,128)(2,1)S(1)} %get-tuple-element.41.grad0.g10), channel_id=1, source_target_pairs={{0,1},{1,2},{2,3},{3,0},{4,5},{5,6},{6,7},{7,4},{8,9},{9,10},{10,1... | collective-permute-start | bytes 393224 | tf_op jit(solution)/shard_map/ppermute | solution.py:273
  59.6 9.5 %copy-start.12 = (bf16[64,1024]{1,0:T(8,128)(2,1)}, bf16[64,1024]{1,0:T(8,128)(2,1)S(1)}, u32[]{:S(2)}) copy-start(bf16[64,1024]{1,0:T(8,128)(2,1)S(1)} %collective-permute-done.12.grad1.g11) | copy-start | bytes 393220
  61.9 6.3 %collective-permute-start.15 = (bf16[14,4,32,128]{3,2,1,0:T(8,128)(2,1)S(1)}, bf16[14,4,32,128]{3,2,1,0:T(8,128)(2,1)S(1)}, u32[]{:S(2)}, u32[]{:S(2)}) collective-permute-start(bf16[14,4,32,128]{3,2,1,0:T(8,128)(2,1)S(1)} %get-tuple-element.43), channel_id=1, source_target_pairs={{0,4},{4,0},{8,12},{12,8},{16,20},{20,16},{24,28},{28,24},{32,36},... | collective-permute-start | bytes 1376264 | tf_op jit(solution)/shard_map/ppermute | solution.py:283
  69.1 17.4 %all-to-all-start.2 = ((bf16[16,4,32,128]{3,2,1,0:T(8,128)(2,1)}), bf16[16,4,32,128]{3,2,1,0:T(8,128)(2,1)S(1)}, u32[]{:S(2)}, u32[]{:S(2)}) async-start(bf16[16,4,32,128]{3,2,1,0:T(8,128)(2,1)} %pair_sum.1.after), calls=%async_computation.2 | async-start | bytes 1048576 | tf_op jit(solution)/shard_map/all_to_all | solution.py:368
  75.8 0.9 copy-start.13
  83.1 36.6 %copy-start.6 = (s32[1,32]{1,0:T(1,128)S(1)}, s32[1,32]{1,0:T(1,128)}, u32[]{:S(2)}) copy-start(s32[1,32]{1,0:T(1,128)} %send_block.3) | copy-start | bytes 388
  83.1 36.6 %copy-start.8 = (s32[1,32]{1,0:T(1,128)S(1)}, s32[1,32]{1,0:T(1,128)}, u32[]{:S(2)}) copy-start(s32[1,32]{1,0:T(1,128)} %send_count.3) | copy-start | bytes 388
  86.5 33.2 %all-to-all-start.1 = ((bf16[32,64,128]{2,1,0:T(8,128)(2,1)}), bf16[32,64,128]{2,1,0:T(8,128)(2,1)S(1)}, u32[]{:S(2)}, u32[]{:S(2)}) async-start(bf16[32,64,128]{2,1,0:T(8,128)(2,1)} %get-tuple-element.45.after), calls=%async_computation.1 | async-start | bytes 1048576 | tf_op jit(solution)/shard_map/all_to_all | solution.py:384
  91.9 2.8 %collective-permute-start.16 = (bf16[32,128]{1,0:T(8,128)(2,1)S(1)}, bf16[32,128]{1,0:T(8,128)(2,1)S(1)}, u32[]{:S(2)}, u32[]{:S(2)}) collective-permute-start(bf16[32,128]{1,0:T(8,128)(2,1)S(1)} %get-tuple-element.47), channel_id=1, source_target_pairs={{0,3},{1,0},{2,1},{3,2},{4,7},{5,4},{6,5},{7,6},{8,11},{9,8},{10,9... | collective-permute-start | bytes 24584 | tf_op jit(solution)/shard_map/ppermute | solution.py:273
  93.5 4.3 %collective-permute-start.17 = (bf16[32,128]{1,0:T(8,128)(2,1)S(1)}, bf16[32,128]{1,0:T(8,128)(2,1)S(1)}, u32[]{:S(2)}, u32[]{:S(2)}) collective-permute-start(bf16[32,128]{1,0:T(8,128)(2,1)S(1)} %get-tuple-element.48), channel_id=1, source_target_pairs={{0,2},{1,3},{2,0},{3,1},{4,6},{5,7},{6,4},{7,5},{8,10},{9,11},{10,... | collective-permute-start | bytes 24584 | tf_op jit(solution)/shard_map/ppermute | solution.py:273
  94.1 4.0 %collective-permute-start.18 = (bf16[32,128]{1,0:T(8,128)(2,1)S(1)}, bf16[32,128]{1,0:T(8,128)(2,1)S(1)}, u32[]{:S(2)}, u32[]{:S(2)}) collective-permute-start(bf16[32,128]{1,0:T(8,128)(2,1)S(1)} %get-tuple-element.49), channel_id=1, source_target_pairs={{0,1},{1,2},{2,3},{3,0},{4,5},{5,6},{6,7},{7,4},{8,9},{9,10},{10,1... | collective-permute-start | bytes 24584 | tf_op jit(solution)/shard_map/ppermute | solution.py:273
  98.2 3.9 %collective-permute-start.21 = (bf16[2,32,256]{2,1,0:T(8,128)(2,1)S(1)}, bf16[2,32,256]{2,1,0:T(8,128)(2,1)S(1)}, u32[]{:S(2)}, u32[]{:S(2)}) collective-permute-start(bf16[2,32,256]{2,1,0:T(8,128)(2,1)S(1)} %assemble.1), channel_id=1, source_target_pairs={{0,96},{4,100},{8,104},{12,108},{16,112},{20,116},{24,120},{28,124... | collective-permute-start | bytes 98312 | tf_op jit(solution)/shard_map/ppermute | solution.py:283
  101.1 4.3 %collective-permute-start.20 = (bf16[2,32,256]{2,1,0:T(8,128)(2,1)S(1)}, bf16[2,32,256]{2,1,0:T(8,128)(2,1)S(1)}, u32[]{:S(2)}, u32[]{:S(2)}) collective-permute-start(bf16[2,32,256]{2,1,0:T(8,128)(2,1)S(1)} %assemble.1), channel_id=1, source_target_pairs={{0,64},{4,68},{8,72},{12,76},{16,80},{20,84},{24,88},{28,92},{32,9... | collective-permute-start | bytes 98312 | tf_op jit(solution)/shard_map/ppermute | solution.py:283
  101.5 4.2 %collective-permute-start.19 = (bf16[2,32,256]{2,1,0:T(8,128)(2,1)S(1)}, bf16[2,32,256]{2,1,0:T(8,128)(2,1)S(1)}, u32[]{:S(2)}, u32[]{:S(2)}) collective-permute-start(bf16[2,32,256]{2,1,0:T(8,128)(2,1)S(1)} %assemble.1), channel_id=1, source_target_pairs={{0,32},{4,36},{8,40},{12,44},{16,48},{20,52},{24,56},{28,60},{32,6... | collective-permute-start | bytes 98312 | tf_op jit(solution)/shard_map/ppermute | solution.py:283
  105.7 7.8 %collective-permute-start.24 = (bf16[4,2,32,256]{3,2,1,0:T(8,128)(2,1)S(1)}, bf16[4,2,32,256]{3,2,1,0:T(8,128)(2,1)S(1)}, u32[]{:S(2)}, u32[]{:S(2)}) collective-permute-start(bf16[4,2,32,256]{3,2,1,0:T(8,128)(2,1)S(1)} %pad_maximum_fusion.refs_0_), channel_id=1, source_target_pairs={{0,24},{4,28},{8,0},{12,4},{16,8},{20,12},{24,16},{28,20},{32,56},... | collective-permute-start | bytes 393224 | tf_op jit(solution)/shard_map/ppermute | solution.py:283
  108.2 6.1 %collective-permute-start.23 = (bf16[4,2,32,256]{3,2,1,0:T(8,128)(2,1)S(1)}, bf16[4,2,32,256]{3,2,1,0:T(8,128)(2,1)S(1)}, u32[]{:S(2)}, u32[]{:S(2)}) collective-permute-start(bf16[4,2,32,256]{3,2,1,0:T(8,128)(2,1)S(1)} %pad_maximum_fusion.refs_0_), channel_id=1, source_target_pairs={{0,16},{4,20},{8,24},{12,28},{16,0},{20,4},{24,8},{28,12},{32,48},... | collective-permute-start | bytes 393224 | tf_op jit(solution)/shard_map/ppermute | solution.py:283
  108.8 9.6 %collective-permute-start.22 = (bf16[4,2,32,256]{3,2,1,0:T(8,128)(2,1)S(1)}, bf16[4,2,32,256]{3,2,1,0:T(8,128)(2,1)S(1)}, u32[]{:S(2)}, u32[]{:S(2)}) collective-permute-start(bf16[4,2,32,256]{3,2,1,0:T(8,128)(2,1)S(1)} %pad_maximum_fusion.refs_0_), channel_id=1, source_target_pairs={{0,8},{4,12},{8,16},{12,20},{16,24},{20,28},{24,0},{28,4},{32,40},... | collective-permute-start | bytes 393224 | tf_op jit(solution)/shard_map/ppermute | solution.py:283
  109.3 12.1 %collective-permute-start.25 = (bf16[4,2,32,256]{3,2,1,0:T(8,128)(2,1)S(1)}, bf16[4,2,32,256]{3,2,1,0:T(8,128)(2,1)S(1)}, u32[]{:S(2)}, u32[]{:S(2)}) collective-permute-start(bf16[4,2,32,256]{3,2,1,0:T(8,128)(2,1)S(1)} %pad_maximum_fusion.refs_0_), channel_id=1, source_target_pairs={{0,4},{4,0},{8,12},{12,8},{16,20},{20,16},{24,28},{28,24},{32,36},... | collective-permute-start | bytes 393224 | tf_op jit(solution)/shard_map/ppermute | solution.py:283
  113.5 7.9 %collective-permute-start.28 = (bf16[4,2,32,256]{3,2,1,0:T(8,128)(2,1)S(1)}, bf16[4,2,32,256]{3,2,1,0:T(8,128)(2,1)S(1)}, u32[]{:S(2)}, u32[]{:S(2)}) collective-permute-start(bf16[4,2,32,256]{3,2,1,0:T(8,128)(2,1)S(1)} %collective-permute-done.24.refs_3_), channel_id=1, source_target_pairs={{0,4},{4,0},{8,12},{12,8},{16,20},{20,16},{24,28},{28,24},{32,36},... | collective-permute-start | bytes 393224 | tf_op jit(solution)/shard_map/ppermute | solution.py:283
  114.3 7.1 %collective-permute-start.27 = (bf16[4,2,32,256]{3,2,1,0:T(8,128)(2,1)S(1)}, bf16[4,2,32,256]{3,2,1,0:T(8,128)(2,1)S(1)}, u32[]{:S(2)}, u32[]{:S(2)}) collective-permute-start(bf16[4,2,32,256]{3,2,1,0:T(8,128)(2,1)S(1)} %collective-permute-done.23.refs_2_), channel_id=1, source_target_pairs={{0,4},{4,0},{8,12},{12,8},{16,20},{20,16},{24,28},{28,24},{32,36},... | collective-permute-start | bytes 393224 | tf_op jit(solution)/shard_map/ppermute | solution.py:283
  118.4 3.1 %collective-permute-start.26 = (bf16[4,2,32,256]{3,2,1,0:T(8,128)(2,1)S(1)}, bf16[4,2,32,256]{3,2,1,0:T(8,128)(2,1)S(1)}, u32[]{:S(2)}, u32[]{:S(2)}) collective-permute-start(bf16[4,2,32,256]{3,2,1,0:T(8,128)(2,1)S(1)} %collective-permute-done.22.refs_1_), channel_id=1, source_target_pairs={{0,4},{4,0},{8,12},{12,8},{16,20},{20,16},{24,28},{28,24},{32,36},... | collective-permute-start | bytes 393224 | tf_op jit(solution)/shard_map/ppermute | solution.py:283

commit v5 on v3

--- a/solution.py
+++ b/solution.py
@@ -15,7 +15,7 @@
 F32 = jnp.float32
 
 
-def call(kernel, name, outs, kinds, scratch=(), flops=0, size=0, limit=48 << 20):
+def call(kernel, name, outs, kinds, scratch=(), flops=0, size=0, limit=24 << 20):
     space = {"s": pltpu.SMEM, "v": pltpu.VMEM, "a": pl.ANY}
     many = isinstance(outs, (list, tuple))
     spec = pl.BlockSpec(memory_space=pltpu.VMEM)
@@ -41,8 +41,7 @@
     return pl.ds(pl.multiple_of(index * BLOCK, BLOCK), BLOCK)
 
 
-def pack_kernel(send_block, send_count, features, after, outgoing):
-    del after
+def pack_kernel(send_block, send_count, features, outgoing):
     for peer in range(outgoing.shape[0]):
         block = features[:, columns(send_block[0, peer])]
         outgoing[peer] = block * send_count[0, peer].astype(F32).astype(BF)
@@ -62,10 +61,10 @@
             pieces[step * PAIRS + pair] = jnp.where(target < 2, low, high)
 
 
-def join_kernel(piece0, piece1, piece2, piece3, weight, flipped):
+def join_kernel(piece0, piece1, piece2, piece3, after, flipped):
+    del after
     for pair in range(PAIRS):
         tile = jnp.concatenate([p[pair] for p in (piece0, piece1, piece2, piece3)], axis=0)
-        weight[:, pair * BLOCK : (pair + 1) * BLOCK] = tile
         flipped[pair * BLOCK : (pair + 1) * BLOCK, :] = tile.T
 
 
@@ -99,18 +98,21 @@
         gathered[OFFSETS * quarter :, block * BLOCK : (block + 1) * BLOCK] = pooled
 
 
-def forward_kernel(
-    half, neighbour, features, incoming, weight, out0, out1, out2, out3, table, gathered
-):
+def forward_kernel(half, neighbour, features, incoming, *refs):
+    pieces, outs, (weight, table, gathered) = refs[:4], refs[4:8], refs[8:]
     quarter, row_count = features.shape
     nblocks = row_count // BLOCK
     extent = nblocks + incoming.shape[0]
+    for step, piece in enumerate(pieces):
+        for pair in range(PAIRS):
+            rows = slice(step * quarter, (step + 1) * quarter)
+            weight[rows, pair * BLOCK : (pair + 1) * BLOCK] = piece[pair]
     fill_table(features, incoming, table, nblocks)
     fill_gathered(neighbour, table, gathered, half * nblocks // 2, extent)
     for tile in range(row_count // 512):
         cut = slice(tile * 256, (tile + 1) * 256)
         total = jnp.dot(weight[...], gathered[:, cut], preferred_element_type=F32)
-        for step, out in enumerate((out0, out1, out2, out3)):
+        for step, out in enumerate(outs):
             out[:, cut] = total[step * quarter : (step + 1) * quarter].astype(out.dtype)
 
 
@@ -152,7 +154,7 @@
 
 
 def weight_second_kernel(
-    place, neighbour, features, incoming, grad0, grad1, grad2, grad3, held, parts, table, gathered, flipped
+    core, neighbour, features, incoming, grad0, grad1, grad2, grad3, held, keep, give, table, gathered, flipped
 ):
     quarter = features.shape[0]
     grads = (grad0, grad1, grad2, grad3)
@@ -161,22 +163,36 @@
     for pair in range(PAIRS):
         rows = slice(pair * BLOCK, (pair + 1) * BLOCK)
         product = jnp.dot(gathered[rows, :], flipped[...], preferred_element_type=F32)
-        upright = (product + held[rows, :]).T.astype(BF)
+        upright = (product + held[rows, :]).T
         for step in range(4):
-            target = lax.rem(place[0] - step + 4, 4)
-            for side in range(2):
-                start = step * quarter + side * half
-                parts[2 * pair + side, target] = upright[start : start + half]
-    for spare in range(2 * PAIRS, parts.shape[0]):
+            low = upright[step * quarter : step * quarter + half]
+            high = upright[step * quarter + half : (step + 1) * quarter]
+            keep[pair, step] = jnp.where(core[0] == 0, low, high)
+            give[pair, step] = jnp.where(core[0] == 0, high, low).astype(BF)
+
+
+def pair_kernel(place, keep, arrived, parts):
+    for step in range(4):
+        target = lax.rem(place[0] - step + 4, 4)
+        for pair in range(PAIRS):
+            parts[pair, target] = (keep[pair, step] + arrived[pair, step].astype(F32)).astype(BF)
+    for spare in range(PAIRS, parts.shape[0]):
         parts[spare] = jnp.zeros(parts.shape[1:], BF)
 
 
+def peer_at(chip, step_y, step_x, flip):
+    y = lax.rem(chip[0] + step_y + 4, 4)
+    x = lax.rem(chip[1] + step_x + 4, 4)
+    return (y * 4 + x) * 2 + (1 - chip[2] if flip else chip[2])
+
+
 def table_kernel(
-    neighbour, weight_t, g00, g01, g02, g03, g10, g11, g12, g13, local, returned, total, spread
+    chip, neighbour, weight_t, g00, g01, g02, g03, g10, g11, g12, g13, after, local, home, away, total, spread
 ):
+    del after
     quarter, row_count = local.shape
     nblocks = row_count // BLOCK
-    extent = nblocks + returned.shape[0]
+    extent = total.shape[0] - 1
     total[...] = jnp.zeros_like(total)
     mean = mean_matrix()
     for tile in range(nblocks // 2):
@@ -204,26 +220,47 @@
             )
     for block in range(nblocks):
         local[:, block * BLOCK : (block + 1) * BLOCK] = total[block]
-    returned[...] = total[nblocks:extent].astype(BF)
-
-
-def return_kernel(send_block, send_count, local, returned, input_grad):
+    for flip, out in enumerate((home, away)):
+        for x in range(4):
+            for y in range(4):
+                out[x, y] = total[nblocks + peer_at(chip, y, x, flip)].astype(BF)
+
+
+def by_x_kernel(home, away, *outs):
+    for x, out in enumerate(outs):
+        for y in range(4):
+            out[y, 0] = home[x, y]
+            out[y, 1] = away[x, y]
+
+
+def by_y_kernel(*refs):
+    for y, out in enumerate(refs[4:]):
+        for x, ref in enumerate(refs[:4]):
+            out[x] = ref[y]
+
+
+def return_kernel(chip, send_block, send_count, local, from0, from1, from2, from3, input_grad):
     input_grad[...] = local[...]
-    for peer in range(returned.shape[0]):
-        factor = send_count[0, peer].astype(F32)
-        input_grad[:, columns(send_block[0, peer])] += returned[peer].astype(F32) * factor
-
-
-def sum_kernel(scale, parts, after, chunk):
+    for y, ref in enumerate((from0, from1, from2, from3)):
+        for x in range(4):
+            for flip in range(2):
+                peer = peer_at(chip, -y, -x, flip)
+                factor = send_count[0, peer].astype(F32)
+                input_grad[:, columns(send_block[0, peer])] += ref[x, flip].astype(F32) * factor
+
+
+def sum_kernel(scale, parts, after, chunks):
     del after
-    quarter = 64
+    half = parts.shape[3] // 2
     total = parts[0].astype(F32)
     for source in range(1, parts.shape[0]):
         total = total + parts[source].astype(F32)
     total = total * scale
     for side in range(2):
-        cut = slice(side * quarter, (side + 1) * quarter)
-        chunk[side] = jnp.concatenate([total[c, :, cut] for c in range(4)], axis=1).astype(BF)
+        cut = slice(side * half, (side + 1) * half)
+        value = jnp.concatenate([total[c, :, cut] for c in range(4)], axis=1).astype(BF)
+        for target in range(chunks.shape[0]):
+            chunks[target, side] = value
 
 
 def unpack_kernel(core, mine, other, conv_grad, coarse_grad):
@@ -243,6 +280,16 @@
     return lax.ppermute(value, axis, [(i, (i + step) % size) for i in range(size)])
 
 
+def move(value, step_y, step_x, flip):
+    moves = []
+    for y in range(4):
+        for x in range(4):
+            for core in range(2):
+                target = ((y + step_y) % 4 * 4 + (x + step_x) % 4) * 2 + (core ^ flip)
+                moves.append(((y * 4 + x) * 2 + core, target))
+    return lax.ppermute(value, "morton", moves)
+
+
 def local_step(features, conv_weight, coarse_weight, out_grad, send_block, send_count, neighbour):
     n_morton = lax.axis_size("morton")
     quarter, row_count = features.shape
@@ -252,26 +299,21 @@
     depth = TERMS * quarter
     flops = 2 * depth * channels * row_count
     place = lax.axis_index("chan").astype(jnp.int32).reshape(1)
+    spot = lax.axis_index("morton").astype(jnp.int32)
+    chip = jnp.stack([spot // 8, spot // 2 % 4, spot % 2])
+    core = (spot % 2).reshape(1)
     shape = jax.ShapeDtypeStruct
 
     pieces = call(
         split_kernel, "split", shape((4 * PAIRS, quarter, BLOCK), BF), "svv", size=2 << 20
     )(place, conv_weight, coarse_weight)
     outgoing = call(
-        pack_kernel, "pack", shape((n_morton, quarter, BLOCK), BF), "ssva", size=64 << 20
-    )(send_block, send_count, features, pieces)
+        pack_kernel, "pack", shape((n_morton, quarter, BLOCK), BF), "ssv", size=1 << 20
+    )(send_block, send_count, features)
     incoming = lax.all_to_all(outgoing, "morton", 0, 0, tiled=True)
 
     pieces = pieces.reshape(4, PAIRS, quarter, BLOCK)
     weights = [pieces[0]] + [shift(pieces[s], "chan", s) for s in (1, 2, 3)]
-    weight, weight_t = call(
-        join_kernel,
-        "join",
-        [shape((channels, depth), BF), shape((depth, channels), BF)],
-        "vvvv",
-        size=3 << 20,
-    )(*weights)
-
     middle = row_count // 2
     big = [pltpu.VMEM((extent + 1, quarter, BLOCK), BF), pltpu.VMEM((depth, middle), BF)]
     turned = [pltpu.VMEM((middle, channels), BF)]
@@ -283,11 +325,11 @@
             functools.partial(forward_kernel, half),
             f"forward{half}",
             [shape(part, F32)] + [shape(part, BF)] * 3,
-            "svvv",
-            big,
+            "svvvvvv",
+            [pltpu.VMEM((channels, depth), BF)] + big,
             flops // 2,
             3 << 20,
-        )(neighbour, features, incoming, weight)
+        )(neighbour, features, incoming, *weights)
         arrived = [shift(partial[s], "chan", -s) for s in (1, 2, 3)]
         output, grad = call(
             activation_end_kernel if half else activation_kernel,
@@ -298,6 +340,9 @@
         )(partial[0], *arrived, out_grad, *((output,) if half else ()))
         grads.append([grad] + [shift(grad, "chan", s) for s in (1, 2, 3)])
 
+    weight_t = call(join_kernel, "join", shape((depth, channels), BF), "vvvva", size=3 << 20)(
+        *weights, grads[0][0]
+    )
     held = call(
         weight_first_kernel,
         "weight_grad0",
@@ -307,63 +352,69 @@
         flops // 2,
         4 << 20,
     )(neighbour, features, incoming, *grads[0])
-    parts = call(
+    piece = (4, quarter // 2, BLOCK)
+    keep, give = call(
         weight_second_kernel,
         "weight_grad1",
-        shape((n_morton, 4, quarter // 2, BLOCK), BF),
+        [shape((PAIRS,) + piece, F32), shape((PAIRS,) + piece, BF)],
         "ssvvvvvvv",
         big + turned,
         flops // 2,
         4 << 20,
-    )(place, neighbour, features, incoming, *grads[1], held)
+    )(core, neighbour, features, incoming, *grads[1], held)
+    chips = n_morton // 2
+    parts = call(pair_kernel, "pair_sum", shape((chips,) + piece, BF), "svv", size=3 << 20)(
+        place, keep, move(give, 0, 0, 1)
+    )
+    same_core = [[2 * c + side for c in range(chips)] for side in range(2)]
+    same_core_all = [[device * 4 + z for device in group for z in range(4)] for group in same_core]
     received = lax.all_to_all(
-        parts.reshape(n_morton * 4, quarter // 2, BLOCK), ("morton", "chan"), 0, 0, tiled=True
+        parts.reshape((4 * chips,) + piece[1:]),
+        ("morton", "chan"),
+        0,
+        0,
+        axis_index_groups=same_core_all,
+        tiled=True,
     ).reshape(parts.shape)
 
-    local, outward = call(
+    blocks = (4, 4, quarter, BLOCK)
+    local, home, away = call(
         table_kernel,
         "table_grad",
-        [shape(wide, F32), shape((n_morton, quarter, BLOCK), BF)],
-        "s" + "v" * 9,
+        [shape(wide, F32), shape(blocks, BF), shape(blocks, BF)],
+        "ss" + "v" * 9 + "a",
         [
             pltpu.VMEM((extent + 1, quarter, BLOCK), F32),
             pltpu.VMEM((OFFSETS * quarter, 256), F32),
         ],
         flops,
         4 << 20,
-    )(neighbour, weight_t, *grads[0], *grads[1])
-    returned = lax.all_to_all(outward, "morton", 0, 0, tiled=True)
-    input_grad = call(return_kernel, "return_add", shape(wide, F32), "ssvv", size=2 << 20)(
-        send_block, send_count, local, returned
+    )(chip, neighbour, weight_t, *grads[0], *grads[1], parts)
+    bundle = [shape((4, 2, quarter, BLOCK), BF)] * 4
+    along_x = call(by_x_kernel, "by_x", bundle, "vv", size=1 << 20)(home, move(away, 0, 0, 1))
+    along_x = [along_x[0]] + [move(along_x[step], 0, step, 0) for step in (1, 2, 3)]
+    along_y = call(by_y_kernel, "by_y", bundle, "vvvv", size=1 << 20)(*along_x)
+    along_y = [along_y[0]] + [move(along_y[step], step, 0, 0) for step in (1, 2, 3)]
+    input_grad = call(return_kernel, "return_add", shape(wide, F32), "sssvvvvv", size=2 << 20)(
+        chip, send_block, send_count, local, *along_y
     )
 
     scale = float(row_count * n_morton) ** (-0.5)
-    chunk = call(
+    chunks = call(
         functools.partial(sum_kernel, scale),
         "sum_parts",
-        shape((2, quarter // 2, channels), BF),
+        shape((chips, 2, quarter // 2, channels), BF),
         "va",
         size=1 << 20,
-    )(received, outward)
-    chips = n_morton // 2
-    same_core = [[2 * chip + core for chip in range(chips)] for core in range(2)]
-    mine = lax.all_to_all(
-        jnp.broadcast_to(chunk, (chips,) + chunk.shape),
-        "morton",
-        0,
-        0,
-        axis_index_groups=same_core,
-        tiled=True,
-    )
-    other = lax.ppermute(mine, "morton", [(i, i ^ 1) for i in range(n_morton)])
-    core = lax.rem(lax.axis_index("morton"), 2).astype(jnp.int32).reshape(1)
+    )(received, home)
+    mine = lax.all_to_all(chunks, "morton", 0, 0, axis_index_groups=same_core, tiled=True)
     conv_grad, coarse_grad = call(
         unpack_kernel,
         "unpack",
         [shape((OFFSETS, quarter, channels), F32), shape((quarter, channels), F32)],
         "svv",
         size=3 << 20,
-    )(core, mine, other)
+    )(core, mine, move(mine, 0, 0, 1))
     return output, input_grad, conv_grad, coarse_grad
 
 

time: 130 us -> 127 us (0.977)
  blocking collectives: 13.2 us -> 0 us
  starting transfers between devices: 41.9 us -> 52.7 us
  local copies, waits for them, and re-layouts: 6.72 us -> 2.54 us
  waiting for transfers between devices: 44.3 us -> 46.9 us
    ppermute x1 -> x9, waiting for transfers between devices: 0.01 us -> 13.7 us  [move(): return lax.ppermute(value, 'morton', moves)]
    ppermute x1 -> x9, starting transfers between devices: 1.88 us -> 15.4 us  [move(): return lax.ppermute(value, 'morton', moves)]
    all_to_all x1 -> x0, blocking collectives: 13.2 us -> none  [local_step(): lax.all_to_all(jnp.broadcast_to(chunk, (chips,) + chunk.shape), 'morton',...]
    all_to_all x2, waiting for transfers between devices: 23.3 us -> 13.6 us  [the longest x1 7.59 us: local_step(): lax.all_to_all(chunks, 'morton', 0, 0, axis_index_groups=same_core, tiled...]
    unnamed x23 -> x21, local copies, waits for them, and re-layouts: 6.61 us -> 2.46 us
    all_to_all x2, starting transfers between devices: 16.1 us -> 12.3 us  [the longest x1 8.77 us: local_step(): lax.all_to_all(parts.reshape((4 * chips,) + piece[1:]), ('morton', 'chan'...]
    ppermute x15, waiting for transfers between devices: 21 us -> 19.6 us  [shift(): lax.ppermute(value, axis, [(i, (i + step) % size) for i in range(size)])]
    pallas_call x6 -> x9, Pallas kernels: 13.4 us -> 13.4 us  [the longest x1 5.82 us: local_step(): call(table_kernel, 'table_grad', [shape(wide, F32), shape(blocks, BF), sh...]
  transfers between devices with their start and end apart: 19 -> 27, of which waited for: 9 -> 14; matrix products, arithmetic and copies ran while one was open for 0% -> 0% of each run, Pallas kernels for 11% -> 11%
where the time goes in v5:
time: 127 us; the launch traced here: 126 us
  starting transfers between devices  52.7 us (41%)
  waiting for transfers between devices  46.9 us (37%)
  Pallas kernels  22.6 us (18%)
  local copies, waits for them, and re-layouts  2.54 us (2%)
    ppermute x15, waiting for transfers between devices, shift(): lax.ppermute(value, axis, [(i, (i + step) % size) for i in range(size)])  19.6 us
    ppermute x15, starting transfers between devices, shift(): lax.ppermute(value, axis, [(i, (i + step) % size) for i in range(size)])  16.4 us
    ppermute x9, starting transfers between devices, move(): return lax.ppermute(value, 'morton', moves)  15.4 us
    ppermute x9, waiting for transfers between devices, move(): return lax.ppermute(value, 'morton', moves)  13.7 us
    all_to_all x1, starting transfers between devices, local_step(): lax.all_to_all(parts.reshape((4 * chips,) + piece[1:]), ('morton', 'chan'...  8.77 us
    all_to_all x1, starting transfers between devices, local_step(): incoming = lax.all_to_all(outgoing, 'morton', 0, 0, tiled=True)  8.59 us
    all_to_all x1, waiting for transfers between devices, local_step(): lax.all_to_all(chunks, 'morton', 0, 0, axis_index_groups=same_core, tiled...  7.59 us
    all_to_all x1, waiting for transfers between devices, local_step(): lax.all_to_all(parts.reshape((4 * chips,) + piece[1:]), ('morton', 'chan'...  5.98 us
  transfers between devices with their start and end apart: 27, of which 14 were waited for; matrix products, arithmetic and copies ran while one was open for 0% of the time, Pallas kernels for 11%

profile of v5, /device:TPU:1, one launch (start us, length us, event | category | flops | bytes accessed | tf_op | source)
XLA Modules:
  0.0 125.8 jit_solution(17807272282548612694)
XLA Ops:
  0.7 1.0 copy-done.2
  1.7 0.7 copy-done.5
  2.3 0.7 copy-done.7
  3.0 1.5 %pack.1 = bf16[32,64,128]{2,1,0:T(8,128)(2,1)} custom-call(s32[1,32]{1,0:T(1,128)S(1)} %copy-done.5, s32[1,32]{1,0:T(1,128)S(1)} %copy-done.7, bf16[64,2048]{1,0:T(8,128)(2,1)S(1)} %copy-done.2), custom_call_target="tpu_custom_call" | custom-call | bytes 1048576 | tf_op jit(solution)/shard_map/pack/pallas_call | solution.py:310
  4.5 8.6 %all-to-all-start = ((bf16[32,64,128]{2,1,0:T(8,128)(2,1)}), bf16[32,64,128]{2,1,0:T(8,128)(2,1)S(1)}, u32[]{:S(2)}, u32[]{:S(2)}) async-start(bf16[32,64,128]{2,1,0:T(8,128)(2,1)} %pack.1), calls=%async_computation | async-start | bytes 1048576 | tf_op jit(solution)/shard_map/all_to_all | solution.py:313
  13.5 3.8 %collective-permute-start.2 = (bf16[14,64,128]{2,1,0:T(8,128)(2,1)S(1)}, bf16[14,64,128]{2,1,0:T(8,128)(2,1)S(1)}, u32[]{:S(2)}, u32[]{:S(2)}) collective-permute-start(bf16[14,64,128]{2,1,0:T(8,128)(2,1)S(1)} %get-tuple-element.58), channel_id=1, source_target_pairs={{0,3},{1,0},{2,1},{3,2},{4,7},{5,4},{6,5},{7,6},{8,11},{9,8},{10,9... | collective-permute-start | bytes 688136 | tf_op jit(solution)/shard_map/ppermute | solution.py:280
  17.4 0.7 collective-permute-start
  18.1 8.9 %collective-permute-done.2.refs_3_.piece3 = bf16[14,64,128]{2,1,0:T(8,128)(2,1)S(1)} collective-permute-done((bf16[14,64,128]{2,1,0:T(8,128)(2,1)S(1)}, bf16[14,64,128]{2,1,0:T(8,128)(2,1)S(1)}, u32[]{:S(2)}, u32[]{:S(2)}) %collective-permute-start.2) | collective-permute-done | bytes 229408 | tf_op jit(solution)/shard_map/ppermute | solution.py:280
  27.0 3.7 %collective-permute-done.refs_1_.piece1 = bf16[14,64,128]{2,1,0:T(8,128)(2,1)S(1)} collective-permute-done((bf16[14,64,128]{2,1,0:T(8,128)(2,1)S(1)}, bf16[14,64,128]{2,1,0:T(8,128)(2,1)S(1)}, u32[]{:S(2)}, u32[]{:S(2)}) %collective-permute-start) | collective-permute-done | bytes 229408 | tf_op jit(solution)/shard_map/ppermute | solution.py:280
  30.7 2.3 %forward0.1 = (f32[64,1024]{1,0:T(8,128)S(1)}, bf16[64,1024]{1,0:T(8,128)(2,1)S(1)}, bf16[64,1024]{1,0:T(8,128)(2,1)S(1)}, bf16[64,1024]{1,0:T(8,128)(2,1)S(1)}) custom-call(s32[27,16]{1,0:T(8,128)S(1)} %copy.11.neighbour, bf16[64,2048]{1,0:T(8,128)(2,1)S(1)} %copy-done.3, bf16[32,64,128]{2,1,0:T(8,128)(2,1)S(1)} %all-to-all-done.incoming, ...), custom_call_target="tpu_custom_call" | custom-call | flops 939524096 | bytes 3145728 | tf_op jit(solution)/shard_map/forward0/pallas_call | solution.py:324
  33.1 0.6 collective-permute-start.7
  33.7 0.8 collective-permute-start.8
  34.5 2.2 %forward1.1 = (f32[64,1024]{1,0:T(8,128)S(1)}, bf16[64,1024]{1,0:T(8,128)(2,1)S(1)}, bf16[64,1024]{1,0:T(8,128)(2,1)S(1)}, bf16[64,1024]{1,0:T(8,128)(2,1)S(1)}) custom-call(s32[27,16]{1,0:T(8,128)S(1)} %copy.11.neighbour, bf16[64,2048]{1,0:T(8,128)(2,1)S(1)} %copy-done.3, bf16[32,64,128]{2,1,0:T(8,128)(2,1)S(1)} %all-to-all-done.incoming, ...), custom_call_target="tpu_custom_call" | custom-call | flops 939524096 | bytes 3145728 | tf_op jit(solution)/shard_map/forward1/pallas_call | solution.py:324
  36.8 2.5 %collective-permute-start.3 = (bf16[64,1024]{1,0:T(8,128)(2,1)S(1)}, bf16[64,1024]{1,0:T(8,128)(2,1)S(1)}, u32[]{:S(2)}, u32[]{:S(2)}) collective-permute-start(bf16[64,1024]{1,0:T(8,128)(2,1)S(1)} %get-tuple-element.32), channel_id=1, source_target_pairs={{0,3},{1,0},{2,1},{3,2},{4,7},{5,4},{6,5},{7,6},{8,11},{9,8},{10,9... | collective-permute-start | bytes 393224 | tf_op jit(solution)/shard_map/ppermute | solution.py:280
  39.3 1.3 %collective-permute-start.4 = (bf16[64,1024]{1,0:T(8,128)(2,1)S(1)}, bf16[64,1024]{1,0:T(8,128)(2,1)S(1)}, u32[]{:S(2)}, u32[]{:S(2)}) collective-permute-start(bf16[64,1024]{1,0:T(8,128)(2,1)S(1)} %get-tuple-element.33), channel_id=1, source_target_pairs={{0,2},{1,3},{2,0},{3,1},{4,6},{5,7},{6,4},{7,5},{8,10},{9,11},{10,... | collective-permute-start | bytes 393224 | tf_op jit(solution)/shard_map/ppermute | solution.py:280
  40.5 0.8 collective-permute-start.5
  41.3 0.8 collective-permute-done.8.part3
  42.3 1.2 collective-permute-start.11
  44.1 0.6 collective-permute-done.4.part2
  44.7 2.4 %collective-permute-done.5.part3 = bf16[64,1024]{1,0:T(8,128)(2,1)S(1)} collective-permute-done((bf16[64,1024]{1,0:T(8,128)(2,1)S(1)}, bf16[64,1024]{1,0:T(8,128)(2,1)S(1)}, u32[]{:S(2)}, u32[]{:S(2)}) %collective-permute-start.5) | collective-permute-done | bytes 131104 | tf_op jit(solution)/shard_map/ppermute | solution.py:280
  47.1 0.8 activation1.1
  48.0 1.0 collective-permute-start.14
  49.0 2.1 %collective-permute-start.13 = (bf16[64,1024]{1,0:T(8,128)(2,1)S(1)}, bf16[64,1024]{1,0:T(8,128)(2,1)S(1)}, u32[]{:S(2)}, u32[]{:S(2)}) collective-permute-start(bf16[64,1024]{1,0:T(8,128)(2,1)S(1)} %get-tuple-element.42.grad0.g10), channel_id=1, source_target_pairs={{0,2},{1,3},{2,0},{3,1},{4,6},{5,7},{6,4},{7,5},{8,10},{9,11},{10,... | collective-permute-start | bytes 393224 | tf_op jit(solution)/shard_map/ppermute | solution.py:280
  51.1 0.9 collective-permute-start.12
  52.0 1.7 %collective-permute-done.9.grad1.g01 = bf16[64,1024]{1,0:T(8,128)(2,1)S(1)} collective-permute-done((bf16[64,1024]{1,0:T(8,128)(2,1)S(1)}, bf16[64,1024]{1,0:T(8,128)(2,1)S(1)}, u32[]{:S(2)}, u32[]{:S(2)}) %collective-permute-start.9) | collective-permute-done | bytes 131104 | tf_op jit(solution)/shard_map/ppermute | solution.py:280
  53.7 2.1 %weight_grad0.1.held = f32[1792,256]{1,0:T(8,128)S(1)} custom-call(s32[27,16]{1,0:T(8,128)S(1)} %copy.11.neighbour, bf16[64,2048]{1,0:T(8,128)(2,1)S(1)} %copy-done.3, bf16[32,64,128]{2,1,0:T(8,128)(2,1)S(1)} %all-to-all-done.incoming, bf16[64,1024]{1,0:T(8,128)(2,1)S(1)} %get-tuple-element.41.after.grad0.g00, ...), custom_call_target="tpu_custom_call" | custom-call | flops 939524096 | bytes 4194304 | tf_op jit(solution)/shard_map/weight_grad0/pallas_call | solution.py:346
  55.8 1.5 %collective-permute-done.12.grad1.g11 = bf16[64,1024]{1,0:T(8,128)(2,1)S(1)} collective-permute-done((bf16[64,1024]{1,0:T(8,128)(2,1)S(1)}, bf16[64,1024]{1,0:T(8,128)(2,1)S(1)}, u32[]{:S(2)}, u32[]{:S(2)}) %collective-permute-start.12) | collective-permute-done | bytes 131104 | tf_op jit(solution)/shard_map/ppermute | solution.py:280
  57.3 2.2 %weight_grad1.1 = (f32[14,4,32,128]{3,2,1,0:T(8,128)S(1)}, bf16[14,4,32,128]{3,2,1,0:T(8,128)(2,1)S(1)}) custom-call(s32[1]{0:T(128)} %bitcast.3.core, s32[27,16]{1,0:T(8,128)S(1)} %copy.11.neighbour, bf16[64,2048]{1,0:T(8,128)(2,1)S(1)} %copy-done.3, bf16[32,64,128]{2,1,0:T(8,128)(2,1)S(1)} %all-to-all-done.incoming, ...), custom_call_target="tpu_custom_call" | custom-call | flops 939524096 | bytes 4194304 | tf_op jit(solution)/shard_map/weight_grad1/pallas_call | solution.py:356
  59.6 4.9 %collective-permute-start.15 = (bf16[14,4,32,128]{3,2,1,0:T(8,128)(2,1)S(1)}, bf16[14,4,32,128]{3,2,1,0:T(8,128)(2,1)S(1)}, u32[]{:S(2)}, u32[]{:S(2)}) collective-permute-start(bf16[14,4,32,128]{3,2,1,0:T(8,128)(2,1)S(1)} %get-tuple-element.44), channel_id=1, source_target_pairs={{0,4},{4,0},{8,12},{12,8},{16,20},{20,16},{24,28},{28,24},{32,36},... | collective-permute-start | bytes 1376264 | tf_op jit(solution)/shard_map/ppermute | solution.py:290
  64.5 1.4 %collective-permute-done.15.arrived = bf16[14,4,32,128]{3,2,1,0:T(8,128)(2,1)S(1)} collective-permute-done((bf16[14,4,32,128]{3,2,1,0:T(8,128)(2,1)S(1)}, bf16[14,4,32,128]{3,2,1,0:T(8,128)(2,1)S(1)}, u32[]{:S(2)}, u32[]{:S(2)}) %collective-permute-start.15) | collective-permute-done | bytes 458784 | tf_op jit(solution)/shard_map/ppermute | solution.py:290
  65.9 0.9 pair_sum.1.after
  66.8 8.8 %all-to-all-start.1 = ((bf16[64,32,128]{2,1,0:T(8,128)(2,1)}), bf16[64,32,128]{2,1,0:T(8,128)(2,1)S(1)}, u32[]{:S(2)}, u32[]{:S(2)}) async-start(bf16[64,32,128]{2,1,0:T(8,128)(2,1)} %bitcast.4), calls=%async_computation.1 | async-start | bytes 1048576 | tf_op jit(solution)/shard_map/all_to_all | solution.py:371
  76.0 5.8 %table_grad.1 = (f32[64,2048]{1,0:T(8,128)S(1)}, bf16[4,4,64,128]{3,2,1,0:T(8,128)(2,1)S(1)}, bf16[4,4,64,128]{3,2,1,0:T(8,128)(2,1)S(1)}) custom-call(s32[3]{0:T(128)S(1)} %pad_add_fusion.chip, s32[27,16]{1,0:T(8,128)S(1)} %copy.11.neighbour, bf16[1792,256]{1,0:T(8,128)(2,1)S(1)} %join.1.weight_t, bf16[64,1024]{1,0:T(8,128)(2,1)S(1)} %get-tuple-element.41.after.grad0.g00, ...), custom_call_target="tpu_custom_call" | custom-call | flops 1879048192 | bytes 4194304 | tf_op jit(solution)/shard_map/table_grad/pallas_call | solution.py:381
  81.8 6.0 %all-to-all-done.1 = bf16[64,32,128]{2,1,0:T(8,128)(2,1)S(1)} async-done(((bf16[64,32,128]{2,1,0:T(8,128)(2,1)}), bf16[64,32,128]{2,1,0:T(8,128)(2,1)S(1)}, u32[]{:S(2)}, u32[]{:S(2)}) %all-to-all-start.1) | async-done | bytes 524320 | tf_op jit(solution)/shard_map/all_to_all | solution.py:371
  87.8 1.0 sum_parts.1
  88.7 3.6 %all-to-all-start.2 = ((bf16[16,2,32,256]{3,2,1,0:T(8,128)(2,1)}), bf16[16,2,32,256]{3,2,1,0:T(8,128)(2,1)S(1)}, u32[]{:S(2)}, u32[]{:S(2)}) async-start(bf16[16,2,32,256]{3,2,1,0:T(8,128)(2,1)} %sum_parts.1), calls=%async_computation.2 | async-start | bytes 1048576 | tf_op jit(solution)/shard_map/all_to_all | solution.py:410
  92.3 2.1 %collective-permute-start.16 = (bf16[4,4,64,128]{3,2,1,0:T(8,128)(2,1)S(1)}, bf16[4,4,64,128]{3,2,1,0:T(8,128)(2,1)S(1)}, u32[]{:S(2)}, u32[]{:S(2)}) collective-permute-start(bf16[4,4,64,128]{3,2,1,0:T(8,128)(2,1)S(1)} %get-tuple-element.47), channel_id=1, source_target_pairs={{0,4},{4,0},{8,12},{12,8},{16,20},{20,16},{24,28},{28,24},{32,36},... | collective-permute-start | bytes 786440 | tf_op jit(solution)/shard_map/ppermute | solution.py:290
  94.4 7.6 %all-to-all-done.2.mine = bf16[16,2,32,256]{3,2,1,0:T(8,128)(2,1)S(1)} async-done(((bf16[16,2,32,256]{3,2,1,0:T(8,128)(2,1)}), bf16[16,2,32,256]{3,2,1,0:T(8,128)(2,1)S(1)}, u32[]{:S(2)}, u32[]{:S(2)}) %all-to-all-start.2) | async-done | bytes 524320 | tf_op jit(solution)/shard_map/all_to_all | solution.py:410
  102.0 2.8 %collective-permute-start.23 = (bf16[16,2,32,256]{3,2,1,0:T(8,128)(2,1)S(1)}, bf16[16,2,32,256]{3,2,1,0:T(8,128)(2,1)S(1)}, u32[]{:S(2)}, u32[]{:S(2)}) collective-permute-start(bf16[16,2,32,256]{3,2,1,0:T(8,128)(2,1)S(1)} %all-to-all-done.2.mine), channel_id=1, source_target_pairs={{0,4},{4,0},{8,12},{12,8},{16,20},{20,16},{24,28},{28,24},{32,36},... | collective-permute-start | bytes 1572872 | tf_op jit(solution)/shard_map/ppermute | solution.py:290
  105.2 1.1 collective-permute-start.18
  106.3 1.4 %collective-permute-start.19 = (bf16[4,2,64,128]{3,2,1,0:T(8,128)(2,1)S(1)}, bf16[4,2,64,128]{3,2,1,0:T(8,128)(2,1)S(1)}, u32[]{:S(2)}, u32[]{:S(2)}) collective-permute-start(bf16[4,2,64,128]{3,2,1,0:T(8,128)(2,1)S(1)} %get-tuple-element.51), channel_id=1, source_target_pairs={{0,24},{4,28},{8,0},{12,4},{16,8},{20,12},{24,16},{28,20},{32,56},... | collective-permute-start | bytes 393224 | tf_op jit(solution)/shard_map/ppermute | solution.py:290
  107.7 6.4 %collective-permute-done.17.refs_1_ = bf16[4,2,64,128]{3,2,1,0:T(8,128)(2,1)S(1)} collective-permute-done((bf16[4,2,64,128]{3,2,1,0:T(8,128)(2,1)S(1)}, bf16[4,2,64,128]{3,2,1,0:T(8,128)(2,1)S(1)}, u32[]{:S(2)}, u32[]{:S(2)}) %collective-permute-start.17) | collective-permute-done | bytes 131104 | tf_op jit(solution)/shard_map/ppermute | solution.py:290
  114.5 1.7 %collective-permute-start.21 = (bf16[4,2,64,128]{3,2,1,0:T(8,128)(2,1)S(1)}, bf16[4,2,64,128]{3,2,1,0:T(8,128)(2,1)S(1)}, u32[]{:S(2)}, u32[]{:S(2)}) collective-permute-start(bf16[4,2,64,128]{3,2,1,0:T(8,128)(2,1)S(1)} %get-tuple-element.54), channel_id=1, source_target_pairs={{0,64},{4,68},{8,72},{12,76},{16,80},{20,84},{24,88},{28,92},{32,9... | collective-permute-start | bytes 393224 | tf_op jit(solution)/shard_map/ppermute | solution.py:290
  116.2 0.9 collective-permute-start.22
  117.2 4.5 %collective-permute-done.20.from1 = bf16[4,2,64,128]{3,2,1,0:T(8,128)(2,1)S(1)} collective-permute-done((bf16[4,2,64,128]{3,2,1,0:T(8,128)(2,1)S(1)}, bf16[4,2,64,128]{3,2,1,0:T(8,128)(2,1)S(1)}, u32[]{:S(2)}, u32[]{:S(2)}) %collective-permute-start.20) | collective-permute-done | bytes 131104 | tf_op jit(solution)/shard_map/ppermute | solution.py:290
  121.7 1.1 collective-permute-done.22.from3
  122.8 1.6 %return_add.1 = f32[64,2048]{1,0:T(8,128)} custom-call(s32[3]{0:T(128)S(1)} %pad_add_fusion.chip, s32[1,32]{1,0:T(1,128)S(1)} %copy-done.6, s32[1,32]{1,0:T(1,128)S(1)} %copy-done.8, f32[64,2048]{1,0:T(8,128)S(1)} %get-tuple-element.45.local, bf16[4,2,64,128]{3,2,1,0:T(8,128)(2,1)S(1)} %get-tuple-element.52.from0, ...), custom_call_target="tpu_custom_call" | custom-call | bytes 2097152 | tf_op jit(solution)/shard_map/return_add/pallas_call | solution.py:398
  124.4 1.3 %unpack.1 = (f32[27,64,256]{2,1,0:T(8,128)}, f32[64,256]{1,0:T(8,128)}) custom-call(s32[1]{0:T(128)} %bitcast.3.core, bf16[16,2,32,256]{3,2,1,0:T(8,128)(2,1)S(1)} %all-to-all-done.2.mine, bf16[16,2,32,256]{3,2,1,0:T(8,128)(2,1)S(1)} %collective-permute-done.23.other), custom_call_target="tpu_custom_call" | custom-call | bytes 3145728 | tf_op jit(solution)/shard_map/unpack/pallas_call | solution.py:411
  (45 shorter events, 2.7 us)
Async XLA Ops:
  0.6 12.4 %copy-start.1 = (bf16[27,64,256]{2,1,0:T(8,128)(2,1)S(1)}, bf16[27,64,256]{2,1,0:T(8,128)(2,1)}, u32[]{:S(2)}) copy-start(bf16[27,64,256]{2,1,0:T(8,128)(2,1)} %conv_weight.1) | copy-start | bytes 2654212
  0.6 1.0 copy-start.2
  1.7 0.7 copy-start.5
  2.3 0.7 copy-start.7
  3.0 10.1 %copy-start.4 = (bf16[64,256]{1,0:T(8,128)(2,1)S(1)}, bf16[64,256]{1,0:T(8,128)(2,1)}, u32[]{:S(2)}) copy-start(bf16[64,256]{1,0:T(8,128)(2,1)} %coarse_weight.1) | copy-start | bytes 98308
  4.5 26.3 %all-to-all-start = ((bf16[32,64,128]{2,1,0:T(8,128)(2,1)}), bf16[32,64,128]{2,1,0:T(8,128)(2,1)S(1)}, u32[]{:S(2)}, u32[]{:S(2)}) async-start(bf16[32,64,128]{2,1,0:T(8,128)(2,1)} %pack.1), calls=%async_computation | async-start | bytes 1048576 | tf_op jit(solution)/shard_map/all_to_all | solution.py:313
  13.1 5.0 %copy-start.9 = (s32[27,16]{0,1:T(8,128)S(1)}, s32[27,16]{0,1:T(8,128)}, u32[]{:S(2)}) copy-start(s32[27,16]{0,1:T(8,128)} %param.13) | copy-start | bytes 5188
  13.1 17.6 %copy-start.3 = (bf16[64,2048]{1,0:T(8,128)(2,1)S(1)}, bf16[64,2048]{1,0:T(8,128)(2,1)}, u32[]{:S(2)}) copy-start(bf16[64,2048]{1,0:T(8,128)(2,1)} %features.9) | copy-start | bytes 786436
  13.5 13.5 %collective-permute-start.2 = (bf16[14,64,128]{2,1,0:T(8,128)(2,1)S(1)}, bf16[14,64,128]{2,1,0:T(8,128)(2,1)S(1)}, u32[]{:S(2)}, u32[]{:S(2)}) collective-permute-start(bf16[14,64,128]{2,1,0:T(8,128)(2,1)S(1)} %get-tuple-element.58), channel_id=1, source_target_pairs={{0,3},{1,0},{2,1},{3,2},{4,7},{5,4},{6,5},{7,6},{8,11},{9,8},{10,9... | collective-permute-start | bytes 688136 | tf_op jit(solution)/shard_map/ppermute | solution.py:280
  17.4 9.7 %collective-permute-start.1 = (bf16[14,64,128]{2,1,0:T(8,128)(2,1)S(1)}, bf16[14,64,128]{2,1,0:T(8,128)(2,1)S(1)}, u32[]{:S(2)}, u32[]{:S(2)}) collective-permute-start(bf16[14,64,128]{2,1,0:T(8,128)(2,1)S(1)} %get-tuple-element.59), channel_id=1, source_target_pairs={{0,2},{1,3},{2,0},{3,1},{4,6},{5,7},{6,4},{7,5},{8,10},{9,11},{10,... | collective-permute-start | bytes 688136 | tf_op jit(solution)/shard_map/ppermute | solution.py:280
  17.4 13.4 %collective-permute-start = (bf16[14,64,128]{2,1,0:T(8,128)(2,1)S(1)}, bf16[14,64,128]{2,1,0:T(8,128)(2,1)S(1)}, u32[]{:S(2)}, u32[]{:S(2)}) collective-permute-start(bf16[14,64,128]{2,1,0:T(8,128)(2,1)S(1)} %get-tuple-element.60), channel_id=1, source_target_pairs={{0,1},{1,2},{2,3},{3,0},{4,5},{5,6},{6,7},{7,4},{8,9},{9,10},{10,1... | collective-permute-start | bytes 688136 | tf_op jit(solution)/shard_map/ppermute | solution.py:280
  33.0 9.1 %copy-start = (bf16[64,2048]{1,0:T(8,128)(2,1)S(1)}, bf16[64,2048]{1,0:T(8,128)(2,1)}, u32[]{:S(2)}) copy-start(bf16[64,2048]{1,0:T(8,128)(2,1)} %out_grad.3) | copy-start | bytes 786436
  33.0 7.5 %collective-permute-start.6 = (bf16[64,1024]{1,0:T(8,128)(2,1)S(1)}, bf16[64,1024]{1,0:T(8,128)(2,1)S(1)}, u32[]{:S(2)}, u32[]{:S(2)}) collective-permute-start(bf16[64,1024]{1,0:T(8,128)(2,1)S(1)} %get-tuple-element.36), channel_id=1, source_target_pairs={{0,3},{1,0},{2,1},{3,2},{4,7},{5,4},{6,5},{7,6},{8,11},{9,8},{10,9... | collective-permute-start | bytes 393224 | tf_op jit(solution)/shard_map/ppermute | solution.py:280
  33.1 8.2 %collective-permute-start.7 = (bf16[64,1024]{1,0:T(8,128)(2,1)S(1)}, bf16[64,1024]{1,0:T(8,128)(2,1)S(1)}, u32[]{:S(2)}, u32[]{:S(2)}) collective-permute-start(bf16[64,1024]{1,0:T(8,128)(2,1)S(1)} %get-tuple-element.37), channel_id=1, source_target_pairs={{0,2},{1,3},{2,0},{3,1},{4,6},{5,7},{6,4},{7,5},{8,10},{9,11},{10,... | collective-permute-start | bytes 393224 | tf_op jit(solution)/shard_map/ppermute | solution.py:280
  33.7 8.3 %collective-permute-start.8 = (bf16[64,1024]{1,0:T(8,128)(2,1)S(1)}, bf16[64,1024]{1,0:T(8,128)(2,1)S(1)}, u32[]{:S(2)}, u32[]{:S(2)}) collective-permute-start(bf16[64,1024]{1,0:T(8,128)(2,1)S(1)} %get-tuple-element.38), channel_id=1, source_target_pairs={{0,1},{1,2},{2,3},{3,0},{4,5},{5,6},{6,7},{7,4},{8,9},{9,10},{10,1... | collective-permute-start | bytes 393224 | tf_op jit(solution)/shard_map/ppermute | solution.py:280
  36.8 7.2 %collective-permute-start.3 = (bf16[64,1024]{1,0:T(8,128)(2,1)S(1)}, bf16[64,1024]{1,0:T(8,128)(2,1)S(1)}, u32[]{:S(2)}, u32[]{:S(2)}) collective-permute-start(bf16[64,1024]{1,0:T(8,128)(2,1)S(1)} %get-tuple-element.32), channel_id=1, source_target_pairs={{0,3},{1,0},{2,1},{3,2},{4,7},{5,4},{6,5},{7,6},{8,11},{9,8},{10,9... | collective-permute-start | bytes 393224 | tf_op jit(solution)/shard_map/ppermute | solution.py:280
  39.3 5.5 %collective-permute-start.4 = (bf16[64,1024]{1,0:T(8,128)(2,1)S(1)}, bf16[64,1024]{1,0:T(8,128)(2,1)S(1)}, u32[]{:S(2)}, u32[]{:S(2)}) collective-permute-start(bf16[64,1024]{1,0:T(8,128)(2,1)S(1)} %get-tuple-element.33), channel_id=1, source_target_pairs={{0,2},{1,3},{2,0},{3,1},{4,6},{5,7},{6,4},{7,5},{8,10},{9,11},{10,... | collective-permute-start | bytes 393224 | tf_op jit(solution)/shard_map/ppermute | solution.py:280
  40.5 6.6 %collective-permute-start.5 = (bf16[64,1024]{1,0:T(8,128)(2,1)S(1)}, bf16[64,1024]{1,0:T(8,128)(2,1)S(1)}, u32[]{:S(2)}, u32[]{:S(2)}) collective-permute-start(bf16[64,1024]{1,0:T(8,128)(2,1)S(1)} %get-tuple-element.34), channel_id=1, source_target_pairs={{0,1},{1,2},{2,3},{3,0},{4,5},{5,6},{6,7},{7,4},{8,9},{9,10},{10,1... | collective-permute-start | bytes 393224 | tf_op jit(solution)/shard_map/ppermute | solution.py:280
  42.3 8.8 %collective-permute-start.11 = (bf16[64,1024]{1,0:T(8,128)(2,1)S(1)}, bf16[64,1024]{1,0:T(8,128)(2,1)S(1)}, u32[]{:S(2)}, u32[]{:S(2)}) collective-permute-start(bf16[64,1024]{1,0:T(8,128)(2,1)S(1)} %get-tuple-element.41.after.grad0.g00), channel_id=1, source_target_pairs={{0,3},{1,0},{2,1},{3,2},{4,7},{5,4},{6,5},{7,6},{8,11},{9,8},{10,9... | collective-permute-start | bytes 393224 | tf_op jit(solution)/shard_map/ppermute | solution.py:280
  43.5 8.5 %collective-permute-start.10 = (bf16[64,1024]{1,0:T(8,128)(2,1)S(1)}, bf16[64,1024]{1,0:T(8,128)(2,1)S(1)}, u32[]{:S(2)}, u32[]{:S(2)}) collective-permute-start(bf16[64,1024]{1,0:T(8,128)(2,1)S(1)} %get-tuple-element.41.after.grad0.g00), channel_id=1, source_target_pairs={{0,2},{1,3},{2,0},{3,1},{4,6},{5,7},{6,4},{7,5},{8,10},{9,11},{10,... | collective-permute-start | bytes 393224 | tf_op jit(solution)/shard_map/ppermute | solution.py:280
  44.0 9.7 %collective-permute-start.9 = (bf16[64,1024]{1,0:T(8,128)(2,1)S(1)}, bf16[64,1024]{1,0:T(8,128)(2,1)S(1)}, u32[]{:S(2)}, u32[]{:S(2)}) collective-permute-start(bf16[64,1024]{1,0:T(8,128)(2,1)S(1)} %get-tuple-element.41.after.grad0.g00), channel_id=1, source_target_pairs={{0,1},{1,2},{2,3},{3,0},{4,5},{5,6},{6,7},{7,4},{8,9},{9,10},{10,1... | collective-permute-start | bytes 393224 | tf_op jit(solution)/shard_map/ppermute | solution.py:280
  48.0 7.8 %collective-permute-start.14 = (bf16[64,1024]{1,0:T(8,128)(2,1)S(1)}, bf16[64,1024]{1,0:T(8,128)(2,1)S(1)}, u32[]{:S(2)}, u32[]{:S(2)}) collective-permute-start(bf16[64,1024]{1,0:T(8,128)(2,1)S(1)} %get-tuple-element.42.grad0.g10), channel_id=1, source_target_pairs={{0,3},{1,0},{2,1},{3,2},{4,7},{5,4},{6,5},{7,6},{8,11},{9,8},{10,9... | collective-permute-start | bytes 393224 | tf_op jit(solution)/shard_map/ppermute | solution.py:280
  49.0 6.8 %collective-permute-start.13 = (bf16[64,1024]{1,0:T(8,128)(2,1)S(1)}, bf16[64,1024]{1,0:T(8,128)(2,1)S(1)}, u32[]{:S(2)}, u32[]{:S(2)}) collective-permute-start(bf16[64,1024]{1,0:T(8,128)(2,1)S(1)} %get-tuple-element.42.grad0.g10), channel_id=1, source_target_pairs={{0,2},{1,3},{2,0},{3,1},{4,6},{5,7},{6,4},{7,5},{8,10},{9,11},{10,... | collective-permute-start | bytes 393224 | tf_op jit(solution)/shard_map/ppermute | solution.py:280
  51.1 6.2 %collective-permute-start.12 = (bf16[64,1024]{1,0:T(8,128)(2,1)S(1)}, bf16[64,1024]{1,0:T(8,128)(2,1)S(1)}, u32[]{:S(2)}, u32[]{:S(2)}) collective-permute-start(bf16[64,1024]{1,0:T(8,128)(2,1)S(1)} %get-tuple-element.42.grad0.g10), channel_id=1, source_target_pairs={{0,1},{1,2},{2,3},{3,0},{4,5},{5,6},{6,7},{7,4},{8,9},{9,10},{10,1... | collective-permute-start | bytes 393224 | tf_op jit(solution)/shard_map/ppermute | solution.py:280
  59.6 6.3 %collective-permute-start.15 = (bf16[14,4,32,128]{3,2,1,0:T(8,128)(2,1)S(1)}, bf16[14,4,32,128]{3,2,1,0:T(8,128)(2,1)S(1)}, u32[]{:S(2)}, u32[]{:S(2)}) collective-permute-start(bf16[14,4,32,128]{3,2,1,0:T(8,128)(2,1)S(1)} %get-tuple-element.44), channel_id=1, source_target_pairs={{0,4},{4,0},{8,12},{12,8},{16,20},{20,16},{24,28},{28,24},{32,36},... | collective-permute-start | bytes 1376264 | tf_op jit(solution)/shard_map/ppermute | solution.py:290
  66.8 21.0 %all-to-all-start.1 = ((bf16[64,32,128]{2,1,0:T(8,128)(2,1)}), bf16[64,32,128]{2,1,0:T(8,128)(2,1)S(1)}, u32[]{:S(2)}, u32[]{:S(2)}) async-start(bf16[64,32,128]{2,1,0:T(8,128)(2,1)} %bitcast.4), calls=%async_computation.1 | async-start | bytes 1048576 | tf_op jit(solution)/shard_map/all_to_all | solution.py:371
  81.8 41.0 %copy-start.6 = (s32[1,32]{1,0:T(1,128)S(1)}, s32[1,32]{1,0:T(1,128)}, u32[]{:S(2)}) copy-start(s32[1,32]{1,0:T(1,128)} %send_block.3) | copy-start | bytes 388
  81.8 41.0 %copy-start.8 = (s32[1,32]{1,0:T(1,128)S(1)}, s32[1,32]{1,0:T(1,128)}, u32[]{:S(2)}) copy-start(s32[1,32]{1,0:T(1,128)} %send_count.3) | copy-start | bytes 388
  88.7 13.2 %all-to-all-start.2 = ((bf16[16,2,32,256]{3,2,1,0:T(8,128)(2,1)}), bf16[16,2,32,256]{3,2,1,0:T(8,128)(2,1)S(1)}, u32[]{:S(2)}, u32[]{:S(2)}) async-start(bf16[16,2,32,256]{3,2,1,0:T(8,128)(2,1)} %sum_parts.1), calls=%async_computation.2 | async-start | bytes 1048576 | tf_op jit(solution)/shard_map/all_to_all | solution.py:410
  92.3 12.5 %collective-permute-start.16 = (bf16[4,4,64,128]{3,2,1,0:T(8,128)(2,1)S(1)}, bf16[4,4,64,128]{3,2,1,0:T(8,128)(2,1)S(1)}, u32[]{:S(2)}, u32[]{:S(2)}) collective-permute-start(bf16[4,4,64,128]{3,2,1,0:T(8,128)(2,1)S(1)} %get-tuple-element.47), channel_id=1, source_target_pairs={{0,4},{4,0},{8,12},{12,8},{16,20},{20,16},{24,28},{28,24},{32,36},... | collective-permute-start | bytes 786440 | tf_op jit(solution)/shard_map/ppermute | solution.py:290
  102.0 22.5 %collective-permute-start.23 = (bf16[16,2,32,256]{3,2,1,0:T(8,128)(2,1)S(1)}, bf16[16,2,32,256]{3,2,1,0:T(8,128)(2,1)S(1)}, u32[]{:S(2)}, u32[]{:S(2)}) collective-permute-start(bf16[16,2,32,256]{3,2,1,0:T(8,128)(2,1)S(1)} %all-to-all-done.2.mine), channel_id=1, source_target_pairs={{0,4},{4,0},{8,12},{12,8},{16,20},{20,16},{24,28},{28,24},{32,36},... | collective-permute-start | bytes 1572872 | tf_op jit(solution)/shard_map/ppermute | solution.py:290
  104.9 9.2 %collective-permute-start.17 = (bf16[4,2,64,128]{3,2,1,0:T(8,128)(2,1)S(1)}, bf16[4,2,64,128]{3,2,1,0:T(8,128)(2,1)S(1)}, u32[]{:S(2)}, u32[]{:S(2)}) collective-permute-start(bf16[4,2,64,128]{3,2,1,0:T(8,128)(2,1)S(1)} %get-tuple-element.49), channel_id=1, source_target_pairs={{0,8},{4,12},{8,16},{12,20},{16,24},{20,28},{24,0},{28,4},{32,40},... | collective-permute-start | bytes 393224 | tf_op jit(solution)/shard_map/ppermute | solution.py:290
  105.2 8.9 %collective-permute-start.18 = (bf16[4,2,64,128]{3,2,1,0:T(8,128)(2,1)S(1)}, bf16[4,2,64,128]{3,2,1,0:T(8,128)(2,1)S(1)}, u32[]{:S(2)}, u32[]{:S(2)}) collective-permute-start(bf16[4,2,64,128]{3,2,1,0:T(8,128)(2,1)S(1)} %get-tuple-element.50), channel_id=1, source_target_pairs={{0,16},{4,20},{8,24},{12,28},{16,0},{20,4},{24,8},{28,12},{32,48},... | collective-permute-start | bytes 393224 | tf_op jit(solution)/shard_map/ppermute | solution.py:290
  106.3 8.1 %collective-permute-start.19 = (bf16[4,2,64,128]{3,2,1,0:T(8,128)(2,1)S(1)}, bf16[4,2,64,128]{3,2,1,0:T(8,128)(2,1)S(1)}, u32[]{:S(2)}, u32[]{:S(2)}) collective-permute-start(bf16[4,2,64,128]{3,2,1,0:T(8,128)(2,1)S(1)} %get-tuple-element.51), channel_id=1, source_target_pairs={{0,24},{4,28},{8,0},{12,4},{16,8},{20,12},{24,16},{28,20},{32,56},... | collective-permute-start | bytes 393224 | tf_op jit(solution)/shard_map/ppermute | solution.py:290
  114.4 7.2 %collective-permute-start.20 = (bf16[4,2,64,128]{3,2,1,0:T(8,128)(2,1)S(1)}, bf16[4,2,64,128]{3,2,1,0:T(8,128)(2,1)S(1)}, u32[]{:S(2)}, u32[]{:S(2)}) collective-permute-start(bf16[4,2,64,128]{3,2,1,0:T(8,128)(2,1)S(1)} %get-tuple-element.53), channel_id=1, source_target_pairs={{0,32},{4,36},{8,40},{12,44},{16,48},{20,52},{24,56},{28,60},{32,6... | collective-permute-start | bytes 393224 | tf_op jit(solution)/shard_map/ppermute | solution.py:290
  114.5 7.2 %collective-permute-start.21 = (bf16[4,2,64,128]{3,2,1,0:T(8,128)(2,1)S(1)}, bf16[4,2,64,128]{3,2,1,0:T(8,128)(2,1)S(1)}, u32[]{:S(2)}, u32[]{:S(2)}) collective-permute-start(bf16[4,2,64,128]{3,2,1,0:T(8,128)(2,1)S(1)} %get-tuple-element.54), channel_id=1, source_target_pairs={{0,64},{4,68},{8,72},{12,76},{16,80},{20,84},{24,88},{28,92},{32,9... | collective-permute-start | bytes 393224 | tf_op jit(solution)/shard_map/ppermute | solution.py:290
  116.2 6.6 %collective-permute-start.22 = (bf16[4,2,64,128]{3,2,1,0:T(8,128)(2,1)S(1)}, bf16[4,2,64,128]{3,2,1,0:T(8,128)(2,1)S(1)}, u32[]{:S(2)}, u32[]{:S(2)}) collective-permute-start(bf16[4,2,64,128]{3,2,1,0:T(8,128)(2,1)S(1)} %get-tuple-element.55), channel_id=1, source_target_pairs={{0,96},{4,100},{8,104},{12,108},{16,112},{20,116},{24,120},{28,124... | collective-permute-start | bytes 393224 | tf_op jit(solution)/shard_map/ppermute | solution.py:290

commit v6 on v5

--- a/solution.py
+++ b/solution.py
@@ -180,14 +180,8 @@
         parts[spare] = jnp.zeros(parts.shape[1:], BF)
 
 
-def peer_at(chip, step_y, step_x, flip):
-    y = lax.rem(chip[0] + step_y + 4, 4)
-    x = lax.rem(chip[1] + step_x + 4, 4)
-    return (y * 4 + x) * 2 + (1 - chip[2] if flip else chip[2])
-
-
 def table_kernel(
-    chip, neighbour, weight_t, g00, g01, g02, g03, g10, g11, g12, g13, after, local, home, away, total, spread
+    core, neighbour, weight_t, g00, g01, g02, g03, g10, g11, g12, g13, after, local, home, away, total, spread
 ):
     del after
     quarter, row_count = local.shape
@@ -220,59 +214,52 @@
             )
     for block in range(nblocks):
         local[:, block * BLOCK : (block + 1) * BLOCK] = total[block]
-    for flip, out in enumerate((home, away)):
-        for x in range(4):
-            for y in range(4):
-                out[x, y] = total[nblocks + peer_at(chip, y, x, flip)].astype(BF)
-
-
-def by_x_kernel(home, away, *outs):
-    for x, out in enumerate(outs):
-        for y in range(4):
-            out[y, 0] = home[x, y]
-            out[y, 1] = away[x, y]
-
-
-def by_y_kernel(*refs):
-    for y, out in enumerate(refs[4:]):
-        for x, ref in enumerate(refs[:4]):
-            out[x] = ref[y]
-
-
-def return_kernel(chip, send_block, send_count, local, from0, from1, from2, from3, input_grad):
+    for chip in range(home.shape[0]):
+        home[chip] = total[nblocks + 2 * chip + core[0]].astype(BF)
+        away[chip] = total[nblocks + 2 * chip + 1 - core[0]].astype(BF)
+
+
+def return_kernel(core, send_block, send_count, local, mixed, input_grad):
     input_grad[...] = local[...]
-    for y, ref in enumerate((from0, from1, from2, from3)):
-        for x in range(4):
-            for flip in range(2):
-                peer = peer_at(chip, -y, -x, flip)
-                factor = send_count[0, peer].astype(F32)
-                input_grad[:, columns(send_block[0, peer])] += ref[x, flip].astype(F32) * factor
-
-
-def sum_kernel(scale, parts, after, chunks):
-    del after
+    for chip in range(mixed.shape[0]):
+        for flip in range(2):
+            peer = 2 * chip + (1 - core[0] if flip else core[0])
+            value = jnp.concatenate([mixed[chip, 4 + 2 * flip], mixed[chip, 5 + 2 * flip]], axis=0)
+            factor = send_count[0, peer].astype(F32)
+            input_grad[:, columns(send_block[0, peer])] += value.astype(F32) * factor
+
+
+def sum_kernel(scale, parts, home, away, mixed):
     half = parts.shape[3] // 2
+    rows = parts.shape[2]
     total = parts[0].astype(F32)
     for source in range(1, parts.shape[0]):
         total = total + parts[source].astype(F32)
     total = total * scale
     for side in range(2):
         cut = slice(side * half, (side + 1) * half)
-        value = jnp.concatenate([total[c, :, cut] for c in range(4)], axis=1).astype(BF)
-        for target in range(chunks.shape[0]):
-            chunks[target, side] = value
+        for pair in range(2):
+            value = jnp.concatenate([total[2 * pair + c, :, cut] for c in range(2)], axis=1)
+            for target in range(mixed.shape[0]):
+                mixed[target, 2 * side + pair] = value.astype(BF)
+    for target in range(mixed.shape[0]):
+        for flip, blocks in enumerate((home, away)):
+            for part in range(2):
+                mixed[target, 4 + 2 * flip + part] = blocks[target, part * rows : (part + 1) * rows]
 
 
 def unpack_kernel(core, mine, other, conv_grad, coarse_grad):
     half = mine.shape[2]
-    for chunks, side in ((mine, core[0]), (other, 1 - core[0])):
+    for mixed, side in ((mine, core[0]), (other, 1 - core[0])):
         rows = pl.ds(pl.multiple_of(side * half, half), half)
         for offset in range(TERMS):
-            value = chunks[offset // 2, offset % 2].astype(F32)
-            if offset < OFFSETS:
-                conv_grad[offset, rows, :] = value
-            else:
-                coarse_grad[rows, :] = value
+            for pair in range(2):
+                value = mixed[offset // 2, 2 * (offset % 2) + pair].astype(F32)
+                cut = slice(pair * BLOCK, (pair + 1) * BLOCK)
+                if offset < OFFSETS:
+                    conv_grad[offset, rows, cut] = value
+                else:
+                    coarse_grad[rows, cut] = value
 
 
 def shift(value, axis, step):
@@ -280,14 +267,9 @@
     return lax.ppermute(value, axis, [(i, (i + step) % size) for i in range(size)])
 
 
-def move(value, step_y, step_x, flip):
-    moves = []
-    for y in range(4):
-        for x in range(4):
-            for core in range(2):
-                target = ((y + step_y) % 4 * 4 + (x + step_x) % 4) * 2 + (core ^ flip)
-                moves.append(((y * 4 + x) * 2 + core, target))
-    return lax.ppermute(value, "morton", moves)
+def swap_cores(value):
+    size = lax.axis_size("morton")
+    return lax.ppermute(value, "morton", [(i, i ^ 1) for i in range(size)])
 
 
 def local_step(features, conv_weight, coarse_weight, out_grad, send_block, send_count, neighbour):
@@ -299,9 +281,7 @@
     depth = TERMS * quarter
     flops = 2 * depth * channels * row_count
     place = lax.axis_index("chan").astype(jnp.int32).reshape(1)
-    spot = lax.axis_index("morton").astype(jnp.int32)
-    chip = jnp.stack([spot // 8, spot // 2 % 4, spot % 2])
-    core = (spot % 2).reshape(1)
+    core = (lax.axis_index("morton") % 2).astype(jnp.int32).reshape(1)
     shape = jax.ShapeDtypeStruct
 
     pieces = call(
@@ -364,7 +344,7 @@
     )(core, neighbour, features, incoming, *grads[1], held)
     chips = n_morton // 2
     parts = call(pair_kernel, "pair_sum", shape((chips,) + piece, BF), "svv", size=3 << 20)(
-        place, keep, move(give, 0, 0, 1)
+        place, keep, swap_cores(give)
     )
     same_core = [[2 * c + side for c in range(chips)] for side in range(2)]
     same_core_all = [[device * 4 + z for device in group for z in range(4)] for group in same_core]
@@ -377,7 +357,7 @@
         tiled=True,
     ).reshape(parts.shape)
 
-    blocks = (4, 4, quarter, BLOCK)
+    blocks = (chips, quarter, BLOCK)
     local, home, away = call(
         table_kernel,
         "table_grad",
@@ -389,32 +369,26 @@
         ],
         flops,
         4 << 20,
-    )(chip, neighbour, weight_t, *grads[0], *grads[1], parts)
-    bundle = [shape((4, 2, quarter, BLOCK), BF)] * 4
-    along_x = call(by_x_kernel, "by_x", bundle, "vv", size=1 << 20)(home, move(away, 0, 0, 1))
-    along_x = [along_x[0]] + [move(along_x[step], 0, step, 0) for step in (1, 2, 3)]
-    along_y = call(by_y_kernel, "by_y", bundle, "vvvv", size=1 << 20)(*along_x)
-    along_y = [along_y[0]] + [move(along_y[step], step, 0, 0) for step in (1, 2, 3)]
-    input_grad = call(return_kernel, "return_add", shape(wide, F32), "sssvvvvv", size=2 << 20)(
-        chip, send_block, send_count, local, *along_y
-    )
-
+    )(core, neighbour, weight_t, *grads[0], *grads[1], parts)
     scale = float(row_count * n_morton) ** (-0.5)
-    chunks = call(
+    mixed = call(
         functools.partial(sum_kernel, scale),
         "sum_parts",
-        shape((chips, 2, quarter // 2, channels), BF),
-        "va",
+        shape((chips, 8, quarter // 2, BLOCK), BF),
+        "vvv",
         size=1 << 20,
-    )(received, home)
-    mine = lax.all_to_all(chunks, "morton", 0, 0, axis_index_groups=same_core, tiled=True)
+    )(received, home, swap_cores(away))
+    mine = lax.all_to_all(mixed, "morton", 0, 0, axis_index_groups=same_core, tiled=True)
+    input_grad = call(return_kernel, "return_add", shape(wide, F32), "sssvv", size=2 << 20)(
+        core, send_block, send_count, local, mine
+    )
     conv_grad, coarse_grad = call(
         unpack_kernel,
         "unpack",
         [shape((OFFSETS, quarter, channels), F32), shape((quarter, channels), F32)],
         "svv",
         size=3 << 20,
-    )(core, mine, move(mine, 0, 0, 1))
+    )(core, mine, swap_cores(mine))
     return output, input_grad, conv_grad, coarse_grad
 
 

time: 127 us -> 113 us (0.89)
  waiting for transfers between devices: 46.9 us -> 27.1 us
  blocking collectives: 0 us -> 18.3 us
  starting transfers between devices: 52.7 us -> 42.3 us
    all_to_all x0 -> x1, blocking collectives: none -> 18.3 us  [local_step(): lax.all_to_all(mixed, 'morton', 0, 0, axis_index_groups=same_core, tiled=...]
    ppermute x9 -> x3, waiting for transfers between devices: 13.7 us -> 3.24 us  [swap_cores(): return lax.ppermute(value, 'morton', [(i, i ^ 1) for i in range(size)])]
    all_to_all x1 -> x0, waiting for transfers between devices: 7.59 us -> none  [local_step(): lax.all_to_all(chunks, 'morton', 0, 0, axis_index_groups=same_core, tiled...]
    ppermute x9 -> x3, starting transfers between devices: 15.4 us -> 8.55 us  [swap_cores(): return lax.ppermute(value, 'morton', [(i, i ^ 1) for i in range(size)])]
    all_to_all x1 -> x0, starting transfers between devices: 3.57 us -> none  [local_step(): lax.all_to_all(chunks, 'morton', 0, 0, axis_index_groups=same_core, tiled...]
    all_to_all x1, waiting for transfers between devices: 5.98 us -> 4.23 us  [local_step(): lax.all_to_all(parts.reshape((4 * chips,) + piece[1:]), ('morton', 'chan'...]
    pallas_call x4 -> x2, Pallas kernels: 2.67 us -> 1.8 us  [the longest x1 1.64 us: local_step(): call(return_kernel, 'return_add', shape(wide, F32), 'sssvv', size=2 << 20)]
  transfers between devices with their start and end apart: 27 -> 20, of which waited for: 14 -> 11; matrix products, arithmetic and copies ran while one was open for 0% -> 0% of each run, Pallas kernels for 11% -> 12%
where the time goes in v6:
time: 113 us
  starting transfers between devices  42.3 us (37%)
  waiting for transfers between devices  27.1 us (24%)
  Pallas kernels  21.8 us (19%)
  blocking collectives  18.3 us (16%)
  local copies, waits for them, and re-layouts  2.54 us (2%)
    ppermute x15, waiting for transfers between devices, shift(): lax.ppermute(value, axis, [(i, (i + step) % size) for i in range(size)])  19.6 us
    all_to_all x1, blocking collectives, local_step(): lax.all_to_all(mixed, 'morton', 0, 0, axis_index_groups=same_core, tiled=...  18.3 us
    ppermute x15, starting transfers between devices, shift(): lax.ppermute(value, axis, [(i, (i + step) % size) for i in range(size)])  16.4 us
    all_to_all x1, starting transfers between devices, local_step(): lax.all_to_all(parts.reshape((4 * chips,) + piece[1:]), ('morton', 'chan'...  8.77 us
    all_to_all x1, starting transfers between devices, local_step(): incoming = lax.all_to_all(outgoing, 'morton', 0, 0, tiled=True)  8.59 us
    ppermute x3, starting transfers between devices, swap_cores(): return lax.ppermute(value, 'morton', [(i, i ^ 1) for i in range(size)])  8.55 us
    pallas_call x1, Pallas kernels, local_step(): call(table_kernel, 'table_grad', [shape(wide, F32), shape(blocks, BF), sh...  5.82 us
    pallas_call x2, Pallas kernels, local_step(): call(functools.partial(forward_kernel, half), f'forward{half}', [shape(pa...  4.5 us
  transfers between devices with their start and end apart: 20, of which 11 were waited for; matrix products, arithmetic and copies ran while one was open for 0% of the time, Pallas kernels for 12%

profile of v6, /device:TPU:1, one launch (start us, length us, event | category | flops | bytes accessed | tf_op | source)
XLA Modules:
  0.0 112.8 jit_solution(4005118127792342728)
XLA Ops:
  0.7 1.0 copy-done.2
  1.7 0.7 copy-done.5
  2.3 0.7 copy-done.7
  3.0 1.5 %pack.1 = bf16[32,64,128]{2,1,0:T(8,128)(2,1)} custom-call(s32[1,32]{1,0:T(1,128)S(1)} %copy-done.5, s32[1,32]{1,0:T(1,128)S(1)} %copy-done.7, bf16[64,2048]{1,0:T(8,128)(2,1)S(1)} %copy-done.2), custom_call_target="tpu_custom_call" | custom-call | bytes 1048576 | tf_op jit(solution)/shard_map/pack/pallas_call | solution.py:290
  4.5 8.6 %all-to-all-start = ((bf16[32,64,128]{2,1,0:T(8,128)(2,1)}), bf16[32,64,128]{2,1,0:T(8,128)(2,1)S(1)}, u32[]{:S(2)}, u32[]{:S(2)}) async-start(bf16[32,64,128]{2,1,0:T(8,128)(2,1)} %pack.1), calls=%async_computation | async-start | bytes 1048576 | tf_op jit(solution)/shard_map/all_to_all | solution.py:293
  13.1 0.3 split.1
  13.5 3.8 %collective-permute-start.2 = (bf16[14,64,128]{2,1,0:T(8,128)(2,1)S(1)}, bf16[14,64,128]{2,1,0:T(8,128)(2,1)S(1)}, u32[]{:S(2)}, u32[]{:S(2)}) collective-permute-start(bf16[14,64,128]{2,1,0:T(8,128)(2,1)S(1)} %get-tuple-element.42), channel_id=1, source_target_pairs={{0,3},{1,0},{2,1},{3,2},{4,7},{5,4},{6,5},{7,6},{8,11},{9,8},{10,9... | collective-permute-start | bytes 688136 | tf_op jit(solution)/shard_map/ppermute | solution.py:267
  17.4 0.7 collective-permute-start
  18.1 8.9 %collective-permute-done.2.refs_3_.piece3 = bf16[14,64,128]{2,1,0:T(8,128)(2,1)S(1)} collective-permute-done((bf16[14,64,128]{2,1,0:T(8,128)(2,1)S(1)}, bf16[14,64,128]{2,1,0:T(8,128)(2,1)S(1)}, u32[]{:S(2)}, u32[]{:S(2)}) %collective-permute-start.2) | collective-permute-done | bytes 229408 | tf_op jit(solution)/shard_map/ppermute | solution.py:267
  27.0 3.7 %collective-permute-done.refs_1_.piece1 = bf16[14,64,128]{2,1,0:T(8,128)(2,1)S(1)} collective-permute-done((bf16[14,64,128]{2,1,0:T(8,128)(2,1)S(1)}, bf16[14,64,128]{2,1,0:T(8,128)(2,1)S(1)}, u32[]{:S(2)}, u32[]{:S(2)}) %collective-permute-start) | collective-permute-done | bytes 229408 | tf_op jit(solution)/shard_map/ppermute | solution.py:267
  30.7 2.3 %forward0.1 = (f32[64,1024]{1,0:T(8,128)S(1)}, bf16[64,1024]{1,0:T(8,128)(2,1)S(1)}, bf16[64,1024]{1,0:T(8,128)(2,1)S(1)}, bf16[64,1024]{1,0:T(8,128)(2,1)S(1)}) custom-call(s32[27,16]{1,0:T(8,128)S(1)} %copy.11.neighbour, bf16[64,2048]{1,0:T(8,128)(2,1)S(1)} %copy-done.3, bf16[32,64,128]{2,1,0:T(8,128)(2,1)S(1)} %all-to-all-done.incoming, ...), custom_call_target="tpu_custom_call" | custom-call | flops 939524096 | bytes 3145728 | tf_op jit(solution)/shard_map/forward0/pallas_call | solution.py:304
  33.0 0.1 collective-permute-start.6
  33.1 0.6 collective-permute-start.7
  33.7 0.8 collective-permute-start.8
  34.5 2.2 %forward1.1 = (f32[64,1024]{1,0:T(8,128)S(1)}, bf16[64,1024]{1,0:T(8,128)(2,1)S(1)}, bf16[64,1024]{1,0:T(8,128)(2,1)S(1)}, bf16[64,1024]{1,0:T(8,128)(2,1)S(1)}) custom-call(s32[27,16]{1,0:T(8,128)S(1)} %copy.11.neighbour, bf16[64,2048]{1,0:T(8,128)(2,1)S(1)} %copy-done.3, bf16[32,64,128]{2,1,0:T(8,128)(2,1)S(1)} %all-to-all-done.incoming, ...), custom_call_target="tpu_custom_call" | custom-call | flops 939524096 | bytes 3145728 | tf_op jit(solution)/shard_map/forward1/pallas_call | solution.py:304
  36.8 2.5 %collective-permute-start.3 = (bf16[64,1024]{1,0:T(8,128)(2,1)S(1)}, bf16[64,1024]{1,0:T(8,128)(2,1)S(1)}, u32[]{:S(2)}, u32[]{:S(2)}) collective-permute-start(bf16[64,1024]{1,0:T(8,128)(2,1)S(1)} %get-tuple-element.24), channel_id=1, source_target_pairs={{0,3},{1,0},{2,1},{3,2},{4,7},{5,4},{6,5},{7,6},{8,11},{9,8},{10,9... | collective-permute-start | bytes 393224 | tf_op jit(solution)/shard_map/ppermute | solution.py:267
  39.3 1.3 %collective-permute-start.4 = (bf16[64,1024]{1,0:T(8,128)(2,1)S(1)}, bf16[64,1024]{1,0:T(8,128)(2,1)S(1)}, u32[]{:S(2)}, u32[]{:S(2)}) collective-permute-start(bf16[64,1024]{1,0:T(8,128)(2,1)S(1)} %get-tuple-element.25), channel_id=1, source_target_pairs={{0,2},{1,3},{2,0},{3,1},{4,6},{5,7},{6,4},{7,5},{8,10},{9,11},{10,... | collective-permute-start | bytes 393224 | tf_op jit(solution)/shard_map/ppermute | solution.py:267
  40.5 0.8 collective-permute-start.5
  41.3 0.8 collective-permute-done.8.part3
  42.1 0.2 activation0.1
  42.3 1.2 %collective-permute-start.11 = (bf16[64,1024]{1,0:T(8,128)(2,1)S(1)}, bf16[64,1024]{1,0:T(8,128)(2,1)S(1)}, u32[]{:S(2)}, u32[]{:S(2)}) collective-permute-start(bf16[64,1024]{1,0:T(8,128)(2,1)S(1)} %get-tuple-element.33.after.grad0.g00), channel_id=1, source_target_pairs={{0,3},{1,0},{2,1},{3,2},{4,7},{5,4},{6,5},{7,6},{8,11},{9,8},{10,9... | collective-permute-start | bytes 393224 | tf_op jit(solution)/shard_map/ppermute | solution.py:267
  43.5 0.5 collective-permute-start.10
  44.0 0.2 collective-permute-start.9
  44.1 0.6 collective-permute-done.4.part2
  44.7 2.4 %collective-permute-done.5.part3 = bf16[64,1024]{1,0:T(8,128)(2,1)S(1)} collective-permute-done((bf16[64,1024]{1,0:T(8,128)(2,1)S(1)}, bf16[64,1024]{1,0:T(8,128)(2,1)S(1)}, u32[]{:S(2)}, u32[]{:S(2)}) %collective-permute-start.5) | collective-permute-done | bytes 131104 | tf_op jit(solution)/shard_map/ppermute | solution.py:267
  47.1 0.8 activation1.1
  48.0 1.0 collective-permute-start.14
  49.0 2.1 %collective-permute-start.13 = (bf16[64,1024]{1,0:T(8,128)(2,1)S(1)}, bf16[64,1024]{1,0:T(8,128)(2,1)S(1)}, u32[]{:S(2)}, u32[]{:S(2)}) collective-permute-start(bf16[64,1024]{1,0:T(8,128)(2,1)S(1)} %get-tuple-element.34.grad0.g10), channel_id=1, source_target_pairs={{0,2},{1,3},{2,0},{3,1},{4,6},{5,7},{6,4},{7,5},{8,10},{9,11},{10,... | collective-permute-start | bytes 393224 | tf_op jit(solution)/shard_map/ppermute | solution.py:267
  51.1 0.9 collective-permute-start.12
  52.0 1.7 %collective-permute-done.9.grad1.g01 = bf16[64,1024]{1,0:T(8,128)(2,1)S(1)} collective-permute-done((bf16[64,1024]{1,0:T(8,128)(2,1)S(1)}, bf16[64,1024]{1,0:T(8,128)(2,1)S(1)}, u32[]{:S(2)}, u32[]{:S(2)}) %collective-permute-start.9) | collective-permute-done | bytes 131104 | tf_op jit(solution)/shard_map/ppermute | solution.py:267
  53.6 2.1 %weight_grad0.1.held = f32[1792,256]{1,0:T(8,128)S(1)} custom-call(s32[27,16]{1,0:T(8,128)S(1)} %copy.11.neighbour, bf16[64,2048]{1,0:T(8,128)(2,1)S(1)} %copy-done.3, bf16[32,64,128]{2,1,0:T(8,128)(2,1)S(1)} %all-to-all-done.incoming, bf16[64,1024]{1,0:T(8,128)(2,1)S(1)} %get-tuple-element.33.after.grad0.g00, ...), custom_call_target="tpu_custom_call" | custom-call | flops 939524096 | bytes 4194304 | tf_op jit(solution)/shard_map/weight_grad0/pallas_call | solution.py:326
  55.8 1.5 %collective-permute-done.12.grad1.g11 = bf16[64,1024]{1,0:T(8,128)(2,1)S(1)} collective-permute-done((bf16[64,1024]{1,0:T(8,128)(2,1)S(1)}, bf16[64,1024]{1,0:T(8,128)(2,1)S(1)}, u32[]{:S(2)}, u32[]{:S(2)}) %collective-permute-start.12) | collective-permute-done | bytes 131104 | tf_op jit(solution)/shard_map/ppermute | solution.py:267
  57.3 2.2 %weight_grad1.1 = (f32[14,4,32,128]{3,2,1,0:T(8,128)S(1)}, bf16[14,4,32,128]{3,2,1,0:T(8,128)(2,1)S(1)}) custom-call(s32[1]{0:T(128)} %bitcast.1.core, s32[27,16]{1,0:T(8,128)S(1)} %copy.11.neighbour, bf16[64,2048]{1,0:T(8,128)(2,1)S(1)} %copy-done.3, bf16[32,64,128]{2,1,0:T(8,128)(2,1)S(1)} %all-to-all-done.incoming, ...), custom_call_target="tpu_custom_call" | custom-call | flops 939524096 | bytes 4194304 | tf_op jit(solution)/shard_map/weight_grad1/pallas_call | solution.py:336
  59.6 4.9 %collective-permute-start.15 = (bf16[14,4,32,128]{3,2,1,0:T(8,128)(2,1)S(1)}, bf16[14,4,32,128]{3,2,1,0:T(8,128)(2,1)S(1)}, u32[]{:S(2)}, u32[]{:S(2)}) collective-permute-start(bf16[14,4,32,128]{3,2,1,0:T(8,128)(2,1)S(1)} %get-tuple-element.36), channel_id=1, source_target_pairs={{0,4},{4,0},{8,12},{12,8},{16,20},{20,16},{24,28},{28,24},{32,36},... | collective-permute-start | bytes 1376264 | tf_op jit(solution)/shard_map/ppermute | solution.py:272
  64.5 1.4 %collective-permute-done.15.arrived = bf16[14,4,32,128]{3,2,1,0:T(8,128)(2,1)S(1)} collective-permute-done((bf16[14,4,32,128]{3,2,1,0:T(8,128)(2,1)S(1)}, bf16[14,4,32,128]{3,2,1,0:T(8,128)(2,1)S(1)}, u32[]{:S(2)}, u32[]{:S(2)}) %collective-permute-start.15) | collective-permute-done | bytes 458784 | tf_op jit(solution)/shard_map/ppermute | solution.py:272
  65.9 0.9 pair_sum.1.after
  66.8 8.8 %all-to-all-start.1 = ((bf16[64,32,128]{2,1,0:T(8,128)(2,1)}), bf16[64,32,128]{2,1,0:T(8,128)(2,1)S(1)}, u32[]{:S(2)}, u32[]{:S(2)}) async-start(bf16[64,32,128]{2,1,0:T(8,128)(2,1)} %bitcast.2), calls=%async_computation.1 | async-start | bytes 1048576 | tf_op jit(solution)/shard_map/all_to_all | solution.py:351
  75.6 0.3 join.1.weight_t
  75.8 5.8 %table_grad.1 = (f32[64,2048]{1,0:T(8,128)S(1)}, bf16[16,64,128]{2,1,0:T(8,128)(2,1)S(1)}, bf16[16,64,128]{2,1,0:T(8,128)(2,1)S(1)}) custom-call(s32[1]{0:T(128)} %bitcast.1.core, s32[27,16]{1,0:T(8,128)S(1)} %copy.11.neighbour, bf16[1792,256]{1,0:T(8,128)(2,1)S(1)} %join.1.weight_t, bf16[64,1024]{1,0:T(8,128)(2,1)S(1)} %get-tuple-element.33.after.grad0.g00, ...), custom_call_target="tpu_custom_call" | custom-call | flops 1879048192 | bytes 4194304 | tf_op jit(solution)/shard_map/table_grad/pallas_call | solution.py:361
  81.7 0.7 collective-permute-start.16
  82.4 1.2 %collective-permute-done.16.away = bf16[16,64,128]{2,1,0:T(8,128)(2,1)S(1)} collective-permute-done((bf16[16,64,128]{2,1,0:T(8,128)(2,1)S(1)}, bf16[16,64,128]{2,1,0:T(8,128)(2,1)S(1)}, u32[]{:S(2)}, u32[]{:S(2)}) %collective-permute-start.16) | collective-permute-done | bytes 262176 | tf_op jit(solution)/shard_map/ppermute | solution.py:272
  83.6 4.2 %all-to-all-done.1 = bf16[64,32,128]{2,1,0:T(8,128)(2,1)S(1)} async-done(((bf16[64,32,128]{2,1,0:T(8,128)(2,1)}), bf16[64,32,128]{2,1,0:T(8,128)(2,1)S(1)}, u32[]{:S(2)}, u32[]{:S(2)}) %all-to-all-start.1) | async-done | bytes 524320 | tf_op jit(solution)/shard_map/all_to_all | solution.py:351
  87.8 0.2 sum_parts.1
  88.0 18.3 %all_to_all.15.mixed.mine = bf16[16,8,32,128]{3,2,1,0:T(8,128)(2,1)S(1)} all-to-all(bf16[16,8,32,128]{3,2,1,0:T(8,128)(2,1)S(1)} %sum_parts.1), channel_id=1, replica_groups={{0,8,16,24,32,40,48,56,64,72,80,88,96,104,112,120},{4,12,20,28,36,44,52..., dimensions={0} | all-to-all | bytes 2097152 | tf_op jit(solution)/shard_map/all_to_all | solution.py:381
  106.2 2.9 %collective-permute-start.17 = (bf16[16,8,32,128]{3,2,1,0:T(8,128)(2,1)S(1)}, bf16[16,8,32,128]{3,2,1,0:T(8,128)(2,1)S(1)}, u32[]{:S(2)}, u32[]{:S(2)}) collective-permute-start(bf16[16,8,32,128]{3,2,1,0:T(8,128)(2,1)S(1)} %all_to_all.15.mixed.mine), channel_id=1, source_target_pairs={{0,4},{4,0},{8,12},{12,8},{16,20},{20,16},{24,28},{28,24},{32,36},... | collective-permute-start | bytes 3145736 | tf_op jit(solution)/shard_map/ppermute | solution.py:272
  109.2 1.6 %return_add.1 = f32[64,2048]{1,0:T(8,128)} custom-call(s32[1]{0:T(128)} %bitcast.1.core, s32[1,32]{1,0:T(1,128)S(1)} %copy-done.6, s32[1,32]{1,0:T(1,128)S(1)} %copy-done.8, f32[64,2048]{1,0:T(8,128)S(1)} %get-tuple-element.37.local, bf16[16,8,32,128]{3,2,1,0:T(8,128)(2,1)S(1)} %all_to_all.15.mixed.mine), custom_call_target="tpu_custom_call" | custom-call | bytes 2097152 | tf_op jit(solution)/shard_map/return_add/pallas_call | solution.py:382
  110.8 0.6 collective-permute-done.17.other
  111.5 1.3 %unpack.1 = (f32[27,64,256]{2,1,0:T(8,128)}, f32[64,256]{1,0:T(8,128)}) custom-call(s32[1]{0:T(128)} %bitcast.1.core, bf16[16,8,32,128]{3,2,1,0:T(8,128)(2,1)S(1)} %all_to_all.15.mixed.mine, bf16[16,8,32,128]{3,2,1,0:T(8,128)(2,1)S(1)} %collective-permute-done.17.other), custom_call_target="tpu_custom_call" | custom-call | bytes 3145728 | tf_op jit(solution)/shard_map/unpack/pallas_call | solution.py:385
  (29 shorter events, 0.2 us)
Async XLA Ops:
  0.6 12.4 %copy-start.1 = (bf16[27,64,256]{2,1,0:T(8,128)(2,1)S(1)}, bf16[27,64,256]{2,1,0:T(8,128)(2,1)}, u32[]{:S(2)}) copy-start(bf16[27,64,256]{2,1,0:T(8,128)(2,1)} %conv_weight.1) | copy-start | bytes 2654212
  0.6 1.0 copy-start.2
  1.7 0.7 copy-start.5
  2.3 0.7 copy-start.7
  3.0 10.1 %copy-start.4 = (bf16[64,256]{1,0:T(8,128)(2,1)S(1)}, bf16[64,256]{1,0:T(8,128)(2,1)}, u32[]{:S(2)}) copy-start(bf16[64,256]{1,0:T(8,128)(2,1)} %coarse_weight.1) | copy-start | bytes 98308
  4.5 26.3 %all-to-all-start = ((bf16[32,64,128]{2,1,0:T(8,128)(2,1)}), bf16[32,64,128]{2,1,0:T(8,128)(2,1)S(1)}, u32[]{:S(2)}, u32[]{:S(2)}) async-start(bf16[32,64,128]{2,1,0:T(8,128)(2,1)} %pack.1), calls=%async_computation | async-start | bytes 1048576 | tf_op jit(solution)/shard_map/all_to_all | solution.py:293
  13.1 5.0 %copy-start.9 = (s32[27,16]{0,1:T(8,128)S(1)}, s32[27,16]{0,1:T(8,128)}, u32[]{:S(2)}) copy-start(s32[27,16]{0,1:T(8,128)} %param.13) | copy-start | bytes 5188
  13.1 17.6 %copy-start.3 = (bf16[64,2048]{1,0:T(8,128)(2,1)S(1)}, bf16[64,2048]{1,0:T(8,128)(2,1)}, u32[]{:S(2)}) copy-start(bf16[64,2048]{1,0:T(8,128)(2,1)} %features.9) | copy-start | bytes 786436
  13.5 13.5 %collective-permute-start.2 = (bf16[14,64,128]{2,1,0:T(8,128)(2,1)S(1)}, bf16[14,64,128]{2,1,0:T(8,128)(2,1)S(1)}, u32[]{:S(2)}, u32[]{:S(2)}) collective-permute-start(bf16[14,64,128]{2,1,0:T(8,128)(2,1)S(1)} %get-tuple-element.42), channel_id=1, source_target_pairs={{0,3},{1,0},{2,1},{3,2},{4,7},{5,4},{6,5},{7,6},{8,11},{9,8},{10,9... | collective-permute-start | bytes 688136 | tf_op jit(solution)/shard_map/ppermute | solution.py:267
  17.4 9.7 %collective-permute-start.1 = (bf16[14,64,128]{2,1,0:T(8,128)(2,1)S(1)}, bf16[14,64,128]{2,1,0:T(8,128)(2,1)S(1)}, u32[]{:S(2)}, u32[]{:S(2)}) collective-permute-start(bf16[14,64,128]{2,1,0:T(8,128)(2,1)S(1)} %get-tuple-element.43), channel_id=1, source_target_pairs={{0,2},{1,3},{2,0},{3,1},{4,6},{5,7},{6,4},{7,5},{8,10},{9,11},{10,... | collective-permute-start | bytes 688136 | tf_op jit(solution)/shard_map/ppermute | solution.py:267
  17.4 13.4 %collective-permute-start = (bf16[14,64,128]{2,1,0:T(8,128)(2,1)S(1)}, bf16[14,64,128]{2,1,0:T(8,128)(2,1)S(1)}, u32[]{:S(2)}, u32[]{:S(2)}) collective-permute-start(bf16[14,64,128]{2,1,0:T(8,128)(2,1)S(1)} %get-tuple-element.44), channel_id=1, source_target_pairs={{0,1},{1,2},{2,3},{3,0},{4,5},{5,6},{6,7},{7,4},{8,9},{9,10},{10,1... | collective-permute-start | bytes 688136 | tf_op jit(solution)/shard_map/ppermute | solution.py:267
  33.0 9.1 %copy-start = (bf16[64,2048]{1,0:T(8,128)(2,1)S(1)}, bf16[64,2048]{1,0:T(8,128)(2,1)}, u32[]{:S(2)}) copy-start(bf16[64,2048]{1,0:T(8,128)(2,1)} %out_grad.3) | copy-start | bytes 786436
  33.0 7.5 %collective-permute-start.6 = (bf16[64,1024]{1,0:T(8,128)(2,1)S(1)}, bf16[64,1024]{1,0:T(8,128)(2,1)S(1)}, u32[]{:S(2)}, u32[]{:S(2)}) collective-permute-start(bf16[64,1024]{1,0:T(8,128)(2,1)S(1)} %get-tuple-element.28), channel_id=1, source_target_pairs={{0,3},{1,0},{2,1},{3,2},{4,7},{5,4},{6,5},{7,6},{8,11},{9,8},{10,9... | collective-permute-start | bytes 393224 | tf_op jit(solution)/shard_map/ppermute | solution.py:267
  33.1 8.2 %collective-permute-start.7 = (bf16[64,1024]{1,0:T(8,128)(2,1)S(1)}, bf16[64,1024]{1,0:T(8,128)(2,1)S(1)}, u32[]{:S(2)}, u32[]{:S(2)}) collective-permute-start(bf16[64,1024]{1,0:T(8,128)(2,1)S(1)} %get-tuple-element.29), channel_id=1, source_target_pairs={{0,2},{1,3},{2,0},{3,1},{4,6},{5,7},{6,4},{7,5},{8,10},{9,11},{10,... | collective-permute-start | bytes 393224 | tf_op jit(solution)/shard_map/ppermute | solution.py:267
  33.7 8.3 %collective-permute-start.8 = (bf16[64,1024]{1,0:T(8,128)(2,1)S(1)}, bf16[64,1024]{1,0:T(8,128)(2,1)S(1)}, u32[]{:S(2)}, u32[]{:S(2)}) collective-permute-start(bf16[64,1024]{1,0:T(8,128)(2,1)S(1)} %get-tuple-element.30), channel_id=1, source_target_pairs={{0,1},{1,2},{2,3},{3,0},{4,5},{5,6},{6,7},{7,4},{8,9},{9,10},{10,1... | collective-permute-start | bytes 393224 | tf_op jit(solution)/shard_map/ppermute | solution.py:267
  36.8 7.2 %collective-permute-start.3 = (bf16[64,1024]{1,0:T(8,128)(2,1)S(1)}, bf16[64,1024]{1,0:T(8,128)(2,1)S(1)}, u32[]{:S(2)}, u32[]{:S(2)}) collective-permute-start(bf16[64,1024]{1,0:T(8,128)(2,1)S(1)} %get-tuple-element.24), channel_id=1, source_target_pairs={{0,3},{1,0},{2,1},{3,2},{4,7},{5,4},{6,5},{7,6},{8,11},{9,8},{10,9... | collective-permute-start | bytes 393224 | tf_op jit(solution)/shard_map/ppermute | solution.py:267
  39.3 5.5 %collective-permute-start.4 = (bf16[64,1024]{1,0:T(8,128)(2,1)S(1)}, bf16[64,1024]{1,0:T(8,128)(2,1)S(1)}, u32[]{:S(2)}, u32[]{:S(2)}) collective-permute-start(bf16[64,1024]{1,0:T(8,128)(2,1)S(1)} %get-tuple-element.25), channel_id=1, source_target_pairs={{0,2},{1,3},{2,0},{3,1},{4,6},{5,7},{6,4},{7,5},{8,10},{9,11},{10,... | collective-permute-start | bytes 393224 | tf_op jit(solution)/shard_map/ppermute | solution.py:267
  40.5 6.6 %collective-permute-start.5 = (bf16[64,1024]{1,0:T(8,128)(2,1)S(1)}, bf16[64,1024]{1,0:T(8,128)(2,1)S(1)}, u32[]{:S(2)}, u32[]{:S(2)}) collective-permute-start(bf16[64,1024]{1,0:T(8,128)(2,1)S(1)} %get-tuple-element.26), channel_id=1, source_target_pairs={{0,1},{1,2},{2,3},{3,0},{4,5},{5,6},{6,7},{7,4},{8,9},{9,10},{10,1... | collective-permute-start | bytes 393224 | tf_op jit(solution)/shard_map/ppermute | solution.py:267
  42.3 8.8 %collective-permute-start.11 = (bf16[64,1024]{1,0:T(8,128)(2,1)S(1)}, bf16[64,1024]{1,0:T(8,128)(2,1)S(1)}, u32[]{:S(2)}, u32[]{:S(2)}) collective-permute-start(bf16[64,1024]{1,0:T(8,128)(2,1)S(1)} %get-tuple-element.33.after.grad0.g00), channel_id=1, source_target_pairs={{0,3},{1,0},{2,1},{3,2},{4,7},{5,4},{6,5},{7,6},{8,11},{9,8},{10,9... | collective-permute-start | bytes 393224 | tf_op jit(solution)/shard_map/ppermute | solution.py:267
  43.5 8.5 %collective-permute-start.10 = (bf16[64,1024]{1,0:T(8,128)(2,1)S(1)}, bf16[64,1024]{1,0:T(8,128)(2,1)S(1)}, u32[]{:S(2)}, u32[]{:S(2)}) collective-permute-start(bf16[64,1024]{1,0:T(8,128)(2,1)S(1)} %get-tuple-element.33.after.grad0.g00), channel_id=1, source_target_pairs={{0,2},{1,3},{2,0},{3,1},{4,6},{5,7},{6,4},{7,5},{8,10},{9,11},{10,... | collective-permute-start | bytes 393224 | tf_op jit(solution)/shard_map/ppermute | solution.py:267
  44.0 9.7 %collective-permute-start.9 = (bf16[64,1024]{1,0:T(8,128)(2,1)S(1)}, bf16[64,1024]{1,0:T(8,128)(2,1)S(1)}, u32[]{:S(2)}, u32[]{:S(2)}) collective-permute-start(bf16[64,1024]{1,0:T(8,128)(2,1)S(1)} %get-tuple-element.33.after.grad0.g00), channel_id=1, source_target_pairs={{0,1},{1,2},{2,3},{3,0},{4,5},{5,6},{6,7},{7,4},{8,9},{9,10},{10,1... | collective-permute-start | bytes 393224 | tf_op jit(solution)/shard_map/ppermute | solution.py:267
  48.0 7.8 %collective-permute-start.14 = (bf16[64,1024]{1,0:T(8,128)(2,1)S(1)}, bf16[64,1024]{1,0:T(8,128)(2,1)S(1)}, u32[]{:S(2)}, u32[]{:S(2)}) collective-permute-start(bf16[64,1024]{1,0:T(8,128)(2,1)S(1)} %get-tuple-element.34.grad0.g10), channel_id=1, source_target_pairs={{0,3},{1,0},{2,1},{3,2},{4,7},{5,4},{6,5},{7,6},{8,11},{9,8},{10,9... | collective-permute-start | bytes 393224 | tf_op jit(solution)/shard_map/ppermute | solution.py:267
  49.0 6.8 %collective-permute-start.13 = (bf16[64,1024]{1,0:T(8,128)(2,1)S(1)}, bf16[64,1024]{1,0:T(8,128)(2,1)S(1)}, u32[]{:S(2)}, u32[]{:S(2)}) collective-permute-start(bf16[64,1024]{1,0:T(8,128)(2,1)S(1)} %get-tuple-element.34.grad0.g10), channel_id=1, source_target_pairs={{0,2},{1,3},{2,0},{3,1},{4,6},{5,7},{6,4},{7,5},{8,10},{9,11},{10,... | collective-permute-start | bytes 393224 | tf_op jit(solution)/shard_map/ppermute | solution.py:267
  51.1 6.2 %collective-permute-start.12 = (bf16[64,1024]{1,0:T(8,128)(2,1)S(1)}, bf16[64,1024]{1,0:T(8,128)(2,1)S(1)}, u32[]{:S(2)}, u32[]{:S(2)}) collective-permute-start(bf16[64,1024]{1,0:T(8,128)(2,1)S(1)} %get-tuple-element.34.grad0.g10), channel_id=1, source_target_pairs={{0,1},{1,2},{2,3},{3,0},{4,5},{5,6},{6,7},{7,4},{8,9},{9,10},{10,1... | collective-permute-start | bytes 393224 | tf_op jit(solution)/shard_map/ppermute | solution.py:267
  59.6 6.3 %collective-permute-start.15 = (bf16[14,4,32,128]{3,2,1,0:T(8,128)(2,1)S(1)}, bf16[14,4,32,128]{3,2,1,0:T(8,128)(2,1)S(1)}, u32[]{:S(2)}, u32[]{:S(2)}) collective-permute-start(bf16[14,4,32,128]{3,2,1,0:T(8,128)(2,1)S(1)} %get-tuple-element.36), channel_id=1, source_target_pairs={{0,4},{4,0},{8,12},{12,8},{16,20},{20,16},{24,28},{28,24},{32,36},... | collective-permute-start | bytes 1376264 | tf_op jit(solution)/shard_map/ppermute | solution.py:272
  66.8 21.0 %all-to-all-start.1 = ((bf16[64,32,128]{2,1,0:T(8,128)(2,1)}), bf16[64,32,128]{2,1,0:T(8,128)(2,1)S(1)}, u32[]{:S(2)}, u32[]{:S(2)}) async-start(bf16[64,32,128]{2,1,0:T(8,128)(2,1)} %bitcast.2), calls=%async_computation.1 | async-start | bytes 1048576 | tf_op jit(solution)/shard_map/all_to_all | solution.py:351
  81.7 1.9 %collective-permute-start.16 = (bf16[16,64,128]{2,1,0:T(8,128)(2,1)S(1)}, bf16[16,64,128]{2,1,0:T(8,128)(2,1)S(1)}, u32[]{:S(2)}, u32[]{:S(2)}) collective-permute-start(bf16[16,64,128]{2,1,0:T(8,128)(2,1)S(1)} %get-tuple-element.39), channel_id=1, source_target_pairs={{0,4},{4,0},{8,12},{12,8},{16,20},{20,16},{24,28},{28,24},{32,36},... | collective-permute-start | bytes 786440 | tf_op jit(solution)/shard_map/ppermute | solution.py:272
  87.8 21.4 %copy-start.6 = (s32[1,32]{1,0:T(1,128)S(1)}, s32[1,32]{1,0:T(1,128)}, u32[]{:S(2)}) copy-start(s32[1,32]{1,0:T(1,128)} %send_block.3) | copy-start | bytes 388
  87.8 21.4 %copy-start.8 = (s32[1,32]{1,0:T(1,128)S(1)}, s32[1,32]{1,0:T(1,128)}, u32[]{:S(2)}) copy-start(s32[1,32]{1,0:T(1,128)} %send_count.3) | copy-start | bytes 388
  106.2 5.2 %collective-permute-start.17 = (bf16[16,8,32,128]{3,2,1,0:T(8,128)(2,1)S(1)}, bf16[16,8,32,128]{3,2,1,0:T(8,128)(2,1)S(1)}, u32[]{:S(2)}, u32[]{:S(2)}) collective-permute-start(bf16[16,8,32,128]{3,2,1,0:T(8,128)(2,1)S(1)} %all_to_all.15.mixed.mine), channel_id=1, source_target_pairs={{0,4},{4,0},{8,12},{12,8},{16,20},{20,16},{24,28},{28,24},{32,36},... | collective-permute-start | bytes 3145736 | tf_op jit(solution)/shard_map/ppermute | solution.py:272

commit v7 on v6

--- a/solution.py
+++ b/solution.py
@@ -55,7 +55,7 @@
         cuts = [slice(t * quarter, (t + 1) * quarter) for t in range(4)]
         tiles = [jnp.concatenate([first[:, c], second[:, c]], axis=1) for c in cuts]
         for step in range(4):
-            target = lax.rem(place[0] + step, 4)
+            target = place[0] ^ step
             low = jnp.where(target == 0, tiles[0], tiles[1])
             high = jnp.where(target == 2, tiles[2], tiles[3])
             pieces[step * PAIRS + pair] = jnp.where(target < 2, low, high)
@@ -173,7 +173,7 @@
 
 def pair_kernel(place, keep, arrived, parts):
     for step in range(4):
-        target = lax.rem(place[0] - step + 4, 4)
+        target = place[0] ^ step
         for pair in range(PAIRS):
             parts[pair, target] = (keep[pair, step] + arrived[pair, step].astype(F32)).astype(BF)
     for spare in range(PAIRS, parts.shape[0]):
@@ -262,9 +262,9 @@
                     coarse_grad[rows, cut] = value
 
 
-def shift(value, axis, step):
-    size = lax.axis_size(axis)
-    return lax.ppermute(value, axis, [(i, (i + step) % size) for i in range(size)])
+def exchange(value, step):
+    size = lax.axis_size("chan")
+    return lax.ppermute(value, "chan", [(i, i ^ step) for i in range(size)])
 
 
 def swap_cores(value):
@@ -293,7 +293,7 @@
     incoming = lax.all_to_all(outgoing, "morton", 0, 0, tiled=True)
 
     pieces = pieces.reshape(4, PAIRS, quarter, BLOCK)
-    weights = [pieces[0]] + [shift(pieces[s], "chan", s) for s in (1, 2, 3)]
+    weights = [pieces[0]] + [exchange(pieces[s], s) for s in (1, 2, 3)]
     middle = row_count // 2
     big = [pltpu.VMEM((extent + 1, quarter, BLOCK), BF), pltpu.VMEM((depth, middle), BF)]
     turned = [pltpu.VMEM((middle, channels), BF)]
@@ -310,7 +310,7 @@
             flops // 2,
             3 << 20,
         )(neighbour, features, incoming, *weights)
-        arrived = [shift(partial[s], "chan", -s) for s in (1, 2, 3)]
+        arrived = [exchange(partial[s], s) for s in (1, 2, 3)]
         output, grad = call(
             activation_end_kernel if half else activation_kernel,
             f"activation{half}",
@@ -318,7 +318,7 @@
             "vvvvvv" if half else "vvvvv",
             size=1 << 20,
         )(partial[0], *arrived, out_grad, *((output,) if half else ()))
-        grads.append([grad] + [shift(grad, "chan", s) for s in (1, 2, 3)])
+        grads.append([grad] + [exchange(grad, s) for s in (1, 2, 3)])
 
     weight_t = call(join_kernel, "join", shape((depth, channels), BF), "vvvva", size=3 << 20)(
         *weights, grads[0][0]

time: 113 us -> 115 us (1.018)
  starting transfers between devices: 42.3 us -> 48.6 us
  waiting for transfers between devices: 27.1 us -> 22.5 us
    ppermute x15, waiting for transfers between devices: 19.6 us -> 15 us  [exchange(): return lax.ppermute(value, 'chan', [(i, i ^ step) for i in range(size)])]
    ppermute x15, starting transfers between devices: 16.4 us -> 20.6 us  [exchange(): return lax.ppermute(value, 'chan', [(i, i ^ step) for i in range(size)])]
    ppermute x3, starting transfers between devices: 8.55 us -> 9.84 us  [swap_cores(): return lax.ppermute(value, 'morton', [(i, i ^ 1) for i in range(size)])]
  transfers between devices with their start and end apart: 20 -> 20, of which waited for: 11 -> 10; matrix products, arithmetic and copies ran while one was open for 0% -> 0% of each run, Pallas kernels for 12% -> 12%
where the time goes in v7:
time: 115 us
  starting transfers between devices  48.6 us (42%)
  waiting for transfers between devices  22.5 us (20%)
  Pallas kernels  21.8 us (19%)
  blocking collectives  18.3 us (16%)
  local copies, waits for them, and re-layouts  2.54 us (2%)
    ppermute x15, starting transfers between devices, exchange(): return lax.ppermute(value, 'chan', [(i, i ^ step) for i in range(size)])  20.6 us
    all_to_all x1, blocking collectives, local_step(): lax.all_to_all(mixed, 'morton', 0, 0, axis_index_groups=same_core, tiled=...  18.3 us
    ppermute x15, waiting for transfers between devices, exchange(): return lax.ppermute(value, 'chan', [(i, i ^ step) for i in range(size)])  15 us
    ppermute x3, starting transfers between devices, swap_cores(): return lax.ppermute(value, 'morton', [(i, i ^ 1) for i in range(size)])  9.84 us
    all_to_all x1, starting transfers between devices, local_step(): lax.all_to_all(parts.reshape((4 * chips,) + piece[1:]), ('morton', 'chan'...  9.62 us
    all_to_all x1, starting transfers between devices, local_step(): incoming = lax.all_to_all(outgoing, 'morton', 0, 0, tiled=True)  8.59 us
    pallas_call x1, Pallas kernels, local_step(): call(table_kernel, 'table_grad', [shape(wide, F32), shape(blocks, BF), sh...  5.81 us
    pallas_call x2, Pallas kernels, local_step(): call(functools.partial(forward_kernel, half), f'forward{half}', [shape(pa...  4.5 us
  transfers between devices with their start and end apart: 20, of which 10 were waited for; matrix products, arithmetic and copies ran while one was open for 0% of the time, Pallas kernels for 12%

profile of v7, /device:TPU:1, one launch (start us, length us, event | category | flops | bytes accessed | tf_op | source)
XLA Modules:
  0.0 114.5 jit_solution(12771078705569493540)
XLA Ops:
  0.7 1.0 copy-done.2
  1.7 0.7 copy-done.5
  2.3 0.7 copy-done.7
  3.0 1.5 %pack.1 = bf16[32,64,128]{2,1,0:T(8,128)(2,1)} custom-call(s32[1,32]{1,0:T(1,128)S(1)} %copy-done.5, s32[1,32]{1,0:T(1,128)S(1)} %copy-done.7, bf16[64,2048]{1,0:T(8,128)(2,1)S(1)} %copy-done.2), custom_call_target="tpu_custom_call" | custom-call | bytes 1048576 | tf_op jit(solution)/shard_map/pack/pallas_call | solution.py:290
  4.5 8.6 %all-to-all-start = ((bf16[32,64,128]{2,1,0:T(8,128)(2,1)}), bf16[32,64,128]{2,1,0:T(8,128)(2,1)S(1)}, u32[]{:S(2)}, u32[]{:S(2)}) async-start(bf16[32,64,128]{2,1,0:T(8,128)(2,1)} %pack.1), calls=%async_computation | async-start | bytes 1048576 | tf_op jit(solution)/shard_map/all_to_all | solution.py:293
  13.1 0.3 split.1
  13.4 0.1 fusion
  13.5 3.8 %collective-permute-start.2 = (bf16[14,64,128]{2,1,0:T(8,128)(2,1)S(1)}, bf16[14,64,128]{2,1,0:T(8,128)(2,1)S(1)}, u32[]{:S(2)}, u32[]{:S(2)}) collective-permute-start(bf16[14,64,128]{2,1,0:T(8,128)(2,1)S(1)} %get-tuple-element.42), channel_id=1, source_target_pairs={{0,3},{1,2},{2,1},{3,0},{4,7},{5,6},{6,5},{7,4},{8,11},{9,10},{10,... | collective-permute-start | bytes 688136 | tf_op jit(solution)/shard_map/ppermute | solution.py:267
  17.4 0.7 collective-permute-start
  18.0 0.1 copy.11.neighbour
  18.1 10.0 %collective-permute-done.2.refs_3_.piece3 = bf16[14,64,128]{2,1,0:T(8,128)(2,1)S(1)} collective-permute-done((bf16[14,64,128]{2,1,0:T(8,128)(2,1)S(1)}, bf16[14,64,128]{2,1,0:T(8,128)(2,1)S(1)}, u32[]{:S(2)}, u32[]{:S(2)}) %collective-permute-start.2) | collective-permute-done | bytes 229408 | tf_op jit(solution)/shard_map/ppermute | solution.py:267
  28.1 0.4 collective-permute-done.refs_1_.piece1
  28.5 2.3 %forward0.1 = (f32[64,1024]{1,0:T(8,128)S(1)}, bf16[64,1024]{1,0:T(8,128)(2,1)S(1)}, bf16[64,1024]{1,0:T(8,128)(2,1)S(1)}, bf16[64,1024]{1,0:T(8,128)(2,1)S(1)}) custom-call(s32[27,16]{1,0:T(8,128)S(1)} %copy.11.neighbour, bf16[64,2048]{1,0:T(8,128)(2,1)S(1)} %copy-done.3, bf16[32,64,128]{2,1,0:T(8,128)(2,1)S(1)} %all-to-all-done.incoming, ...), custom_call_target="tpu_custom_call" | custom-call | flops 939524096 | bytes 3145728 | tf_op jit(solution)/shard_map/forward0/pallas_call | solution.py:304
  30.8 0.0 copy-start
  30.8 0.9 collective-permute-start.6
  31.7 2.7 %collective-permute-start.7 = (bf16[64,1024]{1,0:T(8,128)(2,1)S(1)}, bf16[64,1024]{1,0:T(8,128)(2,1)S(1)}, u32[]{:S(2)}, u32[]{:S(2)}) collective-permute-start(bf16[64,1024]{1,0:T(8,128)(2,1)S(1)} %get-tuple-element.29), channel_id=1, source_target_pairs={{0,2},{1,3},{2,0},{3,1},{4,6},{5,7},{6,4},{7,5},{8,10},{9,11},{10,... | collective-permute-start | bytes 393224 | tf_op jit(solution)/shard_map/ppermute | solution.py:267
  34.3 0.4 collective-permute-start.8
  34.7 2.2 %forward1.1 = (f32[64,1024]{1,0:T(8,128)S(1)}, bf16[64,1024]{1,0:T(8,128)(2,1)S(1)}, bf16[64,1024]{1,0:T(8,128)(2,1)S(1)}, bf16[64,1024]{1,0:T(8,128)(2,1)S(1)}) custom-call(s32[27,16]{1,0:T(8,128)S(1)} %copy.11.neighbour, bf16[64,2048]{1,0:T(8,128)(2,1)S(1)} %copy-done.3, bf16[32,64,128]{2,1,0:T(8,128)(2,1)S(1)} %all-to-all-done.incoming, ...), custom_call_target="tpu_custom_call" | custom-call | flops 939524096 | bytes 3145728 | tf_op jit(solution)/shard_map/forward1/pallas_call | solution.py:304
  37.0 0.1 collective-permute-start.3
  37.1 3.4 %collective-permute-start.4 = (bf16[64,1024]{1,0:T(8,128)(2,1)S(1)}, bf16[64,1024]{1,0:T(8,128)(2,1)S(1)}, u32[]{:S(2)}, u32[]{:S(2)}) collective-permute-start(bf16[64,1024]{1,0:T(8,128)(2,1)S(1)} %get-tuple-element.25), channel_id=1, source_target_pairs={{0,2},{1,3},{2,0},{3,1},{4,6},{5,7},{6,4},{7,5},{8,10},{9,11},{10,... | collective-permute-start | bytes 393224 | tf_op jit(solution)/shard_map/ppermute | solution.py:267
  40.5 0.4 collective-permute-start.5
  40.9 0.9 collective-permute-done.8.part3
  41.8 0.2 activation0.1
  42.0 1.5 %collective-permute-start.11 = (bf16[64,1024]{1,0:T(8,128)(2,1)S(1)}, bf16[64,1024]{1,0:T(8,128)(2,1)S(1)}, u32[]{:S(2)}, u32[]{:S(2)}) collective-permute-start(bf16[64,1024]{1,0:T(8,128)(2,1)S(1)} %get-tuple-element.33.after.grad0.g00), channel_id=1, source_target_pairs={{0,3},{1,2},{2,1},{3,0},{4,7},{5,6},{6,5},{7,4},{8,11},{9,10},{10,... | collective-permute-start | bytes 393224 | tf_op jit(solution)/shard_map/ppermute | solution.py:267
  43.5 1.8 %collective-permute-start.9 = (bf16[64,1024]{1,0:T(8,128)(2,1)S(1)}, bf16[64,1024]{1,0:T(8,128)(2,1)S(1)}, u32[]{:S(2)}, u32[]{:S(2)}) collective-permute-start(bf16[64,1024]{1,0:T(8,128)(2,1)S(1)} %get-tuple-element.33.after.grad0.g00), channel_id=1, source_target_pairs={{0,1},{1,0},{2,3},{3,2},{4,5},{5,4},{6,7},{7,6},{8,9},{9,8},{10,11... | collective-permute-start | bytes 393224 | tf_op jit(solution)/shard_map/ppermute | solution.py:267
  45.3 0.4 collective-permute-done.5.part3
  45.7 0.8 activation1.1
  46.5 2.4 %collective-permute-start.14 = (bf16[64,1024]{1,0:T(8,128)(2,1)S(1)}, bf16[64,1024]{1,0:T(8,128)(2,1)S(1)}, u32[]{:S(2)}, u32[]{:S(2)}) collective-permute-start(bf16[64,1024]{1,0:T(8,128)(2,1)S(1)} %get-tuple-element.34.grad0.g10), channel_id=1, source_target_pairs={{0,3},{1,2},{2,1},{3,0},{4,7},{5,6},{6,5},{7,4},{8,11},{9,10},{10,... | collective-permute-start | bytes 393224 | tf_op jit(solution)/shard_map/ppermute | solution.py:267
  48.9 2.4 %collective-permute-done.11.grad3.g03 = bf16[64,1024]{1,0:T(8,128)(2,1)S(1)} collective-permute-done((bf16[64,1024]{1,0:T(8,128)(2,1)S(1)}, bf16[64,1024]{1,0:T(8,128)(2,1)S(1)}, u32[]{:S(2)}, u32[]{:S(2)}) %collective-permute-start.11) | collective-permute-done | bytes 131104 | tf_op jit(solution)/shard_map/ppermute | solution.py:267
  51.3 2.5 %collective-permute-start.12 = (bf16[64,1024]{1,0:T(8,128)(2,1)S(1)}, bf16[64,1024]{1,0:T(8,128)(2,1)S(1)}, u32[]{:S(2)}, u32[]{:S(2)}) collective-permute-start(bf16[64,1024]{1,0:T(8,128)(2,1)S(1)} %get-tuple-element.34.grad0.g10), channel_id=1, source_target_pairs={{0,1},{1,0},{2,3},{3,2},{4,5},{5,4},{6,7},{7,6},{8,9},{9,8},{10,11... | collective-permute-start | bytes 393224 | tf_op jit(solution)/shard_map/ppermute | solution.py:267
  53.8 2.1 %weight_grad0.1.held = f32[1792,256]{1,0:T(8,128)S(1)} custom-call(s32[27,16]{1,0:T(8,128)S(1)} %copy.11.neighbour, bf16[64,2048]{1,0:T(8,128)(2,1)S(1)} %copy-done.3, bf16[32,64,128]{2,1,0:T(8,128)(2,1)S(1)} %all-to-all-done.incoming, bf16[64,1024]{1,0:T(8,128)(2,1)S(1)} %get-tuple-element.33.after.grad0.g00, ...), custom_call_target="tpu_custom_call" | custom-call | flops 939524096 | bytes 4194304 | tf_op jit(solution)/shard_map/weight_grad0/pallas_call | solution.py:326
  55.9 1.0 collective-permute-done.14.grad3.g13
  56.9 2.2 %weight_grad1.1 = (f32[14,4,32,128]{3,2,1,0:T(8,128)S(1)}, bf16[14,4,32,128]{3,2,1,0:T(8,128)(2,1)S(1)}) custom-call(s32[1]{0:T(128)} %bitcast.1.core, s32[27,16]{1,0:T(8,128)S(1)} %copy.11.neighbour, bf16[64,2048]{1,0:T(8,128)(2,1)S(1)} %copy-done.3, bf16[32,64,128]{2,1,0:T(8,128)(2,1)S(1)} %all-to-all-done.incoming, ...), custom_call_target="tpu_custom_call" | custom-call | flops 939524096 | bytes 4194304 | tf_op jit(solution)/shard_map/weight_grad1/pallas_call | solution.py:336
  59.2 6.2 %collective-permute-start.15 = (bf16[14,4,32,128]{3,2,1,0:T(8,128)(2,1)S(1)}, bf16[14,4,32,128]{3,2,1,0:T(8,128)(2,1)S(1)}, u32[]{:S(2)}, u32[]{:S(2)}) collective-permute-start(bf16[14,4,32,128]{3,2,1,0:T(8,128)(2,1)S(1)} %get-tuple-element.36), channel_id=1, source_target_pairs={{0,4},{4,0},{8,12},{12,8},{16,20},{20,16},{24,28},{28,24},{32,36},... | collective-permute-start | bytes 1376264 | tf_op jit(solution)/shard_map/ppermute | solution.py:272
  65.3 1.4 %collective-permute-done.15.arrived = bf16[14,4,32,128]{3,2,1,0:T(8,128)(2,1)S(1)} collective-permute-done((bf16[14,4,32,128]{3,2,1,0:T(8,128)(2,1)S(1)}, bf16[14,4,32,128]{3,2,1,0:T(8,128)(2,1)S(1)}, u32[]{:S(2)}, u32[]{:S(2)}) %collective-permute-start.15) | collective-permute-done | bytes 458784 | tf_op jit(solution)/shard_map/ppermute | solution.py:272
  66.8 0.9 pair_sum.1.after
  67.7 9.6 %all-to-all-start.1 = ((bf16[64,32,128]{2,1,0:T(8,128)(2,1)}), bf16[64,32,128]{2,1,0:T(8,128)(2,1)S(1)}, u32[]{:S(2)}, u32[]{:S(2)}) async-start(bf16[64,32,128]{2,1,0:T(8,128)(2,1)} %bitcast.2), calls=%async_computation.1 | async-start | bytes 1048576 | tf_op jit(solution)/shard_map/all_to_all | solution.py:351
  77.3 0.3 join.1.weight_t
  77.6 5.8 %table_grad.1 = (f32[64,2048]{1,0:T(8,128)S(1)}, bf16[16,64,128]{2,1,0:T(8,128)(2,1)S(1)}, bf16[16,64,128]{2,1,0:T(8,128)(2,1)S(1)}) custom-call(s32[1]{0:T(128)} %bitcast.1.core, s32[27,16]{1,0:T(8,128)S(1)} %copy.11.neighbour, bf16[1792,256]{1,0:T(8,128)(2,1)S(1)} %join.1.weight_t, bf16[64,1024]{1,0:T(8,128)(2,1)S(1)} %get-tuple-element.33.after.grad0.g00, ...), custom_call_target="tpu_custom_call" | custom-call | flops 1879048192 | bytes 4194304 | tf_op jit(solution)/shard_map/table_grad/pallas_call | solution.py:361
  83.4 0.7 collective-permute-start.16
  84.1 1.2 %collective-permute-done.16.away = bf16[16,64,128]{2,1,0:T(8,128)(2,1)S(1)} collective-permute-done((bf16[16,64,128]{2,1,0:T(8,128)(2,1)S(1)}, bf16[16,64,128]{2,1,0:T(8,128)(2,1)S(1)}, u32[]{:S(2)}, u32[]{:S(2)}) %collective-permute-start.16) | collective-permute-done | bytes 262176 | tf_op jit(solution)/shard_map/ppermute | solution.py:272
  85.3 4.2 %all-to-all-done.1 = bf16[64,32,128]{2,1,0:T(8,128)(2,1)S(1)} async-done(((bf16[64,32,128]{2,1,0:T(8,128)(2,1)}), bf16[64,32,128]{2,1,0:T(8,128)(2,1)S(1)}, u32[]{:S(2)}, u32[]{:S(2)}) %all-to-all-start.1) | async-done | bytes 524320 | tf_op jit(solution)/shard_map/all_to_all | solution.py:351
  89.5 0.2 sum_parts.1
  89.7 18.3 %all_to_all.15.mixed.mine = bf16[16,8,32,128]{3,2,1,0:T(8,128)(2,1)S(1)} all-to-all(bf16[16,8,32,128]{3,2,1,0:T(8,128)(2,1)S(1)} %sum_parts.1), channel_id=1, replica_groups={{0,8,16,24,32,40,48,56,64,72,80,88,96,104,112,120},{4,12,20,28,36,44,52..., dimensions={0} | all-to-all | bytes 2097152 | tf_op jit(solution)/shard_map/all_to_all | solution.py:381
  108.0 2.9 %collective-permute-start.17 = (bf16[16,8,32,128]{3,2,1,0:T(8,128)(2,1)S(1)}, bf16[16,8,32,128]{3,2,1,0:T(8,128)(2,1)S(1)}, u32[]{:S(2)}, u32[]{:S(2)}) collective-permute-start(bf16[16,8,32,128]{3,2,1,0:T(8,128)(2,1)S(1)} %all_to_all.15.mixed.mine), channel_id=1, source_target_pairs={{0,4},{4,0},{8,12},{12,8},{16,20},{20,16},{24,28},{28,24},{32,36},... | collective-permute-start | bytes 3145736 | tf_op jit(solution)/shard_map/ppermute | solution.py:272
  110.9 1.6 %return_add.1 = f32[64,2048]{1,0:T(8,128)} custom-call(s32[1]{0:T(128)} %bitcast.1.core, s32[1,32]{1,0:T(1,128)S(1)} %copy-done.6, s32[1,32]{1,0:T(1,128)S(1)} %copy-done.8, f32[64,2048]{1,0:T(8,128)S(1)} %get-tuple-element.37.local, bf16[16,8,32,128]{3,2,1,0:T(8,128)(2,1)S(1)} %all_to_all.15.mixed.mine), custom_call_target="tpu_custom_call" | custom-call | bytes 2097152 | tf_op jit(solution)/shard_map/return_add/pallas_call | solution.py:382
  112.5 0.6 collective-permute-done.17.other
  113.2 1.3 %unpack.1 = (f32[27,64,256]{2,1,0:T(8,128)}, f32[64,256]{1,0:T(8,128)}) custom-call(s32[1]{0:T(128)} %bitcast.1.core, bf16[16,8,32,128]{3,2,1,0:T(8,128)(2,1)S(1)} %all_to_all.15.mixed.mine, bf16[16,8,32,128]{3,2,1,0:T(8,128)(2,1)S(1)} %collective-permute-done.17.other), custom_call_target="tpu_custom_call" | custom-call | bytes 3145728 | tf_op jit(solution)/shard_map/unpack/pallas_call | solution.py:385
  (29 shorter events, 0.1 us)
Async XLA Ops:
  0.6 12.4 %copy-start.1 = (bf16[27,64,256]{2,1,0:T(8,128)(2,1)S(1)}, bf16[27,64,256]{2,1,0:T(8,128)(2,1)}, u32[]{:S(2)}) copy-start(bf16[27,64,256]{2,1,0:T(8,128)(2,1)} %conv_weight.1) | copy-start | bytes 2654212
  0.6 1.0 copy-start.2
  1.7 0.7 copy-start.5
  2.3 0.7 copy-start.7
  3.0 10.1 %copy-start.4 = (bf16[64,256]{1,0:T(8,128)(2,1)S(1)}, bf16[64,256]{1,0:T(8,128)(2,1)}, u32[]{:S(2)}) copy-start(bf16[64,256]{1,0:T(8,128)(2,1)} %coarse_weight.1) | copy-start | bytes 98308
  4.5 24.0 %all-to-all-start = ((bf16[32,64,128]{2,1,0:T(8,128)(2,1)}), bf16[32,64,128]{2,1,0:T(8,128)(2,1)S(1)}, u32[]{:S(2)}, u32[]{:S(2)}) async-start(bf16[32,64,128]{2,1,0:T(8,128)(2,1)} %pack.1), calls=%async_computation | async-start | bytes 1048576 | tf_op jit(solution)/shard_map/all_to_all | solution.py:293
  13.1 4.9 %copy-start.9 = (s32[27,16]{0,1:T(8,128)S(1)}, s32[27,16]{0,1:T(8,128)}, u32[]{:S(2)}) copy-start(s32[27,16]{0,1:T(8,128)} %param.13) | copy-start | bytes 5188
  13.1 15.4 %copy-start.3 = (bf16[64,2048]{1,0:T(8,128)(2,1)S(1)}, bf16[64,2048]{1,0:T(8,128)(2,1)}, u32[]{:S(2)}) copy-start(bf16[64,2048]{1,0:T(8,128)(2,1)} %features.9) | copy-start | bytes 786436
  13.5 14.6 %collective-permute-start.2 = (bf16[14,64,128]{2,1,0:T(8,128)(2,1)S(1)}, bf16[14,64,128]{2,1,0:T(8,128)(2,1)S(1)}, u32[]{:S(2)}, u32[]{:S(2)}) collective-permute-start(bf16[14,64,128]{2,1,0:T(8,128)(2,1)S(1)} %get-tuple-element.42), channel_id=1, source_target_pairs={{0,3},{1,2},{2,1},{3,0},{4,7},{5,6},{6,5},{7,4},{8,11},{9,10},{10,... | collective-permute-start | bytes 688136 | tf_op jit(solution)/shard_map/ppermute | solution.py:267
  17.4 10.7 %collective-permute-start.1 = (bf16[14,64,128]{2,1,0:T(8,128)(2,1)S(1)}, bf16[14,64,128]{2,1,0:T(8,128)(2,1)S(1)}, u32[]{:S(2)}, u32[]{:S(2)}) collective-permute-start(bf16[14,64,128]{2,1,0:T(8,128)(2,1)S(1)} %get-tuple-element.43), channel_id=1, source_target_pairs={{0,2},{1,3},{2,0},{3,1},{4,6},{5,7},{6,4},{7,5},{8,10},{9,11},{10,... | collective-permute-start | bytes 688136 | tf_op jit(solution)/shard_map/ppermute | solution.py:267
  17.4 11.1 %collective-permute-start = (bf16[14,64,128]{2,1,0:T(8,128)(2,1)S(1)}, bf16[14,64,128]{2,1,0:T(8,128)(2,1)S(1)}, u32[]{:S(2)}, u32[]{:S(2)}) collective-permute-start(bf16[14,64,128]{2,1,0:T(8,128)(2,1)S(1)} %get-tuple-element.44), channel_id=1, source_target_pairs={{0,1},{1,0},{2,3},{3,2},{4,5},{5,4},{6,7},{7,6},{8,9},{9,8},{10,11... | collective-permute-start | bytes 688136 | tf_op jit(solution)/shard_map/ppermute | solution.py:267
  30.8 11.0 %copy-start = (bf16[64,2048]{1,0:T(8,128)(2,1)S(1)}, bf16[64,2048]{1,0:T(8,128)(2,1)}, u32[]{:S(2)}) copy-start(bf16[64,2048]{1,0:T(8,128)(2,1)} %out_grad.3) | copy-start | bytes 786436
  30.8 9.7 %collective-permute-start.6 = (bf16[64,1024]{1,0:T(8,128)(2,1)S(1)}, bf16[64,1024]{1,0:T(8,128)(2,1)S(1)}, u32[]{:S(2)}, u32[]{:S(2)}) collective-permute-start(bf16[64,1024]{1,0:T(8,128)(2,1)S(1)} %get-tuple-element.28), channel_id=1, source_target_pairs={{0,1},{1,0},{2,3},{3,2},{4,5},{5,4},{6,7},{7,6},{8,9},{9,8},{10,11... | collective-permute-start | bytes 393224 | tf_op jit(solution)/shard_map/ppermute | solution.py:267
  31.7 9.3 %collective-permute-start.7 = (bf16[64,1024]{1,0:T(8,128)(2,1)S(1)}, bf16[64,1024]{1,0:T(8,128)(2,1)S(1)}, u32[]{:S(2)}, u32[]{:S(2)}) collective-permute-start(bf16[64,1024]{1,0:T(8,128)(2,1)S(1)} %get-tuple-element.29), channel_id=1, source_target_pairs={{0,2},{1,3},{2,0},{3,1},{4,6},{5,7},{6,4},{7,5},{8,10},{9,11},{10,... | collective-permute-start | bytes 393224 | tf_op jit(solution)/shard_map/ppermute | solution.py:267
  34.3 7.5 %collective-permute-start.8 = (bf16[64,1024]{1,0:T(8,128)(2,1)S(1)}, bf16[64,1024]{1,0:T(8,128)(2,1)S(1)}, u32[]{:S(2)}, u32[]{:S(2)}) collective-permute-start(bf16[64,1024]{1,0:T(8,128)(2,1)S(1)} %get-tuple-element.30), channel_id=1, source_target_pairs={{0,3},{1,2},{2,1},{3,0},{4,7},{5,6},{6,5},{7,4},{8,11},{9,10},{10,... | collective-permute-start | bytes 393224 | tf_op jit(solution)/shard_map/ppermute | solution.py:267
  37.0 6.5 %collective-permute-start.3 = (bf16[64,1024]{1,0:T(8,128)(2,1)S(1)}, bf16[64,1024]{1,0:T(8,128)(2,1)S(1)}, u32[]{:S(2)}, u32[]{:S(2)}) collective-permute-start(bf16[64,1024]{1,0:T(8,128)(2,1)S(1)} %get-tuple-element.24), channel_id=1, source_target_pairs={{0,1},{1,0},{2,3},{3,2},{4,5},{5,4},{6,7},{7,6},{8,9},{9,8},{10,11... | collective-permute-start | bytes 393224 | tf_op jit(solution)/shard_map/ppermute | solution.py:267
  37.1 8.2 %collective-permute-start.4 = (bf16[64,1024]{1,0:T(8,128)(2,1)S(1)}, bf16[64,1024]{1,0:T(8,128)(2,1)S(1)}, u32[]{:S(2)}, u32[]{:S(2)}) collective-permute-start(bf16[64,1024]{1,0:T(8,128)(2,1)S(1)} %get-tuple-element.25), channel_id=1, source_target_pairs={{0,2},{1,3},{2,0},{3,1},{4,6},{5,7},{6,4},{7,5},{8,10},{9,11},{10,... | collective-permute-start | bytes 393224 | tf_op jit(solution)/shard_map/ppermute | solution.py:267
  40.5 5.2 %collective-permute-start.5 = (bf16[64,1024]{1,0:T(8,128)(2,1)S(1)}, bf16[64,1024]{1,0:T(8,128)(2,1)S(1)}, u32[]{:S(2)}, u32[]{:S(2)}) collective-permute-start(bf16[64,1024]{1,0:T(8,128)(2,1)S(1)} %get-tuple-element.26), channel_id=1, source_target_pairs={{0,3},{1,2},{2,1},{3,0},{4,7},{5,6},{6,5},{7,4},{8,11},{9,10},{10,... | collective-permute-start | bytes 393224 | tf_op jit(solution)/shard_map/ppermute | solution.py:267
  42.0 9.3 %collective-permute-start.11 = (bf16[64,1024]{1,0:T(8,128)(2,1)S(1)}, bf16[64,1024]{1,0:T(8,128)(2,1)S(1)}, u32[]{:S(2)}, u32[]{:S(2)}) collective-permute-start(bf16[64,1024]{1,0:T(8,128)(2,1)S(1)} %get-tuple-element.33.after.grad0.g00), channel_id=1, source_target_pairs={{0,3},{1,2},{2,1},{3,0},{4,7},{5,6},{6,5},{7,4},{8,11},{9,10},{10,... | collective-permute-start | bytes 393224 | tf_op jit(solution)/shard_map/ppermute | solution.py:267
  43.5 10.3 %collective-permute-start.10 = (bf16[64,1024]{1,0:T(8,128)(2,1)S(1)}, bf16[64,1024]{1,0:T(8,128)(2,1)S(1)}, u32[]{:S(2)}, u32[]{:S(2)}) collective-permute-start(bf16[64,1024]{1,0:T(8,128)(2,1)S(1)} %get-tuple-element.33.after.grad0.g00), channel_id=1, source_target_pairs={{0,2},{1,3},{2,0},{3,1},{4,6},{5,7},{6,4},{7,5},{8,10},{9,11},{10,... | collective-permute-start | bytes 393224 | tf_op jit(solution)/shard_map/ppermute | solution.py:267
  43.5 10.3 %collective-permute-start.9 = (bf16[64,1024]{1,0:T(8,128)(2,1)S(1)}, bf16[64,1024]{1,0:T(8,128)(2,1)S(1)}, u32[]{:S(2)}, u32[]{:S(2)}) collective-permute-start(bf16[64,1024]{1,0:T(8,128)(2,1)S(1)} %get-tuple-element.33.after.grad0.g00), channel_id=1, source_target_pairs={{0,1},{1,0},{2,3},{3,2},{4,5},{5,4},{6,7},{7,6},{8,9},{9,8},{10,11... | collective-permute-start | bytes 393224 | tf_op jit(solution)/shard_map/ppermute | solution.py:267
  46.5 10.4 %collective-permute-start.14 = (bf16[64,1024]{1,0:T(8,128)(2,1)S(1)}, bf16[64,1024]{1,0:T(8,128)(2,1)S(1)}, u32[]{:S(2)}, u32[]{:S(2)}) collective-permute-start(bf16[64,1024]{1,0:T(8,128)(2,1)S(1)} %get-tuple-element.34.grad0.g10), channel_id=1, source_target_pairs={{0,3},{1,2},{2,1},{3,0},{4,7},{5,6},{6,5},{7,4},{8,11},{9,10},{10,... | collective-permute-start | bytes 393224 | tf_op jit(solution)/shard_map/ppermute | solution.py:267
  48.9 8.0 %collective-permute-start.13 = (bf16[64,1024]{1,0:T(8,128)(2,1)S(1)}, bf16[64,1024]{1,0:T(8,128)(2,1)S(1)}, u32[]{:S(2)}, u32[]{:S(2)}) collective-permute-start(bf16[64,1024]{1,0:T(8,128)(2,1)S(1)} %get-tuple-element.34.grad0.g10), channel_id=1, source_target_pairs={{0,2},{1,3},{2,0},{3,1},{4,6},{5,7},{6,4},{7,5},{8,10},{9,11},{10,... | collective-permute-start | bytes 393224 | tf_op jit(solution)/shard_map/ppermute | solution.py:267
  51.3 5.6 %collective-permute-start.12 = (bf16[64,1024]{1,0:T(8,128)(2,1)S(1)}, bf16[64,1024]{1,0:T(8,128)(2,1)S(1)}, u32[]{:S(2)}, u32[]{:S(2)}) collective-permute-start(bf16[64,1024]{1,0:T(8,128)(2,1)S(1)} %get-tuple-element.34.grad0.g10), channel_id=1, source_target_pairs={{0,1},{1,0},{2,3},{3,2},{4,5},{5,4},{6,7},{7,6},{8,9},{9,8},{10,11... | collective-permute-start | bytes 393224 | tf_op jit(solution)/shard_map/ppermute | solution.py:267
  59.2 7.6 %collective-permute-start.15 = (bf16[14,4,32,128]{3,2,1,0:T(8,128)(2,1)S(1)}, bf16[14,4,32,128]{3,2,1,0:T(8,128)(2,1)S(1)}, u32[]{:S(2)}, u32[]{:S(2)}) collective-permute-start(bf16[14,4,32,128]{3,2,1,0:T(8,128)(2,1)S(1)} %get-tuple-element.36), channel_id=1, source_target_pairs={{0,4},{4,0},{8,12},{12,8},{16,20},{20,16},{24,28},{28,24},{32,36},... | collective-permute-start | bytes 1376264 | tf_op jit(solution)/shard_map/ppermute | solution.py:272
  67.7 21.9 %all-to-all-start.1 = ((bf16[64,32,128]{2,1,0:T(8,128)(2,1)}), bf16[64,32,128]{2,1,0:T(8,128)(2,1)S(1)}, u32[]{:S(2)}, u32[]{:S(2)}) async-start(bf16[64,32,128]{2,1,0:T(8,128)(2,1)} %bitcast.2), calls=%async_computation.1 | async-start | bytes 1048576 | tf_op jit(solution)/shard_map/all_to_all | solution.py:351
  83.4 1.9 %collective-permute-start.16 = (bf16[16,64,128]{2,1,0:T(8,128)(2,1)S(1)}, bf16[16,64,128]{2,1,0:T(8,128)(2,1)S(1)}, u32[]{:S(2)}, u32[]{:S(2)}) collective-permute-start(bf16[16,64,128]{2,1,0:T(8,128)(2,1)S(1)} %get-tuple-element.39), channel_id=1, source_target_pairs={{0,4},{4,0},{8,12},{12,8},{16,20},{20,16},{24,28},{28,24},{32,36},... | collective-permute-start | bytes 786440 | tf_op jit(solution)/shard_map/ppermute | solution.py:272
  89.5 21.4 %copy-start.6 = (s32[1,32]{1,0:T(1,128)S(1)}, s32[1,32]{1,0:T(1,128)}, u32[]{:S(2)}) copy-start(s32[1,32]{1,0:T(1,128)} %send_block.3) | copy-start | bytes 388
  89.5 21.4 %copy-start.8 = (s32[1,32]{1,0:T(1,128)S(1)}, s32[1,32]{1,0:T(1,128)}, u32[]{:S(2)}) copy-start(s32[1,32]{1,0:T(1,128)} %send_count.3) | copy-start | bytes 388
  108.0 5.2 %collective-permute-start.17 = (bf16[16,8,32,128]{3,2,1,0:T(8,128)(2,1)S(1)}, bf16[16,8,32,128]{3,2,1,0:T(8,128)(2,1)S(1)}, u32[]{:S(2)}, u32[]{:S(2)}) collective-permute-start(bf16[16,8,32,128]{3,2,1,0:T(8,128)(2,1)S(1)} %all_to_all.15.mixed.mine), channel_id=1, source_target_pairs={{0,4},{4,0},{8,12},{12,8},{16,20},{20,16},{24,28},{28,24},{32,36},... | collective-permute-start | bytes 3145736 | tf_op jit(solution)/shard_map/ppermute | solution.py:272

commit v8 on v7

--- a/solution.py
+++ b/solution.py
@@ -11,12 +11,13 @@
 TERMS = 28
 PAIRS = TERMS // 2
 BLOCK = 128
+CUTS = (0, 8, 16)
 BF = jnp.bfloat16
 F32 = jnp.float32
 
 
 def call(kernel, name, outs, kinds, scratch=(), flops=0, size=0, limit=24 << 20):
-    space = {"s": pltpu.SMEM, "v": pltpu.VMEM, "a": pl.ANY}
+    space = {"s": pltpu.SMEM, "v": pltpu.VMEM, "a": pl.ANY, "h": pltpu.HBM}
     many = isinstance(outs, (list, tuple))
     spec = pl.BlockSpec(memory_space=pltpu.VMEM)
     return pl.pallas_call(
@@ -41,30 +42,60 @@
     return pl.ds(pl.multiple_of(index * BLOCK, BLOCK), BLOCK)
 
 
-def pack_kernel(send_block, send_count, features, outgoing):
+def pack_kernel(block_hbm, count_hbm, features_hbm, outgoing, send_block, send_count, features, sems):
+    copies = [
+        pltpu.make_async_copy(block_hbm, send_block, sems.at[0]),
+        pltpu.make_async_copy(count_hbm, send_count, sems.at[1]),
+        pltpu.make_async_copy(features_hbm, features, sems.at[2]),
+    ]
+    for copy in copies:
+        copy.start()
+    for copy in copies:
+        copy.wait()
     for peer in range(outgoing.shape[0]):
         block = features[:, columns(send_block[0, peer])]
         outgoing[peer] = block * send_count[0, peer].astype(F32).astype(BF)
 
 
-def split_kernel(place, conv_weight, coarse_weight, pieces):
+def split_kernel(place, core, conv_weight, coarse_weight, own, sent1, sent2, sent3):
     quarter = conv_weight.shape[1]
-    for pair in range(PAIRS):
+    cuts = [slice(t * quarter, (t + 1) * quarter) for t in range(4)]
+
+    def tiles_of(pair):
         first = conv_weight[2 * pair]
         second = conv_weight[2 * pair + 1] if 2 * pair + 1 < OFFSETS else coarse_weight[...]
-        cuts = [slice(t * quarter, (t + 1) * quarter) for t in range(4)]
-        tiles = [jnp.concatenate([first[:, c], second[:, c]], axis=1) for c in cuts]
-        for step in range(4):
-            target = place[0] ^ step
-            low = jnp.where(target == 0, tiles[0], tiles[1])
-            high = jnp.where(target == 2, tiles[2], tiles[3])
-            pieces[step * PAIRS + pair] = jnp.where(target < 2, low, high)
-
-
-def join_kernel(piece0, piece1, piece2, piece3, after, flipped):
-    del after
+        return [jnp.concatenate([first[:, c], second[:, c]], axis=1) for c in cuts]
+
+    def pick(tiles, target):
+        low = jnp.where(target == 0, tiles[0], tiles[1])
+        high = jnp.where(target == 2, tiles[2], tiles[3])
+        return jnp.where(target < 2, low, high)
+
+    half = PAIRS // 2
+    for pair in range(half):
+        low, high = tiles_of(pair), tiles_of(pair + half)
+        own[pair] = pick(low, place[0])
+        own[pair + half] = pick(high, place[0])
+        mine = [jnp.where(core[0] == 0, a, b) for a, b in zip(low, high)]
+        for step, sent in enumerate((sent1, sent2, sent3)):
+            sent[pair] = pick(mine, place[0] ^ (step + 1))
+
+
+def weight_tiles(place, core, pieces, pair):
+    half = PAIRS // 2
+    local = core[0] == pair // half
+    own = pieces[0][pair]
+    first, second, third = (
+        jnp.where(local, pieces[s][pair % half], pieces[s + 3][pair % half]) for s in (1, 2, 3)
+    )
+    odd = place[0] % 2 == 1
+    return own, jnp.where(odd, first, third), second, jnp.where(odd, third, first)
+
+
+def join_kernel(place, core, *refs):
+    flipped = refs[-1]
     for pair in range(PAIRS):
-        tile = jnp.concatenate([p[pair] for p in (piece0, piece1, piece2, piece3)], axis=0)
+        tile = jnp.concatenate(weight_tiles(place, core, refs[:7], pair), axis=0)
         flipped[pair * BLOCK : (pair + 1) * BLOCK, :] = tile.T
 
 
@@ -98,18 +129,18 @@
         gathered[OFFSETS * quarter :, block * BLOCK : (block + 1) * BLOCK] = pooled
 
 
-def forward_kernel(half, neighbour, features, incoming, *refs):
-    pieces, outs, (weight, table, gathered) = refs[:4], refs[4:8], refs[8:]
+def forward_kernel(first, place, core, neighbour, features, incoming, *refs):
+    pieces, outs, (weight, table, gathered) = refs[:7], refs[7:11], refs[11:]
     quarter, row_count = features.shape
     nblocks = row_count // BLOCK
     extent = nblocks + incoming.shape[0]
-    for step, piece in enumerate(pieces):
-        for pair in range(PAIRS):
+    for pair in range(PAIRS):
+        for step, tile in enumerate(weight_tiles(place, core, pieces, pair)):
             rows = slice(step * quarter, (step + 1) * quarter)
-            weight[rows, pair * BLOCK : (pair + 1) * BLOCK] = piece[pair]
+            weight[rows, pair * BLOCK : (pair + 1) * BLOCK] = tile
     fill_table(features, incoming, table, nblocks)
-    fill_gathered(neighbour, table, gathered, half * nblocks // 2, extent)
-    for tile in range(row_count // 512):
+    fill_gathered(neighbour, table, gathered, first, extent)
+    for tile in range(gathered.shape[1] // 256):
         cut = slice(tile * 256, (tile + 1) * 256)
         total = jnp.dot(weight[...], gathered[:, cut], preferred_element_type=F32)
         for step, out in enumerate(outs):
@@ -123,42 +154,54 @@
     return (pre * sigma).astype(BF), grad.astype(BF)
 
 
-def activation_kernel(own, part1, part2, part3, out_grad, output, grad):
-    middle = own.shape[1]
-    output[...], grad[...] = activate(own, part1, part2, part3, out_grad[:, :middle])
-
-
-def activation_end_kernel(own, part1, part2, part3, out_grad, before, output, grad):
-    middle = own.shape[1]
-    output[:, :middle] = before[...]
-    output[:, middle:], grad[...] = activate(own, part1, part2, part3, out_grad[:, middle:])
-
-
-def prepare_weight(half, neighbour, features, incoming, grads, table, gathered, flipped):
+def activation_kernel(first, own, part1, part2, part3, out_grad, output, grad):
+    cut = slice(first * BLOCK, first * BLOCK + own.shape[1])
+    output[...], grad[...] = activate(own, part1, part2, part3, out_grad[:, cut])
+
+
+def activation_end_kernel(first, own, part1, part2, part3, out_grad, *refs):
+    output, grad = refs[-2:]
+    start = 0
+    for before in refs[:-2]:
+        output[:, start : start + before.shape[1]] = before[...]
+        start += before.shape[1]
+    cut = slice(first * BLOCK, first * BLOCK + own.shape[1])
+    output[:, cut], grad[...] = activate(own, part1, part2, part3, out_grad[:, cut])
+
+
+def prepare_weight(first, neighbour, features, incoming, grads, table, gathered, flipped):
     nblocks = features.shape[1] // BLOCK
     extent = nblocks + incoming.shape[0]
     fill_table(features, incoming, table, nblocks)
-    fill_gathered(neighbour, table, gathered, half * nblocks // 2, extent)
-    for block in range(nblocks // 2):
+    fill_gathered(neighbour, table, gathered, first, extent)
+    for block in range(gathered.shape[1] // BLOCK):
         cut = slice(block * BLOCK, (block + 1) * BLOCK)
         tall = jnp.concatenate([g[:, cut] for g in grads], axis=0)
         flipped[cut, :] = tall.T
 
 
 def weight_first_kernel(
-    neighbour, features, incoming, grad0, grad1, grad2, grad3, held, table, gathered, flipped
+    first, neighbour, features, incoming, grad0, grad1, grad2, grad3, held, table, gathered, flipped
 ):
     grads = (grad0, grad1, grad2, grad3)
-    prepare_weight(0, neighbour, features, incoming, grads, table, gathered, flipped)
+    prepare_weight(first, neighbour, features, incoming, grads, table, gathered, flipped)
     held[...] = jnp.dot(gathered[...], flipped[...], preferred_element_type=F32)
 
 
-def weight_second_kernel(
-    core, neighbour, features, incoming, grad0, grad1, grad2, grad3, held, keep, give, table, gathered, flipped
+def weight_more_kernel(
+    first, neighbour, features, incoming, grad0, grad1, grad2, grad3, held, more, table, gathered, flipped
+):
+    grads = (grad0, grad1, grad2, grad3)
+    prepare_weight(first, neighbour, features, incoming, grads, table, gathered, flipped)
+    more[...] = held[...] + jnp.dot(gathered[...], flipped[...], preferred_element_type=F32)
+
+
+def weight_last_kernel(
+    first, core, neighbour, features, incoming, grad0, grad1, grad2, grad3, held, keep, give, table, gathered, flipped
 ):
     quarter = features.shape[0]
     grads = (grad0, grad1, grad2, grad3)
-    prepare_weight(1, neighbour, features, incoming, grads, table, gathered, flipped)
+    prepare_weight(first, neighbour, features, incoming, grads, table, gathered, flipped)
     half = quarter // 2
     for pair in range(PAIRS):
         rows = slice(pair * BLOCK, (pair + 1) * BLOCK)
@@ -173,26 +216,27 @@
 
 def pair_kernel(place, keep, arrived, parts):
     for step in range(4):
-        target = place[0] ^ step
+        target = lax.rem(place[0] - step + 4, 4)
         for pair in range(PAIRS):
             parts[pair, target] = (keep[pair, step] + arrived[pair, step].astype(F32)).astype(BF)
     for spare in range(PAIRS, parts.shape[0]):
         parts[spare] = jnp.zeros(parts.shape[1:], BF)
 
 
-def table_kernel(
-    core, neighbour, weight_t, g00, g01, g02, g03, g10, g11, g12, g13, after, local, home, away, total, spread
-):
-    del after
+def table_kernel(core, neighbour, weight_t, *refs):
+    local, home, away, total, spread = refs[-5:]
+    grads = refs[: 4 * (len(CUTS) - 1)]
     quarter, row_count = local.shape
     nblocks = row_count // BLOCK
     extent = total.shape[0] - 1
     total[...] = jnp.zeros_like(total)
     mean = mean_matrix()
     for tile in range(nblocks // 2):
-        grads = (g00, g01, g02, g03) if tile < nblocks // 4 else (g10, g11, g12, g13)
-        start = tile % (nblocks // 4) * 256
-        tall = jnp.concatenate([g[:, start : start + 256] for g in grads], axis=0)
+        part = sum(2 * tile >= cut for cut in CUTS[1:])
+        start = (2 * tile - CUTS[part]) * BLOCK
+        tall = jnp.concatenate(
+            [g[:, start : start + 256] for g in grads[4 * part : 4 * part + 4]], axis=0
+        )
         product = jnp.dot(weight_t[...], tall, preferred_element_type=F32)
         spread[...] = product[: OFFSETS * quarter]
 
@@ -262,6 +306,11 @@
                     coarse_grad[rows, cut] = value
 
 
+def shift(value, step):
+    size = lax.axis_size("chan")
+    return lax.ppermute(value, "chan", [(i, (i + step) % size) for i in range(size)])
+
+
 def exchange(value, step):
     size = lax.axis_size("chan")
     return lax.ppermute(value, "chan", [(i, i ^ step) for i in range(size)])
@@ -284,64 +333,78 @@
     core = (lax.axis_index("morton") % 2).astype(jnp.int32).reshape(1)
     shape = jax.ShapeDtypeStruct
 
-    pieces = call(
-        split_kernel, "split", shape((4 * PAIRS, quarter, BLOCK), BF), "svv", size=2 << 20
-    )(place, conv_weight, coarse_weight)
     outgoing = call(
-        pack_kernel, "pack", shape((n_morton, quarter, BLOCK), BF), "ssv", size=1 << 20
+        pack_kernel, "pack", shape((n_morton, quarter, BLOCK), BF), "hhh",
+        [
+            pltpu.SMEM((1, n_morton), jnp.int32),
+            pltpu.SMEM((1, n_morton), jnp.int32),
+            pltpu.VMEM((quarter, row_count), BF),
+            pltpu.SemaphoreType.DMA((3,)),
+        ],
+        size=1 << 20,
+        limit=60 << 20,
     )(send_block, send_count, features)
     incoming = lax.all_to_all(outgoing, "morton", 0, 0, tiled=True)
 
-    pieces = pieces.reshape(4, PAIRS, quarter, BLOCK)
-    weights = [pieces[0]] + [exchange(pieces[s], s) for s in (1, 2, 3)]
-    middle = row_count // 2
-    big = [pltpu.VMEM((extent + 1, quarter, BLOCK), BF), pltpu.VMEM((depth, middle), BF)]
-    turned = [pltpu.VMEM((middle, channels), BF)]
-    wide, part = (quarter, row_count), (quarter, middle)
-    grads = []
-    output = ()
-    for half in range(2):
+    half_piece = shape((PAIRS // 2, quarter, BLOCK), BF)
+    own_piece, *sent = call(
+        split_kernel,
+        "split",
+        [shape((PAIRS, quarter, BLOCK), BF)] + [half_piece] * 3,
+        "ssvv",
+        size=2 << 20,
+    )(place, core, conv_weight, coarse_weight)
+    came = [exchange(value, step) for step, value in zip((1, 2, 3), sent)]
+    weights = [own_piece] + came + [swap_cores(value) for value in came]
+
+    table = pltpu.VMEM((extent + 1, quarter, BLOCK), BF)
+    wide, piece = (quarter, row_count), (4, quarter // 2, BLOCK)
+    grads, outputs = [], []
+    for first, end in zip(CUTS, CUTS[1:]):
+        width = (end - first) * BLOCK
+        part = (quarter, width)
         partial = call(
-            functools.partial(forward_kernel, half),
-            f"forward{half}",
+            functools.partial(forward_kernel, first),
+            f"forward{first}",
             [shape(part, F32)] + [shape(part, BF)] * 3,
-            "svvvvvv",
-            [pltpu.VMEM((channels, depth), BF)] + big,
-            flops // 2,
+            "sss" + "v" * 9,
+            [pltpu.VMEM((channels, depth), BF), table, pltpu.VMEM((depth, width), BF)],
+            flops * width // row_count,
             3 << 20,
-        )(neighbour, features, incoming, *weights)
-        arrived = [exchange(partial[s], s) for s in (1, 2, 3)]
+        )(place, core, neighbour, features, incoming, *weights)
+        arrived = [shift(partial[s], -s) for s in (1, 2, 3)]
+        last = end == CUTS[-1]
         output, grad = call(
-            activation_end_kernel if half else activation_kernel,
-            f"activation{half}",
-            [shape(wide if half else part, BF), shape(part, BF)],
-            "vvvvvv" if half else "vvvvv",
+            functools.partial(activation_end_kernel if last else activation_kernel, first),
+            f"activation{first}",
+            [shape(wide if last else part, BF), shape(part, BF)],
+            "vvvvv" + "v" * (len(outputs) if last else 0),
             size=1 << 20,
-        )(partial[0], *arrived, out_grad, *((output,) if half else ()))
-        grads.append([grad] + [exchange(grad, s) for s in (1, 2, 3)])
-
-    weight_t = call(join_kernel, "join", shape((depth, channels), BF), "vvvva", size=3 << 20)(
-        *weights, grads[0][0]
-    )
-    held = call(
-        weight_first_kernel,
-        "weight_grad0",
-        shape((depth, channels), F32),
-        "svvvvvv",
-        big + turned,
-        flops // 2,
-        4 << 20,
-    )(neighbour, features, incoming, *grads[0])
-    piece = (4, quarter // 2, BLOCK)
-    keep, give = call(
-        weight_second_kernel,
-        "weight_grad1",
-        [shape((PAIRS,) + piece, F32), shape((PAIRS,) + piece, BF)],
-        "ssvvvvvvv",
-        big + turned,
-        flops // 2,
-        4 << 20,
-    )(core, neighbour, features, incoming, *grads[1], held)
+        )(partial[0], *arrived, out_grad, *(outputs if last else ()))
+        outputs.append(output)
+        grads.append([grad] + [shift(grad, s) for s in (1, 2, 3)])
+
+    weight_t = call(join_kernel, "join", shape((depth, channels), BF), "ss" + "v" * 7 + "a", size=3 << 20)(
+        place, core, *weights, grads[0][0]
+    )
+    held = ()
+    for (first, end), given in zip(zip(CUTS, CUTS[1:]), grads):
+        width = (end - first) * BLOCK
+        last = end == CUTS[-1]
+        kernel = weight_last_kernel if last else weight_more_kernel if held else weight_first_kernel
+        sums = [shape((PAIRS,) + piece, F32), shape((PAIRS,) + piece, BF)]
+        result = call(
+            functools.partial(kernel, first),
+            f"weight_grad{first}",
+            sums if last else shape((depth, channels), F32),
+            "s" * (1 + last) + "v" * (6 + len(held)),
+            [table, pltpu.VMEM((depth, width), BF), pltpu.VMEM((width, channels), BF)],
+            flops * width // row_count,
+            4 << 20,
+        )(*((core,) if last else ()), neighbour, features, incoming, *given, *held)
+        held = (result,)
+    keep, give = result
+    output = outputs[-1]
     chips = n_morton // 2
     parts = call(pair_kernel, "pair_sum", shape((chips,) + piece, BF), "svv", size=3 << 20)(
         place, keep, swap_cores(give)
@@ -362,14 +425,14 @@
         table_kernel,
         "table_grad",
         [shape(wide, F32), shape(blocks, BF), shape(blocks, BF)],
-        "ss" + "v" * 9 + "a",
+        "ssv" + "v" * 4 * len(grads) + "a",
         [
             pltpu.VMEM((extent + 1, quarter, BLOCK), F32),
             pltpu.VMEM((OFFSETS * quarter, 256), F32),
         ],
         flops,
         4 << 20,
-    )(core, neighbour, weight_t, *grads[0], *grads[1], parts)
+    )(core, neighbour, weight_t, *(g for given in grads for g in given), parts)
     scale = float(row_count * n_morton) ** (-0.5)
     mixed = call(
         functools.partial(sum_kernel, scale),

time: 115 us -> 109 us (0.948)
  starting transfers between devices: 48.6 us -> 44 us
  local copies, waits for them, and re-layouts: 2.54 us -> 0.12 us
    ppermute x15 -> x3, starting transfers between devices: 20.6 us -> 5.02 us  [exchange(): return lax.ppermute(value, 'chan', [(i, i ^ step) for i in range(size)])]
    ppermute x0 -> x12, starting transfers between devices: none -> 10.9 us  [shift(): lax.ppermute(value, 'chan', [(i, (i + step) % size) for i in range(size)])]
    ppermute x15 -> x3, waiting for transfers between devices: 15 us -> 6.18 us  [exchange(): return lax.ppermute(value, 'chan', [(i, i ^ step) for i in range(size)])]
    ppermute x0 -> x12, waiting for transfers between devices: none -> 7.91 us  [shift(): lax.ppermute(value, 'chan', [(i, (i + step) % size) for i in range(size)])]
    unnamed x21 -> x15, local copies, waits for them, and re-layouts: 2.45 us -> 0.12 us
    ppermute x3 -> x6, starting transfers between devices: 9.84 us -> 10.8 us  [swap_cores(): return lax.ppermute(value, 'morton', [(i, i ^ 1) for i in range(size)])]
    ppermute x3 -> x6, waiting for transfers between devices: 3.24 us -> 4.12 us  [swap_cores(): return lax.ppermute(value, 'morton', [(i, i ^ 1) for i in range(size)])]
  transfers between devices with their start and end apart: 20 -> 23, of which waited for: 10 -> 12; matrix products, arithmetic and copies ran while one was open for 0% -> 0% of each run, Pallas kernels for 12% -> 12%
where the time goes in v8:
time: 109 us; the launch traced here: 108 us
  starting transfers between devices  44 us (40%)
  Pallas kernels  22.5 us (21%)
  waiting for transfers between devices  22.5 us (21%)
  blocking collectives  18.3 us (17%)
    all_to_all x1, blocking collectives, local_step(): lax.all_to_all(mixed, 'morton', 0, 0, axis_index_groups=same_core, tiled=...  18.3 us
    ppermute x12, starting transfers between devices, shift(): lax.ppermute(value, 'chan', [(i, (i + step) % size) for i in range(size)])  10.9 us
    ppermute x6, starting transfers between devices, swap_cores(): return lax.ppermute(value, 'morton', [(i, i ^ 1) for i in range(size)])  10.8 us
    all_to_all x1, starting transfers between devices, local_step(): lax.all_to_all(parts.reshape((4 * chips,) + piece[1:]), ('morton', 'chan'...  8.75 us
    all_to_all x1, starting transfers between devices, local_step(): incoming = lax.all_to_all(outgoing, 'morton', 0, 0, tiled=True)  8.6 us
    ppermute x12, waiting for transfers between devices, shift(): lax.ppermute(value, 'chan', [(i, (i + step) % size) for i in range(size)])  7.91 us
    ppermute x3, waiting for transfers between devices, exchange(): return lax.ppermute(value, 'chan', [(i, i ^ step) for i in range(size)])  6.18 us
    pallas_call x1, Pallas kernels, local_step(): call(table_kernel, 'table_grad', [shape(wide, F32), shape(blocks, BF), sh...  5.78 us
  transfers between devices with their start and end apart: 23, of which 12 were waited for; matrix products, arithmetic and copies ran while one was open for 0% of the time, Pallas kernels for 12%

profile of v8, /device:TPU:1, one launch (start us, length us, event | category | flops | bytes accessed | tf_op | source)
XLA Modules:
  0.0 108.2 jit_solution(14186319811921429736)
XLA Ops:
  0.7 2.0 %pack.1 = bf16[32,64,128]{2,1,0:T(8,128)(2,1)} custom-call(s32[1,32]{1,0:T(1,128)} %send_block.1, s32[1,32]{1,0:T(1,128)} %send_count.1, bf16[64,2048]{1,0:T(8,128)(2,1)} %features.7), custom_call_target="tpu_custom_call" | custom-call | bytes 1048576 | tf_op jit(solution)/shard_map/pack/pallas_call | solution.py:336
  2.7 8.6 %all-to-all-start = ((bf16[32,64,128]{2,1,0:T(8,128)(2,1)}), bf16[32,64,128]{2,1,0:T(8,128)(2,1)S(1)}, u32[]{:S(2)}, u32[]{:S(2)}) async-start(bf16[32,64,128]{2,1,0:T(8,128)(2,1)} %pack.1), calls=%async_computation | async-start | bytes 1048576 | tf_op jit(solution)/shard_map/all_to_all | solution.py:347
  11.3 0.3 split.1
  11.6 1.7 %collective-permute-start = (bf16[7,64,128]{2,1,0:T(8,128)(2,1)S(1)}, bf16[7,64,128]{2,1,0:T(8,128)(2,1)S(1)}, u32[]{:S(2)}, u32[]{:S(2)}) collective-permute-start(bf16[7,64,128]{2,1,0:T(8,128)(2,1)S(1)} %get-tuple-element.28), channel_id=1, source_target_pairs={{0,1},{1,0},{2,3},{3,2},{4,5},{5,4},{6,7},{7,6},{8,9},{9,8},{10,11... | collective-permute-start | bytes 344072 | tf_op jit(solution)/shard_map/ppermute | solution.py:316
  13.4 3.3 %collective-permute-start.1 = (bf16[7,64,128]{2,1,0:T(8,128)(2,1)S(1)}, bf16[7,64,128]{2,1,0:T(8,128)(2,1)S(1)}, u32[]{:S(2)}, u32[]{:S(2)}) collective-permute-start(bf16[7,64,128]{2,1,0:T(8,128)(2,1)S(1)} %get-tuple-element.29), channel_id=1, source_target_pairs={{0,2},{1,3},{2,0},{3,1},{4,6},{5,7},{6,4},{7,5},{8,10},{9,11},{10,... | collective-permute-start | bytes 344072 | tf_op jit(solution)/shard_map/ppermute | solution.py:316
  16.7 0.8 collective-permute-start.3
  17.5 4.7 %collective-permute-done.1.refs_2_ = bf16[7,64,128]{2,1,0:T(8,128)(2,1)S(1)} collective-permute-done((bf16[7,64,128]{2,1,0:T(8,128)(2,1)S(1)}, bf16[7,64,128]{2,1,0:T(8,128)(2,1)S(1)}, u32[]{:S(2)}, u32[]{:S(2)}) %collective-permute-start.1) | collective-permute-done | bytes 114720 | tf_op jit(solution)/shard_map/ppermute | solution.py:316
  22.2 1.1 %collective-permute-start.4 = (bf16[7,64,128]{2,1,0:T(8,128)(2,1)S(1)}, bf16[7,64,128]{2,1,0:T(8,128)(2,1)S(1)}, u32[]{:S(2)}, u32[]{:S(2)}) collective-permute-start(bf16[7,64,128]{2,1,0:T(8,128)(2,1)S(1)} %collective-permute-done.1.refs_2_), channel_id=1, source_target_pairs={{0,4},{4,0},{8,12},{12,8},{16,20},{20,16},{24,28},{28,24},{32,36},... | collective-permute-start | bytes 344072 | tf_op jit(solution)/shard_map/ppermute | solution.py:321
  23.3 1.4 %collective-permute-done.2.refs_3_ = bf16[7,64,128]{2,1,0:T(8,128)(2,1)S(1)} collective-permute-done((bf16[7,64,128]{2,1,0:T(8,128)(2,1)S(1)}, bf16[7,64,128]{2,1,0:T(8,128)(2,1)S(1)}, u32[]{:S(2)}, u32[]{:S(2)}) %collective-permute-start.2) | collective-permute-done | bytes 114720 | tf_op jit(solution)/shard_map/ppermute | solution.py:316
  24.8 0.7 collective-permute-start.5
  25.6 0.9 collective-permute-done.5.refs_6_
  26.4 2.4 %forward0.1 = (f32[64,1024]{1,0:T(8,128)S(1)}, bf16[64,1024]{1,0:T(8,128)(2,1)S(1)}, bf16[64,1024]{1,0:T(8,128)(2,1)S(1)}, bf16[64,1024]{1,0:T(8,128)(2,1)S(1)}) custom-call(s32[1]{0:T(128)} %bitcast.place, s32[1]{0:T(128)} %bitcast.1.core, s32[27,16]{1,0:T(8,128)S(1)} %copy.11.neighbour, bf16[64,2048]{1,0:T(8,128)(2,1)S(1)} %copy-done.2, ...), custom_call_target="tpu_custom_call" | custom-call | flops 939524096 | bytes 3145728 | tf_op jit(solution)/shard_map/forward0/pallas_call | solution.py:366
  28.8 0.2 collective-permute-start.9
  29.1 0.4 collective-permute-start.10
  29.4 0.9 collective-permute-start.11
  30.4 2.4 %forward8.1 = (f32[64,1024]{1,0:T(8,128)S(1)}, bf16[64,1024]{1,0:T(8,128)(2,1)S(1)}, bf16[64,1024]{1,0:T(8,128)(2,1)S(1)}, bf16[64,1024]{1,0:T(8,128)(2,1)S(1)}) custom-call(s32[1]{0:T(128)} %bitcast.place, s32[1]{0:T(128)} %bitcast.1.core, s32[27,16]{1,0:T(8,128)S(1)} %copy.11.neighbour, bf16[64,2048]{1,0:T(8,128)(2,1)S(1)} %copy-done.2, ...), custom_call_target="tpu_custom_call" | custom-call | flops 939524096 | bytes 3145728 | tf_op jit(solution)/shard_map/forward8/pallas_call | solution.py:366
  32.7 2.5 %collective-permute-start.6 = (bf16[64,1024]{1,0:T(8,128)(2,1)S(1)}, bf16[64,1024]{1,0:T(8,128)(2,1)S(1)}, u32[]{:S(2)}, u32[]{:S(2)}) collective-permute-start(bf16[64,1024]{1,0:T(8,128)(2,1)S(1)} %get-tuple-element.32), channel_id=1, source_target_pairs={{0,3},{1,0},{2,1},{3,2},{4,7},{5,4},{6,5},{7,6},{8,11},{9,8},{10,9... | collective-permute-start | bytes 393224 | tf_op jit(solution)/shard_map/ppermute | solution.py:311
  35.2 1.3 %collective-permute-start.7 = (bf16[64,1024]{1,0:T(8,128)(2,1)S(1)}, bf16[64,1024]{1,0:T(8,128)(2,1)S(1)}, u32[]{:S(2)}, u32[]{:S(2)}) collective-permute-start(bf16[64,1024]{1,0:T(8,128)(2,1)S(1)} %get-tuple-element.33), channel_id=1, source_target_pairs={{0,2},{1,3},{2,0},{3,1},{4,6},{5,7},{6,4},{7,5},{8,10},{9,11},{10,... | collective-permute-start | bytes 393224 | tf_op jit(solution)/shard_map/ppermute | solution.py:311
  36.5 0.8 collective-permute-start.8
  37.2 1.5 %collective-permute-done.11.part3 = bf16[64,1024]{1,0:T(8,128)(2,1)S(1)} collective-permute-done((bf16[64,1024]{1,0:T(8,128)(2,1)S(1)}, bf16[64,1024]{1,0:T(8,128)(2,1)S(1)}, u32[]{:S(2)}, u32[]{:S(2)}) %collective-permute-start.11) | collective-permute-done | bytes 131104 | tf_op jit(solution)/shard_map/ppermute | solution.py:311
  38.8 0.2 activation0.1
  39.0 0.4 collective-permute-start.14
  39.4 0.5 collective-permute-start.13
  39.9 0.6 collective-permute-start.12
  40.6 3.8 %collective-permute-done.8.part3 = bf16[64,1024]{1,0:T(8,128)(2,1)S(1)} collective-permute-done((bf16[64,1024]{1,0:T(8,128)(2,1)S(1)}, bf16[64,1024]{1,0:T(8,128)(2,1)S(1)}, u32[]{:S(2)}, u32[]{:S(2)}) %collective-permute-start.8) | collective-permute-done | bytes 131104 | tf_op jit(solution)/shard_map/ppermute | solution.py:311
  44.4 0.8 activation8.1
  45.2 0.1 collective-permute-start.17
  45.3 2.4 %collective-permute-start.16 = (bf16[64,1024]{1,0:T(8,128)(2,1)S(1)}, bf16[64,1024]{1,0:T(8,128)(2,1)S(1)}, u32[]{:S(2)}, u32[]{:S(2)}) collective-permute-start(bf16[64,1024]{1,0:T(8,128)(2,1)S(1)} %get-tuple-element.42.grad0.refs_4_), channel_id=1, source_target_pairs={{0,2},{1,3},{2,0},{3,1},{4,6},{5,7},{6,4},{7,5},{8,10},{9,11},{10,... | collective-permute-start | bytes 393224 | tf_op jit(solution)/shard_map/ppermute | solution.py:311
  47.7 0.9 collective-permute-start.15
  48.5 1.2 %collective-permute-done.12.grad1.refs_1_ = bf16[64,1024]{1,0:T(8,128)(2,1)S(1)} collective-permute-done((bf16[64,1024]{1,0:T(8,128)(2,1)S(1)}, bf16[64,1024]{1,0:T(8,128)(2,1)S(1)}, u32[]{:S(2)}, u32[]{:S(2)}) %collective-permute-start.12) | collective-permute-done | bytes 131104 | tf_op jit(solution)/shard_map/ppermute | solution.py:311
  49.7 2.1 %weight_grad0.1.held = f32[1792,256]{1,0:T(8,128)S(1)} custom-call(s32[27,16]{1,0:T(8,128)S(1)} %copy.11.neighbour, bf16[64,2048]{1,0:T(8,128)(2,1)S(1)} %copy-done.2, bf16[32,64,128]{2,1,0:T(8,128)(2,1)S(1)} %all-to-all-done.incoming, bf16[64,1024]{1,0:T(8,128)(2,1)S(1)} %get-tuple-element.41.refs_7_.grad0.refs_0_, ...), custom_call_target="tpu_custom_call" | custom-call | flops 939524096 | bytes 4194304 | tf_op jit(solution)/shard_map/weight_grad0/pallas_call | solution.py:396
  51.9 1.3 %collective-permute-done.15.grad1.refs_5_ = bf16[64,1024]{1,0:T(8,128)(2,1)S(1)} collective-permute-done((bf16[64,1024]{1,0:T(8,128)(2,1)S(1)}, bf16[64,1024]{1,0:T(8,128)(2,1)S(1)}, u32[]{:S(2)}, u32[]{:S(2)}) %collective-permute-start.15) | collective-permute-done | bytes 131104 | tf_op jit(solution)/shard_map/ppermute | solution.py:311
  53.2 2.2 %weight_grad8.1 = (f32[14,4,32,128]{3,2,1,0:T(8,128)S(1)}, bf16[14,4,32,128]{3,2,1,0:T(8,128)(2,1)S(1)}) custom-call(s32[1]{0:T(128)} %bitcast.1.core, s32[27,16]{1,0:T(8,128)S(1)} %copy.11.neighbour, bf16[64,2048]{1,0:T(8,128)(2,1)S(1)} %copy-done.2, bf16[32,64,128]{2,1,0:T(8,128)(2,1)S(1)} %all-to-all-done.incoming, ...), custom_call_target="tpu_custom_call" | custom-call | flops 939524096 | bytes 4194304 | tf_op jit(solution)/shard_map/weight_grad8/pallas_call | solution.py:396
  55.4 4.5 %collective-permute-start.18 = (bf16[14,4,32,128]{3,2,1,0:T(8,128)(2,1)S(1)}, bf16[14,4,32,128]{3,2,1,0:T(8,128)(2,1)S(1)}, u32[]{:S(2)}, u32[]{:S(2)}) collective-permute-start(bf16[14,4,32,128]{3,2,1,0:T(8,128)(2,1)S(1)} %get-tuple-element.44), channel_id=1, source_target_pairs={{0,4},{4,0},{8,12},{12,8},{16,20},{20,16},{24,28},{28,24},{32,36},... | collective-permute-start | bytes 1376264 | tf_op jit(solution)/shard_map/ppermute | solution.py:321
  59.9 1.4 %collective-permute-done.18.arrived = bf16[14,4,32,128]{3,2,1,0:T(8,128)(2,1)S(1)} collective-permute-done((bf16[14,4,32,128]{3,2,1,0:T(8,128)(2,1)S(1)}, bf16[14,4,32,128]{3,2,1,0:T(8,128)(2,1)S(1)}, u32[]{:S(2)}, u32[]{:S(2)}) %collective-permute-start.18) | collective-permute-done | bytes 458784 | tf_op jit(solution)/shard_map/ppermute | solution.py:321
  61.3 0.9 pair_sum.1.refs_8_
  62.2 8.7 %all-to-all-start.1 = ((bf16[64,32,128]{2,1,0:T(8,128)(2,1)}), bf16[64,32,128]{2,1,0:T(8,128)(2,1)S(1)}, u32[]{:S(2)}, u32[]{:S(2)}) async-start(bf16[64,32,128]{2,1,0:T(8,128)(2,1)} %bitcast.2), calls=%async_computation.1 | async-start | bytes 1048576 | tf_op jit(solution)/shard_map/all_to_all | solution.py:414
  71.0 0.3 join.1.weight_t
  71.3 5.8 %table_grad.1 = (f32[64,2048]{1,0:T(8,128)S(1)}, bf16[16,64,128]{2,1,0:T(8,128)(2,1)S(1)}, bf16[16,64,128]{2,1,0:T(8,128)(2,1)S(1)}) custom-call(s32[1]{0:T(128)} %bitcast.1.core, s32[27,16]{1,0:T(8,128)S(1)} %copy.11.neighbour, bf16[1792,256]{1,0:T(8,128)(2,1)S(1)} %join.1.weight_t, bf16[64,1024]{1,0:T(8,128)(2,1)S(1)} %get-tuple-element.41.refs_7_.grad0.refs_0_, ...), custom_call_target="tpu_custom_call" | custom-call | flops 1879048192 | bytes 4194304 | tf_op jit(solution)/shard_map/table_grad/pallas_call | solution.py:424
  77.1 0.7 collective-permute-start.19
  77.8 1.2 %collective-permute-done.19.away = bf16[16,64,128]{2,1,0:T(8,128)(2,1)S(1)} collective-permute-done((bf16[16,64,128]{2,1,0:T(8,128)(2,1)S(1)}, bf16[16,64,128]{2,1,0:T(8,128)(2,1)S(1)}, u32[]{:S(2)}, u32[]{:S(2)}) %collective-permute-start.19) | collective-permute-done | bytes 262176 | tf_op jit(solution)/shard_map/ppermute | solution.py:321
  79.0 4.2 %all-to-all-done.1 = bf16[64,32,128]{2,1,0:T(8,128)(2,1)S(1)} async-done(((bf16[64,32,128]{2,1,0:T(8,128)(2,1)}), bf16[64,32,128]{2,1,0:T(8,128)(2,1)S(1)}, u32[]{:S(2)}, u32[]{:S(2)}) %all-to-all-start.1) | async-done | bytes 524320 | tf_op jit(solution)/shard_map/all_to_all | solution.py:414
  83.2 0.2 sum_parts.1
  83.4 18.3 %all_to_all.15.mixed.mine = bf16[16,8,32,128]{3,2,1,0:T(8,128)(2,1)S(1)} all-to-all(bf16[16,8,32,128]{3,2,1,0:T(8,128)(2,1)S(1)} %sum_parts.1), channel_id=1, replica_groups={{0,8,16,24,32,40,48,56,64,72,80,88,96,104,112,120},{4,12,20,28,36,44,52..., dimensions={0} | all-to-all | bytes 2097152 | tf_op jit(solution)/shard_map/all_to_all | solution.py:444
  101.6 2.9 %collective-permute-start.20 = (bf16[16,8,32,128]{3,2,1,0:T(8,128)(2,1)S(1)}, bf16[16,8,32,128]{3,2,1,0:T(8,128)(2,1)S(1)}, u32[]{:S(2)}, u32[]{:S(2)}) collective-permute-start(bf16[16,8,32,128]{3,2,1,0:T(8,128)(2,1)S(1)} %all_to_all.15.mixed.mine), channel_id=1, source_target_pairs={{0,4},{4,0},{8,12},{12,8},{16,20},{20,16},{24,28},{28,24},{32,36},... | collective-permute-start | bytes 3145736 | tf_op jit(solution)/shard_map/ppermute | solution.py:321
  104.6 1.6 %return_add.1 = f32[64,2048]{1,0:T(8,128)} custom-call(s32[1]{0:T(128)} %bitcast.1.core, s32[1,32]{1,0:T(1,128)S(1)} %copy-done.4, s32[1,32]{1,0:T(1,128)S(1)} %copy-done.5, f32[64,2048]{1,0:T(8,128)S(1)} %get-tuple-element.45.local, bf16[16,8,32,128]{3,2,1,0:T(8,128)(2,1)S(1)} %all_to_all.15.mixed.mine), custom_call_target="tpu_custom_call" | custom-call | bytes 2097152 | tf_op jit(solution)/shard_map/return_add/pallas_call | solution.py:445
  106.2 0.6 collective-permute-done.20.other
  106.9 1.3 %unpack.1 = (f32[27,64,256]{2,1,0:T(8,128)}, f32[64,256]{1,0:T(8,128)}) custom-call(s32[1]{0:T(128)} %bitcast.1.core, bf16[16,8,32,128]{3,2,1,0:T(8,128)(2,1)S(1)} %all_to_all.15.mixed.mine, bf16[16,8,32,128]{3,2,1,0:T(8,128)(2,1)S(1)} %collective-permute-done.20.other), custom_call_target="tpu_custom_call" | custom-call | bytes 3145728 | tf_op jit(solution)/shard_map/unpack/pallas_call | solution.py:448
  (28 shorter events, 0.2 us)
Async XLA Ops:
  0.6 25.8 %copy-start.2 = (bf16[64,2048]{1,0:T(8,128)(2,1)S(1)}, bf16[64,2048]{1,0:T(8,128)(2,1)}, u32[]{:S(2)}) copy-start(bf16[64,2048]{1,0:T(8,128)(2,1)} %features.7) | copy-start | bytes 786436
  0.6 10.7 %copy-start.3 = (bf16[64,256]{1,0:T(8,128)(2,1)S(1)}, bf16[64,256]{1,0:T(8,128)(2,1)}, u32[]{:S(2)}) copy-start(bf16[64,256]{1,0:T(8,128)(2,1)} %coarse_weight.1) | copy-start | bytes 98308
  0.7 10.7 %copy-start.1 = (bf16[27,64,256]{2,1,0:T(8,128)(2,1)S(1)}, bf16[27,64,256]{2,1,0:T(8,128)(2,1)}, u32[]{:S(2)}) copy-start(bf16[27,64,256]{2,1,0:T(8,128)(2,1)} %conv_weight.1) | copy-start | bytes 2654212
  0.7 24.8 %copy-start.6 = (s32[27,16]{0,1:T(8,128)S(1)}, s32[27,16]{0,1:T(8,128)}, u32[]{:S(2)}) copy-start(s32[27,16]{0,1:T(8,128)} %param.13) | copy-start | bytes 5188
  2.7 23.7 %all-to-all-start = ((bf16[32,64,128]{2,1,0:T(8,128)(2,1)}), bf16[32,64,128]{2,1,0:T(8,128)(2,1)S(1)}, u32[]{:S(2)}, u32[]{:S(2)}) async-start(bf16[32,64,128]{2,1,0:T(8,128)(2,1)} %pack.1), calls=%async_computation | async-start | bytes 1048576 | tf_op jit(solution)/shard_map/all_to_all | solution.py:347
  11.6 5.0 %collective-permute-start = (bf16[7,64,128]{2,1,0:T(8,128)(2,1)S(1)}, bf16[7,64,128]{2,1,0:T(8,128)(2,1)S(1)}, u32[]{:S(2)}, u32[]{:S(2)}) collective-permute-start(bf16[7,64,128]{2,1,0:T(8,128)(2,1)S(1)} %get-tuple-element.28), channel_id=1, source_target_pairs={{0,1},{1,0},{2,3},{3,2},{4,5},{5,4},{6,7},{7,6},{8,9},{9,8},{10,11... | collective-permute-start | bytes 344072 | tf_op jit(solution)/shard_map/ppermute | solution.py:316
  13.4 8.9 %collective-permute-start.1 = (bf16[7,64,128]{2,1,0:T(8,128)(2,1)S(1)}, bf16[7,64,128]{2,1,0:T(8,128)(2,1)S(1)}, u32[]{:S(2)}, u32[]{:S(2)}) collective-permute-start(bf16[7,64,128]{2,1,0:T(8,128)(2,1)S(1)} %get-tuple-element.29), channel_id=1, source_target_pairs={{0,2},{1,3},{2,0},{3,1},{4,6},{5,7},{6,4},{7,5},{8,10},{9,11},{10,... | collective-permute-start | bytes 344072 | tf_op jit(solution)/shard_map/ppermute | solution.py:316
  16.7 8.1 %collective-permute-start.2 = (bf16[7,64,128]{2,1,0:T(8,128)(2,1)S(1)}, bf16[7,64,128]{2,1,0:T(8,128)(2,1)S(1)}, u32[]{:S(2)}, u32[]{:S(2)}) collective-permute-start(bf16[7,64,128]{2,1,0:T(8,128)(2,1)S(1)} %get-tuple-element.30), channel_id=1, source_target_pairs={{0,3},{1,2},{2,1},{3,0},{4,7},{5,6},{6,5},{7,4},{8,11},{9,10},{10,... | collective-permute-start | bytes 344072 | tf_op jit(solution)/shard_map/ppermute | solution.py:316
  16.7 8.9 %collective-permute-start.3 = (bf16[7,64,128]{2,1,0:T(8,128)(2,1)S(1)}, bf16[7,64,128]{2,1,0:T(8,128)(2,1)S(1)}, u32[]{:S(2)}, u32[]{:S(2)}) collective-permute-start(bf16[7,64,128]{2,1,0:T(8,128)(2,1)S(1)} %collective-permute-done.refs_1_), channel_id=1, source_target_pairs={{0,4},{4,0},{8,12},{12,8},{16,20},{20,16},{24,28},{28,24},{32,36},... | collective-permute-start | bytes 344072 | tf_op jit(solution)/shard_map/ppermute | solution.py:321
  22.2 3.3 %collective-permute-start.4 = (bf16[7,64,128]{2,1,0:T(8,128)(2,1)S(1)}, bf16[7,64,128]{2,1,0:T(8,128)(2,1)S(1)}, u32[]{:S(2)}, u32[]{:S(2)}) collective-permute-start(bf16[7,64,128]{2,1,0:T(8,128)(2,1)S(1)} %collective-permute-done.1.refs_2_), channel_id=1, source_target_pairs={{0,4},{4,0},{8,12},{12,8},{16,20},{20,16},{24,28},{28,24},{32,36},... | collective-permute-start | bytes 344072 | tf_op jit(solution)/shard_map/ppermute | solution.py:321
  24.8 1.7 %collective-permute-start.5 = (bf16[7,64,128]{2,1,0:T(8,128)(2,1)S(1)}, bf16[7,64,128]{2,1,0:T(8,128)(2,1)S(1)}, u32[]{:S(2)}, u32[]{:S(2)}) collective-permute-start(bf16[7,64,128]{2,1,0:T(8,128)(2,1)S(1)} %collective-permute-done.2.refs_3_), channel_id=1, source_target_pairs={{0,4},{4,0},{8,12},{12,8},{16,20},{20,16},{24,28},{28,24},{32,36},... | collective-permute-start | bytes 344072 | tf_op jit(solution)/shard_map/ppermute | solution.py:321
  28.8 10.0 %copy-start = (bf16[64,2048]{1,0:T(8,128)(2,1)S(1)}, bf16[64,2048]{1,0:T(8,128)(2,1)}, u32[]{:S(2)}) copy-start(bf16[64,2048]{1,0:T(8,128)(2,1)} %out_grad.3) | copy-start | bytes 786436
  28.8 7.6 %collective-permute-start.9 = (bf16[64,1024]{1,0:T(8,128)(2,1)S(1)}, bf16[64,1024]{1,0:T(8,128)(2,1)S(1)}, u32[]{:S(2)}, u32[]{:S(2)}) collective-permute-start(bf16[64,1024]{1,0:T(8,128)(2,1)S(1)} %get-tuple-element.36), channel_id=1, source_target_pairs={{0,3},{1,0},{2,1},{3,2},{4,7},{5,4},{6,5},{7,6},{8,11},{9,8},{10,9... | collective-permute-start | bytes 393224 | tf_op jit(solution)/shard_map/ppermute | solution.py:311
  29.1 8.2 %collective-permute-start.10 = (bf16[64,1024]{1,0:T(8,128)(2,1)S(1)}, bf16[64,1024]{1,0:T(8,128)(2,1)S(1)}, u32[]{:S(2)}, u32[]{:S(2)}) collective-permute-start(bf16[64,1024]{1,0:T(8,128)(2,1)S(1)} %get-tuple-element.37), channel_id=1, source_target_pairs={{0,2},{1,3},{2,0},{3,1},{4,6},{5,7},{6,4},{7,5},{8,10},{9,11},{10,... | collective-permute-start | bytes 393224 | tf_op jit(solution)/shard_map/ppermute | solution.py:311
  29.4 9.4 %collective-permute-start.11 = (bf16[64,1024]{1,0:T(8,128)(2,1)S(1)}, bf16[64,1024]{1,0:T(8,128)(2,1)S(1)}, u32[]{:S(2)}, u32[]{:S(2)}) collective-permute-start(bf16[64,1024]{1,0:T(8,128)(2,1)S(1)} %get-tuple-element.38), channel_id=1, source_target_pairs={{0,1},{1,2},{2,3},{3,0},{4,5},{5,6},{6,7},{7,4},{8,9},{9,10},{10,1... | collective-permute-start | bytes 393224 | tf_op jit(solution)/shard_map/ppermute | solution.py:311
  32.7 7.2 %collective-permute-start.6 = (bf16[64,1024]{1,0:T(8,128)(2,1)S(1)}, bf16[64,1024]{1,0:T(8,128)(2,1)S(1)}, u32[]{:S(2)}, u32[]{:S(2)}) collective-permute-start(bf16[64,1024]{1,0:T(8,128)(2,1)S(1)} %get-tuple-element.32), channel_id=1, source_target_pairs={{0,3},{1,0},{2,1},{3,2},{4,7},{5,4},{6,5},{7,6},{8,11},{9,8},{10,9... | collective-permute-start | bytes 393224 | tf_op jit(solution)/shard_map/ppermute | solution.py:311
  35.2 5.4 %collective-permute-start.7 = (bf16[64,1024]{1,0:T(8,128)(2,1)S(1)}, bf16[64,1024]{1,0:T(8,128)(2,1)S(1)}, u32[]{:S(2)}, u32[]{:S(2)}) collective-permute-start(bf16[64,1024]{1,0:T(8,128)(2,1)S(1)} %get-tuple-element.33), channel_id=1, source_target_pairs={{0,2},{1,3},{2,0},{3,1},{4,6},{5,7},{6,4},{7,5},{8,10},{9,11},{10,... | collective-permute-start | bytes 393224 | tf_op jit(solution)/shard_map/ppermute | solution.py:311
  36.5 7.9 %collective-permute-start.8 = (bf16[64,1024]{1,0:T(8,128)(2,1)S(1)}, bf16[64,1024]{1,0:T(8,128)(2,1)S(1)}, u32[]{:S(2)}, u32[]{:S(2)}) collective-permute-start(bf16[64,1024]{1,0:T(8,128)(2,1)S(1)} %get-tuple-element.34), channel_id=1, source_target_pairs={{0,1},{1,2},{2,3},{3,0},{4,5},{5,6},{6,7},{7,4},{8,9},{9,10},{10,1... | collective-permute-start | bytes 393224 | tf_op jit(solution)/shard_map/ppermute | solution.py:311
  39.0 8.7 %collective-permute-start.14 = (bf16[64,1024]{1,0:T(8,128)(2,1)S(1)}, bf16[64,1024]{1,0:T(8,128)(2,1)S(1)}, u32[]{:S(2)}, u32[]{:S(2)}) collective-permute-start(bf16[64,1024]{1,0:T(8,128)(2,1)S(1)} %get-tuple-element.41.refs_7_.grad0.refs_0_), channel_id=1, source_target_pairs={{0,3},{1,0},{2,1},{3,2},{4,7},{5,4},{6,5},{7,6},{8,11},{9,8},{10,9... | collective-permute-start | bytes 393224 | tf_op jit(solution)/shard_map/ppermute | solution.py:311
  39.4 9.1 %collective-permute-start.13 = (bf16[64,1024]{1,0:T(8,128)(2,1)S(1)}, bf16[64,1024]{1,0:T(8,128)(2,1)S(1)}, u32[]{:S(2)}, u32[]{:S(2)}) collective-permute-start(bf16[64,1024]{1,0:T(8,128)(2,1)S(1)} %get-tuple-element.41.refs_7_.grad0.refs_0_), channel_id=1, source_target_pairs={{0,2},{1,3},{2,0},{3,1},{4,6},{5,7},{6,4},{7,5},{8,10},{9,11},{10,... | collective-permute-start | bytes 393224 | tf_op jit(solution)/shard_map/ppermute | solution.py:311
  39.9 9.8 %collective-permute-start.12 = (bf16[64,1024]{1,0:T(8,128)(2,1)S(1)}, bf16[64,1024]{1,0:T(8,128)(2,1)S(1)}, u32[]{:S(2)}, u32[]{:S(2)}) collective-permute-start(bf16[64,1024]{1,0:T(8,128)(2,1)S(1)} %get-tuple-element.41.refs_7_.grad0.refs_0_), channel_id=1, source_target_pairs={{0,1},{1,2},{2,3},{3,0},{4,5},{5,6},{6,7},{7,4},{8,9},{9,10},{10,1... | collective-permute-start | bytes 393224 | tf_op jit(solution)/shard_map/ppermute | solution.py:311
  45.2 6.6 %collective-permute-start.17 = (bf16[64,1024]{1,0:T(8,128)(2,1)S(1)}, bf16[64,1024]{1,0:T(8,128)(2,1)S(1)}, u32[]{:S(2)}, u32[]{:S(2)}) collective-permute-start(bf16[64,1024]{1,0:T(8,128)(2,1)S(1)} %get-tuple-element.42.grad0.refs_4_), channel_id=1, source_target_pairs={{0,3},{1,0},{2,1},{3,2},{4,7},{5,4},{6,5},{7,6},{8,11},{9,8},{10,9... | collective-permute-start | bytes 393224 | tf_op jit(solution)/shard_map/ppermute | solution.py:311
  45.3 6.5 %collective-permute-start.16 = (bf16[64,1024]{1,0:T(8,128)(2,1)S(1)}, bf16[64,1024]{1,0:T(8,128)(2,1)S(1)}, u32[]{:S(2)}, u32[]{:S(2)}) collective-permute-start(bf16[64,1024]{1,0:T(8,128)(2,1)S(1)} %get-tuple-element.42.grad0.refs_4_), channel_id=1, source_target_pairs={{0,2},{1,3},{2,0},{3,1},{4,6},{5,7},{6,4},{7,5},{8,10},{9,11},{10,... | collective-permute-start | bytes 393224 | tf_op jit(solution)/shard_map/ppermute | solution.py:311
  47.7 5.5 %collective-permute-start.15 = (bf16[64,1024]{1,0:T(8,128)(2,1)S(1)}, bf16[64,1024]{1,0:T(8,128)(2,1)S(1)}, u32[]{:S(2)}, u32[]{:S(2)}) collective-permute-start(bf16[64,1024]{1,0:T(8,128)(2,1)S(1)} %get-tuple-element.42.grad0.refs_4_), channel_id=1, source_target_pairs={{0,1},{1,2},{2,3},{3,0},{4,5},{5,6},{6,7},{7,4},{8,9},{9,10},{10,1... | collective-permute-start | bytes 393224 | tf_op jit(solution)/shard_map/ppermute | solution.py:311
  55.4 5.9 %collective-permute-start.18 = (bf16[14,4,32,128]{3,2,1,0:T(8,128)(2,1)S(1)}, bf16[14,4,32,128]{3,2,1,0:T(8,128)(2,1)S(1)}, u32[]{:S(2)}, u32[]{:S(2)}) collective-permute-start(bf16[14,4,32,128]{3,2,1,0:T(8,128)(2,1)S(1)} %get-tuple-element.44), channel_id=1, source_target_pairs={{0,4},{4,0},{8,12},{12,8},{16,20},{20,16},{24,28},{28,24},{32,36},... | collective-permute-start | bytes 1376264 | tf_op jit(solution)/shard_map/ppermute | solution.py:321
  62.2 21.0 %all-to-all-start.1 = ((bf16[64,32,128]{2,1,0:T(8,128)(2,1)}), bf16[64,32,128]{2,1,0:T(8,128)(2,1)S(1)}, u32[]{:S(2)}, u32[]{:S(2)}) async-start(bf16[64,32,128]{2,1,0:T(8,128)(2,1)} %bitcast.2), calls=%async_computation.1 | async-start | bytes 1048576 | tf_op jit(solution)/shard_map/all_to_all | solution.py:414
  77.1 1.9 %collective-permute-start.19 = (bf16[16,64,128]{2,1,0:T(8,128)(2,1)S(1)}, bf16[16,64,128]{2,1,0:T(8,128)(2,1)S(1)}, u32[]{:S(2)}, u32[]{:S(2)}) collective-permute-start(bf16[16,64,128]{2,1,0:T(8,128)(2,1)S(1)} %get-tuple-element.47), channel_id=1, source_target_pairs={{0,4},{4,0},{8,12},{12,8},{16,20},{20,16},{24,28},{28,24},{32,36},... | collective-permute-start | bytes 786440 | tf_op jit(solution)/shard_map/ppermute | solution.py:321
  83.2 21.4 %copy-start.4 = (s32[1,32]{1,0:T(1,128)S(1)}, s32[1,32]{1,0:T(1,128)}, u32[]{:S(2)}) copy-start(s32[1,32]{1,0:T(1,128)} %send_block.1) | copy-start | bytes 388
  83.2 21.4 %copy-start.5 = (s32[1,32]{1,0:T(1,128)S(1)}, s32[1,32]{1,0:T(1,128)}, u32[]{:S(2)}) copy-start(s32[1,32]{1,0:T(1,128)} %send_count.1) | copy-start | bytes 388
  101.6 5.2 %collective-permute-start.20 = (bf16[16,8,32,128]{3,2,1,0:T(8,128)(2,1)S(1)}, bf16[16,8,32,128]{3,2,1,0:T(8,128)(2,1)S(1)}, u32[]{:S(2)}, u32[]{:S(2)}) collective-permute-start(bf16[16,8,32,128]{3,2,1,0:T(8,128)(2,1)S(1)} %all_to_all.15.mixed.mine), channel_id=1, source_target_pairs={{0,4},{4,0},{8,12},{12,8},{16,20},{20,16},{24,28},{28,24},{32,36},... | collective-permute-start | bytes 3145736 | tf_op jit(solution)/shard_map/ppermute | solution.py:321

commit v9 on v8

--- a/solution.py
+++ b/solution.py
@@ -129,8 +129,8 @@
         gathered[OFFSETS * quarter :, block * BLOCK : (block + 1) * BLOCK] = pooled
 
 
-def forward_kernel(first, place, core, neighbour, features, incoming, *refs):
-    pieces, outs, (weight, table, gathered) = refs[:7], refs[7:11], refs[11:]
+def forward_kernel(place, core, neighbour, features, incoming, *refs):
+    pieces, outs, (weight, table, gathered) = refs[:7], refs[7:-3], refs[-3:]
     quarter, row_count = features.shape
     nblocks = row_count // BLOCK
     extent = nblocks + incoming.shape[0]
@@ -139,12 +139,14 @@
             rows = slice(step * quarter, (step + 1) * quarter)
             weight[rows, pair * BLOCK : (pair + 1) * BLOCK] = tile
     fill_table(features, incoming, table, nblocks)
-    fill_gathered(neighbour, table, gathered, first, extent)
-    for tile in range(gathered.shape[1] // 256):
-        cut = slice(tile * 256, (tile + 1) * 256)
-        total = jnp.dot(weight[...], gathered[:, cut], preferred_element_type=F32)
-        for step, out in enumerate(outs):
-            out[:, cut] = total[step * quarter : (step + 1) * quarter].astype(out.dtype)
+    for part, first in enumerate(CUTS[:-1]):
+        width = outs[4 * part].shape[1]
+        fill_gathered(neighbour, table, gathered.at[:, :width], first, extent)
+        for tile in range(width // 256):
+            cut = slice(tile * 256, (tile + 1) * 256)
+            total = jnp.dot(weight[...], gathered[:, cut], preferred_element_type=F32)
+            for step, out in enumerate(outs[4 * part : 4 * part + 4]):
+                out[:, cut] = total[step * quarter : (step + 1) * quarter].astype(out.dtype)
 
 
 def activate(own, part1, part2, part3, out_grad):
@@ -360,18 +362,19 @@
     table = pltpu.VMEM((extent + 1, quarter, BLOCK), BF)
     wide, piece = (quarter, row_count), (4, quarter // 2, BLOCK)
     grads, outputs = [], []
-    for first, end in zip(CUTS, CUTS[1:]):
-        width = (end - first) * BLOCK
-        part = (quarter, width)
-        partial = call(
-            functools.partial(forward_kernel, first),
-            f"forward{first}",
-            [shape(part, F32)] + [shape(part, BF)] * 3,
-            "sss" + "v" * 9,
-            [pltpu.VMEM((channels, depth), BF), table, pltpu.VMEM((depth, width), BF)],
-            flops * width // row_count,
-            3 << 20,
-        )(place, core, neighbour, features, incoming, *weights)
+    widths = [(end - first) * BLOCK for first, end in zip(CUTS, CUTS[1:])]
+    partials = call(
+        forward_kernel,
+        "forward",
+        [shape((quarter, w), BF if s else F32) for w in widths for s in range(4)],
+        "sss" + "v" * 9,
+        [pltpu.VMEM((channels, depth), BF), table, pltpu.VMEM((depth, max(widths)), BF)],
+        flops,
+        3 << 20,
+    )(place, core, neighbour, features, incoming, *weights)
+    for index, (first, end) in enumerate(zip(CUTS, CUTS[1:])):
+        part = (quarter, widths[index])
+        partial = partials[4 * index : 4 * index + 4]
         arrived = [shift(partial[s], -s) for s in (1, 2, 3)]
         last = end == CUTS[-1]
         output, grad = call(

time: 109 us -> 108 us (level)
  waiting for transfers between devices: 22.5 us -> 28.4 us
  starting transfers between devices: 44 us -> 38.3 us
    ppermute x12, waiting for transfers between devices: 7.91 us -> 13.8 us  [shift(): lax.ppermute(value, 'chan', [(i, (i + step) % size) for i in range(size)])]
    ppermute x6, starting transfers between devices: 10.8 us -> 7.73 us  [swap_cores(): return lax.ppermute(value, 'morton', [(i, i ^ 1) for i in range(size)])]
    ppermute x12, starting transfers between devices: 10.9 us -> 8.96 us  [shift(): lax.ppermute(value, 'chan', [(i, (i + step) % size) for i in range(size)])]
    pallas_call x2 -> x1, Pallas kernels: 4.72 us -> 4.38 us  [local_step(): call(forward_kernel, 'forward', [shape((quarter, w), BF if s else F32) fo...]
  transfers between devices with their start and end apart: 23 -> 23, of which waited for: 12 -> 13; matrix products, arithmetic and copies ran while one was open for 0% -> 0% of each run, Pallas kernels for 12% -> 10%
where the time goes in v9:
time: 108 us
  starting transfers between devices  38.3 us (35%)
  waiting for transfers between devices  28.4 us (26%)
  Pallas kernels  22.2 us (21%)
  blocking collectives  18.3 us (17%)
    all_to_all x1, blocking collectives, local_step(): lax.all_to_all(mixed, 'morton', 0, 0, axis_index_groups=same_core, tiled=...  18.3 us
    ppermute x12, waiting for transfers between devices, shift(): lax.ppermute(value, 'chan', [(i, (i + step) % size) for i in range(size)])  13.8 us
    ppermute x12, starting transfers between devices, shift(): lax.ppermute(value, 'chan', [(i, (i + step) % size) for i in range(size)])  8.96 us
    all_to_all x1, starting transfers between devices, local_step(): incoming = lax.all_to_all(outgoing, 'morton', 0, 0, tiled=True)  8.6 us
    all_to_all x1, starting transfers between devices, local_step(): lax.all_to_all(parts.reshape((4 * chips,) + piece[1:]), ('morton', 'chan'...  8.02 us
    ppermute x6, starting transfers between devices, swap_cores(): return lax.ppermute(value, 'morton', [(i, i ^ 1) for i in range(size)])  7.73 us
    ppermute x3, waiting for transfers between devices, exchange(): return lax.ppermute(value, 'chan', [(i, i ^ step) for i in range(size)])  6.18 us
    pallas_call x1, Pallas kernels, local_step(): call(table_kernel, 'table_grad', [shape(wide, F32), shape(blocks, BF), sh...  5.79 us
  transfers between devices with their start and end apart: 23, of which 13 were waited for; matrix products, arithmetic and copies ran while one was open for 0% of the time, Pallas kernels for 10%

profile of v9, /device:TPU:1, one launch (start us, length us, event | category | flops | bytes accessed | tf_op | source)
XLA Modules:
  0.0 108.0 jit_solution(13427170977509636953)
XLA Ops:
  0.7 2.0 %pack.1 = bf16[32,64,128]{2,1,0:T(8,128)(2,1)} custom-call(s32[1,32]{1,0:T(1,128)} %send_block.1, s32[1,32]{1,0:T(1,128)} %send_count.1, bf16[64,2048]{1,0:T(8,128)(2,1)} %features.5), custom_call_target="tpu_custom_call" | custom-call | bytes 1048576 | tf_op jit(solution)/shard_map/pack/pallas_call | solution.py:338
  2.7 8.6 %all-to-all-start = ((bf16[32,64,128]{2,1,0:T(8,128)(2,1)}), bf16[32,64,128]{2,1,0:T(8,128)(2,1)S(1)}, u32[]{:S(2)}, u32[]{:S(2)}) async-start(bf16[32,64,128]{2,1,0:T(8,128)(2,1)} %pack.1), calls=%async_computation | async-start | bytes 1048576 | tf_op jit(solution)/shard_map/all_to_all | solution.py:349
  11.3 0.3 split.1
  11.6 1.7 %collective-permute-start = (bf16[7,64,128]{2,1,0:T(8,128)(2,1)S(1)}, bf16[7,64,128]{2,1,0:T(8,128)(2,1)S(1)}, u32[]{:S(2)}, u32[]{:S(2)}) collective-permute-start(bf16[7,64,128]{2,1,0:T(8,128)(2,1)S(1)} %get-tuple-element.28), channel_id=1, source_target_pairs={{0,1},{1,0},{2,3},{3,2},{4,5},{5,4},{6,7},{7,6},{8,9},{9,8},{10,11... | collective-permute-start | bytes 344072 | tf_op jit(solution)/shard_map/ppermute | solution.py:318
  13.4 3.3 %collective-permute-start.1 = (bf16[7,64,128]{2,1,0:T(8,128)(2,1)S(1)}, bf16[7,64,128]{2,1,0:T(8,128)(2,1)S(1)}, u32[]{:S(2)}, u32[]{:S(2)}) collective-permute-start(bf16[7,64,128]{2,1,0:T(8,128)(2,1)S(1)} %get-tuple-element.29), channel_id=1, source_target_pairs={{0,2},{1,3},{2,0},{3,1},{4,6},{5,7},{6,4},{7,5},{8,10},{9,11},{10,... | collective-permute-start | bytes 344072 | tf_op jit(solution)/shard_map/ppermute | solution.py:318
  16.7 0.8 collective-permute-start.3
  17.5 4.7 %collective-permute-done.1.refs_2_ = bf16[7,64,128]{2,1,0:T(8,128)(2,1)S(1)} collective-permute-done((bf16[7,64,128]{2,1,0:T(8,128)(2,1)S(1)}, bf16[7,64,128]{2,1,0:T(8,128)(2,1)S(1)}, u32[]{:S(2)}, u32[]{:S(2)}) %collective-permute-start.1) | collective-permute-done | bytes 114720 | tf_op jit(solution)/shard_map/ppermute | solution.py:318
  22.2 1.1 %collective-permute-start.4 = (bf16[7,64,128]{2,1,0:T(8,128)(2,1)S(1)}, bf16[7,64,128]{2,1,0:T(8,128)(2,1)S(1)}, u32[]{:S(2)}, u32[]{:S(2)}) collective-permute-start(bf16[7,64,128]{2,1,0:T(8,128)(2,1)S(1)} %collective-permute-done.1.refs_2_), channel_id=1, source_target_pairs={{0,4},{4,0},{8,12},{12,8},{16,20},{20,16},{24,28},{28,24},{32,36},... | collective-permute-start | bytes 344072 | tf_op jit(solution)/shard_map/ppermute | solution.py:323
  23.3 1.4 %collective-permute-done.2.refs_3_ = bf16[7,64,128]{2,1,0:T(8,128)(2,1)S(1)} collective-permute-done((bf16[7,64,128]{2,1,0:T(8,128)(2,1)S(1)}, bf16[7,64,128]{2,1,0:T(8,128)(2,1)S(1)}, u32[]{:S(2)}, u32[]{:S(2)}) %collective-permute-start.2) | collective-permute-done | bytes 114720 | tf_op jit(solution)/shard_map/ppermute | solution.py:318
  24.8 0.7 collective-permute-start.5
  25.5 0.1 copy.11.neighbour
  25.6 0.9 collective-permute-done.5.refs_6_
  26.4 4.4 %forward.1 = (f32[64,1024]{1,0:T(8,128)S(1)}, bf16[64,1024]{1,0:T(8,128)(2,1)S(1)}, bf16[64,1024]{1,0:T(8,128)(2,1)S(1)}, bf16[64,1024]{1,0:T(8,128)(2,1)S(1)}, ...) custom-call(s32[1]{0:T(128)} %bitcast.place, ...), custom_call_target="tpu_custom_call" | custom-call | flops 1879048192 | bytes 3145728 | tf_op jit(solution)/shard_map/forward/pallas_call | solution.py:366
  30.8 0.2 collective-permute-start.9
  31.1 0.4 collective-permute-start.10
  31.4 0.9 collective-permute-start.11
  32.4 2.4 %collective-permute-start.6 = (bf16[64,1024]{1,0:T(8,128)(2,1)S(1)}, bf16[64,1024]{1,0:T(8,128)(2,1)S(1)}, u32[]{:S(2)}, u32[]{:S(2)}) collective-permute-start(bf16[64,1024]{1,0:T(8,128)(2,1)S(1)} %get-tuple-element.32), channel_id=1, source_target_pairs={{0,3},{1,0},{2,1},{3,2},{4,7},{5,4},{6,5},{7,6},{8,11},{9,8},{10,9... | collective-permute-start | bytes 393224 | tf_op jit(solution)/shard_map/ppermute | solution.py:313
  34.8 1.2 %collective-permute-start.7 = (bf16[64,1024]{1,0:T(8,128)(2,1)S(1)}, bf16[64,1024]{1,0:T(8,128)(2,1)S(1)}, u32[]{:S(2)}, u32[]{:S(2)}) collective-permute-start(bf16[64,1024]{1,0:T(8,128)(2,1)S(1)} %get-tuple-element.33), channel_id=1, source_target_pairs={{0,2},{1,3},{2,0},{3,1},{4,6},{5,7},{6,4},{7,5},{8,10},{9,11},{10,... | collective-permute-start | bytes 393224 | tf_op jit(solution)/shard_map/ppermute | solution.py:313
  35.9 0.9 collective-permute-start.8
  36.9 4.8 %collective-permute-done.11.part3 = bf16[64,1024]{1,0:T(8,128)(2,1)S(1)} collective-permute-done((bf16[64,1024]{1,0:T(8,128)(2,1)S(1)}, bf16[64,1024]{1,0:T(8,128)(2,1)S(1)}, u32[]{:S(2)}, u32[]{:S(2)}) %collective-permute-start.11) | collective-permute-done | bytes 131104 | tf_op jit(solution)/shard_map/ppermute | solution.py:313
  41.6 0.2 activation0.1
  41.8 0.1 collective-permute-start.14
  41.9 0.1 collective-permute-start.13
  42.0 1.4 %collective-permute-start.12 = (bf16[64,1024]{1,0:T(8,128)(2,1)S(1)}, bf16[64,1024]{1,0:T(8,128)(2,1)S(1)}, u32[]{:S(2)}, u32[]{:S(2)}) collective-permute-start(bf16[64,1024]{1,0:T(8,128)(2,1)S(1)} %get-tuple-element.41.refs_7_.grad0.refs_0_), channel_id=1, source_target_pairs={{0,1},{1,2},{2,3},{3,0},{4,5},{5,6},{6,7},{7,4},{8,9},{9,10},{10,1... | collective-permute-start | bytes 393224 | tf_op jit(solution)/shard_map/ppermute | solution.py:313
  43.4 3.2 %collective-permute-done.8.part3 = bf16[64,1024]{1,0:T(8,128)(2,1)S(1)} collective-permute-done((bf16[64,1024]{1,0:T(8,128)(2,1)S(1)}, bf16[64,1024]{1,0:T(8,128)(2,1)S(1)}, u32[]{:S(2)}, u32[]{:S(2)}) %collective-permute-start.8) | collective-permute-done | bytes 131104 | tf_op jit(solution)/shard_map/ppermute | solution.py:313
  46.6 0.8 activation8.1
  47.4 0.4 collective-permute-start.16
  47.8 1.1 %collective-permute-start.15 = (bf16[64,1024]{1,0:T(8,128)(2,1)S(1)}, bf16[64,1024]{1,0:T(8,128)(2,1)S(1)}, u32[]{:S(2)}, u32[]{:S(2)}) collective-permute-start(bf16[64,1024]{1,0:T(8,128)(2,1)S(1)} %get-tuple-element.42.grad0.refs_4_), channel_id=1, source_target_pairs={{0,1},{1,2},{2,3},{3,0},{4,5},{5,6},{6,7},{7,4},{8,9},{9,10},{10,1... | collective-permute-start | bytes 393224 | tf_op jit(solution)/shard_map/ppermute | solution.py:313
  48.9 2.2 %collective-permute-done.12.grad1.refs_1_ = bf16[64,1024]{1,0:T(8,128)(2,1)S(1)} collective-permute-done((bf16[64,1024]{1,0:T(8,128)(2,1)S(1)}, bf16[64,1024]{1,0:T(8,128)(2,1)S(1)}, u32[]{:S(2)}, u32[]{:S(2)}) %collective-permute-start.12) | collective-permute-done | bytes 131104 | tf_op jit(solution)/shard_map/ppermute | solution.py:313
  51.1 2.1 %weight_grad0.1.held = f32[1792,256]{1,0:T(8,128)S(1)} custom-call(s32[27,16]{1,0:T(8,128)S(1)} %copy.11.neighbour, bf16[64,2048]{1,0:T(8,128)(2,1)S(1)} %copy-done.2, bf16[32,64,128]{2,1,0:T(8,128)(2,1)S(1)} %all-to-all-done.incoming, bf16[64,1024]{1,0:T(8,128)(2,1)S(1)} %get-tuple-element.41.refs_7_.grad0.refs_0_, ...), custom_call_target="tpu_custom_call" | custom-call | flops 939524096 | bytes 4194304 | tf_op jit(solution)/shard_map/weight_grad0/pallas_call | solution.py:399
  53.2 0.3 collective-permute-done.16.grad2.refs_6_
  53.5 3.2 %collective-permute-done.15.grad1.refs_5_ = bf16[64,1024]{1,0:T(8,128)(2,1)S(1)} collective-permute-done((bf16[64,1024]{1,0:T(8,128)(2,1)S(1)}, bf16[64,1024]{1,0:T(8,128)(2,1)S(1)}, u32[]{:S(2)}, u32[]{:S(2)}) %collective-permute-start.15) | collective-permute-done | bytes 131104 | tf_op jit(solution)/shard_map/ppermute | solution.py:313
  56.8 2.2 %weight_grad8.1 = (f32[14,4,32,128]{3,2,1,0:T(8,128)S(1)}, bf16[14,4,32,128]{3,2,1,0:T(8,128)(2,1)S(1)}) custom-call(s32[1]{0:T(128)} %bitcast.1.core, s32[27,16]{1,0:T(8,128)S(1)} %copy.11.neighbour, bf16[64,2048]{1,0:T(8,128)(2,1)S(1)} %copy-done.2, bf16[32,64,128]{2,1,0:T(8,128)(2,1)S(1)} %all-to-all-done.incoming, ...), custom_call_target="tpu_custom_call" | custom-call | flops 939524096 | bytes 4194304 | tf_op jit(solution)/shard_map/weight_grad8/pallas_call | solution.py:399
  59.0 1.4 %collective-permute-start.18 = (bf16[14,4,32,128]{3,2,1,0:T(8,128)(2,1)S(1)}, bf16[14,4,32,128]{3,2,1,0:T(8,128)(2,1)S(1)}, u32[]{:S(2)}, u32[]{:S(2)}) collective-permute-start(bf16[14,4,32,128]{3,2,1,0:T(8,128)(2,1)S(1)} %get-tuple-element.44), channel_id=1, source_target_pairs={{0,4},{4,0},{8,12},{12,8},{16,20},{20,16},{24,28},{28,24},{32,36},... | collective-permute-start | bytes 1376264 | tf_op jit(solution)/shard_map/ppermute | solution.py:323
  60.5 1.4 %collective-permute-done.18.arrived = bf16[14,4,32,128]{3,2,1,0:T(8,128)(2,1)S(1)} collective-permute-done((bf16[14,4,32,128]{3,2,1,0:T(8,128)(2,1)S(1)}, bf16[14,4,32,128]{3,2,1,0:T(8,128)(2,1)S(1)}, u32[]{:S(2)}, u32[]{:S(2)}) %collective-permute-start.18) | collective-permute-done | bytes 458784 | tf_op jit(solution)/shard_map/ppermute | solution.py:323
  61.9 0.9 pair_sum.1.refs_8_
  62.8 8.0 %all-to-all-start.1 = ((bf16[64,32,128]{2,1,0:T(8,128)(2,1)}), bf16[64,32,128]{2,1,0:T(8,128)(2,1)S(1)}, u32[]{:S(2)}, u32[]{:S(2)}) async-start(bf16[64,32,128]{2,1,0:T(8,128)(2,1)} %bitcast.2), calls=%async_computation.1 | async-start | bytes 1048576 | tf_op jit(solution)/shard_map/all_to_all | solution.py:417
  70.8 0.3 join.1.weight_t
  71.1 5.8 %table_grad.1 = (f32[64,2048]{1,0:T(8,128)S(1)}, bf16[16,64,128]{2,1,0:T(8,128)(2,1)S(1)}, bf16[16,64,128]{2,1,0:T(8,128)(2,1)S(1)}) custom-call(s32[1]{0:T(128)} %bitcast.1.core, s32[27,16]{1,0:T(8,128)S(1)} %copy.11.neighbour, bf16[1792,256]{1,0:T(8,128)(2,1)S(1)} %join.1.weight_t, bf16[64,1024]{1,0:T(8,128)(2,1)S(1)} %get-tuple-element.41.refs_7_.grad0.refs_0_, ...), custom_call_target="tpu_custom_call" | custom-call | flops 1879048192 | bytes 4194304 | tf_op jit(solution)/shard_map/table_grad/pallas_call | solution.py:427
  76.9 0.7 collective-permute-start.19
  77.7 1.2 %collective-permute-done.19.away = bf16[16,64,128]{2,1,0:T(8,128)(2,1)S(1)} collective-permute-done((bf16[16,64,128]{2,1,0:T(8,128)(2,1)S(1)}, bf16[16,64,128]{2,1,0:T(8,128)(2,1)S(1)}, u32[]{:S(2)}, u32[]{:S(2)}) %collective-permute-start.19) | collective-permute-done | bytes 262176 | tf_op jit(solution)/shard_map/ppermute | solution.py:323
  78.8 4.2 %all-to-all-done.1 = bf16[64,32,128]{2,1,0:T(8,128)(2,1)S(1)} async-done(((bf16[64,32,128]{2,1,0:T(8,128)(2,1)}), bf16[64,32,128]{2,1,0:T(8,128)(2,1)S(1)}, u32[]{:S(2)}, u32[]{:S(2)}) %all-to-all-start.1) | async-done | bytes 524320 | tf_op jit(solution)/shard_map/all_to_all | solution.py:417
  83.1 0.2 sum_parts.1
  83.2 18.3 %all_to_all.15.mixed.mine = bf16[16,8,32,128]{3,2,1,0:T(8,128)(2,1)S(1)} all-to-all(bf16[16,8,32,128]{3,2,1,0:T(8,128)(2,1)S(1)} %sum_parts.1), channel_id=1, replica_groups={{0,8,16,24,32,40,48,56,64,72,80,88,96,104,112,120},{4,12,20,28,36,44,52..., dimensions={0} | all-to-all | bytes 2097152 | tf_op jit(solution)/shard_map/all_to_all | solution.py:447
  101.5 2.9 %collective-permute-start.20 = (bf16[16,8,32,128]{3,2,1,0:T(8,128)(2,1)S(1)}, bf16[16,8,32,128]{3,2,1,0:T(8,128)(2,1)S(1)}, u32[]{:S(2)}, u32[]{:S(2)}) collective-permute-start(bf16[16,8,32,128]{3,2,1,0:T(8,128)(2,1)S(1)} %all_to_all.15.mixed.mine), channel_id=1, source_target_pairs={{0,4},{4,0},{8,12},{12,8},{16,20},{20,16},{24,28},{28,24},{32,36},... | collective-permute-start | bytes 3145736 | tf_op jit(solution)/shard_map/ppermute | solution.py:323
  104.4 1.6 %return_add.1 = f32[64,2048]{1,0:T(8,128)} custom-call(s32[1]{0:T(128)} %bitcast.1.core, s32[1,32]{1,0:T(1,128)S(1)} %copy-done.4, s32[1,32]{1,0:T(1,128)S(1)} %copy-done.5, f32[64,2048]{1,0:T(8,128)S(1)} %get-tuple-element.45.local, bf16[16,8,32,128]{3,2,1,0:T(8,128)(2,1)S(1)} %all_to_all.15.mixed.mine), custom_call_target="tpu_custom_call" | custom-call | bytes 2097152 | tf_op jit(solution)/shard_map/return_add/pallas_call | solution.py:448
  106.1 0.6 collective-permute-done.20.other
  106.7 1.3 %unpack.1 = (f32[27,64,256]{2,1,0:T(8,128)}, f32[64,256]{1,0:T(8,128)}) custom-call(s32[1]{0:T(128)} %bitcast.1.core, bf16[16,8,32,128]{3,2,1,0:T(8,128)(2,1)S(1)} %all_to_all.15.mixed.mine, bf16[16,8,32,128]{3,2,1,0:T(8,128)(2,1)S(1)} %collective-permute-done.20.other), custom_call_target="tpu_custom_call" | custom-call | bytes 3145728 | tf_op jit(solution)/shard_map/unpack/pallas_call | solution.py:451
  (27 shorter events, 0.1 us)
Async XLA Ops:
  0.6 25.8 %copy-start.2 = (bf16[64,2048]{1,0:T(8,128)(2,1)S(1)}, bf16[64,2048]{1,0:T(8,128)(2,1)}, u32[]{:S(2)}) copy-start(bf16[64,2048]{1,0:T(8,128)(2,1)} %features.5) | copy-start | bytes 786436
  0.6 10.7 %copy-start.3 = (bf16[64,256]{1,0:T(8,128)(2,1)S(1)}, bf16[64,256]{1,0:T(8,128)(2,1)}, u32[]{:S(2)}) copy-start(bf16[64,256]{1,0:T(8,128)(2,1)} %coarse_weight.1) | copy-start | bytes 98308
  0.7 10.7 %copy-start.1 = (bf16[27,64,256]{2,1,0:T(8,128)(2,1)S(1)}, bf16[27,64,256]{2,1,0:T(8,128)(2,1)}, u32[]{:S(2)}) copy-start(bf16[27,64,256]{2,1,0:T(8,128)(2,1)} %conv_weight.1) | copy-start | bytes 2654212
  0.7 24.8 %copy-start.6 = (s32[27,16]{0,1:T(8,128)S(1)}, s32[27,16]{0,1:T(8,128)}, u32[]{:S(2)}) copy-start(s32[27,16]{0,1:T(8,128)} %param.13) | copy-start | bytes 5188
  2.7 23.7 %all-to-all-start = ((bf16[32,64,128]{2,1,0:T(8,128)(2,1)}), bf16[32,64,128]{2,1,0:T(8,128)(2,1)S(1)}, u32[]{:S(2)}, u32[]{:S(2)}) async-start(bf16[32,64,128]{2,1,0:T(8,128)(2,1)} %pack.1), calls=%async_computation | async-start | bytes 1048576 | tf_op jit(solution)/shard_map/all_to_all | solution.py:349
  11.6 5.0 %collective-permute-start = (bf16[7,64,128]{2,1,0:T(8,128)(2,1)S(1)}, bf16[7,64,128]{2,1,0:T(8,128)(2,1)S(1)}, u32[]{:S(2)}, u32[]{:S(2)}) collective-permute-start(bf16[7,64,128]{2,1,0:T(8,128)(2,1)S(1)} %get-tuple-element.28), channel_id=1, source_target_pairs={{0,1},{1,0},{2,3},{3,2},{4,5},{5,4},{6,7},{7,6},{8,9},{9,8},{10,11... | collective-permute-start | bytes 344072 | tf_op jit(solution)/shard_map/ppermute | solution.py:318
  13.4 8.9 %collective-permute-start.1 = (bf16[7,64,128]{2,1,0:T(8,128)(2,1)S(1)}, bf16[7,64,128]{2,1,0:T(8,128)(2,1)S(1)}, u32[]{:S(2)}, u32[]{:S(2)}) collective-permute-start(bf16[7,64,128]{2,1,0:T(8,128)(2,1)S(1)} %get-tuple-element.29), channel_id=1, source_target_pairs={{0,2},{1,3},{2,0},{3,1},{4,6},{5,7},{6,4},{7,5},{8,10},{9,11},{10,... | collective-permute-start | bytes 344072 | tf_op jit(solution)/shard_map/ppermute | solution.py:318
  16.7 8.1 %collective-permute-start.2 = (bf16[7,64,128]{2,1,0:T(8,128)(2,1)S(1)}, bf16[7,64,128]{2,1,0:T(8,128)(2,1)S(1)}, u32[]{:S(2)}, u32[]{:S(2)}) collective-permute-start(bf16[7,64,128]{2,1,0:T(8,128)(2,1)S(1)} %get-tuple-element.30), channel_id=1, source_target_pairs={{0,3},{1,2},{2,1},{3,0},{4,7},{5,6},{6,5},{7,4},{8,11},{9,10},{10,... | collective-permute-start | bytes 344072 | tf_op jit(solution)/shard_map/ppermute | solution.py:318
  16.7 8.9 %collective-permute-start.3 = (bf16[7,64,128]{2,1,0:T(8,128)(2,1)S(1)}, bf16[7,64,128]{2,1,0:T(8,128)(2,1)S(1)}, u32[]{:S(2)}, u32[]{:S(2)}) collective-permute-start(bf16[7,64,128]{2,1,0:T(8,128)(2,1)S(1)} %collective-permute-done.refs_1_), channel_id=1, source_target_pairs={{0,4},{4,0},{8,12},{12,8},{16,20},{20,16},{24,28},{28,24},{32,36},... | collective-permute-start | bytes 344072 | tf_op jit(solution)/shard_map/ppermute | solution.py:323
  22.2 3.3 %collective-permute-start.4 = (bf16[7,64,128]{2,1,0:T(8,128)(2,1)S(1)}, bf16[7,64,128]{2,1,0:T(8,128)(2,1)S(1)}, u32[]{:S(2)}, u32[]{:S(2)}) collective-permute-start(bf16[7,64,128]{2,1,0:T(8,128)(2,1)S(1)} %collective-permute-done.1.refs_2_), channel_id=1, source_target_pairs={{0,4},{4,0},{8,12},{12,8},{16,20},{20,16},{24,28},{28,24},{32,36},... | collective-permute-start | bytes 344072 | tf_op jit(solution)/shard_map/ppermute | solution.py:323
  24.8 1.7 %collective-permute-start.5 = (bf16[7,64,128]{2,1,0:T(8,128)(2,1)S(1)}, bf16[7,64,128]{2,1,0:T(8,128)(2,1)S(1)}, u32[]{:S(2)}, u32[]{:S(2)}) collective-permute-start(bf16[7,64,128]{2,1,0:T(8,128)(2,1)S(1)} %collective-permute-done.2.refs_3_), channel_id=1, source_target_pairs={{0,4},{4,0},{8,12},{12,8},{16,20},{20,16},{24,28},{28,24},{32,36},... | collective-permute-start | bytes 344072 | tf_op jit(solution)/shard_map/ppermute | solution.py:323
  26.4 15.2 %copy-start = (bf16[64,2048]{1,0:T(8,128)(2,1)S(1)}, bf16[64,2048]{1,0:T(8,128)(2,1)}, u32[]{:S(2)}) copy-start(bf16[64,2048]{1,0:T(8,128)(2,1)} %out_grad.3) | copy-start | bytes 786436
  30.8 5.1 %collective-permute-start.9 = (bf16[64,1024]{1,0:T(8,128)(2,1)S(1)}, bf16[64,1024]{1,0:T(8,128)(2,1)S(1)}, u32[]{:S(2)}, u32[]{:S(2)}) collective-permute-start(bf16[64,1024]{1,0:T(8,128)(2,1)S(1)} %get-tuple-element.36), channel_id=1, source_target_pairs={{0,3},{1,0},{2,1},{3,2},{4,7},{5,4},{6,5},{7,6},{8,11},{9,8},{10,9... | collective-permute-start | bytes 393224 | tf_op jit(solution)/shard_map/ppermute | solution.py:313
  31.1 5.8 %collective-permute-start.10 = (bf16[64,1024]{1,0:T(8,128)(2,1)S(1)}, bf16[64,1024]{1,0:T(8,128)(2,1)S(1)}, u32[]{:S(2)}, u32[]{:S(2)}) collective-permute-start(bf16[64,1024]{1,0:T(8,128)(2,1)S(1)} %get-tuple-element.37), channel_id=1, source_target_pairs={{0,2},{1,3},{2,0},{3,1},{4,6},{5,7},{6,4},{7,5},{8,10},{9,11},{10,... | collective-permute-start | bytes 393224 | tf_op jit(solution)/shard_map/ppermute | solution.py:313
  31.4 10.2 %collective-permute-start.11 = (bf16[64,1024]{1,0:T(8,128)(2,1)S(1)}, bf16[64,1024]{1,0:T(8,128)(2,1)S(1)}, u32[]{:S(2)}, u32[]{:S(2)}) collective-permute-start(bf16[64,1024]{1,0:T(8,128)(2,1)S(1)} %get-tuple-element.38), channel_id=1, source_target_pairs={{0,1},{1,2},{2,3},{3,0},{4,5},{5,6},{6,7},{7,4},{8,9},{9,10},{10,1... | collective-permute-start | bytes 393224 | tf_op jit(solution)/shard_map/ppermute | solution.py:313
  32.4 9.6 %collective-permute-start.6 = (bf16[64,1024]{1,0:T(8,128)(2,1)S(1)}, bf16[64,1024]{1,0:T(8,128)(2,1)S(1)}, u32[]{:S(2)}, u32[]{:S(2)}) collective-permute-start(bf16[64,1024]{1,0:T(8,128)(2,1)S(1)} %get-tuple-element.32), channel_id=1, source_target_pairs={{0,3},{1,0},{2,1},{3,2},{4,7},{5,4},{6,5},{7,6},{8,11},{9,8},{10,9... | collective-permute-start | bytes 393224 | tf_op jit(solution)/shard_map/ppermute | solution.py:313
  34.8 8.6 %collective-permute-start.7 = (bf16[64,1024]{1,0:T(8,128)(2,1)S(1)}, bf16[64,1024]{1,0:T(8,128)(2,1)S(1)}, u32[]{:S(2)}, u32[]{:S(2)}) collective-permute-start(bf16[64,1024]{1,0:T(8,128)(2,1)S(1)} %get-tuple-element.33), channel_id=1, source_target_pairs={{0,2},{1,3},{2,0},{3,1},{4,6},{5,7},{6,4},{7,5},{8,10},{9,11},{10,... | collective-permute-start | bytes 393224 | tf_op jit(solution)/shard_map/ppermute | solution.py:313
  35.9 10.6 %collective-permute-start.8 = (bf16[64,1024]{1,0:T(8,128)(2,1)S(1)}, bf16[64,1024]{1,0:T(8,128)(2,1)S(1)}, u32[]{:S(2)}, u32[]{:S(2)}) collective-permute-start(bf16[64,1024]{1,0:T(8,128)(2,1)S(1)} %get-tuple-element.34), channel_id=1, source_target_pairs={{0,1},{1,2},{2,3},{3,0},{4,5},{5,6},{6,7},{7,4},{8,9},{9,10},{10,1... | collective-permute-start | bytes 393224 | tf_op jit(solution)/shard_map/ppermute | solution.py:313
  41.8 6.0 %collective-permute-start.14 = (bf16[64,1024]{1,0:T(8,128)(2,1)S(1)}, bf16[64,1024]{1,0:T(8,128)(2,1)S(1)}, u32[]{:S(2)}, u32[]{:S(2)}) collective-permute-start(bf16[64,1024]{1,0:T(8,128)(2,1)S(1)} %get-tuple-element.41.refs_7_.grad0.refs_0_), channel_id=1, source_target_pairs={{0,3},{1,0},{2,1},{3,2},{4,7},{5,4},{6,5},{7,6},{8,11},{9,8},{10,9... | collective-permute-start | bytes 393224 | tf_op jit(solution)/shard_map/ppermute | solution.py:313
  41.9 7.0 %collective-permute-start.13 = (bf16[64,1024]{1,0:T(8,128)(2,1)S(1)}, bf16[64,1024]{1,0:T(8,128)(2,1)S(1)}, u32[]{:S(2)}, u32[]{:S(2)}) collective-permute-start(bf16[64,1024]{1,0:T(8,128)(2,1)S(1)} %get-tuple-element.41.refs_7_.grad0.refs_0_), channel_id=1, source_target_pairs={{0,2},{1,3},{2,0},{3,1},{4,6},{5,7},{6,4},{7,5},{8,10},{9,11},{10,... | collective-permute-start | bytes 393224 | tf_op jit(solution)/shard_map/ppermute | solution.py:313
  42.0 9.1 %collective-permute-start.12 = (bf16[64,1024]{1,0:T(8,128)(2,1)S(1)}, bf16[64,1024]{1,0:T(8,128)(2,1)S(1)}, u32[]{:S(2)}, u32[]{:S(2)}) collective-permute-start(bf16[64,1024]{1,0:T(8,128)(2,1)S(1)} %get-tuple-element.41.refs_7_.grad0.refs_0_), channel_id=1, source_target_pairs={{0,1},{1,2},{2,3},{3,0},{4,5},{5,6},{6,7},{7,4},{8,9},{9,10},{10,1... | collective-permute-start | bytes 393224 | tf_op jit(solution)/shard_map/ppermute | solution.py:313
  47.4 5.8 %collective-permute-start.17 = (bf16[64,1024]{1,0:T(8,128)(2,1)S(1)}, bf16[64,1024]{1,0:T(8,128)(2,1)S(1)}, u32[]{:S(2)}, u32[]{:S(2)}) collective-permute-start(bf16[64,1024]{1,0:T(8,128)(2,1)S(1)} %get-tuple-element.42.grad0.refs_4_), channel_id=1, source_target_pairs={{0,3},{1,0},{2,1},{3,2},{4,7},{5,4},{6,5},{7,6},{8,11},{9,8},{10,9... | collective-permute-start | bytes 393224 | tf_op jit(solution)/shard_map/ppermute | solution.py:313
  47.4 6.1 %collective-permute-start.16 = (bf16[64,1024]{1,0:T(8,128)(2,1)S(1)}, bf16[64,1024]{1,0:T(8,128)(2,1)S(1)}, u32[]{:S(2)}, u32[]{:S(2)}) collective-permute-start(bf16[64,1024]{1,0:T(8,128)(2,1)S(1)} %get-tuple-element.42.grad0.refs_4_), channel_id=1, source_target_pairs={{0,2},{1,3},{2,0},{3,1},{4,6},{5,7},{6,4},{7,5},{8,10},{9,11},{10,... | collective-permute-start | bytes 393224 | tf_op jit(solution)/shard_map/ppermute | solution.py:313
  47.8 9.0 %collective-permute-start.15 = (bf16[64,1024]{1,0:T(8,128)(2,1)S(1)}, bf16[64,1024]{1,0:T(8,128)(2,1)S(1)}, u32[]{:S(2)}, u32[]{:S(2)}) collective-permute-start(bf16[64,1024]{1,0:T(8,128)(2,1)S(1)} %get-tuple-element.42.grad0.refs_4_), channel_id=1, source_target_pairs={{0,1},{1,2},{2,3},{3,0},{4,5},{5,6},{6,7},{7,4},{8,9},{9,10},{10,1... | collective-permute-start | bytes 393224 | tf_op jit(solution)/shard_map/ppermute | solution.py:313
  59.0 2.9 %collective-permute-start.18 = (bf16[14,4,32,128]{3,2,1,0:T(8,128)(2,1)S(1)}, bf16[14,4,32,128]{3,2,1,0:T(8,128)(2,1)S(1)}, u32[]{:S(2)}, u32[]{:S(2)}) collective-permute-start(bf16[14,4,32,128]{3,2,1,0:T(8,128)(2,1)S(1)} %get-tuple-element.44), channel_id=1, source_target_pairs={{0,4},{4,0},{8,12},{12,8},{16,20},{20,16},{24,28},{28,24},{32,36},... | collective-permute-start | bytes 1376264 | tf_op jit(solution)/shard_map/ppermute | solution.py:323
  62.8 20.3 %all-to-all-start.1 = ((bf16[64,32,128]{2,1,0:T(8,128)(2,1)}), bf16[64,32,128]{2,1,0:T(8,128)(2,1)S(1)}, u32[]{:S(2)}, u32[]{:S(2)}) async-start(bf16[64,32,128]{2,1,0:T(8,128)(2,1)} %bitcast.2), calls=%async_computation.1 | async-start | bytes 1048576 | tf_op jit(solution)/shard_map/all_to_all | solution.py:417
  76.9 1.9 %collective-permute-start.19 = (bf16[16,64,128]{2,1,0:T(8,128)(2,1)S(1)}, bf16[16,64,128]{2,1,0:T(8,128)(2,1)S(1)}, u32[]{:S(2)}, u32[]{:S(2)}) collective-permute-start(bf16[16,64,128]{2,1,0:T(8,128)(2,1)S(1)} %get-tuple-element.47), channel_id=1, source_target_pairs={{0,4},{4,0},{8,12},{12,8},{16,20},{20,16},{24,28},{28,24},{32,36},... | collective-permute-start | bytes 786440 | tf_op jit(solution)/shard_map/ppermute | solution.py:323
  83.1 21.4 %copy-start.4 = (s32[1,32]{1,0:T(1,128)S(1)}, s32[1,32]{1,0:T(1,128)}, u32[]{:S(2)}) copy-start(s32[1,32]{1,0:T(1,128)} %send_block.1) | copy-start | bytes 388
  83.1 21.4 %copy-start.5 = (s32[1,32]{1,0:T(1,128)S(1)}, s32[1,32]{1,0:T(1,128)}, u32[]{:S(2)}) copy-start(s32[1,32]{1,0:T(1,128)} %send_count.1) | copy-start | bytes 388
  101.5 5.2 %collective-permute-start.20 = (bf16[16,8,32,128]{3,2,1,0:T(8,128)(2,1)S(1)}, bf16[16,8,32,128]{3,2,1,0:T(8,128)(2,1)S(1)}, u32[]{:S(2)}, u32[]{:S(2)}) collective-permute-start(bf16[16,8,32,128]{3,2,1,0:T(8,128)(2,1)S(1)} %all_to_all.15.mixed.mine), channel_id=1, source_target_pairs={{0,4},{4,0},{8,12},{12,8},{16,20},{20,16},{24,28},{28,24},{32,36},... | collective-permute-start | bytes 3145736 | tf_op jit(solution)/shard_map/ppermute | solution.py:323

commit v10 on v9

--- a/solution.py
+++ b/solution.py
@@ -111,42 +111,42 @@
     return jnp.where(named < 0, extent, named)
 
 
-def fill_gathered(neighbour, table, gathered, first, extent):
+def gather(neighbour, table, gathered, first, blocks, offsets):
     quarter = table.shape[1]
-    nblocks = gathered.shape[1] // BLOCK
-
-    def step(offset, carry):
-        rows = pl.ds(pl.multiple_of(offset * quarter, quarter), quarter)
-        for block in range(nblocks):
-            picked = table[slot(neighbour, offset, first + block, extent)]
-            gathered[rows, block * BLOCK : (block + 1) * BLOCK] = picked
-        return carry
-
-    lax.fori_loop(0, OFFSETS, step, 0, unroll=27)
-    mean = mean_matrix()
-    for block in range(nblocks):
-        pooled = jnp.dot(table[first + block], mean, preferred_element_type=F32).astype(BF)
-        gathered[OFFSETS * quarter :, block * BLOCK : (block + 1) * BLOCK] = pooled
+    extent = table.shape[0] - 1
+    for offset in offsets:
+        rows = slice(offset * quarter, (offset + 1) * quarter)
+        for block in blocks:
+            cut = slice(block * BLOCK, (block + 1) * BLOCK)
+            if offset < OFFSETS:
+                gathered[rows, cut] = table[slot(neighbour, offset, first + block, extent)]
+            else:
+                pooled = jnp.dot(table[first + block], mean_matrix(), preferred_element_type=F32)
+                gathered[rows, cut] = pooled.astype(BF)
 
 
 def forward_kernel(place, core, neighbour, features, incoming, *refs):
     pieces, outs, (weight, table, gathered) = refs[:7], refs[7:-3], refs[-3:]
     quarter, row_count = features.shape
     nblocks = row_count // BLOCK
-    extent = nblocks + incoming.shape[0]
     for pair in range(PAIRS):
         for step, tile in enumerate(weight_tiles(place, core, pieces, pair)):
             rows = slice(step * quarter, (step + 1) * quarter)
             weight[rows, pair * BLOCK : (pair + 1) * BLOCK] = tile
     fill_table(features, incoming, table, nblocks)
-    for part, first in enumerate(CUTS[:-1]):
-        width = outs[4 * part].shape[1]
-        fill_gathered(neighbour, table, gathered.at[:, :width], first, extent)
-        for tile in range(width // 256):
-            cut = slice(tile * 256, (tile + 1) * 256)
-            total = jnp.dot(weight[...], gathered[:, cut], preferred_element_type=F32)
-            for step, out in enumerate(outs[4 * part : 4 * part + 4]):
-                out[:, cut] = total[step * quarter : (step + 1) * quarter].astype(out.dtype)
+    for tile in range(nblocks // 2):
+        if tile == 0:
+            gather(neighbour, table, gathered, 0, range(2), range(TERMS))
+        if tile < nblocks // 2 - 1:
+            ahead = range(2 * tile + 2, 2 * tile + 4)
+            gather(neighbour, table, gathered, 0, ahead, range(TERMS))
+        read = slice(tile * 256, (tile + 1) * 256)
+        total = jnp.dot(weight[...], gathered[:, read], preferred_element_type=F32)
+        part = sum(2 * tile >= cut for cut in CUTS[1:])
+        start = (2 * tile - CUTS[part]) * BLOCK
+        for step, out in enumerate(outs[4 * part : 4 * part + 4]):
+            value = total[step * quarter : (step + 1) * quarter]
+            out[:, start : start + 256] = value.astype(out.dtype)
 
 
 def activate(own, part1, part2, part3, out_grad):
@@ -171,43 +171,42 @@
     output[:, cut], grad[...] = activate(own, part1, part2, part3, out_grad[:, cut])
 
 
-def prepare_weight(first, neighbour, features, incoming, grads, table, gathered, flipped):
+def weight_products(first, neighbour, features, incoming, grads, table, gathered, flipped):
     nblocks = features.shape[1] // BLOCK
-    extent = nblocks + incoming.shape[0]
+    blocks = range(gathered.shape[1] // BLOCK)
     fill_table(features, incoming, table, nblocks)
-    fill_gathered(neighbour, table, gathered, first, extent)
-    for block in range(gathered.shape[1] // BLOCK):
+    for block in blocks:
         cut = slice(block * BLOCK, (block + 1) * BLOCK)
         tall = jnp.concatenate([g[:, cut] for g in grads], axis=0)
         flipped[cut, :] = tall.T
+    for pair in range(PAIRS):
+        if pair == 0:
+            gather(neighbour, table, gathered, first, blocks, range(2))
+        if pair < PAIRS - 1:
+            gather(neighbour, table, gathered, first, blocks, range(2 * pair + 2, 2 * pair + 4))
+        rows = slice(pair * BLOCK, (pair + 1) * BLOCK)
+        yield pair, rows, jnp.dot(gathered[rows, :], flipped[...], preferred_element_type=F32)
 
 
 def weight_first_kernel(
     first, neighbour, features, incoming, grad0, grad1, grad2, grad3, held, table, gathered, flipped
 ):
     grads = (grad0, grad1, grad2, grad3)
-    prepare_weight(first, neighbour, features, incoming, grads, table, gathered, flipped)
-    held[...] = jnp.dot(gathered[...], flipped[...], preferred_element_type=F32)
-
-
-def weight_more_kernel(
-    first, neighbour, features, incoming, grad0, grad1, grad2, grad3, held, more, table, gathered, flipped
-):
-    grads = (grad0, grad1, grad2, grad3)
-    prepare_weight(first, neighbour, features, incoming, grads, table, gathered, flipped)
-    more[...] = held[...] + jnp.dot(gathered[...], flipped[...], preferred_element_type=F32)
+    for _, rows, product in weight_products(
+        first, neighbour, features, incoming, grads, table, gathered, flipped
+    ):
+        held[rows, :] = product
 
 
 def weight_last_kernel(
     first, core, neighbour, features, incoming, grad0, grad1, grad2, grad3, held, keep, give, table, gathered, flipped
 ):
     quarter = features.shape[0]
+    half = quarter // 2
     grads = (grad0, grad1, grad2, grad3)
-    prepare_weight(first, neighbour, features, incoming, grads, table, gathered, flipped)
-    half = quarter // 2
-    for pair in range(PAIRS):
-        rows = slice(pair * BLOCK, (pair + 1) * BLOCK)
-        product = jnp.dot(gathered[rows, :], flipped[...], preferred_element_type=F32)
+    for pair, rows, product in weight_products(
+        first, neighbour, features, incoming, grads, table, gathered, flipped
+    ):
         upright = (product + held[rows, :]).T
         for step in range(4):
             low = upright[step * quarter : step * quarter + half]
@@ -368,7 +367,7 @@
         "forward",
         [shape((quarter, w), BF if s else F32) for w in widths for s in range(4)],
         "sss" + "v" * 9,
-        [pltpu.VMEM((channels, depth), BF), table, pltpu.VMEM((depth, max(widths)), BF)],
+        [pltpu.VMEM((channels, depth), BF), table, pltpu.VMEM((depth, row_count), BF)],
         flops,
         3 << 20,
     )(place, core, neighbour, features, incoming, *weights)
@@ -394,7 +393,7 @@
     for (first, end), given in zip(zip(CUTS, CUTS[1:]), grads):
         width = (end - first) * BLOCK
         last = end == CUTS[-1]
-        kernel = weight_last_kernel if last else weight_more_kernel if held else weight_first_kernel
+        kernel = weight_last_kernel if last else weight_first_kernel
         sums = [shape((PAIRS,) + piece, F32), shape((PAIRS,) + piece, BF)]
         result = call(
             functools.partial(kernel, first),

time: 108 us -> 108 us (level)
  no operation moved by 1% of the time
where the time goes in v10:
time: 108 us; the launch traced here: 107 us
  starting transfers between devices  38.3 us (35%)
  waiting for transfers between devices  28.3 us (26%)
  Pallas kernels  21.5 us (20%)
  blocking collectives  18.3 us (17%)
    all_to_all x1, blocking collectives, local_step(): lax.all_to_all(mixed, 'morton', 0, 0, axis_index_groups=same_core, tiled=...  18.3 us
    ppermute x12, waiting for transfers between devices, shift(): lax.ppermute(value, 'chan', [(i, (i + step) % size) for i in range(size)])  13.7 us
    ppermute x12, starting transfers between devices, shift(): lax.ppermute(value, 'chan', [(i, (i + step) % size) for i in range(size)])  8.96 us
    all_to_all x1, starting transfers between devices, local_step(): incoming = lax.all_to_all(outgoing, 'morton', 0, 0, tiled=True)  8.6 us
    all_to_all x1, starting transfers between devices, local_step(): lax.all_to_all(parts.reshape((4 * chips,) + piece[1:]), ('morton', 'chan'...  8.01 us
    ppermute x6, starting transfers between devices, swap_cores(): return lax.ppermute(value, 'morton', [(i, i ^ 1) for i in range(size)])  7.73 us
    ppermute x3, waiting for transfers between devices, exchange(): return lax.ppermute(value, 'chan', [(i, i ^ step) for i in range(size)])  6.18 us
    pallas_call x1, Pallas kernels, local_step(): call(table_kernel, 'table_grad', [shape(wide, F32), shape(blocks, BF), sh...  5.78 us
  transfers between devices with their start and end apart: 23, of which 13 were waited for; matrix products, arithmetic and copies ran while one was open for 0% of the time, Pallas kernels for 10%

profile of v10, /device:TPU:1, one launch (start us, length us, event | category | flops | bytes accessed | tf_op | source)
XLA Modules:
  0.0 107.3 jit_solution(5198791795795451176)
XLA Ops:
  0.7 2.0 %pack.1 = bf16[32,64,128]{2,1,0:T(8,128)(2,1)} custom-call(s32[1,32]{1,0:T(1,128)} %send_block.1, s32[1,32]{1,0:T(1,128)} %send_count.1, bf16[64,2048]{1,0:T(8,128)(2,1)} %features.5), custom_call_target="tpu_custom_call" | custom-call | bytes 1048576 | tf_op jit(solution)/shard_map/pack/pallas_call | solution.py:337
  2.7 8.6 %all-to-all-start = ((bf16[32,64,128]{2,1,0:T(8,128)(2,1)}), bf16[32,64,128]{2,1,0:T(8,128)(2,1)S(1)}, u32[]{:S(2)}, u32[]{:S(2)}) async-start(bf16[32,64,128]{2,1,0:T(8,128)(2,1)} %pack.1), calls=%async_computation | async-start | bytes 1048576 | tf_op jit(solution)/shard_map/all_to_all | solution.py:348
  11.3 0.3 split.1
  11.6 1.7 %collective-permute-start = (bf16[7,64,128]{2,1,0:T(8,128)(2,1)S(1)}, bf16[7,64,128]{2,1,0:T(8,128)(2,1)S(1)}, u32[]{:S(2)}, u32[]{:S(2)}) collective-permute-start(bf16[7,64,128]{2,1,0:T(8,128)(2,1)S(1)} %get-tuple-element.28), channel_id=1, source_target_pairs={{0,1},{1,0},{2,3},{3,2},{4,5},{5,4},{6,7},{7,6},{8,9},{9,8},{10,11... | collective-permute-start | bytes 344072 | tf_op jit(solution)/shard_map/ppermute | solution.py:317
  13.4 3.3 %collective-permute-start.1 = (bf16[7,64,128]{2,1,0:T(8,128)(2,1)S(1)}, bf16[7,64,128]{2,1,0:T(8,128)(2,1)S(1)}, u32[]{:S(2)}, u32[]{:S(2)}) collective-permute-start(bf16[7,64,128]{2,1,0:T(8,128)(2,1)S(1)} %get-tuple-element.29), channel_id=1, source_target_pairs={{0,2},{1,3},{2,0},{3,1},{4,6},{5,7},{6,4},{7,5},{8,10},{9,11},{10,... | collective-permute-start | bytes 344072 | tf_op jit(solution)/shard_map/ppermute | solution.py:317
  16.7 0.8 collective-permute-start.3
  17.5 4.7 %collective-permute-done.1.refs_2_ = bf16[7,64,128]{2,1,0:T(8,128)(2,1)S(1)} collective-permute-done((bf16[7,64,128]{2,1,0:T(8,128)(2,1)S(1)}, bf16[7,64,128]{2,1,0:T(8,128)(2,1)S(1)}, u32[]{:S(2)}, u32[]{:S(2)}) %collective-permute-start.1) | collective-permute-done | bytes 114720 | tf_op jit(solution)/shard_map/ppermute | solution.py:317
  22.2 1.1 %collective-permute-start.4 = (bf16[7,64,128]{2,1,0:T(8,128)(2,1)S(1)}, bf16[7,64,128]{2,1,0:T(8,128)(2,1)S(1)}, u32[]{:S(2)}, u32[]{:S(2)}) collective-permute-start(bf16[7,64,128]{2,1,0:T(8,128)(2,1)S(1)} %collective-permute-done.1.refs_2_), channel_id=1, source_target_pairs={{0,4},{4,0},{8,12},{12,8},{16,20},{20,16},{24,28},{28,24},{32,36},... | collective-permute-start | bytes 344072 | tf_op jit(solution)/shard_map/ppermute | solution.py:322
  23.3 1.4 %collective-permute-done.2.refs_3_ = bf16[7,64,128]{2,1,0:T(8,128)(2,1)S(1)} collective-permute-done((bf16[7,64,128]{2,1,0:T(8,128)(2,1)S(1)}, bf16[7,64,128]{2,1,0:T(8,128)(2,1)S(1)}, u32[]{:S(2)}, u32[]{:S(2)}) %collective-permute-start.2) | collective-permute-done | bytes 114720 | tf_op jit(solution)/shard_map/ppermute | solution.py:317
  24.8 0.7 collective-permute-start.5
  25.5 0.1 copy.11.neighbour
  25.6 0.9 collective-permute-done.5.refs_6_
  26.4 3.5 %forward.1 = (f32[64,1024]{1,0:T(8,128)S(1)}, bf16[64,1024]{1,0:T(8,128)(2,1)S(1)}, bf16[64,1024]{1,0:T(8,128)(2,1)S(1)}, bf16[64,1024]{1,0:T(8,128)(2,1)S(1)}, ...) custom-call(s32[1]{0:T(128)} %bitcast.place, ...), custom_call_target="tpu_custom_call" | custom-call | flops 1879048192 | bytes 3145728 | tf_op jit(solution)/shard_map/forward/pallas_call | solution.py:365
  30.0 0.2 collective-permute-start.9
  30.2 0.4 collective-permute-start.10
  30.6 0.9 collective-permute-start.11
  31.5 2.4 %collective-permute-start.6 = (bf16[64,1024]{1,0:T(8,128)(2,1)S(1)}, bf16[64,1024]{1,0:T(8,128)(2,1)S(1)}, u32[]{:S(2)}, u32[]{:S(2)}) collective-permute-start(bf16[64,1024]{1,0:T(8,128)(2,1)S(1)} %get-tuple-element.32), channel_id=1, source_target_pairs={{0,3},{1,0},{2,1},{3,2},{4,7},{5,4},{6,5},{7,6},{8,11},{9,8},{10,9... | collective-permute-start | bytes 393224 | tf_op jit(solution)/shard_map/ppermute | solution.py:312
  33.9 1.2 %collective-permute-start.7 = (bf16[64,1024]{1,0:T(8,128)(2,1)S(1)}, bf16[64,1024]{1,0:T(8,128)(2,1)S(1)}, u32[]{:S(2)}, u32[]{:S(2)}) collective-permute-start(bf16[64,1024]{1,0:T(8,128)(2,1)S(1)} %get-tuple-element.33), channel_id=1, source_target_pairs={{0,2},{1,3},{2,0},{3,1},{4,6},{5,7},{6,4},{7,5},{8,10},{9,11},{10,... | collective-permute-start | bytes 393224 | tf_op jit(solution)/shard_map/ppermute | solution.py:312
  35.1 0.9 collective-permute-start.8
  36.0 4.8 %collective-permute-done.11.part3 = bf16[64,1024]{1,0:T(8,128)(2,1)S(1)} collective-permute-done((bf16[64,1024]{1,0:T(8,128)(2,1)S(1)}, bf16[64,1024]{1,0:T(8,128)(2,1)S(1)}, u32[]{:S(2)}, u32[]{:S(2)}) %collective-permute-start.11) | collective-permute-done | bytes 131104 | tf_op jit(solution)/shard_map/ppermute | solution.py:312
  40.8 0.2 activation0.1
  41.0 0.1 collective-permute-start.14
  41.0 0.1 collective-permute-start.13
  41.2 1.4 %collective-permute-start.12 = (bf16[64,1024]{1,0:T(8,128)(2,1)S(1)}, bf16[64,1024]{1,0:T(8,128)(2,1)S(1)}, u32[]{:S(2)}, u32[]{:S(2)}) collective-permute-start(bf16[64,1024]{1,0:T(8,128)(2,1)S(1)} %get-tuple-element.41.refs_7_.grad0.refs_0_), channel_id=1, source_target_pairs={{0,1},{1,2},{2,3},{3,0},{4,5},{5,6},{6,7},{7,4},{8,9},{9,10},{10,1... | collective-permute-start | bytes 393224 | tf_op jit(solution)/shard_map/ppermute | solution.py:312
  42.5 3.2 %collective-permute-done.8.part3 = bf16[64,1024]{1,0:T(8,128)(2,1)S(1)} collective-permute-done((bf16[64,1024]{1,0:T(8,128)(2,1)S(1)}, bf16[64,1024]{1,0:T(8,128)(2,1)S(1)}, u32[]{:S(2)}, u32[]{:S(2)}) %collective-permute-start.8) | collective-permute-done | bytes 131104 | tf_op jit(solution)/shard_map/ppermute | solution.py:312
  45.7 0.8 activation8.1
  46.6 0.4 collective-permute-start.16
  46.9 1.1 %collective-permute-start.15 = (bf16[64,1024]{1,0:T(8,128)(2,1)S(1)}, bf16[64,1024]{1,0:T(8,128)(2,1)S(1)}, u32[]{:S(2)}, u32[]{:S(2)}) collective-permute-start(bf16[64,1024]{1,0:T(8,128)(2,1)S(1)} %get-tuple-element.42.grad0.refs_4_), channel_id=1, source_target_pairs={{0,1},{1,2},{2,3},{3,0},{4,5},{5,6},{6,7},{7,4},{8,9},{9,10},{10,1... | collective-permute-start | bytes 393224 | tf_op jit(solution)/shard_map/ppermute | solution.py:312
  48.0 2.2 %collective-permute-done.12.grad1.refs_1_ = bf16[64,1024]{1,0:T(8,128)(2,1)S(1)} collective-permute-done((bf16[64,1024]{1,0:T(8,128)(2,1)S(1)}, bf16[64,1024]{1,0:T(8,128)(2,1)S(1)}, u32[]{:S(2)}, u32[]{:S(2)}) %collective-permute-start.12) | collective-permute-done | bytes 131104 | tf_op jit(solution)/shard_map/ppermute | solution.py:312
  50.2 2.2 %weight_grad0.1.held = f32[1792,256]{1,0:T(8,128)S(1)} custom-call(s32[27,16]{1,0:T(8,128)S(1)} %copy.11.neighbour, bf16[64,2048]{1,0:T(8,128)(2,1)S(1)} %copy-done.2, bf16[32,64,128]{2,1,0:T(8,128)(2,1)S(1)} %all-to-all-done.incoming, bf16[64,1024]{1,0:T(8,128)(2,1)S(1)} %get-tuple-element.41.refs_7_.grad0.refs_0_, ...), custom_call_target="tpu_custom_call" | custom-call | flops 939524096 | bytes 4194304 | tf_op jit(solution)/shard_map/weight_grad0/pallas_call | solution.py:398
  52.5 0.2 collective-permute-done.16.grad2.refs_6_
  52.7 3.2 %collective-permute-done.15.grad1.refs_5_ = bf16[64,1024]{1,0:T(8,128)(2,1)S(1)} collective-permute-done((bf16[64,1024]{1,0:T(8,128)(2,1)S(1)}, bf16[64,1024]{1,0:T(8,128)(2,1)S(1)}, u32[]{:S(2)}, u32[]{:S(2)}) %collective-permute-start.15) | collective-permute-done | bytes 131104 | tf_op jit(solution)/shard_map/ppermute | solution.py:312
  55.9 2.3 %weight_grad8.1 = (f32[14,4,32,128]{3,2,1,0:T(8,128)S(1)}, bf16[14,4,32,128]{3,2,1,0:T(8,128)(2,1)S(1)}) custom-call(s32[1]{0:T(128)} %bitcast.1.core, s32[27,16]{1,0:T(8,128)S(1)} %copy.11.neighbour, bf16[64,2048]{1,0:T(8,128)(2,1)S(1)} %copy-done.2, bf16[32,64,128]{2,1,0:T(8,128)(2,1)S(1)} %all-to-all-done.incoming, ...), custom_call_target="tpu_custom_call" | custom-call | flops 939524096 | bytes 4194304 | tf_op jit(solution)/shard_map/weight_grad8/pallas_call | solution.py:398
  58.2 1.4 %collective-permute-start.18 = (bf16[14,4,32,128]{3,2,1,0:T(8,128)(2,1)S(1)}, bf16[14,4,32,128]{3,2,1,0:T(8,128)(2,1)S(1)}, u32[]{:S(2)}, u32[]{:S(2)}) collective-permute-start(bf16[14,4,32,128]{3,2,1,0:T(8,128)(2,1)S(1)} %get-tuple-element.44), channel_id=1, source_target_pairs={{0,4},{4,0},{8,12},{12,8},{16,20},{20,16},{24,28},{28,24},{32,36},... | collective-permute-start | bytes 1376264 | tf_op jit(solution)/shard_map/ppermute | solution.py:322
  59.7 1.4 %collective-permute-done.18.arrived = bf16[14,4,32,128]{3,2,1,0:T(8,128)(2,1)S(1)} collective-permute-done((bf16[14,4,32,128]{3,2,1,0:T(8,128)(2,1)S(1)}, bf16[14,4,32,128]{3,2,1,0:T(8,128)(2,1)S(1)}, u32[]{:S(2)}, u32[]{:S(2)}) %collective-permute-start.18) | collective-permute-done | bytes 458784 | tf_op jit(solution)/shard_map/ppermute | solution.py:322
  61.1 0.9 pair_sum.1.refs_8_
  62.0 8.0 %all-to-all-start.1 = ((bf16[64,32,128]{2,1,0:T(8,128)(2,1)}), bf16[64,32,128]{2,1,0:T(8,128)(2,1)S(1)}, u32[]{:S(2)}, u32[]{:S(2)}) async-start(bf16[64,32,128]{2,1,0:T(8,128)(2,1)} %bitcast.2), calls=%async_computation.1 | async-start | bytes 1048576 | tf_op jit(solution)/shard_map/all_to_all | solution.py:416
  70.0 0.3 join.1.weight_t
  70.3 5.8 %table_grad.1 = (f32[64,2048]{1,0:T(8,128)S(1)}, bf16[16,64,128]{2,1,0:T(8,128)(2,1)S(1)}, bf16[16,64,128]{2,1,0:T(8,128)(2,1)S(1)}) custom-call(s32[1]{0:T(128)} %bitcast.1.core, s32[27,16]{1,0:T(8,128)S(1)} %copy.11.neighbour, bf16[1792,256]{1,0:T(8,128)(2,1)S(1)} %join.1.weight_t, bf16[64,1024]{1,0:T(8,128)(2,1)S(1)} %get-tuple-element.41.refs_7_.grad0.refs_0_, ...), custom_call_target="tpu_custom_call" | custom-call | flops 1879048192 | bytes 4194304 | tf_op jit(solution)/shard_map/table_grad/pallas_call | solution.py:426
  76.1 0.7 collective-permute-start.19
  76.9 1.2 %collective-permute-done.19.away = bf16[16,64,128]{2,1,0:T(8,128)(2,1)S(1)} collective-permute-done((bf16[16,64,128]{2,1,0:T(8,128)(2,1)S(1)}, bf16[16,64,128]{2,1,0:T(8,128)(2,1)S(1)}, u32[]{:S(2)}, u32[]{:S(2)}) %collective-permute-start.19) | collective-permute-done | bytes 262176 | tf_op jit(solution)/shard_map/ppermute | solution.py:322
  78.0 4.2 %all-to-all-done.1 = bf16[64,32,128]{2,1,0:T(8,128)(2,1)S(1)} async-done(((bf16[64,32,128]{2,1,0:T(8,128)(2,1)}), bf16[64,32,128]{2,1,0:T(8,128)(2,1)S(1)}, u32[]{:S(2)}, u32[]{:S(2)}) %all-to-all-start.1) | async-done | bytes 524320 | tf_op jit(solution)/shard_map/all_to_all | solution.py:416
  82.3 0.2 sum_parts.1
  82.4 18.3 %all_to_all.15.mixed.mine = bf16[16,8,32,128]{3,2,1,0:T(8,128)(2,1)S(1)} all-to-all(bf16[16,8,32,128]{3,2,1,0:T(8,128)(2,1)S(1)} %sum_parts.1), channel_id=1, replica_groups={{0,8,16,24,32,40,48,56,64,72,80,88,96,104,112,120},{4,12,20,28,36,44,52..., dimensions={0} | all-to-all | bytes 2097152 | tf_op jit(solution)/shard_map/all_to_all | solution.py:446
  100.7 2.9 %collective-permute-start.20 = (bf16[16,8,32,128]{3,2,1,0:T(8,128)(2,1)S(1)}, bf16[16,8,32,128]{3,2,1,0:T(8,128)(2,1)S(1)}, u32[]{:S(2)}, u32[]{:S(2)}) collective-permute-start(bf16[16,8,32,128]{3,2,1,0:T(8,128)(2,1)S(1)} %all_to_all.15.mixed.mine), channel_id=1, source_target_pairs={{0,4},{4,0},{8,12},{12,8},{16,20},{20,16},{24,28},{28,24},{32,36},... | collective-permute-start | bytes 3145736 | tf_op jit(solution)/shard_map/ppermute | solution.py:322
  103.6 1.6 %return_add.1 = f32[64,2048]{1,0:T(8,128)} custom-call(s32[1]{0:T(128)} %bitcast.1.core, s32[1,32]{1,0:T(1,128)S(1)} %copy-done.4, s32[1,32]{1,0:T(1,128)S(1)} %copy-done.5, f32[64,2048]{1,0:T(8,128)S(1)} %get-tuple-element.45.local, bf16[16,8,32,128]{3,2,1,0:T(8,128)(2,1)S(1)} %all_to_all.15.mixed.mine), custom_call_target="tpu_custom_call" | custom-call | bytes 2097152 | tf_op jit(solution)/shard_map/return_add/pallas_call | solution.py:447
  105.3 0.6 collective-permute-done.20.other
  105.9 1.3 %unpack.1 = (f32[27,64,256]{2,1,0:T(8,128)}, f32[64,256]{1,0:T(8,128)}) custom-call(s32[1]{0:T(128)} %bitcast.1.core, bf16[16,8,32,128]{3,2,1,0:T(8,128)(2,1)S(1)} %all_to_all.15.mixed.mine, bf16[16,8,32,128]{3,2,1,0:T(8,128)(2,1)S(1)} %collective-permute-done.20.other), custom_call_target="tpu_custom_call" | custom-call | bytes 3145728 | tf_op jit(solution)/shard_map/unpack/pallas_call | solution.py:450
  (27 shorter events, 0.1 us)
Async XLA Ops:
  0.6 25.8 %copy-start.2 = (bf16[64,2048]{1,0:T(8,128)(2,1)S(1)}, bf16[64,2048]{1,0:T(8,128)(2,1)}, u32[]{:S(2)}) copy-start(bf16[64,2048]{1,0:T(8,128)(2,1)} %features.5) | copy-start | bytes 786436
  0.6 10.7 %copy-start.3 = (bf16[64,256]{1,0:T(8,128)(2,1)S(1)}, bf16[64,256]{1,0:T(8,128)(2,1)}, u32[]{:S(2)}) copy-start(bf16[64,256]{1,0:T(8,128)(2,1)} %coarse_weight.1) | copy-start | bytes 98308
  0.7 10.7 %copy-start.1 = (bf16[27,64,256]{2,1,0:T(8,128)(2,1)S(1)}, bf16[27,64,256]{2,1,0:T(8,128)(2,1)}, u32[]{:S(2)}) copy-start(bf16[27,64,256]{2,1,0:T(8,128)(2,1)} %conv_weight.1) | copy-start | bytes 2654212
  0.7 24.8 %copy-start.6 = (s32[27,16]{0,1:T(8,128)S(1)}, s32[27,16]{0,1:T(8,128)}, u32[]{:S(2)}) copy-start(s32[27,16]{0,1:T(8,128)} %param.13) | copy-start | bytes 5188
  2.7 23.7 %all-to-all-start = ((bf16[32,64,128]{2,1,0:T(8,128)(2,1)}), bf16[32,64,128]{2,1,0:T(8,128)(2,1)S(1)}, u32[]{:S(2)}, u32[]{:S(2)}) async-start(bf16[32,64,128]{2,1,0:T(8,128)(2,1)} %pack.1), calls=%async_computation | async-start | bytes 1048576 | tf_op jit(solution)/shard_map/all_to_all | solution.py:348
  11.6 5.0 %collective-permute-start = (bf16[7,64,128]{2,1,0:T(8,128)(2,1)S(1)}, bf16[7,64,128]{2,1,0:T(8,128)(2,1)S(1)}, u32[]{:S(2)}, u32[]{:S(2)}) collective-permute-start(bf16[7,64,128]{2,1,0:T(8,128)(2,1)S(1)} %get-tuple-element.28), channel_id=1, source_target_pairs={{0,1},{1,0},{2,3},{3,2},{4,5},{5,4},{6,7},{7,6},{8,9},{9,8},{10,11... | collective-permute-start | bytes 344072 | tf_op jit(solution)/shard_map/ppermute | solution.py:317
  13.4 8.9 %collective-permute-start.1 = (bf16[7,64,128]{2,1,0:T(8,128)(2,1)S(1)}, bf16[7,64,128]{2,1,0:T(8,128)(2,1)S(1)}, u32[]{:S(2)}, u32[]{:S(2)}) collective-permute-start(bf16[7,64,128]{2,1,0:T(8,128)(2,1)S(1)} %get-tuple-element.29), channel_id=1, source_target_pairs={{0,2},{1,3},{2,0},{3,1},{4,6},{5,7},{6,4},{7,5},{8,10},{9,11},{10,... | collective-permute-start | bytes 344072 | tf_op jit(solution)/shard_map/ppermute | solution.py:317
  16.7 8.1 %collective-permute-start.2 = (bf16[7,64,128]{2,1,0:T(8,128)(2,1)S(1)}, bf16[7,64,128]{2,1,0:T(8,128)(2,1)S(1)}, u32[]{:S(2)}, u32[]{:S(2)}) collective-permute-start(bf16[7,64,128]{2,1,0:T(8,128)(2,1)S(1)} %get-tuple-element.30), channel_id=1, source_target_pairs={{0,3},{1,2},{2,1},{3,0},{4,7},{5,6},{6,5},{7,4},{8,11},{9,10},{10,... | collective-permute-start | bytes 344072 | tf_op jit(solution)/shard_map/ppermute | solution.py:317
  16.7 8.9 %collective-permute-start.3 = (bf16[7,64,128]{2,1,0:T(8,128)(2,1)S(1)}, bf16[7,64,128]{2,1,0:T(8,128)(2,1)S(1)}, u32[]{:S(2)}, u32[]{:S(2)}) collective-permute-start(bf16[7,64,128]{2,1,0:T(8,128)(2,1)S(1)} %collective-permute-done.refs_1_), channel_id=1, source_target_pairs={{0,4},{4,0},{8,12},{12,8},{16,20},{20,16},{24,28},{28,24},{32,36},... | collective-permute-start | bytes 344072 | tf_op jit(solution)/shard_map/ppermute | solution.py:322
  22.2 3.3 %collective-permute-start.4 = (bf16[7,64,128]{2,1,0:T(8,128)(2,1)S(1)}, bf16[7,64,128]{2,1,0:T(8,128)(2,1)S(1)}, u32[]{:S(2)}, u32[]{:S(2)}) collective-permute-start(bf16[7,64,128]{2,1,0:T(8,128)(2,1)S(1)} %collective-permute-done.1.refs_2_), channel_id=1, source_target_pairs={{0,4},{4,0},{8,12},{12,8},{16,20},{20,16},{24,28},{28,24},{32,36},... | collective-permute-start | bytes 344072 | tf_op jit(solution)/shard_map/ppermute | solution.py:322
  24.8 1.7 %collective-permute-start.5 = (bf16[7,64,128]{2,1,0:T(8,128)(2,1)S(1)}, bf16[7,64,128]{2,1,0:T(8,128)(2,1)S(1)}, u32[]{:S(2)}, u32[]{:S(2)}) collective-permute-start(bf16[7,64,128]{2,1,0:T(8,128)(2,1)S(1)} %collective-permute-done.2.refs_3_), channel_id=1, source_target_pairs={{0,4},{4,0},{8,12},{12,8},{16,20},{20,16},{24,28},{28,24},{32,36},... | collective-permute-start | bytes 344072 | tf_op jit(solution)/shard_map/ppermute | solution.py:322
  26.4 14.4 %copy-start = (bf16[64,2048]{1,0:T(8,128)(2,1)S(1)}, bf16[64,2048]{1,0:T(8,128)(2,1)}, u32[]{:S(2)}) copy-start(bf16[64,2048]{1,0:T(8,128)(2,1)} %out_grad.3) | copy-start | bytes 786436
  30.0 5.1 %collective-permute-start.9 = (bf16[64,1024]{1,0:T(8,128)(2,1)S(1)}, bf16[64,1024]{1,0:T(8,128)(2,1)S(1)}, u32[]{:S(2)}, u32[]{:S(2)}) collective-permute-start(bf16[64,1024]{1,0:T(8,128)(2,1)S(1)} %get-tuple-element.36), channel_id=1, source_target_pairs={{0,3},{1,0},{2,1},{3,2},{4,7},{5,4},{6,5},{7,6},{8,11},{9,8},{10,9... | collective-permute-start | bytes 393224 | tf_op jit(solution)/shard_map/ppermute | solution.py:312
  30.2 5.8 %collective-permute-start.10 = (bf16[64,1024]{1,0:T(8,128)(2,1)S(1)}, bf16[64,1024]{1,0:T(8,128)(2,1)S(1)}, u32[]{:S(2)}, u32[]{:S(2)}) collective-permute-start(bf16[64,1024]{1,0:T(8,128)(2,1)S(1)} %get-tuple-element.37), channel_id=1, source_target_pairs={{0,2},{1,3},{2,0},{3,1},{4,6},{5,7},{6,4},{7,5},{8,10},{9,11},{10,... | collective-permute-start | bytes 393224 | tf_op jit(solution)/shard_map/ppermute | solution.py:312
  30.6 10.2 %collective-permute-start.11 = (bf16[64,1024]{1,0:T(8,128)(2,1)S(1)}, bf16[64,1024]{1,0:T(8,128)(2,1)S(1)}, u32[]{:S(2)}, u32[]{:S(2)}) collective-permute-start(bf16[64,1024]{1,0:T(8,128)(2,1)S(1)} %get-tuple-element.38), channel_id=1, source_target_pairs={{0,1},{1,2},{2,3},{3,0},{4,5},{5,6},{6,7},{7,4},{8,9},{9,10},{10,1... | collective-permute-start | bytes 393224 | tf_op jit(solution)/shard_map/ppermute | solution.py:312
  31.5 9.6 %collective-permute-start.6 = (bf16[64,1024]{1,0:T(8,128)(2,1)S(1)}, bf16[64,1024]{1,0:T(8,128)(2,1)S(1)}, u32[]{:S(2)}, u32[]{:S(2)}) collective-permute-start(bf16[64,1024]{1,0:T(8,128)(2,1)S(1)} %get-tuple-element.32), channel_id=1, source_target_pairs={{0,3},{1,0},{2,1},{3,2},{4,7},{5,4},{6,5},{7,6},{8,11},{9,8},{10,9... | collective-permute-start | bytes 393224 | tf_op jit(solution)/shard_map/ppermute | solution.py:312
  33.9 8.6 %collective-permute-start.7 = (bf16[64,1024]{1,0:T(8,128)(2,1)S(1)}, bf16[64,1024]{1,0:T(8,128)(2,1)S(1)}, u32[]{:S(2)}, u32[]{:S(2)}) collective-permute-start(bf16[64,1024]{1,0:T(8,128)(2,1)S(1)} %get-tuple-element.33), channel_id=1, source_target_pairs={{0,2},{1,3},{2,0},{3,1},{4,6},{5,7},{6,4},{7,5},{8,10},{9,11},{10,... | collective-permute-start | bytes 393224 | tf_op jit(solution)/shard_map/ppermute | solution.py:312
  35.1 10.6 %collective-permute-start.8 = (bf16[64,1024]{1,0:T(8,128)(2,1)S(1)}, bf16[64,1024]{1,0:T(8,128)(2,1)S(1)}, u32[]{:S(2)}, u32[]{:S(2)}) collective-permute-start(bf16[64,1024]{1,0:T(8,128)(2,1)S(1)} %get-tuple-element.34), channel_id=1, source_target_pairs={{0,1},{1,2},{2,3},{3,0},{4,5},{5,6},{6,7},{7,4},{8,9},{9,10},{10,1... | collective-permute-start | bytes 393224 | tf_op jit(solution)/shard_map/ppermute | solution.py:312
  41.0 6.0 %collective-permute-start.14 = (bf16[64,1024]{1,0:T(8,128)(2,1)S(1)}, bf16[64,1024]{1,0:T(8,128)(2,1)S(1)}, u32[]{:S(2)}, u32[]{:S(2)}) collective-permute-start(bf16[64,1024]{1,0:T(8,128)(2,1)S(1)} %get-tuple-element.41.refs_7_.grad0.refs_0_), channel_id=1, source_target_pairs={{0,3},{1,0},{2,1},{3,2},{4,7},{5,4},{6,5},{7,6},{8,11},{9,8},{10,9... | collective-permute-start | bytes 393224 | tf_op jit(solution)/shard_map/ppermute | solution.py:312
  41.0 7.0 %collective-permute-start.13 = (bf16[64,1024]{1,0:T(8,128)(2,1)S(1)}, bf16[64,1024]{1,0:T(8,128)(2,1)S(1)}, u32[]{:S(2)}, u32[]{:S(2)}) collective-permute-start(bf16[64,1024]{1,0:T(8,128)(2,1)S(1)} %get-tuple-element.41.refs_7_.grad0.refs_0_), channel_id=1, source_target_pairs={{0,2},{1,3},{2,0},{3,1},{4,6},{5,7},{6,4},{7,5},{8,10},{9,11},{10,... | collective-permute-start | bytes 393224 | tf_op jit(solution)/shard_map/ppermute | solution.py:312
  41.2 9.1 %collective-permute-start.12 = (bf16[64,1024]{1,0:T(8,128)(2,1)S(1)}, bf16[64,1024]{1,0:T(8,128)(2,1)S(1)}, u32[]{:S(2)}, u32[]{:S(2)}) collective-permute-start(bf16[64,1024]{1,0:T(8,128)(2,1)S(1)} %get-tuple-element.41.refs_7_.grad0.refs_0_), channel_id=1, source_target_pairs={{0,1},{1,2},{2,3},{3,0},{4,5},{5,6},{6,7},{7,4},{8,9},{9,10},{10,1... | collective-permute-start | bytes 393224 | tf_op jit(solution)/shard_map/ppermute | solution.py:312
  46.6 5.9 %collective-permute-start.17 = (bf16[64,1024]{1,0:T(8,128)(2,1)S(1)}, bf16[64,1024]{1,0:T(8,128)(2,1)S(1)}, u32[]{:S(2)}, u32[]{:S(2)}) collective-permute-start(bf16[64,1024]{1,0:T(8,128)(2,1)S(1)} %get-tuple-element.42.grad0.refs_4_), channel_id=1, source_target_pairs={{0,3},{1,0},{2,1},{3,2},{4,7},{5,4},{6,5},{7,6},{8,11},{9,8},{10,9... | collective-permute-start | bytes 393224 | tf_op jit(solution)/shard_map/ppermute | solution.py:312
  46.6 6.1 %collective-permute-start.16 = (bf16[64,1024]{1,0:T(8,128)(2,1)S(1)}, bf16[64,1024]{1,0:T(8,128)(2,1)S(1)}, u32[]{:S(2)}, u32[]{:S(2)}) collective-permute-start(bf16[64,1024]{1,0:T(8,128)(2,1)S(1)} %get-tuple-element.42.grad0.refs_4_), channel_id=1, source_target_pairs={{0,2},{1,3},{2,0},{3,1},{4,6},{5,7},{6,4},{7,5},{8,10},{9,11},{10,... | collective-permute-start | bytes 393224 | tf_op jit(solution)/shard_map/ppermute | solution.py:312
  46.9 9.0 %collective-permute-start.15 = (bf16[64,1024]{1,0:T(8,128)(2,1)S(1)}, bf16[64,1024]{1,0:T(8,128)(2,1)S(1)}, u32[]{:S(2)}, u32[]{:S(2)}) collective-permute-start(bf16[64,1024]{1,0:T(8,128)(2,1)S(1)} %get-tuple-element.42.grad0.refs_4_), channel_id=1, source_target_pairs={{0,1},{1,2},{2,3},{3,0},{4,5},{5,6},{6,7},{7,4},{8,9},{9,10},{10,1... | collective-permute-start | bytes 393224 | tf_op jit(solution)/shard_map/ppermute | solution.py:312
  58.2 2.9 %collective-permute-start.18 = (bf16[14,4,32,128]{3,2,1,0:T(8,128)(2,1)S(1)}, bf16[14,4,32,128]{3,2,1,0:T(8,128)(2,1)S(1)}, u32[]{:S(2)}, u32[]{:S(2)}) collective-permute-start(bf16[14,4,32,128]{3,2,1,0:T(8,128)(2,1)S(1)} %get-tuple-element.44), channel_id=1, source_target_pairs={{0,4},{4,0},{8,12},{12,8},{16,20},{20,16},{24,28},{28,24},{32,36},... | collective-permute-start | bytes 1376264 | tf_op jit(solution)/shard_map/ppermute | solution.py:322
  62.0 20.3 %all-to-all-start.1 = ((bf16[64,32,128]{2,1,0:T(8,128)(2,1)}), bf16[64,32,128]{2,1,0:T(8,128)(2,1)S(1)}, u32[]{:S(2)}, u32[]{:S(2)}) async-start(bf16[64,32,128]{2,1,0:T(8,128)(2,1)} %bitcast.2), calls=%async_computation.1 | async-start | bytes 1048576 | tf_op jit(solution)/shard_map/all_to_all | solution.py:416
  76.1 1.9 %collective-permute-start.19 = (bf16[16,64,128]{2,1,0:T(8,128)(2,1)S(1)}, bf16[16,64,128]{2,1,0:T(8,128)(2,1)S(1)}, u32[]{:S(2)}, u32[]{:S(2)}) collective-permute-start(bf16[16,64,128]{2,1,0:T(8,128)(2,1)S(1)} %get-tuple-element.47), channel_id=1, source_target_pairs={{0,4},{4,0},{8,12},{12,8},{16,20},{20,16},{24,28},{28,24},{32,36},... | collective-permute-start | bytes 786440 | tf_op jit(solution)/shard_map/ppermute | solution.py:322
  82.3 21.4 %copy-start.4 = (s32[1,32]{1,0:T(1,128)S(1)}, s32[1,32]{1,0:T(1,128)}, u32[]{:S(2)}) copy-start(s32[1,32]{1,0:T(1,128)} %send_block.1) | copy-start | bytes 388
  82.3 21.4 %copy-start.5 = (s32[1,32]{1,0:T(1,128)S(1)}, s32[1,32]{1,0:T(1,128)}, u32[]{:S(2)}) copy-start(s32[1,32]{1,0:T(1,128)} %send_count.1) | copy-start | bytes 388
  100.7 5.2 %collective-permute-start.20 = (bf16[16,8,32,128]{3,2,1,0:T(8,128)(2,1)S(1)}, bf16[16,8,32,128]{3,2,1,0:T(8,128)(2,1)S(1)}, u32[]{:S(2)}, u32[]{:S(2)}) collective-permute-start(bf16[16,8,32,128]{3,2,1,0:T(8,128)(2,1)S(1)} %all_to_all.15.mixed.mine), channel_id=1, source_target_pairs={{0,4},{4,0},{8,12},{12,8},{16,20},{20,16},{24,28},{28,24},{32,36},... | collective-permute-start | bytes 3145736 | tf_op jit(solution)/shard_map/ppermute | solution.py:322

commit v11 on v10

--- a/solution.py
+++ b/solution.py
@@ -16,10 +16,10 @@
 F32 = jnp.float32
 
 
-def call(kernel, name, outs, kinds, scratch=(), flops=0, size=0, limit=24 << 20):
+def call(kernel, name, outs, kinds, scratch=(), flops=0, size=0, limit=24 << 20, space_out=pltpu.VMEM):
     space = {"s": pltpu.SMEM, "v": pltpu.VMEM, "a": pl.ANY, "h": pltpu.HBM}
     many = isinstance(outs, (list, tuple))
-    spec = pl.BlockSpec(memory_space=pltpu.VMEM)
+    spec = pl.BlockSpec(memory_space=space_out)
     return pl.pallas_call(
         kernel,
         name=name,
@@ -42,7 +42,7 @@
     return pl.ds(pl.multiple_of(index * BLOCK, BLOCK), BLOCK)
 
 
-def pack_kernel(block_hbm, count_hbm, features_hbm, outgoing, send_block, send_count, features, sems):
+def pack_kernel(block_hbm, count_hbm, features_hbm, out_hbm, send_block, send_count, features, outgoing, sems, out_sems):
     copies = [
         pltpu.make_async_copy(block_hbm, send_block, sems.at[0]),
         pltpu.make_async_copy(count_hbm, send_count, sems.at[1]),
@@ -52,9 +52,18 @@
         copy.start()
     for copy in copies:
         copy.wait()
-    for peer in range(outgoing.shape[0]):
-        block = features[:, columns(send_block[0, peer])]
-        outgoing[peer] = block * send_count[0, peer].astype(F32).astype(BF)
+    groups = out_sems.shape[0]
+    size = outgoing.shape[0] // groups
+    sent = []
+    for group in range(groups):
+        for peer in range(group * size, (group + 1) * size):
+            block = features[:, columns(send_block[0, peer])]
+            outgoing[peer] = block * send_count[0, peer].astype(F32).astype(BF)
+        part = pl.ds(group * size, size)
+        sent.append(pltpu.make_async_copy(outgoing.at[part], out_hbm.at[part], out_sems.at[group]))
+        sent[-1].start()
+    for copy in sent:
+        copy.wait()
 
 
 def split_kernel(place, core, conv_weight, coarse_weight, own, sent1, sent2, sent3):
@@ -340,10 +349,13 @@
             pltpu.SMEM((1, n_morton), jnp.int32),
             pltpu.SMEM((1, n_morton), jnp.int32),
             pltpu.VMEM((quarter, row_count), BF),
+            pltpu.VMEM((n_morton, quarter, BLOCK), BF),
             pltpu.SemaphoreType.DMA((3,)),
+            pltpu.SemaphoreType.DMA((4,)),
         ],
         size=1 << 20,
         limit=60 << 20,
+        space_out=pltpu.HBM,
     )(send_block, send_count, features)
     incoming = lax.all_to_all(outgoing, "morton", 0, 0, tiled=True)
 
@@ -453,7 +465,7 @@
         [shape((OFFSETS, quarter, channels), F32), shape((quarter, channels), F32)],
         "svv",
         size=3 << 20,
-    )(core, mine, swap_cores(mine))
+    )(core, mine, swap_cores(mine[:, :4]))
     return output, input_grad, conv_grad, coarse_grad
 
 

time: 108 us -> 107 us (level)
  transfers between devices with their start and end apart: 23 -> 23, of which waited for: 13 -> 12; matrix products, arithmetic and copies ran while one was open for 0% -> 0% of each run, Pallas kernels for 10% -> 11%
where the time goes in v11:
time: 107 us
  starting transfers between devices  38.4 us (36%)
  waiting for transfers between devices  27.6 us (26%)
  Pallas kernels  21.4 us (20%)
  blocking collectives  18.3 us (17%)
    all_to_all x1, blocking collectives, local_step(): lax.all_to_all(mixed, 'morton', 0, 0, axis_index_groups=same_core, tiled=...  18.3 us
    ppermute x12, waiting for transfers between devices, shift(): lax.ppermute(value, 'chan', [(i, (i + step) % size) for i in range(size)])  13.7 us
    ppermute x12, starting transfers between devices, shift(): lax.ppermute(value, 'chan', [(i, (i + step) % size) for i in range(size)])  8.96 us
    all_to_all x1, starting transfers between devices, local_step(): incoming = lax.all_to_all(outgoing, 'morton', 0, 0, tiled=True)  8.6 us
    all_to_all x1, starting transfers between devices, local_step(): lax.all_to_all(parts.reshape((4 * chips,) + piece[1:]), ('morton', 'chan'...  8.02 us
    ppermute x6, starting transfers between devices, swap_cores(): return lax.ppermute(value, 'morton', [(i, i ^ 1) for i in range(size)])  7.81 us
    ppermute x3, waiting for transfers between devices, exchange(): return lax.ppermute(value, 'chan', [(i, i ^ step) for i in range(size)])  6.18 us
    pallas_call x1, Pallas kernels, local_step(): call(table_kernel, 'table_grad', [shape(wide, F32), shape(blocks, BF), sh...  5.79 us
  transfers between devices with their start and end apart: 23, of which 12 were waited for; matrix products, arithmetic and copies ran while one was open for 0% of the time, Pallas kernels for 11%

profile of v11, /device:TPU:1, one launch (start us, length us, event | category | flops | bytes accessed | tf_op | source)
XLA Modules:
  0.0 106.7 jit_solution(1372427660763641251)
XLA Ops:
  0.7 1.9 %pack.1 = bf16[32,64,128]{2,1,0:T(8,128)(2,1)} custom-call(s32[1,32]{1,0:T(1,128)} %send_block.1, s32[1,32]{1,0:T(1,128)} %send_count.1, bf16[64,2048]{1,0:T(8,128)(2,1)} %features.5), custom_call_target="tpu_custom_call" | custom-call | bytes 1048576 | tf_op jit(solution)/shard_map/pack/pallas_call | solution.py:346
  2.6 8.6 %all-to-all-start = ((bf16[32,64,128]{2,1,0:T(8,128)(2,1)}), bf16[32,64,128]{2,1,0:T(8,128)(2,1)S(1)}, u32[]{:S(2)}, u32[]{:S(2)}) async-start(bf16[32,64,128]{2,1,0:T(8,128)(2,1)} %pack.1), calls=%async_computation | async-start | bytes 1048576 | tf_op jit(solution)/shard_map/all_to_all | solution.py:360
  11.2 0.3 split.1
  11.6 1.7 %collective-permute-start = (bf16[7,64,128]{2,1,0:T(8,128)(2,1)S(1)}, bf16[7,64,128]{2,1,0:T(8,128)(2,1)S(1)}, u32[]{:S(2)}, u32[]{:S(2)}) collective-permute-start(bf16[7,64,128]{2,1,0:T(8,128)(2,1)S(1)} %get-tuple-element.28), channel_id=1, source_target_pairs={{0,1},{1,0},{2,3},{3,2},{4,5},{5,4},{6,7},{7,6},{8,9},{9,8},{10,11... | collective-permute-start | bytes 344072 | tf_op jit(solution)/shard_map/ppermute | solution.py:326
  13.3 3.3 %collective-permute-start.1 = (bf16[7,64,128]{2,1,0:T(8,128)(2,1)S(1)}, bf16[7,64,128]{2,1,0:T(8,128)(2,1)S(1)}, u32[]{:S(2)}, u32[]{:S(2)}) collective-permute-start(bf16[7,64,128]{2,1,0:T(8,128)(2,1)S(1)} %get-tuple-element.29), channel_id=1, source_target_pairs={{0,2},{1,3},{2,0},{3,1},{4,6},{5,7},{6,4},{7,5},{8,10},{9,11},{10,... | collective-permute-start | bytes 344072 | tf_op jit(solution)/shard_map/ppermute | solution.py:326
  16.6 0.8 collective-permute-start.3
  17.4 4.7 %collective-permute-done.1.refs_2_ = bf16[7,64,128]{2,1,0:T(8,128)(2,1)S(1)} collective-permute-done((bf16[7,64,128]{2,1,0:T(8,128)(2,1)S(1)}, bf16[7,64,128]{2,1,0:T(8,128)(2,1)S(1)}, u32[]{:S(2)}, u32[]{:S(2)}) %collective-permute-start.1) | collective-permute-done | bytes 114720 | tf_op jit(solution)/shard_map/ppermute | solution.py:326
  22.1 1.1 %collective-permute-start.4 = (bf16[7,64,128]{2,1,0:T(8,128)(2,1)S(1)}, bf16[7,64,128]{2,1,0:T(8,128)(2,1)S(1)}, u32[]{:S(2)}, u32[]{:S(2)}) collective-permute-start(bf16[7,64,128]{2,1,0:T(8,128)(2,1)S(1)} %collective-permute-done.1.refs_2_), channel_id=1, source_target_pairs={{0,4},{4,0},{8,12},{12,8},{16,20},{20,16},{24,28},{28,24},{32,36},... | collective-permute-start | bytes 344072 | tf_op jit(solution)/shard_map/ppermute | solution.py:331
  23.2 1.4 %collective-permute-done.2.refs_3_ = bf16[7,64,128]{2,1,0:T(8,128)(2,1)S(1)} collective-permute-done((bf16[7,64,128]{2,1,0:T(8,128)(2,1)S(1)}, bf16[7,64,128]{2,1,0:T(8,128)(2,1)S(1)}, u32[]{:S(2)}, u32[]{:S(2)}) %collective-permute-start.2) | collective-permute-done | bytes 114720 | tf_op jit(solution)/shard_map/ppermute | solution.py:326
  24.7 0.7 collective-permute-start.5
  25.4 0.1 copy.11.neighbour
  25.5 0.9 collective-permute-done.5.refs_6_
  26.4 3.5 %forward.1 = (f32[64,1024]{1,0:T(8,128)S(1)}, bf16[64,1024]{1,0:T(8,128)(2,1)S(1)}, bf16[64,1024]{1,0:T(8,128)(2,1)S(1)}, bf16[64,1024]{1,0:T(8,128)(2,1)S(1)}, ...) custom-call(s32[1]{0:T(128)} %bitcast.place, ...), custom_call_target="tpu_custom_call" | custom-call | flops 1879048192 | bytes 3145728 | tf_op jit(solution)/shard_map/forward/pallas_call | solution.py:377
  29.9 0.2 collective-permute-start.9
  30.1 0.4 collective-permute-start.10
  30.5 0.9 collective-permute-start.11
  31.4 2.4 %collective-permute-start.6 = (bf16[64,1024]{1,0:T(8,128)(2,1)S(1)}, bf16[64,1024]{1,0:T(8,128)(2,1)S(1)}, u32[]{:S(2)}, u32[]{:S(2)}) collective-permute-start(bf16[64,1024]{1,0:T(8,128)(2,1)S(1)} %get-tuple-element.32), channel_id=1, source_target_pairs={{0,3},{1,0},{2,1},{3,2},{4,7},{5,4},{6,5},{7,6},{8,11},{9,8},{10,9... | collective-permute-start | bytes 393224 | tf_op jit(solution)/shard_map/ppermute | solution.py:321
  33.8 1.2 %collective-permute-start.7 = (bf16[64,1024]{1,0:T(8,128)(2,1)S(1)}, bf16[64,1024]{1,0:T(8,128)(2,1)S(1)}, u32[]{:S(2)}, u32[]{:S(2)}) collective-permute-start(bf16[64,1024]{1,0:T(8,128)(2,1)S(1)} %get-tuple-element.33), channel_id=1, source_target_pairs={{0,2},{1,3},{2,0},{3,1},{4,6},{5,7},{6,4},{7,5},{8,10},{9,11},{10,... | collective-permute-start | bytes 393224 | tf_op jit(solution)/shard_map/ppermute | solution.py:321
  35.0 0.9 collective-permute-start.8
  35.9 0.1 collective-permute-done.10.part2
  35.9 4.8 %collective-permute-done.11.part3 = bf16[64,1024]{1,0:T(8,128)(2,1)S(1)} collective-permute-done((bf16[64,1024]{1,0:T(8,128)(2,1)S(1)}, bf16[64,1024]{1,0:T(8,128)(2,1)S(1)}, u32[]{:S(2)}, u32[]{:S(2)}) %collective-permute-start.11) | collective-permute-done | bytes 131104 | tf_op jit(solution)/shard_map/ppermute | solution.py:321
  40.7 0.2 activation0.1
  40.9 0.1 collective-permute-start.14
  41.0 0.1 collective-permute-start.13
  41.1 1.4 %collective-permute-start.12 = (bf16[64,1024]{1,0:T(8,128)(2,1)S(1)}, bf16[64,1024]{1,0:T(8,128)(2,1)S(1)}, u32[]{:S(2)}, u32[]{:S(2)}) collective-permute-start(bf16[64,1024]{1,0:T(8,128)(2,1)S(1)} %get-tuple-element.41.refs_7_.grad0.refs_0_), channel_id=1, source_target_pairs={{0,1},{1,2},{2,3},{3,0},{4,5},{5,6},{6,7},{7,4},{8,9},{9,10},{10,1... | collective-permute-start | bytes 393224 | tf_op jit(solution)/shard_map/ppermute | solution.py:321
  42.4 3.2 %collective-permute-done.8.part3 = bf16[64,1024]{1,0:T(8,128)(2,1)S(1)} collective-permute-done((bf16[64,1024]{1,0:T(8,128)(2,1)S(1)}, bf16[64,1024]{1,0:T(8,128)(2,1)S(1)}, u32[]{:S(2)}, u32[]{:S(2)}) %collective-permute-start.8) | collective-permute-done | bytes 131104 | tf_op jit(solution)/shard_map/ppermute | solution.py:321
  45.6 0.8 activation8.1
  46.5 0.4 collective-permute-start.16
  46.8 1.1 %collective-permute-start.15 = (bf16[64,1024]{1,0:T(8,128)(2,1)S(1)}, bf16[64,1024]{1,0:T(8,128)(2,1)S(1)}, u32[]{:S(2)}, u32[]{:S(2)}) collective-permute-start(bf16[64,1024]{1,0:T(8,128)(2,1)S(1)} %get-tuple-element.42.grad0.refs_4_), channel_id=1, source_target_pairs={{0,1},{1,2},{2,3},{3,0},{4,5},{5,6},{6,7},{7,4},{8,9},{9,10},{10,1... | collective-permute-start | bytes 393224 | tf_op jit(solution)/shard_map/ppermute | solution.py:321
  47.9 2.2 %collective-permute-done.12.grad1.refs_1_ = bf16[64,1024]{1,0:T(8,128)(2,1)S(1)} collective-permute-done((bf16[64,1024]{1,0:T(8,128)(2,1)S(1)}, bf16[64,1024]{1,0:T(8,128)(2,1)S(1)}, u32[]{:S(2)}, u32[]{:S(2)}) %collective-permute-start.12) | collective-permute-done | bytes 131104 | tf_op jit(solution)/shard_map/ppermute | solution.py:321
  50.2 2.2 %weight_grad0.1.held = f32[1792,256]{1,0:T(8,128)S(1)} custom-call(s32[27,16]{1,0:T(8,128)S(1)} %copy.11.neighbour, bf16[64,2048]{1,0:T(8,128)(2,1)S(1)} %copy-done.2, bf16[32,64,128]{2,1,0:T(8,128)(2,1)S(1)} %all-to-all-done.incoming, bf16[64,1024]{1,0:T(8,128)(2,1)S(1)} %get-tuple-element.41.refs_7_.grad0.refs_0_, ...), custom_call_target="tpu_custom_call" | custom-call | flops 939524096 | bytes 4194304 | tf_op jit(solution)/shard_map/weight_grad0/pallas_call | solution.py:410
  52.4 0.2 collective-permute-done.16.grad2.refs_6_
  52.6 3.2 %collective-permute-done.15.grad1.refs_5_ = bf16[64,1024]{1,0:T(8,128)(2,1)S(1)} collective-permute-done((bf16[64,1024]{1,0:T(8,128)(2,1)S(1)}, bf16[64,1024]{1,0:T(8,128)(2,1)S(1)}, u32[]{:S(2)}, u32[]{:S(2)}) %collective-permute-start.15) | collective-permute-done | bytes 131104 | tf_op jit(solution)/shard_map/ppermute | solution.py:321
  55.9 2.3 %weight_grad8.1 = (f32[14,4,32,128]{3,2,1,0:T(8,128)S(1)}, bf16[14,4,32,128]{3,2,1,0:T(8,128)(2,1)S(1)}) custom-call(s32[1]{0:T(128)} %bitcast.1.core, s32[27,16]{1,0:T(8,128)S(1)} %copy.11.neighbour, bf16[64,2048]{1,0:T(8,128)(2,1)S(1)} %copy-done.2, bf16[32,64,128]{2,1,0:T(8,128)(2,1)S(1)} %all-to-all-done.incoming, ...), custom_call_target="tpu_custom_call" | custom-call | flops 939524096 | bytes 4194304 | tf_op jit(solution)/shard_map/weight_grad8/pallas_call | solution.py:410
  58.2 1.4 %collective-permute-start.18 = (bf16[14,4,32,128]{3,2,1,0:T(8,128)(2,1)S(1)}, bf16[14,4,32,128]{3,2,1,0:T(8,128)(2,1)S(1)}, u32[]{:S(2)}, u32[]{:S(2)}) collective-permute-start(bf16[14,4,32,128]{3,2,1,0:T(8,128)(2,1)S(1)} %get-tuple-element.44), channel_id=1, source_target_pairs={{0,4},{4,0},{8,12},{12,8},{16,20},{20,16},{24,28},{28,24},{32,36},... | collective-permute-start | bytes 1376264 | tf_op jit(solution)/shard_map/ppermute | solution.py:331
  59.6 1.4 %collective-permute-done.18.arrived = bf16[14,4,32,128]{3,2,1,0:T(8,128)(2,1)S(1)} collective-permute-done((bf16[14,4,32,128]{3,2,1,0:T(8,128)(2,1)S(1)}, bf16[14,4,32,128]{3,2,1,0:T(8,128)(2,1)S(1)}, u32[]{:S(2)}, u32[]{:S(2)}) %collective-permute-start.18) | collective-permute-done | bytes 458784 | tf_op jit(solution)/shard_map/ppermute | solution.py:331
  61.1 0.9 pair_sum.1.refs_8_
  61.9 8.0 %all-to-all-start.1 = ((bf16[64,32,128]{2,1,0:T(8,128)(2,1)}), bf16[64,32,128]{2,1,0:T(8,128)(2,1)S(1)}, u32[]{:S(2)}, u32[]{:S(2)}) async-start(bf16[64,32,128]{2,1,0:T(8,128)(2,1)} %bitcast.2), calls=%async_computation.1 | async-start | bytes 1048576 | tf_op jit(solution)/shard_map/all_to_all | solution.py:428
  70.0 0.3 join.1.weight_t
  70.3 5.8 %table_grad.1 = (f32[64,2048]{1,0:T(8,128)S(1)}, bf16[16,64,128]{2,1,0:T(8,128)(2,1)S(1)}, bf16[16,64,128]{2,1,0:T(8,128)(2,1)S(1)}) custom-call(s32[1]{0:T(128)} %bitcast.1.core, s32[27,16]{1,0:T(8,128)S(1)} %copy.11.neighbour, bf16[1792,256]{1,0:T(8,128)(2,1)S(1)} %join.1.weight_t, bf16[64,1024]{1,0:T(8,128)(2,1)S(1)} %get-tuple-element.41.refs_7_.grad0.refs_0_, ...), custom_call_target="tpu_custom_call" | custom-call | flops 1879048192 | bytes 4194304 | tf_op jit(solution)/shard_map/table_grad/pallas_call | solution.py:438
  76.0 0.7 collective-permute-start.19
  76.8 1.2 %collective-permute-done.19.away = bf16[16,64,128]{2,1,0:T(8,128)(2,1)S(1)} collective-permute-done((bf16[16,64,128]{2,1,0:T(8,128)(2,1)S(1)}, bf16[16,64,128]{2,1,0:T(8,128)(2,1)S(1)}, u32[]{:S(2)}, u32[]{:S(2)}) %collective-permute-start.19) | collective-permute-done | bytes 262176 | tf_op jit(solution)/shard_map/ppermute | solution.py:331
  77.9 4.2 %all-to-all-done.1 = bf16[64,32,128]{2,1,0:T(8,128)(2,1)S(1)} async-done(((bf16[64,32,128]{2,1,0:T(8,128)(2,1)}), bf16[64,32,128]{2,1,0:T(8,128)(2,1)S(1)}, u32[]{:S(2)}, u32[]{:S(2)}) %all-to-all-start.1) | async-done | bytes 524320 | tf_op jit(solution)/shard_map/all_to_all | solution.py:428
  82.2 0.2 sum_parts.1
  82.4 18.3 %all_to_all.15.mixed.mine = bf16[16,8,32,128]{3,2,1,0:T(8,128)(2,1)S(1)} all-to-all(bf16[16,8,32,128]{3,2,1,0:T(8,128)(2,1)S(1)} %sum_parts.1), channel_id=1, replica_groups={{0,8,16,24,32,40,48,56,64,72,80,88,96,104,112,120},{4,12,20,28,36,44,52..., dimensions={0} | all-to-all | bytes 2097152 | tf_op jit(solution)/shard_map/all_to_all | solution.py:458
  100.7 3.0 %collective-permute-start.20 = (bf16[16,4,32,128]{3,2,1,0:T(8,128)(2,1)S(1)}, bf16[16,4,32,128]{3,2,1,0:T(8,128)(2,1)S(1)}, u32[]{:S(2)}, u32[]{:S(2)}) collective-permute-start(bf16[16,4,32,128]{3,2,1,0:T(8,128)(2,1)S(1)} %slice.4), channel_id=1, source_target_pairs={{0,4},{4,0},{8,12},{12,8},{16,20},{20,16},{24,28},{28,24},{32,36},... | collective-permute-start | bytes 1572872 | tf_op jit(solution)/shard_map/ppermute | solution.py:331
  103.7 1.6 %return_add.1 = f32[64,2048]{1,0:T(8,128)} custom-call(s32[1]{0:T(128)} %bitcast.1.core, s32[1,32]{1,0:T(1,128)S(1)} %copy-done.4, s32[1,32]{1,0:T(1,128)S(1)} %copy-done.5, f32[64,2048]{1,0:T(8,128)S(1)} %get-tuple-element.45.local, bf16[16,8,32,128]{3,2,1,0:T(8,128)(2,1)S(1)} %all_to_all.15.mixed.mine), custom_call_target="tpu_custom_call" | custom-call | bytes 2097152 | tf_op jit(solution)/shard_map/return_add/pallas_call | solution.py:459
  105.3 1.3 %unpack.1 = (f32[27,64,256]{2,1,0:T(8,128)}, f32[64,256]{1,0:T(8,128)}) custom-call(s32[1]{0:T(128)} %bitcast.1.core, bf16[16,8,32,128]{3,2,1,0:T(8,128)(2,1)S(1)} %all_to_all.15.mixed.mine, bf16[16,4,32,128]{3,2,1,0:T(8,128)(2,1)S(1)} %collective-permute-done.20.other), custom_call_target="tpu_custom_call" | custom-call | bytes 3145728 | tf_op jit(solution)/shard_map/unpack/pallas_call | solution.py:462
  (28 shorter events, 0.1 us)
Async XLA Ops:
  0.6 25.7 %copy-start.2 = (bf16[64,2048]{1,0:T(8,128)(2,1)S(1)}, bf16[64,2048]{1,0:T(8,128)(2,1)}, u32[]{:S(2)}) copy-start(bf16[64,2048]{1,0:T(8,128)(2,1)} %features.5) | copy-start | bytes 786436
  0.6 10.6 %copy-start.3 = (bf16[64,256]{1,0:T(8,128)(2,1)S(1)}, bf16[64,256]{1,0:T(8,128)(2,1)}, u32[]{:S(2)}) copy-start(bf16[64,256]{1,0:T(8,128)(2,1)} %coarse_weight.1) | copy-start | bytes 98308
  0.7 10.6 %copy-start.1 = (bf16[27,64,256]{2,1,0:T(8,128)(2,1)S(1)}, bf16[27,64,256]{2,1,0:T(8,128)(2,1)}, u32[]{:S(2)}) copy-start(bf16[27,64,256]{2,1,0:T(8,128)(2,1)} %conv_weight.1) | copy-start | bytes 2654212
  0.7 24.7 %copy-start.6 = (s32[27,16]{0,1:T(8,128)S(1)}, s32[27,16]{0,1:T(8,128)}, u32[]{:S(2)}) copy-start(s32[27,16]{0,1:T(8,128)} %param.13) | copy-start | bytes 5188
  2.6 23.7 %all-to-all-start = ((bf16[32,64,128]{2,1,0:T(8,128)(2,1)}), bf16[32,64,128]{2,1,0:T(8,128)(2,1)S(1)}, u32[]{:S(2)}, u32[]{:S(2)}) async-start(bf16[32,64,128]{2,1,0:T(8,128)(2,1)} %pack.1), calls=%async_computation | async-start | bytes 1048576 | tf_op jit(solution)/shard_map/all_to_all | solution.py:360
  11.6 5.0 %collective-permute-start = (bf16[7,64,128]{2,1,0:T(8,128)(2,1)S(1)}, bf16[7,64,128]{2,1,0:T(8,128)(2,1)S(1)}, u32[]{:S(2)}, u32[]{:S(2)}) collective-permute-start(bf16[7,64,128]{2,1,0:T(8,128)(2,1)S(1)} %get-tuple-element.28), channel_id=1, source_target_pairs={{0,1},{1,0},{2,3},{3,2},{4,5},{5,4},{6,7},{7,6},{8,9},{9,8},{10,11... | collective-permute-start | bytes 344072 | tf_op jit(solution)/shard_map/ppermute | solution.py:326
  13.3 8.9 %collective-permute-start.1 = (bf16[7,64,128]{2,1,0:T(8,128)(2,1)S(1)}, bf16[7,64,128]{2,1,0:T(8,128)(2,1)S(1)}, u32[]{:S(2)}, u32[]{:S(2)}) collective-permute-start(bf16[7,64,128]{2,1,0:T(8,128)(2,1)S(1)} %get-tuple-element.29), channel_id=1, source_target_pairs={{0,2},{1,3},{2,0},{3,1},{4,6},{5,7},{6,4},{7,5},{8,10},{9,11},{10,... | collective-permute-start | bytes 344072 | tf_op jit(solution)/shard_map/ppermute | solution.py:326
  16.6 8.1 %collective-permute-start.2 = (bf16[7,64,128]{2,1,0:T(8,128)(2,1)S(1)}, bf16[7,64,128]{2,1,0:T(8,128)(2,1)S(1)}, u32[]{:S(2)}, u32[]{:S(2)}) collective-permute-start(bf16[7,64,128]{2,1,0:T(8,128)(2,1)S(1)} %get-tuple-element.30), channel_id=1, source_target_pairs={{0,3},{1,2},{2,1},{3,0},{4,7},{5,6},{6,5},{7,4},{8,11},{9,10},{10,... | collective-permute-start | bytes 344072 | tf_op jit(solution)/shard_map/ppermute | solution.py:326
  16.6 8.9 %collective-permute-start.3 = (bf16[7,64,128]{2,1,0:T(8,128)(2,1)S(1)}, bf16[7,64,128]{2,1,0:T(8,128)(2,1)S(1)}, u32[]{:S(2)}, u32[]{:S(2)}) collective-permute-start(bf16[7,64,128]{2,1,0:T(8,128)(2,1)S(1)} %collective-permute-done.refs_1_), channel_id=1, source_target_pairs={{0,4},{4,0},{8,12},{12,8},{16,20},{20,16},{24,28},{28,24},{32,36},... | collective-permute-start | bytes 344072 | tf_op jit(solution)/shard_map/ppermute | solution.py:331
  22.1 3.3 %collective-permute-start.4 = (bf16[7,64,128]{2,1,0:T(8,128)(2,1)S(1)}, bf16[7,64,128]{2,1,0:T(8,128)(2,1)S(1)}, u32[]{:S(2)}, u32[]{:S(2)}) collective-permute-start(bf16[7,64,128]{2,1,0:T(8,128)(2,1)S(1)} %collective-permute-done.1.refs_2_), channel_id=1, source_target_pairs={{0,4},{4,0},{8,12},{12,8},{16,20},{20,16},{24,28},{28,24},{32,36},... | collective-permute-start | bytes 344072 | tf_op jit(solution)/shard_map/ppermute | solution.py:331
  24.7 1.7 %collective-permute-start.5 = (bf16[7,64,128]{2,1,0:T(8,128)(2,1)S(1)}, bf16[7,64,128]{2,1,0:T(8,128)(2,1)S(1)}, u32[]{:S(2)}, u32[]{:S(2)}) collective-permute-start(bf16[7,64,128]{2,1,0:T(8,128)(2,1)S(1)} %collective-permute-done.2.refs_3_), channel_id=1, source_target_pairs={{0,4},{4,0},{8,12},{12,8},{16,20},{20,16},{24,28},{28,24},{32,36},... | collective-permute-start | bytes 344072 | tf_op jit(solution)/shard_map/ppermute | solution.py:331
  26.4 14.4 %copy-start = (bf16[64,2048]{1,0:T(8,128)(2,1)S(1)}, bf16[64,2048]{1,0:T(8,128)(2,1)}, u32[]{:S(2)}) copy-start(bf16[64,2048]{1,0:T(8,128)(2,1)} %out_grad.3) | copy-start | bytes 786436
  29.9 5.1 %collective-permute-start.9 = (bf16[64,1024]{1,0:T(8,128)(2,1)S(1)}, bf16[64,1024]{1,0:T(8,128)(2,1)S(1)}, u32[]{:S(2)}, u32[]{:S(2)}) collective-permute-start(bf16[64,1024]{1,0:T(8,128)(2,1)S(1)} %get-tuple-element.36), channel_id=1, source_target_pairs={{0,3},{1,0},{2,1},{3,2},{4,7},{5,4},{6,5},{7,6},{8,11},{9,8},{10,9... | collective-permute-start | bytes 393224 | tf_op jit(solution)/shard_map/ppermute | solution.py:321
  30.1 5.8 %collective-permute-start.10 = (bf16[64,1024]{1,0:T(8,128)(2,1)S(1)}, bf16[64,1024]{1,0:T(8,128)(2,1)S(1)}, u32[]{:S(2)}, u32[]{:S(2)}) collective-permute-start(bf16[64,1024]{1,0:T(8,128)(2,1)S(1)} %get-tuple-element.37), channel_id=1, source_target_pairs={{0,2},{1,3},{2,0},{3,1},{4,6},{5,7},{6,4},{7,5},{8,10},{9,11},{10,... | collective-permute-start | bytes 393224 | tf_op jit(solution)/shard_map/ppermute | solution.py:321
  30.5 10.2 %collective-permute-start.11 = (bf16[64,1024]{1,0:T(8,128)(2,1)S(1)}, bf16[64,1024]{1,0:T(8,128)(2,1)S(1)}, u32[]{:S(2)}, u32[]{:S(2)}) collective-permute-start(bf16[64,1024]{1,0:T(8,128)(2,1)S(1)} %get-tuple-element.38), channel_id=1, source_target_pairs={{0,1},{1,2},{2,3},{3,0},{4,5},{5,6},{6,7},{7,4},{8,9},{9,10},{10,1... | collective-permute-start | bytes 393224 | tf_op jit(solution)/shard_map/ppermute | solution.py:321
  31.4 9.6 %collective-permute-start.6 = (bf16[64,1024]{1,0:T(8,128)(2,1)S(1)}, bf16[64,1024]{1,0:T(8,128)(2,1)S(1)}, u32[]{:S(2)}, u32[]{:S(2)}) collective-permute-start(bf16[64,1024]{1,0:T(8,128)(2,1)S(1)} %get-tuple-element.32), channel_id=1, source_target_pairs={{0,3},{1,0},{2,1},{3,2},{4,7},{5,4},{6,5},{7,6},{8,11},{9,8},{10,9... | collective-permute-start | bytes 393224 | tf_op jit(solution)/shard_map/ppermute | solution.py:321
  33.8 8.6 %collective-permute-start.7 = (bf16[64,1024]{1,0:T(8,128)(2,1)S(1)}, bf16[64,1024]{1,0:T(8,128)(2,1)S(1)}, u32[]{:S(2)}, u32[]{:S(2)}) collective-permute-start(bf16[64,1024]{1,0:T(8,128)(2,1)S(1)} %get-tuple-element.33), channel_id=1, source_target_pairs={{0,2},{1,3},{2,0},{3,1},{4,6},{5,7},{6,4},{7,5},{8,10},{9,11},{10,... | collective-permute-start | bytes 393224 | tf_op jit(solution)/shard_map/ppermute | solution.py:321
  35.0 10.6 %collective-permute-start.8 = (bf16[64,1024]{1,0:T(8,128)(2,1)S(1)}, bf16[64,1024]{1,0:T(8,128)(2,1)S(1)}, u32[]{:S(2)}, u32[]{:S(2)}) collective-permute-start(bf16[64,1024]{1,0:T(8,128)(2,1)S(1)} %get-tuple-element.34), channel_id=1, source_target_pairs={{0,1},{1,2},{2,3},{3,0},{4,5},{5,6},{6,7},{7,4},{8,9},{9,10},{10,1... | collective-permute-start | bytes 393224 | tf_op jit(solution)/shard_map/ppermute | solution.py:321
  40.9 6.0 %collective-permute-start.14 = (bf16[64,1024]{1,0:T(8,128)(2,1)S(1)}, bf16[64,1024]{1,0:T(8,128)(2,1)S(1)}, u32[]{:S(2)}, u32[]{:S(2)}) collective-permute-start(bf16[64,1024]{1,0:T(8,128)(2,1)S(1)} %get-tuple-element.41.refs_7_.grad0.refs_0_), channel_id=1, source_target_pairs={{0,3},{1,0},{2,1},{3,2},{4,7},{5,4},{6,5},{7,6},{8,11},{9,8},{10,9... | collective-permute-start | bytes 393224 | tf_op jit(solution)/shard_map/ppermute | solution.py:321
  41.0 7.0 %collective-permute-start.13 = (bf16[64,1024]{1,0:T(8,128)(2,1)S(1)}, bf16[64,1024]{1,0:T(8,128)(2,1)S(1)}, u32[]{:S(2)}, u32[]{:S(2)}) collective-permute-start(bf16[64,1024]{1,0:T(8,128)(2,1)S(1)} %get-tuple-element.41.refs_7_.grad0.refs_0_), channel_id=1, source_target_pairs={{0,2},{1,3},{2,0},{3,1},{4,6},{5,7},{6,4},{7,5},{8,10},{9,11},{10,... | collective-permute-start | bytes 393224 | tf_op jit(solution)/shard_map/ppermute | solution.py:321
  41.1 9.1 %collective-permute-start.12 = (bf16[64,1024]{1,0:T(8,128)(2,1)S(1)}, bf16[64,1024]{1,0:T(8,128)(2,1)S(1)}, u32[]{:S(2)}, u32[]{:S(2)}) collective-permute-start(bf16[64,1024]{1,0:T(8,128)(2,1)S(1)} %get-tuple-element.41.refs_7_.grad0.refs_0_), channel_id=1, source_target_pairs={{0,1},{1,2},{2,3},{3,0},{4,5},{5,6},{6,7},{7,4},{8,9},{9,10},{10,1... | collective-permute-start | bytes 393224 | tf_op jit(solution)/shard_map/ppermute | solution.py:321
  46.5 5.9 %collective-permute-start.17 = (bf16[64,1024]{1,0:T(8,128)(2,1)S(1)}, bf16[64,1024]{1,0:T(8,128)(2,1)S(1)}, u32[]{:S(2)}, u32[]{:S(2)}) collective-permute-start(bf16[64,1024]{1,0:T(8,128)(2,1)S(1)} %get-tuple-element.42.grad0.refs_4_), channel_id=1, source_target_pairs={{0,3},{1,0},{2,1},{3,2},{4,7},{5,4},{6,5},{7,6},{8,11},{9,8},{10,9... | collective-permute-start | bytes 393224 | tf_op jit(solution)/shard_map/ppermute | solution.py:321
  46.5 6.1 %collective-permute-start.16 = (bf16[64,1024]{1,0:T(8,128)(2,1)S(1)}, bf16[64,1024]{1,0:T(8,128)(2,1)S(1)}, u32[]{:S(2)}, u32[]{:S(2)}) collective-permute-start(bf16[64,1024]{1,0:T(8,128)(2,1)S(1)} %get-tuple-element.42.grad0.refs_4_), channel_id=1, source_target_pairs={{0,2},{1,3},{2,0},{3,1},{4,6},{5,7},{6,4},{7,5},{8,10},{9,11},{10,... | collective-permute-start | bytes 393224 | tf_op jit(solution)/shard_map/ppermute | solution.py:321
  46.8 9.0 %collective-permute-start.15 = (bf16[64,1024]{1,0:T(8,128)(2,1)S(1)}, bf16[64,1024]{1,0:T(8,128)(2,1)S(1)}, u32[]{:S(2)}, u32[]{:S(2)}) collective-permute-start(bf16[64,1024]{1,0:T(8,128)(2,1)S(1)} %get-tuple-element.42.grad0.refs_4_), channel_id=1, source_target_pairs={{0,1},{1,2},{2,3},{3,0},{4,5},{5,6},{6,7},{7,4},{8,9},{9,10},{10,1... | collective-permute-start | bytes 393224 | tf_op jit(solution)/shard_map/ppermute | solution.py:321
  58.2 2.9 %collective-permute-start.18 = (bf16[14,4,32,128]{3,2,1,0:T(8,128)(2,1)S(1)}, bf16[14,4,32,128]{3,2,1,0:T(8,128)(2,1)S(1)}, u32[]{:S(2)}, u32[]{:S(2)}) collective-permute-start(bf16[14,4,32,128]{3,2,1,0:T(8,128)(2,1)S(1)} %get-tuple-element.44), channel_id=1, source_target_pairs={{0,4},{4,0},{8,12},{12,8},{16,20},{20,16},{24,28},{28,24},{32,36},... | collective-permute-start | bytes 1376264 | tf_op jit(solution)/shard_map/ppermute | solution.py:331
  61.9 20.3 %all-to-all-start.1 = ((bf16[64,32,128]{2,1,0:T(8,128)(2,1)}), bf16[64,32,128]{2,1,0:T(8,128)(2,1)S(1)}, u32[]{:S(2)}, u32[]{:S(2)}) async-start(bf16[64,32,128]{2,1,0:T(8,128)(2,1)} %bitcast.2), calls=%async_computation.1 | async-start | bytes 1048576 | tf_op jit(solution)/shard_map/all_to_all | solution.py:428
  76.0 1.9 %collective-permute-start.19 = (bf16[16,64,128]{2,1,0:T(8,128)(2,1)S(1)}, bf16[16,64,128]{2,1,0:T(8,128)(2,1)S(1)}, u32[]{:S(2)}, u32[]{:S(2)}) collective-permute-start(bf16[16,64,128]{2,1,0:T(8,128)(2,1)S(1)} %get-tuple-element.47), channel_id=1, source_target_pairs={{0,4},{4,0},{8,12},{12,8},{16,20},{20,16},{24,28},{28,24},{32,36},... | collective-permute-start | bytes 786440 | tf_op jit(solution)/shard_map/ppermute | solution.py:331
  82.4 21.3 %copy-start.4 = (s32[1,32]{1,0:T(1,128)S(1)}, s32[1,32]{1,0:T(1,128)}, u32[]{:S(2)}) copy-start(s32[1,32]{1,0:T(1,128)} %send_block.1) | copy-start | bytes 388
  82.4 21.3 %copy-start.5 = (s32[1,32]{1,0:T(1,128)S(1)}, s32[1,32]{1,0:T(1,128)}, u32[]{:S(2)}) copy-start(s32[1,32]{1,0:T(1,128)} %send_count.1) | copy-start | bytes 388
  100.7 4.7 %collective-permute-start.20 = (bf16[16,4,32,128]{3,2,1,0:T(8,128)(2,1)S(1)}, bf16[16,4,32,128]{3,2,1,0:T(8,128)(2,1)S(1)}, u32[]{:S(2)}, u32[]{:S(2)}) collective-permute-start(bf16[16,4,32,128]{3,2,1,0:T(8,128)(2,1)S(1)} %slice.4), channel_id=1, source_target_pairs={{0,4},{4,0},{8,12},{12,8},{16,20},{20,16},{24,28},{28,24},{32,36},... | collective-permute-start | bytes 1572872 | tf_op jit(solution)/shard_map/ppermute | solution.py:331
